TPU v7x, 128 devices: a whole 4x4x4 slice. The times are simulated.
128 devices in a mesh: fsdp: 8 (over x, z_hi), ctx: 4 (over z_lo, core), tp: 4 (over y).
Axes of the slice: x: 4, y: 4, z: 4 (z_hi: 2, z_lo: 2; z = z_hi * 2 + z_lo), core: 2. Of those that a mesh axis runs over, the one named last changes fastest.
Arguments:
- hidden_in: bfloat16 [8192, 1536], P(('fsdp', 'ctx')), may hold values from -6 to 6
- cotangent: bfloat16 [8192, 1536], P(('fsdp', 'ctx')), may hold values from -6 to 6
- seq_lengths: int32 [32], replicated, may hold values from 1 to 1021, as said below
- deal_order: int32 [8192], replicated, may hold values from 0 to 8191, as said below
- mixer_gain: bfloat16 [1536], P(('fsdp', 'ctx')), may hold values from 0.5 to 1.5
- mixer_project: bfloat16 [1536, 3, 1536], P(('fsdp', 'ctx'), None, 'tp'), may hold values from -0.15625 to 0.15625
- mixer_kernel: bfloat16 [3, 1536], replicated, may hold values from -2.390625 to 2.390625
- mixer_output: bfloat16 [1536, 1536], P('tp', ('fsdp', 'ctx')), may hold values from -0.15625 to 0.15625
- first_gain: bfloat16 [1536], P(('fsdp', 'ctx')), may hold values from 0.5 to 1.5
- first_gateup: bfloat16 [1536, 2, 6912], P(('fsdp', 'ctx'), None, 'tp'), may hold values from -0.15625 to 0.15625
- first_down: bfloat16 [6912, 1536], P('tp', ('fsdp', 'ctx')), may hold values from -0.078125 to 0.078125
- attend_gain: bfloat16 [1536], P(('fsdp', 'ctx')), may hold values from 0.5 to 1.5
- attend_project: bfloat16 [1536, 2560], P(('fsdp', 'ctx'), 'tp'), may hold values from -0.15625 to 0.15625
- query_gain: bfloat16 [64], replicated, may hold values from 0.5 to 1.5
- key_gain: bfloat16 [64], replicated, may hold values from 0.5 to 1.5
- attend_output: bfloat16 [1536, 1536], P('tp', ('fsdp', 'ctx')), may hold values from -0.875 to 0.875
- second_gain: bfloat16 [1536], P(('fsdp', 'ctx')), may hold values from 0.5 to 1.5
- second_gateup: bfloat16 [1536, 2, 6912], P(('fsdp', 'ctx'), None, 'tp'), may hold values from -0.15625 to 0.15625
- second_down: bfloat16 [6912, 1536], P('tp', ('fsdp', 'ctx')), may hold values from -0.078125 to 0.078125
Outputs:
- layer_out: bfloat16 [8192, 1536], P(('fsdp', 'ctx'))
- input_gradient: bfloat16 [8192, 1536], P(('fsdp', 'ctx'))
- mixer_gain_gradient: float32 [1536], P(('fsdp', 'ctx'))
- mixer_project_gradient: float32 [1536, 3, 1536], P(('fsdp', 'ctx'), None, 'tp')
- mixer_kernel_gradient: float32 [3, 1536], replicated
- mixer_output_gradient: float32 [1536, 1536], P('tp', ('fsdp', 'ctx'))
- first_gain_gradient: float32 [1536], P(('fsdp', 'ctx'))
- first_gateup_gradient: float32 [1536, 2, 6912], P(('fsdp', 'ctx'), None, 'tp')
- first_down_gradient: float32 [6912, 1536], P('tp', ('fsdp', 'ctx'))
- attend_gain_gradient: float32 [1536], P(('fsdp', 'ctx'))
- attend_project_gradient: float32 [1536, 2560], P(('fsdp', 'ctx'), 'tp')
- query_gain_gradient: float32 [64], replicated
- key_gain_gradient: float32 [64], replicated
- attend_output_gradient: float32 [1536, 1536], P('tp', ('fsdp', 'ctx'))
- second_gain_gradient: float32 [1536], P(('fsdp', 'ctx'))
- second_gateup_gradient: float32 [1536, 2, 6912], P(('fsdp', 'ctx'), None, 'tp')
- second_down_gradient: float32 [6912, 1536], P('tp', ('fsdp', 'ctx'))
Inputs may be any that keep to these rules, and one draw needn't show every extreme that they name: `seq_lengths`: sequences 4 * g to 4 * g + 3 fill dealt rows g * 1024 to (g + 1) * 1024 - 1 exactly; in each such group one sequence covers all but at most 128 of its rows. deal_order is a permutation. Dealt rows come in aligned blocks of 8; each block holds 8 consecutive arrival tokens in order, starting at a multiple of 8; the 256 dealt rows of each device take exactly one block from the 256 arrival rows of every device.
All inputs are finite; a program needn't handle non-finite values.
Results may differ from a plain program's by a relative error of at most 0.02.
The roundings to bfloat16 on the way count: a program that leaves them out, or rounds other values in their place, can miss the bound.
Values may be sent and summed in bfloat16 or wider, within the bound.
No kernel may reach another device: no remote copies, remote signals or barrier semaphores. Data moves between devices by JAX's collectives and lax.ppermute only.
A program may use at most 256 MiB of HBM per device.

v0:
```python
import jax
import jax.numpy as jnp
from jax import lax
from jax.sharding import PartitionSpec as P

H = 24
KVH = 8
HD = 64


EPSILON = 1e-05
ROPE_BASE = 1000000.0
NEGATIVE = -1e30


def from_behind(block, axis, distance):
    devices = range(lax.axis_size(axis))
    route = [(i - distance, i) for i in devices if i - distance in devices]
    return lax.ppermute(block, axis, route)


def norm_rows(values, scales):
    return values * lax.rsqrt(jnp.mean(values * values, axis=-1, keepdims=True) + EPSILON) * scales


def rotate(values, places):
    half_dim = values.shape[-1] // 2
    frequency = ROPE_BASE ** (-(jnp.arange(half_dim).astype(jnp.float32) * 2.0 / values.shape[-1]))
    angles = places.astype(jnp.float32)[:, None] * frequency[None, :]
    shape_out = (values.shape[0],) + (1,) * (values.ndim - 2) + (half_dim,)
    cosine = jnp.cos(angles).reshape(shape_out)
    sine_part = jnp.sin(angles).reshape(shape_out)
    first_half = values[..., :half_dim]
    second_half = values[..., half_dim:]
    return jnp.concatenate(
        [
            first_half * cosine - second_half * sine_part,
            second_half * cosine + first_half * sine_part,
        ],
        axis=-1,
    )


def locate(lengths, positions):
    seq_ends = jnp.cumsum(lengths)
    segment = jnp.sum((positions[:, None] >= seq_ends[None, :]).astype(jnp.int32), axis=1)
    starts = seq_ends - lengths
    first_row = jnp.sum(
        jnp.where(segment[:, None] == jnp.arange(lengths.shape[0])[None, :], starts[None, :], 0),
        axis=1,
    )
    return (segment, positions - first_row)


def shortconv(extended, kernel_in, segment):
    kernel_taps = kernel_in.shape[0]
    out_rows = extended.shape[0] - kernel_taps + 1
    result = kernel_in[0] * extended[kernel_taps - 1 :]
    for t in range(1, kernel_taps):
        earlier = extended[kernel_taps - 1 - t : kernel_taps - 1 - t + out_rows]
        same_seq = (
            segment[kernel_taps - 1 - t : kernel_taps - 1 - t + out_rows]
            == segment[kernel_taps - 1 :]
        ).astype(jnp.float32)[:, None]
        result = result + kernel_in[t] * earlier * same_seq
    return result


def branch_sum(partial_rows):
    return lax.psum(partial_rows, "tp")


def input_sum(partial_rows):
    return lax.psum(partial_rows, "tp")


def fetch_layer(members):
    return (
        lax.all_gather(members[0], ("fsdp", "ctx"), axis=0, tiled=True),
        lax.all_gather(members[1], ("fsdp", "ctx"), axis=0, tiled=True),
        lax.all_gather(members[2], ("fsdp", "ctx"), axis=1, tiled=True),
        lax.all_gather(members[3], ("fsdp", "ctx"), axis=0, tiled=True),
        lax.all_gather(members[4], ("fsdp", "ctx"), axis=0, tiled=True),
        lax.all_gather(members[5], ("fsdp", "ctx"), axis=1, tiled=True),
    )


def fetch_again(members):
    return (
        lax.all_gather(members[0], ("fsdp", "ctx"), axis=0, tiled=True),
        lax.all_gather(members[1], ("fsdp", "ctx"), axis=0, tiled=True),
        lax.all_gather(members[2], ("fsdp", "ctx"), axis=1, tiled=True),
        lax.all_gather(members[3], ("fsdp", "ctx"), axis=0, tiled=True),
        lax.all_gather(members[4], ("fsdp", "ctx"), axis=0, tiled=True),
        lax.all_gather(members[5], ("fsdp", "ctx"), axis=1, tiled=True),
    )


def reduce_layer(members):
    return (
        lax.psum_scatter(members[0], ("fsdp", "ctx"), scatter_dimension=0, tiled=True),
        lax.psum_scatter(members[1], ("fsdp", "ctx"), scatter_dimension=0, tiled=True),
        lax.psum_scatter(members[2], ("fsdp", "ctx"), scatter_dimension=1, tiled=True),
        lax.psum_scatter(members[3], ("fsdp", "ctx"), scatter_dimension=0, tiled=True),
        lax.psum_scatter(members[4], ("fsdp", "ctx"), scatter_dimension=0, tiled=True),
        lax.psum_scatter(members[5], ("fsdp", "ctx"), scatter_dimension=1, tiled=True),
    )


def ffn_forward(stream, scales, gate_weight, down_proj):
    normed_in = norm_rows(stream, scales.astype(jnp.float32)).astype(jnp.bfloat16)
    gate_up = jnp.einsum("td,dwf->twf", normed_in, gate_weight, preferred_element_type=jnp.float32)
    active = (jax.nn.silu(gate_up[:, 0]) * gate_up[:, 1]).astype(jnp.bfloat16)
    result = stream + branch_sum(jnp.dot(active, down_proj, preferred_element_type=jnp.float32))
    return (result, (normed_in, gate_up, active))


def ffn_backward(stream, kept_rows, scales, gate_weight, down_proj, upward):
    normed_in, gate_up, active = kept_rows
    rounded_back = upward.astype(jnp.bfloat16)
    d_active = jnp.dot(rounded_back, down_proj.T, preferred_element_type=jnp.float32)
    down_gradient = jnp.dot(active.T, rounded_back, preferred_element_type=jnp.float32)
    unused, pullback = jax.vjp(
        lambda gate_in, up_in: jax.nn.silu(gate_in) * up_in, gate_up[:, 0], gate_up[:, 1]
    )
    d_gate, d_up = pullback(d_active)
    d_both = jnp.stack([d_gate, d_up], axis=1).astype(jnp.bfloat16)
    gateup_gradient = jnp.einsum(
        "td,twf->dwf", normed_in, d_both, preferred_element_type=jnp.float32
    )
    d_normed = input_sum(
        jnp.einsum("twf,dwf->td", d_both, gate_weight, preferred_element_type=jnp.float32)
    )
    unused, pullback = jax.vjp(norm_rows, stream, scales.astype(jnp.float32))
    d_stream, gain_gradient = pullback(d_normed)
    return (upward + d_stream, gain_gradient, gateup_gradient, down_gradient)


def body(
    hidden_in,
    cotangent,
    seq_lengths,
    deal_order,
    mixer_gain,
    mixer_project,
    mixer_kernel,
    mixer_output,
    first_gain,
    first_gateup,
    first_down,
    attend_gain,
    attend_project,
    query_gain,
    key_gain,
    attend_output,
    second_gain,
    second_gateup,
    second_down,
):
    shards = lax.axis_size(("fsdp", "ctx"))
    contexts = lax.axis_size("ctx")
    row_count, model_width = hidden_in.shape
    piece_rows = row_count // shards
    device = lax.axis_index(("fsdp", "ctx"))
    piece_table = deal_order.reshape(shards, shards, piece_rows)[:, :, 0]
    anchor = piece_table // row_count
    anchor_piece = piece_table % row_count // piece_rows
    send_piece = jnp.sum(jnp.where(anchor == device, anchor_piece, 0), axis=1)
    my_anchor = lax.dynamic_index_in_dim(anchor, device, 0, keepdims=False)
    arrived = (
        lax.all_to_all(
            hidden_in.reshape(shards, piece_rows, model_width)[send_piece],
            ("fsdp", "ctx"),
            split_axis=0,
            concat_axis=0,
            tiled=True,
        ),
        lax.all_to_all(
            cotangent.reshape(shards, piece_rows, model_width)[send_piece],
            ("fsdp", "ctx"),
            split_axis=0,
            concat_axis=0,
            tiled=True,
        ),
    )
    stream0 = arrived[0][my_anchor].reshape(row_count, model_width).astype(jnp.float32)
    upstream = arrived[1][my_anchor].reshape(row_count, model_width).astype(jnp.float32)
    kernel_taps = mixer_kernel.shape[0]
    local_rows = device * row_count + jnp.arange(row_count)
    segment, places = locate(seq_lengths, local_rows)
    halo_segment, unused = locate(
        seq_lengths, local_rows[0] - kernel_taps + 1 + jnp.arange(row_count + kernel_taps - 1)
    )
    group_rows = lax.axis_index("fsdp") * contexts * row_count + jnp.arange(contexts * row_count)
    key_segment, key_places = locate(seq_lengths, group_rows)
    allowed = (segment[:, None] == key_segment[None, :]) & (key_places[None, :] <= places[:, None])
    first_set = fetch_layer(
        (mixer_gain, mixer_project, mixer_output, first_gain, first_gateup, first_down)
    )
    gain_a, project_a, output_a, gain_f, gateup_f, down_f = first_set
    channels = output_a.shape[0]
    kernel_local = lax.dynamic_slice_in_dim(
        mixer_kernel, lax.axis_index("tp") * channels, channels, 1
    ).astype(jnp.float32)
    mixer_in = norm_rows(stream0, gain_a.astype(jnp.float32)).astype(jnp.bfloat16)
    proj_a = jnp.einsum("td,dwc->twc", mixer_in, project_a, preferred_element_type=jnp.float32)
    product = (proj_a[:, 0] * proj_a[:, 2]).astype(jnp.bfloat16)
    halo_rows = from_behind(product[row_count - kernel_taps + 1 :], "ctx", 1)
    extended = jnp.concatenate([halo_rows, product]).astype(jnp.float32)
    conv_out = shortconv(extended, kernel_local, halo_segment)
    gated_rows = (proj_a[:, 1] * conv_out).astype(jnp.bfloat16)
    stream1 = stream0 + branch_sum(
        jnp.dot(gated_rows, output_a, preferred_element_type=jnp.float32)
    )
    stream2, kept_first = ffn_forward(stream1, gain_f, gateup_f, down_f)
    second_set = fetch_layer(
        (attend_gain, attend_project, attend_output, second_gain, second_gateup, second_down)
    )
    gain_b, project_b, output_b, gain_s, gateup_s, down_s = second_set
    groups = H // KVH
    score_scale = HD ** (-0.5)
    qgain_f = query_gain.astype(jnp.float32)
    kgain_f = key_gain.astype(jnp.float32)

    def qk_maps(query_in, key_in, gain_q, gain_k):
        return (
            rotate(norm_rows(query_in, gain_q), places),
            rotate(norm_rows(key_in, gain_k), places),
        )

    attend_in = norm_rows(stream2, gain_b.astype(jnp.float32)).astype(jnp.bfloat16)
    proj_b = jnp.dot(attend_in, project_b, preferred_element_type=jnp.float32).reshape(
        row_count, -1, groups + 2, HD
    )
    query_raw = proj_b[:, :, :groups]
    key_raw = proj_b[:, :, groups]
    query_f, key_f = qk_maps(query_raw, key_raw, qgain_f, kgain_f)
    query_b = query_f.astype(jnp.bfloat16)
    key_b = key_f.astype(jnp.bfloat16)
    value_b = proj_b[:, :, groups + 1].astype(jnp.bfloat16)
    key_all, value_all = (
        lax.all_gather(key_b, "ctx", axis=0, tiled=True),
        lax.all_gather(value_b, "ctx", axis=0, tiled=True),
    )
    scores = (
        jnp.einsum("tkgd,nkd->kgtn", query_b, key_all, preferred_element_type=jnp.float32)
        * score_scale
    )
    masked = jnp.where(allowed, scores, NEGATIVE)
    row_top = jnp.max(masked, axis=-1, keepdims=True)
    exponent = jnp.exp(masked - row_top)
    row_total = jnp.sum(exponent, axis=-1, keepdims=True)
    softmax_rows = exponent / row_total
    log_total = row_top + jnp.log(row_total)
    attended = (
        jnp.einsum(
            "kgtn,nkd->tkgd",
            softmax_rows.astype(jnp.bfloat16),
            value_all,
            preferred_element_type=jnp.float32,
        )
        .astype(jnp.bfloat16)
        .reshape(row_count, -1)
    )
    stream3 = stream2 + branch_sum(jnp.dot(attended, output_b, preferred_element_type=jnp.float32))
    stream4, kept_second = ffn_forward(stream3, gain_s, gateup_s, down_s)
    second_back = fetch_again(
        (attend_gain, attend_project, attend_output, second_gain, second_gateup, second_down)
    )
    gain_b, project_b, output_b, gain_s, gateup_s, down_s = second_back
    d_stream3, gain_s_grad, gateup_s_grad, down_s_grad = ffn_backward(
        stream3, kept_second, gain_s, gateup_s, down_s, upstream
    )
    rounded_back = d_stream3.astype(jnp.bfloat16)
    d_attended = jnp.dot(rounded_back, output_b.T, preferred_element_type=jnp.float32)
    output_b_grad = jnp.dot(attended.T, rounded_back, preferred_element_type=jnp.float32)
    d_attended_b = d_attended.astype(jnp.bfloat16).reshape(row_count, -1, groups, HD)
    scores_again = (
        jnp.einsum("tkgd,nkd->kgtn", query_b, key_all, preferred_element_type=jnp.float32)
        * score_scale
    )
    probs_again = jnp.where(allowed, jnp.exp(scores_again - log_total), 0.0)
    d_probs = jnp.einsum(
        "tkgd,nkd->kgtn", d_attended_b, value_all, preferred_element_type=jnp.float32
    )
    d_values = jnp.einsum(
        "kgtn,tkgd->nkd",
        probs_again.astype(jnp.bfloat16),
        d_attended_b,
        preferred_element_type=jnp.float32,
    )
    inner_sum = jnp.sum(probs_again * d_probs, axis=-1, keepdims=True)
    d_scores = (probs_again * (d_probs - inner_sum)).astype(jnp.bfloat16)
    d_query = (
        jnp.einsum("kgtn,nkd->tkgd", d_scores, key_all, preferred_element_type=jnp.float32)
        * score_scale
    )
    d_keys = (
        jnp.einsum("kgtn,tkgd->nkd", d_scores, query_b, preferred_element_type=jnp.float32)
        * score_scale
    )
    d_key_local, d_value_local = (
        lax.psum_scatter(d_keys, "ctx", scatter_dimension=0, tiled=True),
        lax.psum_scatter(d_values, "ctx", scatter_dimension=0, tiled=True),
    )
    unused, pullback = jax.vjp(qk_maps, query_raw, key_raw, qgain_f, kgain_f)
    d_query_raw, d_key_raw, qgain_grad, kgain_grad = pullback((d_query, d_key_local))
    d_proj_b = jnp.concatenate(
        [d_query_raw, d_key_raw[:, :, None], d_value_local[:, :, None]], axis=2
    )
    d_proj_b = d_proj_b.astype(jnp.bfloat16).reshape(row_count, -1)
    project_b_grad = jnp.dot(attend_in.T, d_proj_b, preferred_element_type=jnp.float32)
    d_attend_in = input_sum(jnp.dot(d_proj_b, project_b.T, preferred_element_type=jnp.float32))
    unused, pullback = jax.vjp(norm_rows, stream2, gain_b.astype(jnp.float32))
    d_norm_b, gain_b_grad = pullback(d_attend_in)
    d_stream2 = d_stream3 + d_norm_b
    second_grads = reduce_layer(
        (gain_b_grad, project_b_grad, output_b_grad, gain_s_grad, gateup_s_grad, down_s_grad)
    )
    first_back = fetch_again(
        (mixer_gain, mixer_project, mixer_output, first_gain, first_gateup, first_down)
    )
    gain_a, project_a, output_a, gain_f, gateup_f, down_f = first_back
    d_stream1, gain_f_grad, gateup_f_grad, down_f_grad = ffn_backward(
        stream1, kept_first, gain_f, gateup_f, down_f, d_stream2
    )
    rounded_back = d_stream1.astype(jnp.bfloat16)
    d_gated = jnp.dot(rounded_back, output_a.T, preferred_element_type=jnp.float32)
    output_a_grad = jnp.dot(gated_rows.T, rounded_back, preferred_element_type=jnp.float32)
    d_cgate = d_gated * conv_out
    d_conv = d_gated * proj_a[:, 1]
    unused, pullback = jax.vjp(
        lambda ext_rows, kernel_in: shortconv(ext_rows, kernel_in, halo_segment),
        extended,
        kernel_local,
    )
    d_extended, kernel_grad = pullback(d_conv)
    returned = from_behind(d_extended[: kernel_taps - 1], "ctx", -1)
    d_product = d_extended[kernel_taps - 1 :] + jnp.concatenate(
        [jnp.zeros((row_count - kernel_taps + 1, channels), jnp.float32), returned]
    )
    d_proj_a = jnp.stack(
        [d_product * proj_a[:, 2], d_cgate, d_product * proj_a[:, 0]], axis=1
    ).astype(jnp.bfloat16)
    project_a_grad = jnp.einsum(
        "td,twc->dwc", mixer_in, d_proj_a, preferred_element_type=jnp.float32
    )
    d_mixer_in = input_sum(
        jnp.einsum("twc,dwc->td", d_proj_a, project_a, preferred_element_type=jnp.float32)
    )
    unused, pullback = jax.vjp(norm_rows, stream0, gain_a.astype(jnp.float32))
    d_norm_a, gain_a_grad = pullback(d_mixer_in)
    d_stream0 = d_stream1 + d_norm_a
    first_grads = reduce_layer(
        (gain_a_grad, project_a_grad, output_a_grad, gain_f_grad, gateup_f_grad, down_f_grad)
    )
    kernel_full = lax.dynamic_update_slice_in_dim(
        jnp.zeros(mixer_kernel.shape, jnp.float32), kernel_grad, lax.axis_index("tp") * channels, 1
    )
    kernel_total, qgain_total, kgain_total = lax.psum(
        (kernel_full, qgain_grad, kgain_grad), ("fsdp", "ctx", "tp")
    )
    slot_for_anchor = jnp.sum(
        jnp.where(
            my_anchor[None, :] == jnp.arange(shards)[:, None], jnp.arange(shards)[None, :], 0
        ),
        axis=1,
    )
    dest_for_piece = jnp.sum(
        jnp.where(
            send_piece[None, :] == jnp.arange(shards)[:, None], jnp.arange(shards)[None, :], 0
        ),
        axis=1,
    )
    out_rows = stream4.astype(jnp.bfloat16).reshape(shards, piece_rows, model_width)[
        slot_for_anchor
    ]
    grad_rows = d_stream0.astype(jnp.bfloat16).reshape(shards, piece_rows, model_width)[
        slot_for_anchor
    ]
    homeward = (
        lax.all_to_all(out_rows, ("fsdp", "ctx"), split_axis=0, concat_axis=0, tiled=True),
        lax.all_to_all(grad_rows, ("fsdp", "ctx"), split_axis=0, concat_axis=0, tiled=True),
    )
    layer_out = homeward[0][dest_for_piece].reshape(row_count, model_width)
    input_gradient = homeward[1][dest_for_piece].reshape(row_count, model_width)
    return (
        layer_out,
        input_gradient,
        first_grads[0],
        first_grads[1],
        kernel_total,
        first_grads[2],
        first_grads[3],
        first_grads[4],
        first_grads[5],
        second_grads[0],
        second_grads[1],
        qgain_total,
        kgain_total,
        second_grads[2],
        second_grads[3],
        second_grads[4],
        second_grads[5],
    )


def solution(mesh):
    return jax.shard_map(
        body,
        mesh=mesh,
        in_specs=(
            P(("fsdp", "ctx"), None),
            P(("fsdp", "ctx"), None),
            P(),
            P(),
            P(("fsdp", "ctx")),
            P(("fsdp", "ctx"), None, "tp"),
            P(),
            P("tp", ("fsdp", "ctx")),
            P(("fsdp", "ctx")),
            P(("fsdp", "ctx"), None, "tp"),
            P("tp", ("fsdp", "ctx")),
            P(("fsdp", "ctx")),
            P(("fsdp", "ctx"), "tp"),
            P(),
            P(),
            P("tp", ("fsdp", "ctx")),
            P(("fsdp", "ctx")),
            P(("fsdp", "ctx"), None, "tp"),
            P("tp", ("fsdp", "ctx")),
        ),
        out_specs=(
            P(("fsdp", "ctx"), None),
            P(("fsdp", "ctx"), None),
            P(("fsdp", "ctx")),
            P(("fsdp", "ctx"), None, "tp"),
            P(),
            P("tp", ("fsdp", "ctx")),
            P(("fsdp", "ctx")),
            P(("fsdp", "ctx"), None, "tp"),
            P("tp", ("fsdp", "ctx")),
            P(("fsdp", "ctx")),
            P(("fsdp", "ctx"), "tp"),
            P(),
            P(),
            P("tp", ("fsdp", "ctx")),
            P(("fsdp", "ctx")),
            P(("fsdp", "ctx"), None, "tp"),
            P("tp", ("fsdp", "ctx")),
        ),
        check_vma=False,
    )
```

profile of v0, /device:TPU:1, one launch (start us, length us, event | category | flops | bytes accessed | tf_op | source)
XLA Modules:
  0.0 1805.0 jit_solution(18318523663704563732)
XLA Ops:
  11.8 9.4 all-to-all-start
  24.4 123.8 %all-reduce.22 = (bf16[1536]{0:T(1024)(128)(2,1)S(1)}, bf16[1536]{0:T(1024)(128)(2,1)S(1)}, bf16[1536]{0:T(1024)(128)(2,1)S(1)}, bf16[1536]{0:T(1024)(128)(2,1)}) all-reduce(bf16[1536]{0:T(1024)(128)(2,1)S(1)} %dynamic-update-slice, bf16[1536]{0:T(1024)(128)(2,1)S(1)} %dynamic-update-slice.1, ...), channel_id=1, replica_groups=mesh['fsdp'=8,'ctx'=4,'tp'=4] {'fsdp','ctx'}, use_global_device_ids=true, to_apply=%add.11 | all-reduce | flops 6144 | bytes 24576
  168.1 44.8 %all-reduce.31.cloned.1.call-done = f32[256,1536]{1,0:T(8,128)} async-done(((f32[256,1536]{1,0:T(8,128)}), f32[256,1536]{1,0:T(8,128)}) %all-reduce.31.cloned.1.call-update) | async-done | bytes 1572880 | tf_op jit(solution)/shard_map/psum | solution.py:70
  214.7 60.9 %all-gather.14.cloned.1.call-done = bf16[1536,2,1728]{2,0,1:T(8,128)(2,1)} async-done(((bf16[48,2,1728]{2,0,1:T(8,128)(2,1)}), bf16[1536,2,1728]{2,0,1:T(8,128)(2,1)}) %all-gather.14.cloned.1.call-update) | async-done | bytes 10616848 | tf_op jit(solution)/shard_map/all_gather | solution.py:83
  275.6 7.3 fusion.100
  286.4 38.8 %all-gather.16.cloned.1.call-done = bf16[1728,1536]{0,1:T(8,128)(2,1)} async-done(((bf16[1728,48]{0,1:T(8,128)(2,1)}), bf16[1728,1536]{0,1:T(8,128)(2,1)}) %all-gather.16.cloned.1.call-update) | async-done | bytes 5308432 | tf_op jit(solution)/shard_map/all_gather | solution.py:84
  325.2 5.7 fusion.141
  334.3 45.8 %all-reduce.33.cloned.1.call-done = f32[256,1536]{1,0:T(8,128)} async-done(((f32[256,1536]{1,0:T(8,128)}), f32[256,1536]{1,0:T(8,128)}) %all-reduce.33.cloned.1.call-update) | async-done | bytes 1572880 | tf_op jit(solution)/shard_map/psum | solution.py:70
  382.2 44.5 %all-gather.18.cloned.1.call-done = bf16[1536,640]{1,0:T(8,128)(2,1)} async-done(((bf16[48,640]{1,0:T(8,128)(2,1)}), bf16[1536,640]{1,0:T(8,128)(2,1)}) %all-gather.18.cloned.1.call-update) | async-done | bytes 1966096 | tf_op jit(solution)/shard_map/all_gather | solution.py:80
  429.6 5.9 all_gather.63
  435.6 5.9 all-gather
  447.8 23.6 %all-gather.20.cloned.1.call-done = bf16[384,1536]{0,1:T(8,128)(2,1)} async-done(((bf16[384,48]{0,1:T(8,128)(2,1)}), bf16[384,1536]{0,1:T(8,128)(2,1)}) %all-gather.20.cloned.1.call-update) | async-done | bytes 1179664 | tf_op jit(solution)/shard_map/all_gather | solution.py:81
  479.7 5.2 all-to-all-start.2
  486.0 13.3 all-to-all-done.2
  501.9 22.0 %all-reduce.35.cloned.1.call-done = f32[256,1536]{1,0:T(8,128)} async-done(((f32[256,1536]{1,0:T(8,128)}), f32[256,1536]{1,0:T(8,128)}) %all-reduce.35.cloned.1.call-update) | async-done | bytes 1572880 | tf_op jit(solution)/shard_map/psum | solution.py:70
  526.6 59.9 %all-gather.22.cloned.1.call-done = bf16[1536,2,1728]{2,0,1:T(8,128)(2,1)} async-done(((bf16[48,2,1728]{2,0,1:T(8,128)(2,1)}), bf16[1536,2,1728]{2,0,1:T(8,128)(2,1)}) %all-gather.22.cloned.1.call-update) | async-done | bytes 10616848 | tf_op jit(solution)/shard_map/all_gather | solution.py:83
  586.5 10.8 fusion.97
  597.4 38.9 %all-gather.24.cloned.1.call-done = bf16[1728,1536]{0,1:T(8,128)(2,1)} async-done(((bf16[1728,48]{0,1:T(8,128)(2,1)}), bf16[1728,1536]{0,1:T(8,128)(2,1)}) %all-gather.24.cloned.1.call-update) | async-done | bytes 5308432 | tf_op jit(solution)/shard_map/all_gather | solution.py:84
  636.2 6.6 fusion.54
  644.1 4.3 convolution_bitcast_fusion.2
  649.5 48.1 %all-reduce.37.cloned.1.call-done = f32[256,1536]{1,0:T(8,128)} async-done(((f32[256,1536]{1,0:T(8,128)}), f32[256,1536]{1,0:T(8,128)}) %all-reduce.37.cloned.1.call-update) | async-done | bytes 1572880 | tf_op jit(solution)/shard_map/psum | solution.py:74
  706.9 7.5 fusion
  714.5 4.5 fusion.2
  726.0 5.0 fusion.38
  734.7 6.9 reduce-scatter.11.cloned.1.call-done
  745.3 18.2 %reduce-scatter.13.cloned.1.call-done = f32[256,2,64]{0,2,1:T(8,128)} async-done(((f32[1024,2,64]{0,2,1:T(8,128)}), f32[256,2,64]{0,2,1:T(8,128)}) %reduce-scatter.13.cloned.1.call-update) | async-done | bytes 131088 | tf_op jit(solution)/shard_map/reduce_scatter | solution.py:304
  769.1 50.6 %all-reduce.39.cloned.1.call-done = f32[256,1536]{1,0:T(8,128)} async-done(((f32[256,1536]{1,0:T(8,128)}), f32[256,1536]{1,0:T(8,128)}) %all-reduce.39.cloned.1.call-update) | async-done | bytes 1572880 | tf_op jit(solution)/shard_map/psum | solution.py:74
  824.1 6.2 fusion.53
  831.5 4.3 convolution_bitcast_fusion.1
  835.9 6.5 fusion.49
  842.4 44.1 %all-reduce.41.cloned.1.call-done = f32[256,1536]{1,0:T(8,128)} async-done(((f32[256,1536]{1,0:T(8,128)}), f32[256,1536]{1,0:T(8,128)}) %all-reduce.41.cloned.1.call-update) | async-done | bytes 1572880 | tf_op jit(solution)/shard_map/psum | solution.py:74
  903.4 13.1 fusion.46
  916.6 12.7 fusion.45
  941.2 7.8 fusion.51
  950.0 4.2 fusion.82
  955.9 5.6 fusion.68
  962.5 15.6 all-reduce.43.cloned.1.call-done
  981.2 7.8 all-to-all-start.1
  995.6 7.7 all-to-all-done.1
  1008.0 68.5 %all-reduce.19 = (f32[3,1536]{1,0:T(4,128)}, f32[64]{0:T(128)}, f32[64]{0:T(128)}) all-reduce(f32[3,1536]{1,0:T(4,128)S(1)} %add_dynamic-update-slice_fusion, f32[64]{0:T(128)S(1)} %copy-done.80, f32[64]{0:T(128)S(1)} %copy-done.81), channel_id=1, replica_groups=mesh['fsdp'=8,'ctx'=4,'tp'=4] {'fsdp','ctx','tp'}, use_global_device_ids=true, to_apply=%region_40.41 | all-reduce | flops 4736 | bytes 37888 | tf_op jit(solution)/shard_map/psum | solution.py:360
  1076.5 122.8 %all-reduce.20 = (f32[1536]{0:T(1024)S(1)}, f32[1536]{0:T(1024)S(1)}, f32[1536]{0:T(1024)S(1)}, f32[1536]{0:T(1024)S(1)}) all-reduce(f32[1536]{0:T(1024)S(1)} %get-tuple-element.108, f32[1536]{0:T(1024)S(1)} %get-tuple-element.106, f32[1536]{0:T(1024)S(1)} %get-tuple-element.104, ...), channel_id=5, replica_groups=mesh['fsdp'=8,'ctx'=4,'tp'=4] {'fsdp','ctx'}, use_global_device_ids=true, to_apply=%region_35.36.clone | all-reduce | flops 6144 | bytes 49152
  1207.1 41.1 %reduce-scatter.19.cloned.1.call-done = f32[48,2,1728]{2,0,1:T(8,128)} async-done(((f32[1536,2,1728]{2,0,1:T(8,128)}), f32[48,2,1728]{2,0,1:T(8,128)}) %reduce-scatter.19.cloned.1.call-update) | async-done | bytes 663568 | tf_op jit(solution)/shard_map/reduce_scatter | solution.py:105
  1250.7 79.1 %reduce-scatter.25.cloned.1.call-done = f32[384,48]{0,1:T(8,128)} async-done(((f32[384,1536]{0,1:T(8,128)}), f32[384,48]{0,1:T(8,128)}) %reduce-scatter.25.cloned.1.call-update) | async-done | bytes 73744 | tf_op jit(solution)/shard_map/reduce_scatter | solution.py:103
  1329.7 85.9 %reduce-scatter.23.cloned.1.call-done = f32[48,640]{1,0:T(8,128)} async-done(((f32[1536,640]{1,0:T(8,128)}), f32[48,640]{1,0:T(8,128)}) %reduce-scatter.23.cloned.1.call-update) | async-done | bytes 122896 | tf_op jit(solution)/shard_map/reduce_scatter | solution.py:102
  1415.6 83.1 %reduce-scatter.17.cloned.1.call-done = f32[384,48]{0,1:T(8,128)} async-done(((f32[384,1536]{0,1:T(8,128)}), f32[384,48]{0,1:T(8,128)}) %reduce-scatter.17.cloned.1.call-update) | async-done | bytes 73744 | tf_op jit(solution)/shard_map/reduce_scatter | solution.py:103
  1498.7 103.7 %reduce-scatter.29.cloned.1.call-done = f32[1728,48]{0,1:T(8,128)} async-done(((f32[1728,1536]{0,1:T(8,128)}), f32[1728,48]{0,1:T(8,128)}) %reduce-scatter.29.cloned.1.call-update) | async-done | bytes 331792 | tf_op jit(solution)/shard_map/reduce_scatter | solution.py:106
  1602.4 91.3 %reduce-scatter.15.cloned.1.call-done = f32[48,3,384]{2,0,1:T(8,128)} async-done(((f32[1536,3,384]{2,0,1:T(8,128)}), f32[48,3,384]{2,0,1:T(8,128)}) %reduce-scatter.15.cloned.1.call-update) | async-done | bytes 221200 | tf_op jit(solution)/shard_map/reduce_scatter | solution.py:102
  1693.7 104.3 %reduce-scatter.21.cloned.1.call-done = f32[1728,48]{0,1:T(8,128)} async-done(((f32[1728,1536]{0,1:T(8,128)}), f32[1728,48]{0,1:T(8,128)}) %reduce-scatter.21.cloned.1.call-update) | async-done | bytes 331792 | tf_op jit(solution)/shard_map/reduce_scatter | solution.py:106
  (403 shorter events, 153.6 us)
Async XLA Ops:
  7.2 144.3 %all-gather.10.cloned.1.call-start = ((), (), s32[]{:S(2)}) async-start(), calls=%async_computation.14 | async-start | bytes 3649536 | tf_op jit(solution)/shard_map/all_gather | solution.py:80
  9.7 139.0 %copy-start.85 = (s32[32]{0:T(128)S(1)}, s32[32]{0:T(128)}, u32[]{:S(2)}) copy-start(s32[32]{0:T(128)} %param.21) | copy-start | bytes 388
  9.8 139.8 %copy-start.68 = (s32[32,32]{1,0:T(8,128)}, s32[32,32]{1,0:T(8,128)S(1)}, u32[]{:S(2)}) copy-start(s32[32,32]{1,0:T(8,128)S(1)} %get-tuple-element.162) | copy-start | bytes 12292
  11.8 138.7 %all-to-all-start = ((bf16[32,8,1536]{2,1,0:T(8,128)(2,1)}), bf16[32,8,1536]{2,1,0:T(8,128)(2,1)S(1)}, u32[]{:S(2)}, u32[]{:S(2)}) async-start(bf16[32,8,1536]{2,1,0:T(8,128)(2,1)} %gather_fusion), calls=%async_computation | async-start | bytes 1572864 | tf_op jit(solution)/shard_map/all_to_all | solution.py:171
  21.3 142.1 %all-gather.12.cloned.1.call-start = ((), (), s32[]{:S(2)}) async-start(), calls=%async_computation.15 | async-start | bytes 1216512 | tf_op jit(solution)/shard_map/all_gather | solution.py:81
  22.0 190.9 %all-reduce.31.cloned.1.call-start = ((), (), s32[]{:S(2)}) async-start(), calls=%async_computation.16 | async-start | bytes 3145728 | tf_op jit(solution)/shard_map/psum | solution.py:70
  154.9 7.5 collective-permute-start
  166.6 109.0 %all-gather.14.cloned.1.call-start = ((), (), s32[]{:S(2)}) async-start(), calls=%async_computation.17 | async-start | bytes 11354112 | tf_op jit(solution)/shard_map/all_gather | solution.py:83
  167.5 157.7 %all-gather.16.cloned.1.call-start = ((), (), s32[]{:S(2)}) async-start(), calls=%async_computation.18 | async-start | bytes 5677056 | tf_op jit(solution)/shard_map/all_gather | solution.py:84
  168.1 212.0 %all-reduce.33.cloned.1.call-start = ((), (), s32[]{:S(2)}) async-start(), calls=%async_computation.19 | async-start | bytes 3145728 | tf_op jit(solution)/shard_map/psum | solution.py:70
  214.6 68.3 %copy-start.3 = (f32[256,1536]{1,0:T(8,128)}, f32[256,1536]{1,0:T(8,128)S(1)}, u32[]{:S(2)}) copy-start(f32[256,1536]{1,0:T(8,128)S(1)} %get-tuple-element.141) | copy-start | bytes 4718596
  214.7 68.3 %copy-start.69 = (f32[256]{0:T(256)}, f32[256]{0:T(256)S(1)}, u32[]{:S(2)}) copy-start(f32[256]{0:T(256)S(1)} %get-tuple-element.140) | copy-start | bytes 3076
  214.7 68.3 %copy-start.49 = (f32[256]{0:T(256)}, f32[256]{0:T(256)S(1)}, u32[]{:S(2)}) copy-start(f32[256]{0:T(256)S(1)} %fusion.106) | copy-start | bytes 3076
  286.3 46.7 %copy-start.92 = (bf16[64]{0:T(256)(128)(2,1)S(1)}, bf16[64]{0:T(256)(128)(2,1)}, u32[]{:S(2)}) copy-start(bf16[64]{0:T(256)(128)(2,1)} %param.32) | copy-start | bytes 388
  286.3 46.7 %copy-start.93 = (bf16[64]{0:T(256)(128)(2,1)S(1)}, bf16[64]{0:T(256)(128)(2,1)}, u32[]{:S(2)}) copy-start(bf16[64]{0:T(256)(128)(2,1)} %param.33) | copy-start | bytes 388
  330.8 95.9 %all-gather.18.cloned.1.call-start = ((), (), s32[]{:S(2)}) async-start(), calls=%async_computation.20 | async-start | bytes 2027520 | tf_op jit(solution)/shard_map/all_gather | solution.py:80
  331.6 139.8 %all-gather.20.cloned.1.call-start = ((), (), s32[]{:S(2)}) async-start(), calls=%async_computation.21 | async-start | bytes 1216512 | tf_op jit(solution)/shard_map/all_gather | solution.py:81
  332.3 191.5 %all-reduce.35.cloned.1.call-start = ((), (), s32[]{:S(2)}) async-start(), calls=%async_computation.22 | async-start | bytes 3145728 | tf_op jit(solution)/shard_map/psum | solution.py:70
  333.0 102.4 %copy-start.78 = (f32[64]{0:T(128)}, f32[64]{0:T(128)S(1)}, u32[]{:S(2)}) copy-start(f32[64]{0:T(128)S(1)} %convert_element_type.177) | copy-start | bytes 772
  333.1 96.4 %copy-start.79 = (f32[64]{0:T(128)}, f32[64]{0:T(128)S(1)}, u32[]{:S(2)}) copy-start(f32[64]{0:T(128)S(1)} %convert_element_type.174) | copy-start | bytes 772
  382.2 47.1 %copy-start.71 = (f32[256]{0:T(256)}, f32[256]{0:T(256)S(1)}, u32[]{:S(2)}) copy-start(f32[256]{0:T(256)S(1)} %get-tuple-element.138) | copy-start | bytes 3076
  382.2 47.1 %copy-start.51 = (f32[256]{0:T(256)}, f32[256]{0:T(256)S(1)}, u32[]{:S(2)}) copy-start(f32[256]{0:T(256)S(1)} %fusion.107) | copy-start | bytes 3076
  474.6 111.9 %all-gather.22.cloned.1.call-start = ((), (), s32[]{:S(2)}) async-start(), calls=%async_computation.23 | async-start | bytes 11354112 | tf_op jit(solution)/shard_map/all_gather | solution.py:83
  476.4 159.8 %all-gather.24.cloned.1.call-start = ((), (), s32[]{:S(2)}) async-start(), calls=%async_computation.24 | async-start | bytes 5677056 | tf_op jit(solution)/shard_map/all_gather | solution.py:84
  479.7 19.5 %all-to-all-start.2 = ((bf16[32,8,1536]{2,1,0:T(8,128)(2,1)}), bf16[32,8,1536]{2,1,0:T(8,128)(2,1)}, u32[]{:S(2)}, u32[]{:S(2)}) async-start(bf16[32,8,1536]{2,1,0:T(8,128)(2,1)} %gather_fusion.4), calls=%async_computation.2 | async-start | bytes 1572864 | tf_op jit(solution)/shard_map/all_to_all | solution.py:178
  485.0 212.6 %all-reduce.37.cloned.1.call-start = ((), (), s32[]{:S(2)}) async-start(), calls=%async_computation.25 | async-start | bytes 3145728 | tf_op jit(solution)/shard_map/psum | solution.py:74
  526.6 70.8 %copy-start.73 = (f32[256]{0:T(256)}, f32[256]{0:T(256)S(1)}, u32[]{:S(2)}) copy-start(f32[256]{0:T(256)S(1)} %get-tuple-element.134) | copy-start | bytes 3076
  526.6 70.8 %copy-start.53 = (f32[256]{0:T(256)}, f32[256]{0:T(256)S(1)}, u32[]{:S(2)}) copy-start(f32[256]{0:T(256)S(1)} %fusion.108) | copy-start | bytes 3076
  648.4 93.2 %reduce-scatter.11.cloned.1.call-start = ((), (), s32[]{:S(2)}) async-start(), calls=%async_computation.26 | async-start | bytes 655360 | tf_op jit(solution)/shard_map/reduce_scatter | solution.py:303
  722.5 41.0 %reduce-scatter.13.cloned.1.call-start = ((), (), s32[]{:S(2)}) async-start(), calls=%async_computation.27 | async-start | bytes 655360 | tf_op jit(solution)/shard_map/reduce_scatter | solution.py:304
  731.0 88.7 %all-reduce.39.cloned.1.call-start = ((), (), s32[]{:S(2)}) async-start(), calls=%async_computation.28 | async-start | bytes 3145728 | tf_op jit(solution)/shard_map/psum | solution.py:74
  765.3 54.4 %copy-start.52 = (f32[256]{0:T(256)S(1)}, f32[256]{0:T(256)}, u32[]{:S(2)}) copy-start(f32[256]{0:T(256)} %copy-done.51) | copy-start | bytes 3076
  768.9 52.7 %copy-start.72 = (f32[256]{0:T(256)S(1)}, f32[256]{0:T(256)}, u32[]{:S(2)}) copy-start(f32[256]{0:T(256)} %copy-done.71) | copy-start | bytes 3076
  768.9 117.6 %all-reduce.41.cloned.1.call-start = ((), (), s32[]{:S(2)}) async-start(), calls=%async_computation.29 | async-start | bytes 3145728 | tf_op jit(solution)/shard_map/psum | solution.py:74
  835.8 50.7 %copy-start.50 = (f32[256]{0:T(256)S(1)}, f32[256]{0:T(256)}, u32[]{:S(2)}) copy-start(f32[256]{0:T(256)} %copy-done.49) | copy-start | bytes 3076
  835.8 142.3 %all-reduce.43.cloned.1.call-start = ((), (), s32[]{:S(2)}) async-start(), calls=%async_computation.38 | async-start | bytes 6291456 | tf_op jit(solution)/shard_map/psum | solution.py:70
  894.2 5.4 collective-permute-start.1
  902.8 301.9 %reduce-scatter.27.cloned.1.call-start = ((), (), s32[]{:S(2)}) async-start(), calls=%async_computation.36 | async-start | bytes 22708224 | tf_op jit(solution)/shard_map/reduce_scatter | solution.py:105
  916.5 331.7 %reduce-scatter.19.cloned.1.call-start = ((), (), s32[]{:S(2)}) async-start(), calls=%async_computation.32 | async-start | bytes 22708224 | tf_op jit(solution)/shard_map/reduce_scatter | solution.py:105
  929.3 400.4 %reduce-scatter.25.cloned.1.call-start = ((), (), s32[]{:S(2)}) async-start(), calls=%async_computation.35 | async-start | bytes 2433024 | tf_op jit(solution)/shard_map/reduce_scatter | solution.py:103
  933.7 481.9 %reduce-scatter.23.cloned.1.call-start = ((), (), s32[]{:S(2)}) async-start(), calls=%async_computation.34 | async-start | bytes 4055040 | tf_op jit(solution)/shard_map/reduce_scatter | solution.py:102
  936.6 562.1 %reduce-scatter.17.cloned.1.call-start = ((), (), s32[]{:S(2)}) async-start(), calls=%async_computation.31 | async-start | bytes 2433024 | tf_op jit(solution)/shard_map/reduce_scatter | solution.py:103
  940.1 662.3 %reduce-scatter.29.cloned.1.call-start = ((), (), s32[]{:S(2)}) async-start(), calls=%async_computation.37 | async-start | bytes 11354112 | tf_op jit(solution)/shard_map/reduce_scatter | solution.py:106
  949.1 744.6 %reduce-scatter.15.cloned.1.call-start = ((), (), s32[]{:S(2)}) async-start(), calls=%async_computation.30 | async-start | bytes 7299072 | tf_op jit(solution)/shard_map/reduce_scatter | solution.py:102
  954.3 843.8 %reduce-scatter.21.cloned.1.call-start = ((), (), s32[]{:S(2)}) async-start(), calls=%async_computation.33 | async-start | bytes 11354112 | tf_op jit(solution)/shard_map/reduce_scatter | solution.py:106
  981.2 22.0 %all-to-all-start.1 = ((bf16[32,8,1536]{2,1,0:T(8,128)(2,1)}), bf16[32,8,1536]{2,1,0:T(8,128)(2,1)S(1)}, u32[]{:S(2)}, u32[]{:S(2)}) async-start(bf16[32,8,1536]{2,1,0:T(8,128)(2,1)} %gather_fusion.2), calls=%async_computation.1 | async-start | bytes 1572864 | tf_op jit(solution)/shard_map/all_to_all | solution.py:382
  1003.2 199.9 %all-to-all-start.3 = ((bf16[32,8,1536]{2,1,0:T(8,128)(2,1)}), bf16[32,8,1536]{2,1,0:T(8,128)(2,1)S(1)}, u32[]{:S(2)}, u32[]{:S(2)}) async-start(bf16[32,8,1536]{2,1,0:T(8,128)(2,1)} %gather_fusion.6), calls=%async_computation.5 | async-start | bytes 1572864 | tf_op jit(solution)/shard_map/all_to_all | solution.py:383
  1203.2 594.9 %copy-start.1 = (bf16[256,1536]{1,0:T(8,128)(2,1)S(1)}, bf16[256,1536]{1,0:T(8,128)(2,1)}, u32[]{:S(2)}) copy-start(bf16[256,1536]{1,0:T(8,128)(2,1)} %param.19) | copy-start | bytes 2359300
  (82 other events, 483.2 us)
Sparse Core Ops, SparseCore 0:
  10.4 51.9 all-gather.9
  64.7 42.3 all-gather.11
  166.7 46.1 all-reduce.30
  215.7 59.8 all-gather.13
  277.7 47.4 all-gather.15
  331.0 49.0 all-reduce.32
  382.4 44.3 all-gather.17
  429.1 42.2 all-gather.19
  474.7 49.1 all-reduce.34
  526.6 59.8 all-gather.21
  588.8 47.4 all-gather.23
  648.5 49.0 all-reduce.36
  722.6 18.9 reduce-scatter.10
  744.4 19.0 reduce-scatter.12
  769.0 50.6 all-reduce.38
  835.9 50.5 all-reduce.40
  902.9 75.1 all-reduce.42
  982.0 131.2 reduce-scatter.26
  1117.7 130.4 reduce-scatter.18
  1252.2 77.5 reduce-scatter.24
  1334.5 81.0 reduce-scatter.22
  1420.2 78.5 reduce-scatter.16
  1503.1 99.3 reduce-scatter.28
  1607.2 86.5 reduce-scatter.14
  1698.6 99.4 reduce-scatter.20
where the time goes:
time: 1810 us
  waiting for transfers between devices  1180 us (65%)
  blocking collectives  327 us (18%)
  matrix products  144 us (8%)
  local copies, waits for them, and re-layouts  50.3 us (3%)
  other arithmetic  48.2 us (3%)
  starting transfers between devices  35.3 us (2%)
    unnamed x2, blocking collectives  247 us
    reduce_scatter x2, waiting for transfers between devices, reduce_layer(): lax.psum_scatter(members[5], ('fsdp', 'ctx'), scatter_dimension=1, tiled=...  208 us
    reduce_scatter x2, waiting for transfers between devices, reduce_layer(): lax.psum_scatter(members[1], ('fsdp', 'ctx'), scatter_dimension=0, tiled=...  177 us
    reduce_scatter x2, waiting for transfers between devices, reduce_layer(): lax.psum_scatter(members[2], ('fsdp', 'ctx'), scatter_dimension=1, tiled=...  162 us
    psum x3, waiting for transfers between devices, input_sum(): return lax.psum(partial_rows, 'tp')  143 us
    psum x4, waiting for transfers between devices, branch_sum(): return lax.psum(partial_rows, 'tp')  128 us
    all_gather x2, waiting for transfers between devices, fetch_layer(): lax.all_gather(members[4], ('fsdp', 'ctx'), axis=0, tiled=True)  121 us
    all_gather x2, waiting for transfers between devices, fetch_layer(): lax.all_gather(members[5], ('fsdp', 'ctx'), axis=1, tiled=True)  77.7 us
  transfers between devices with their start and end apart: 31, of which 26 were waited for; matrix products, arithmetic and copies ran while one was open for 8% of the time, Pallas kernels for 0%

commit v1 on v0

v1 whole, which is shorter than its diff:
```python
import jax
import jax.numpy as jnp
from jax import lax
from jax.sharding import PartitionSpec as P

H = 24
KVH = 8
HD = 64

EPSILON = 1e-05
ROPE_BASE = 1000000.0
NEGATIVE = -1e30

TOKEN_AXES = ("fsdp", "ctx")
RING = 4
CORES = 2
F32 = jnp.float32
BF16 = jnp.bfloat16


def norm_rows(values, scales):
    return values * lax.rsqrt(jnp.mean(values * values, axis=-1, keepdims=True) + EPSILON) * scales


def rotate(values, cosine, sine):
    half_dim = values.shape[-1] // 2
    shape_out = (values.shape[0],) + (1,) * (values.ndim - 2) + (half_dim,)
    cosine = cosine.reshape(shape_out)
    sine = sine.reshape(shape_out)
    first_half = values[..., :half_dim]
    second_half = values[..., half_dim:]
    return jnp.concatenate(
        [
            first_half * cosine - second_half * sine,
            second_half * cosine + first_half * sine,
        ],
        axis=-1,
    )


def locate(lengths, positions):
    seq_ends = jnp.cumsum(lengths)
    segment = jnp.sum((positions[:, None] >= seq_ends[None, :]).astype(jnp.int32), axis=1)
    starts = seq_ends - lengths
    first_row = jnp.sum(
        jnp.where(segment[:, None] == jnp.arange(lengths.shape[0])[None, :], starts[None, :], 0),
        axis=1,
    )
    return (segment, positions - first_row)


def shortconv(extended, kernel_in, segment):
    kernel_taps = kernel_in.shape[0]
    out_rows = extended.shape[0] - kernel_taps + 1
    result = kernel_in[0] * extended[kernel_taps - 1 :]
    for t in range(1, kernel_taps):
        earlier = extended[kernel_taps - 1 - t : kernel_taps - 1 - t + out_rows]
        same_seq = (
            segment[kernel_taps - 1 - t : kernel_taps - 1 - t + out_rows]
            == segment[kernel_taps - 1 :]
        ).astype(F32)[:, None]
        result = result + kernel_in[t] * earlier * same_seq
    return result


def from_behind(block, axis, distance):
    devices = range(lax.axis_size(axis))
    route = [(i - distance, i) for i in devices if i - distance in devices]
    return lax.ppermute(block, axis, route)


def shift_chip(block, along_x, distance):
    route = []
    for x in range(RING):
        for z in range(RING):
            for core in range(CORES):
                to_x = (x + distance) % RING if along_x else x
                to_z = z if along_x else (z + distance) % RING
                route.append(
                    ((x * RING + z) * CORES + core, (to_x * RING + to_z) * CORES + core)
                )
    return lax.ppermute(block, TOKEN_AXES, route)


def swap_ctx(block, mask):
    return lax.ppermute(block, "ctx", [(i, i ^ mask) for i in range(lax.axis_size("ctx"))])


def shift_tp(block, distance):
    members = lax.axis_size("tp")
    return lax.ppermute(block, "tp", [(i, (i + distance) % members) for i in range(members)])


def tp_gather(shard):
    members = lax.axis_size("tp")
    return jnp.concatenate([shard] + [shift_tp(shard, k) for k in range(1, members)], axis=0)


def tp_reduce(partial):
    members = lax.axis_size("tp")
    rows = partial.shape[0] // members
    total = partial[:rows].astype(F32)
    for k in range(1, members):
        total = total + shift_tp(partial[k * rows : (k + 1) * rows], -k).astype(F32)
    return total


def reorder(rows):
    members = lax.axis_size("tp")
    own = lax.axis_index("tp")
    chunk = rows.shape[0] // members
    return jnp.concatenate(
        [
            lax.dynamic_slice_in_dim(rows, (own - k) % members * chunk, chunk, 0)
            for k in range(members)
        ],
        axis=0,
    )


def times(left, right):
    return lax.dot_general(left, right, (((1,), (0,)), ((), ())), preferred_element_type=F32)


def times_t(left, right):
    return lax.dot_general(left, right, (((1,), (1,)), ((), ())), preferred_element_type=F32)


def pair(rows):
    return jnp.concatenate([rows, swap_ctx(rows, 1)], axis=0)


def block_order(x_first):
    device = lax.axis_index(TOKEN_AXES)
    core = device % CORES
    z = device // CORES % RING
    x = device // (CORES * RING)
    outer, inner = jnp.meshgrid(jnp.arange(RING), jnp.arange(RING), indexing="ij")
    step_x, step_z = (outer, inner) if x_first else (inner, outer)
    return ((((x + step_x) % RING) * RING + (z + step_z) % RING) * CORES + core).reshape(-1)


def left_blocks(paired, x_first):
    tokens, width = paired.shape
    shards = lax.axis_size(TOKEN_AXES)
    columns = paired.T.reshape(shards, width // shards, tokens)
    picked = jnp.take(columns, block_order(x_first), axis=0, mode="clip")
    return picked.reshape(RING, -1, tokens)


def reduce_gradient(left, right, x_first):
    parts = [times(left[k], right).astype(BF16) for k in range(RING)]
    rows = parts[0].shape[0] // RING
    got = [parts[0]] + [shift_chip(parts[k], x_first, k) for k in range(1, RING)]
    sums = [
        sum(part[m * rows : (m + 1) * rows].astype(F32) for part in got) for m in range(RING)
    ]
    total = sums[0]
    for m in range(1, RING):
        total = total + shift_chip(sums[m].astype(BF16), not x_first, m).astype(F32)
    return total


def ffn_forward(stream, gain, gateup, down_t):
    hidden = down_t.shape[1]
    normed = tp_gather(norm_rows(stream, gain).astype(BF16))
    gate = times(normed, gateup[:, :hidden])
    up = times(normed, gateup[:, hidden:])
    active = (jax.nn.silu(gate) * up).astype(BF16)
    result = stream + tp_reduce(times_t(active, down_t).astype(BF16))
    return result, (normed, gate, up, active)


def ffn_backward(stream, kept, gain, gateup, down_t, upward, back, down_x_first):
    normed, gate, up, active = kept
    d_active = times(back, down_t)
    unused, pullback = jax.vjp(lambda a, b: jax.nn.silu(a) * b, gate, up)
    d_gate, d_up = pullback(d_active)
    d_gate = d_gate.astype(BF16)
    d_up = d_up.astype(BF16)
    d_both = jnp.concatenate([d_gate, d_up], axis=1)
    d_normed = tp_reduce(times_t(d_both, gateup).astype(BF16))
    unused, pullback = jax.vjp(norm_rows, stream, gain)
    d_stream, d_gain = pullback(d_normed)
    normed_pair = pair(normed)
    back_pair = pair(back)
    gate_grad = reduce_gradient(left_blocks(normed_pair, True), pair(d_gate), True)
    up_grad = reduce_gradient(left_blocks(normed_pair, False), pair(d_up), False)
    down_grad = reduce_gradient(
        left_blocks(back_pair, down_x_first), pair(active), down_x_first
    )
    return upward + d_stream, d_gain, gate_grad, up_grad, down_grad


def body(
    hidden_in,
    cotangent,
    seq_lengths,
    deal_order,
    mixer_gain,
    mixer_project,
    mixer_kernel,
    mixer_output,
    first_gain,
    first_gateup,
    first_down,
    attend_gain,
    attend_project,
    query_gain,
    key_gain,
    attend_output,
    second_gain,
    second_gateup,
    second_down,
):
    shards = lax.axis_size(TOKEN_AXES)
    contexts = lax.axis_size("ctx")
    members = lax.axis_size("tp")
    row_count, width = hidden_in.shape
    piece_rows = row_count // shards
    chunk = row_count // members
    device = lax.axis_index(TOKEN_AXES)
    own = lax.axis_index("tp")
    depth = mixer_gain.shape[0]
    channels = mixer_output.shape[0]
    hidden = first_down.shape[0]
    heads_width = attend_output.shape[0]

    first_pack = jnp.concatenate(
        [
            mixer_project.reshape(depth, -1),
            mixer_output.T,
            first_gateup.reshape(depth, -1),
            first_down.T,
        ],
        axis=1,
    )
    second_pack = jnp.concatenate(
        [
            attend_project,
            attend_output.T,
            second_gateup.reshape(depth, -1),
            second_down.T,
        ],
        axis=1,
    )
    first_all = lax.all_gather(first_pack, TOKEN_AXES, axis=0, tiled=True)
    second_all = lax.all_gather(second_pack, TOKEN_AXES, axis=0, tiled=True)
    cut = 3 * channels
    project_a = first_all[:, :cut]
    output_a_t = first_all[:, cut : cut + channels]
    cut = cut + channels
    gateup_f = first_all[:, cut : cut + 2 * hidden]
    down_f_t = first_all[:, cut + 2 * hidden :]
    cut = attend_project.shape[1]
    project_b = second_all[:, :cut]
    output_b_t = second_all[:, cut : cut + heads_width]
    cut = cut + heads_width
    gateup_s = second_all[:, cut : cut + 2 * hidden]
    down_s_t = second_all[:, cut + 2 * hidden :]

    piece_table = deal_order.reshape(shards, shards, piece_rows)[:, :, 0]
    anchor = piece_table // row_count
    anchor_piece = piece_table % row_count // piece_rows
    send_piece = jnp.sum(jnp.where(anchor == device, anchor_piece, 0), axis=1)
    my_anchor = lax.dynamic_index_in_dim(anchor, device, 0, keepdims=False)
    gains_row = jnp.concatenate(
        [mixer_gain, first_gain, attend_gain, second_gain, jnp.zeros((width - 4 * depth,), BF16)]
    )
    outgoing = jnp.concatenate(
        [
            hidden_in.reshape(shards, piece_rows, width)[send_piece],
            cotangent.reshape(shards, piece_rows, width)[send_piece],
            jnp.broadcast_to(gains_row, (shards, 8, width)),
        ],
        axis=1,
    )
    arrived = lax.all_to_all(outgoing, TOKEN_AXES, split_axis=0, concat_axis=0, tiled=True)
    tokens = arrived[:, :piece_rows][my_anchor].reshape(row_count, width)
    back_s = arrived[:, piece_rows : 2 * piece_rows][my_anchor].reshape(row_count, width)
    gains = (
        arrived[:, 2 * piece_rows, : 4 * depth]
        .reshape(shards, 4, depth)
        .transpose(1, 0, 2)
        .reshape(4, width)
        .astype(F32)
    )
    gain_a, gain_f, gain_b, gain_s = gains[0], gains[1], gains[2], gains[3]
    stream0 = lax.dynamic_slice_in_dim(tokens, own * chunk, chunk, 0).astype(F32)
    upstream = lax.dynamic_slice_in_dim(back_s, own * chunk, chunk, 0).astype(F32)
    back_s = reorder(back_s)

    kernel_taps = mixer_kernel.shape[0]
    halo = kernel_taps - 1
    local_rows = device * row_count + jnp.arange(row_count)
    halo_segment, unused = locate(
        seq_lengths, local_rows[0] - halo + jnp.arange(row_count + halo)
    )
    offsets = reorder(jnp.arange(row_count))
    segment, places = locate(seq_lengths, device * row_count + offsets)
    ctx = lax.axis_index("ctx")
    group_rows = jnp.concatenate(
        [
            (lax.axis_index("fsdp") * contexts + (ctx ^ mask)) * row_count + offsets
            for mask in range(contexts)
        ]
    )
    key_segment, key_places = locate(seq_lengths, group_rows)
    allowed = (segment[:, None] == key_segment[None, :]) & (key_places[None, :] <= places[:, None])
    half_dim = HD // 2
    frequency = ROPE_BASE ** (-(jnp.arange(half_dim).astype(F32) * 2.0 / HD))
    angles = places.astype(F32)[:, None] * frequency[None, :]
    cosine = jnp.cos(angles)
    sine = jnp.sin(angles)

    kernel_local = lax.dynamic_slice_in_dim(mixer_kernel, own * channels, channels, 1).astype(F32)
    mixer_in = norm_rows(tokens.astype(F32), gain_a).astype(BF16)
    halo_pad = 16
    halo_in = from_behind(mixer_in[row_count - halo_pad :], "ctx", 1)
    proj_a = times(jnp.concatenate([halo_in, mixer_in]), project_a)
    proj_b_part = proj_a[:, :channels]
    proj_c_part = proj_a[halo_pad:, channels : 2 * channels]
    proj_x_part = proj_a[:, 2 * channels :]
    extended = (proj_b_part * proj_x_part)[halo_pad - halo :].astype(BF16).astype(F32)
    conv_out = shortconv(extended, kernel_local, halo_segment)
    gated_rows = reorder((proj_c_part * conv_out).astype(BF16))
    stream1 = stream0 + tp_reduce(times_t(gated_rows, output_a_t).astype(BF16))
    stream2, kept_first = ffn_forward(stream1, gain_f, gateup_f, down_f_t)

    groups = H // KVH
    score_scale = HD ** (-0.5)
    qgain_f = query_gain.astype(F32)
    kgain_f = key_gain.astype(F32)

    def qk_maps(query_in, key_in, gain_q, gain_k):
        return (
            rotate(norm_rows(query_in, gain_q), cosine, sine),
            rotate(norm_rows(key_in, gain_k), cosine, sine),
        )

    attend_in = tp_gather(norm_rows(stream2, gain_b).astype(BF16))
    proj_b = times(attend_in, project_b).reshape(row_count, -1, groups + 2, HD)
    kv_heads = proj_b.shape[1]
    query_raw = proj_b[:, :, :groups]
    key_raw = proj_b[:, :, groups]
    query_f, key_f = qk_maps(query_raw, key_raw, qgain_f, kgain_f)
    query_b = query_f.astype(BF16)
    key_value = jnp.concatenate(
        [
            key_f.astype(BF16).reshape(row_count, -1),
            proj_b[:, :, groups + 1].astype(BF16).reshape(row_count, -1),
        ],
        axis=1,
    )
    key_value_all = jnp.concatenate(
        [key_value] + [swap_ctx(key_value, mask) for mask in range(1, contexts)], axis=0
    )
    key_all = key_value_all[:, : kv_heads * HD].reshape(-1, kv_heads, HD)
    value_all = key_value_all[:, kv_heads * HD :].reshape(-1, kv_heads, HD)
    scores = (
        jnp.einsum("tkgd,nkd->kgtn", query_b, key_all, preferred_element_type=F32) * score_scale
    )
    masked = jnp.where(allowed, scores, NEGATIVE)
    row_top = jnp.max(masked, axis=-1, keepdims=True)
    exponent = jnp.exp(masked - row_top)
    row_total = jnp.sum(exponent, axis=-1, keepdims=True)
    softmax_rows = exponent / row_total
    log_total = row_top + jnp.log(row_total)
    attended = (
        jnp.einsum(
            "kgtn,nkd->tkgd", softmax_rows.astype(BF16), value_all, preferred_element_type=F32
        )
        .astype(BF16)
        .reshape(row_count, -1)
    )
    stream3 = stream2 + tp_reduce(times_t(attended, output_b_t).astype(BF16))
    stream4, kept_second = ffn_forward(stream3, gain_s, gateup_s, down_s_t)

    d_stream3, gain_s_grad, gate_s_grad, up_s_grad, down_s_grad = ffn_backward(
        stream3, kept_second, gain_s, gateup_s, down_s_t, upstream, back_s, True
    )
    back_b = tp_gather(d_stream3.astype(BF16))
    d_attended_b = times(back_b, output_b_t).astype(BF16).reshape(row_count, -1, groups, HD)
    scores_again = (
        jnp.einsum("tkgd,nkd->kgtn", query_b, key_all, preferred_element_type=F32) * score_scale
    )
    probs_again = jnp.where(allowed, jnp.exp(scores_again - log_total), 0.0)
    d_probs = jnp.einsum("tkgd,nkd->kgtn", d_attended_b, value_all, preferred_element_type=F32)
    d_values = jnp.einsum(
        "kgtn,tkgd->nkd", probs_again.astype(BF16), d_attended_b, preferred_element_type=F32
    )
    inner_sum = jnp.sum(probs_again * d_probs, axis=-1, keepdims=True)
    d_scores = (probs_again * (d_probs - inner_sum)).astype(BF16)
    d_query = (
        jnp.einsum("kgtn,nkd->tkgd", d_scores, key_all, preferred_element_type=F32) * score_scale
    )
    d_keys = (
        jnp.einsum("kgtn,tkgd->nkd", d_scores, query_b, preferred_element_type=F32) * score_scale
    )
    d_key_value = jnp.concatenate(
        [d_keys.reshape(-1, kv_heads * HD), d_values.reshape(-1, kv_heads * HD)], axis=1
    )
    d_local = d_key_value[:row_count]
    for mask in range(1, contexts):
        part = d_key_value[mask * row_count : (mask + 1) * row_count].astype(BF16)
        d_local = d_local + swap_ctx(part, mask).astype(F32)
    d_key_local = d_local[:, : kv_heads * HD].reshape(row_count, kv_heads, HD)
    d_value_local = d_local[:, kv_heads * HD :].reshape(row_count, kv_heads, HD)
    unused, pullback = jax.vjp(qk_maps, query_raw, key_raw, qgain_f, kgain_f)
    d_query_raw, d_key_raw, qgain_grad, kgain_grad = pullback((d_query, d_key_local))
    d_proj_b = (
        jnp.concatenate([d_query_raw, d_key_raw[:, :, None], d_value_local[:, :, None]], axis=2)
        .astype(BF16)
        .reshape(row_count, -1)
    )
    d_attend_in = tp_reduce(times_t(d_proj_b, project_b).astype(BF16))
    unused, pullback = jax.vjp(norm_rows, stream2, gain_b)
    d_norm_b, gain_b_grad = pullback(d_attend_in)
    d_stream2 = d_stream3 + d_norm_b
    project_b_grad = reduce_gradient(left_blocks(pair(attend_in), False), pair(d_proj_b), False)
    output_b_grad = reduce_gradient(left_blocks(pair(back_b), False), pair(attended), False)

    back_f = tp_gather(d_stream2.astype(BF16))
    d_stream1, gain_f_grad, gate_f_grad, up_f_grad, down_f_grad = ffn_backward(
        stream1, kept_first, gain_f, gateup_f, down_f_t, d_stream2, back_f, False
    )
    back_a = tp_gather(d_stream1.astype(BF16))
    d_gated = reorder(times(back_a, output_a_t))
    d_cgate = d_gated * conv_out
    d_conv = d_gated * proj_c_part
    unused, pullback = jax.vjp(
        lambda ext_rows, kernel_in: shortconv(ext_rows, kernel_in, halo_segment),
        extended,
        kernel_local,
    )
    d_extended, kernel_grad = pullback(d_conv)
    returned = from_behind(d_extended[:halo], "ctx", -1)
    d_product = d_extended[halo:] + jnp.concatenate(
        [jnp.zeros((row_count - halo, channels), F32), returned]
    )
    d_proj_a = jnp.concatenate(
        [
            d_product * proj_x_part[halo_pad:],
            d_cgate,
            d_product * proj_b_part[halo_pad:],
        ],
        axis=1,
    ).astype(BF16)
    d_mixer_in = tp_reduce(times_t(reorder(d_proj_a), project_a).astype(BF16))
    unused, pullback = jax.vjp(norm_rows, stream0, gain_a)
    d_norm_a, gain_a_grad = pullback(d_mixer_in)
    d_stream0 = d_stream1 + d_norm_a
    project_a_grad = reduce_gradient(left_blocks(pair(mixer_in), True), pair(d_proj_a), True)
    output_a_grad = reduce_gradient(left_blocks(pair(back_a), False), pair(gated_rows), False)

    slot_for_anchor = jnp.sum(
        jnp.where(
            my_anchor[None, :] == jnp.arange(shards)[:, None], jnp.arange(shards)[None, :], 0
        ),
        axis=1,
    )
    dest_for_piece = jnp.sum(
        jnp.where(
            send_piece[None, :] == jnp.arange(shards)[:, None], jnp.arange(shards)[None, :], 0
        ),
        axis=1,
    )
    pieces = shards // members
    slot_place = (own - slot_for_anchor // pieces) % members * pieces + slot_for_anchor % pieces
    out_rows = tp_gather(stream4.astype(BF16)).reshape(shards, piece_rows, width)[slot_place]
    out_home = lax.all_to_all(out_rows, TOKEN_AXES, split_axis=0, concat_axis=0, tiled=True)
    layer_out = out_home[dest_for_piece].reshape(row_count, width)

    def row_of(values):
        flat = values.reshape(-1)
        return jnp.concatenate([flat, jnp.zeros((width - flat.shape[0],), F32)])

    small = jnp.stack(
        [
            gain_a_grad,
            gain_f_grad,
            gain_b_grad,
            gain_s_grad,
            row_of(jnp.concatenate([qgain_grad, kgain_grad])),
            row_of(kernel_grad),
        ]
        + [jnp.zeros((width,), F32)] * 10
    )
    last = tp_gather(jnp.concatenate([d_stream0.astype(BF16), small.astype(BF16)]))
    last = last.reshape(members, chunk + 16, width)
    grad_rows = last[:, :chunk].reshape(shards, piece_rows, width)[slot_place]
    smalls = last[:, chunk:].astype(F32)
    summed = jnp.sum(smalls[:, :5], axis=0)
    gain_sums = summed[:4].reshape(4, shards, depth).transpose(1, 0, 2).reshape(shards, 4 * depth)
    head_sums = summed[4, : 2 * HD]
    kernel_rows = reorder(smalls[:, 5, : kernel_taps * channels])
    kernel_rows = kernel_rows.reshape(members, kernel_taps, channels).transpose(1, 0, 2)
    shared = jnp.concatenate([kernel_rows.reshape(-1), head_sums])
    fill = 4 * width - 4 * depth - shared.shape[0]
    small_rows = jnp.concatenate(
        [
            gain_sums,
            jnp.broadcast_to(shared, (shards, shared.shape[0])),
            jnp.zeros((shards, fill), F32),
        ],
        axis=1,
    ).astype(BF16)
    home = lax.all_to_all(
        jnp.concatenate([grad_rows, small_rows.reshape(shards, 4, width)], axis=1),
        TOKEN_AXES,
        split_axis=0,
        concat_axis=0,
        tiled=True,
    )
    input_gradient = home[:, :piece_rows][dest_for_piece].reshape(row_count, width)
    totals = jnp.sum(home[:, piece_rows:].astype(F32), axis=0).reshape(-1)
    gain_totals = totals[: 4 * depth].reshape(4, depth)
    kernel_end = 4 * depth + kernel_taps * width
    kernel_total = totals[4 * depth : kernel_end].reshape(kernel_taps, width)
    qgain_total = totals[kernel_end : kernel_end + HD]
    kgain_total = totals[kernel_end + HD : kernel_end + 2 * HD]

    return (
        layer_out,
        input_gradient,
        gain_totals[0],
        project_a_grad.reshape(depth, 3, channels),
        kernel_total,
        output_a_grad.T,
        gain_totals[1],
        jnp.stack([gate_f_grad, up_f_grad], axis=1),
        down_f_grad.T,
        gain_totals[2],
        project_b_grad,
        qgain_total,
        kgain_total,
        output_b_grad.T,
        gain_totals[3],
        jnp.stack([gate_s_grad, up_s_grad], axis=1),
        down_s_grad.T,
    )


def solution(mesh):
    tokens = P(TOKEN_AXES, None)
    rows = P(TOKEN_AXES)
    three = P(TOKEN_AXES, None, "tp")
    two = P(TOKEN_AXES, "tp")
    turned = P("tp", TOKEN_AXES)
    return jax.shard_map(
        body,
        mesh=mesh,
        in_specs=(
            tokens, tokens, P(), P(),
            rows, three, P(), turned,
            rows, three, turned,
            rows, two, P(), P(), turned,
            rows, three, turned,
        ),
        out_specs=(
            tokens, tokens,
            rows, three, P(), turned,
            rows, three, turned,
            rows, two, P(), P(), turned,
            rows, three, turned,
        ),
        check_vma=False,
    )
```

time: 1810 us -> 878 us (0.49)
  waiting for transfers between devices: 1180 us -> 251 us
  blocking collectives: 327 us -> 0 us
  starting transfers between devices: 35.3 us -> 225 us
  local copies, waits for them, and re-layouts: 50.3 us -> 112 us
  matrix products: 144 us -> 188 us
  other arithmetic: 48.2 us -> 69.8 us
    reduce_scatter x10 -> x0, waiting for transfers between devices: 613 us -> none  [the longest x2 208 us: reduce_layer(): lax.psum_scatter(members[5], ('fsdp', 'ctx'), scatter_dimension=1, tiled=...]
    psum x7 -> x0, waiting for transfers between devices: 271 us -> none  [the longest x3 143 us: input_sum(): return lax.psum(partial_rows, 'tp')]
    unnamed x2 -> x0, blocking collectives: 247 us -> none
    ppermute x0 -> x132, starting transfers between devices: none -> 195 us  [the longest x60 90 us: shift_chip(): return lax.ppermute(block, TOKEN_AXES, route)]
    all_gather x8 -> x2, waiting for transfers between devices: 267 us -> 93.2 us  [the longest x1 69 us: body(): second_all = lax.all_gather(second_pack, TOKEN_AXES, axis=0, tiled=True)]
    ppermute x0 -> x132, waiting for transfers between devices: none -> 128 us  [the longest x60 67.7 us: shift_chip(): return lax.ppermute(block, TOKEN_AXES, route)]
    psum x1 -> x0, blocking collectives: 68.5 us -> none  [body(): lax.psum((kernel_full, qgain_grad, kgain_grad), ('fsdp', 'ctx', 'tp'))]
    dot_general x29 -> x63, matrix products: 136 us -> 183 us  [the longest x50 144 us: times(): lax.dot_general(left, right, (((1,), (0,)), ((), ())), preferred_element_...]
  transfers between devices with their start and end apart: 31 -> 139, of which waited for: 26 -> 42; matrix products, arithmetic and copies ran while one was open for 8% -> 37% of each run, Pallas kernels for 0% -> 0%
where the time goes in v1:
time: 878 us; the launch traced here: 864 us
  waiting for transfers between devices  251 us (29%)
  starting transfers between devices  225 us (26%)
  matrix products  188 us (21%)
  local copies, waits for them, and re-layouts  112 us (13%)
  other arithmetic  69.8 us (8%)
  between operations  18.5 us (2%)
    dot_general x50, matrix products, times(): lax.dot_general(left, right, (((1,), (0,)), ((), ())), preferred_element_...  144 us
    ppermute x60, starting transfers between devices, shift_chip(): return lax.ppermute(block, TOKEN_AXES, route)  90 us
    all_gather x1, waiting for transfers between devices, body(): second_all = lax.all_gather(second_pack, TOKEN_AXES, axis=0, tiled=True)  69 us
    ppermute x60, waiting for transfers between devices, shift_chip(): return lax.ppermute(block, TOKEN_AXES, route)  67.7 us
    ppermute x48, waiting for transfers between devices, shift_tp(): lax.ppermute(block, 'tp', [(i, (i + distance) % members) for i in range(m...  54.7 us
    ppermute x48, starting transfers between devices, shift_tp(): lax.ppermute(block, 'tp', [(i, (i + distance) % members) for i in range(m...  54.4 us
    ppermute x24, starting transfers between devices, swap_ctx(): lax.ppermute(block, 'ctx', [(i, i ^ mask) for i in range(lax.axis_size('c...  50.8 us
    dot_general x8, matrix products, times_t(): lax.dot_general(left, right, (((1,), (1,)), ((), ())), preferred_element_...  32.4 us
  transfers between devices with their start and end apart: 139, of which 42 were waited for; matrix products, arithmetic and copies ran while one was open for 37% of the time, Pallas kernels for 0%

profile of v1, /device:TPU:1, one launch (start us, length us, event | category | flops | bytes accessed | tf_op | source)
XLA Modules:
  0.0 864.0 jit_solution(4552924559734266261)
XLA Ops:
  16.8 9.6 %all-to-all-start = ((bf16[32,24,1536]{2,1,0:T(8,128)(2,1)}), bf16[32,24,1536]{2,1,0:T(8,128)(2,1)S(1)}, u32[]{:S(2)}, u32[]{:S(2)}) async-start(bf16[32,24,1536]{2,1,0:T(8,128)(2,1)} %pad_maximum_fusion), calls=%async_computation | async-start | bytes 4718592 | tf_op jit(solution)/shard_map/all_to_all | solution.py:278
  36.7 29.8 %all-to-all-done = bf16[32,24,1536]{2,1,0:T(8,128)(2,1)S(1)} async-done(((bf16[32,24,1536]{2,1,0:T(8,128)(2,1)}), bf16[32,24,1536]{2,1,0:T(8,128)(2,1)S(1)}, u32[]{:S(2)}, u32[]{:S(2)}) %all-to-all-start) | async-done | bytes 2359328 | tf_op jit(solution)/shard_map/all_to_all | solution.py:278
  89.2 3.1 gather_fusion.17
  97.1 24.2 %all-gather.3.cloned.1.call-done = bf16[1536,6720]{1,0:T(8,128)(2,1)} async-done(((bf16[48,6720]{1,0:T(8,128)(2,1)}), bf16[1536,6720]{1,0:T(8,128)(2,1)}) %all-gather.3.cloned.1.call-update) | async-done | bytes 20643856 | tf_op jit(solution)/shard_map/all_gather | solution.py:247
  121.3 3.2 fusion.34
  133.2 69.0 %all-gather.5.cloned.1.call-done = bf16[1536,6208]{1,0:T(8,128)(2,1)} async-done(((bf16[48,6208]{1,0:T(8,128)(2,1)}), bf16[1536,6208]{1,0:T(8,128)(2,1)}) %all-gather.5.cloned.1.call-update) | async-done | bytes 19070992 | tf_op jit(solution)/shard_map/all_gather | solution.py:248
  202.2 6.2 fusion.18
  219.6 5.2 collective-permute-done.5
  224.8 4.9 fusion.16
  229.8 6.3 multiply_convert_fusion.3
  248.8 5.0 collective-permute-done.9
  257.4 8.5 collective-permute-done.10
  290.1 7.5 collective-permute-done.16
  297.6 3.8 collective-permute-done.18
  315.8 7.9 fusion.10
  323.7 6.7 fusion.53
  330.5 5.1 fusion.48
  339.1 7.1 fusion.39
  383.5 5.0 fusion.4
  395.6 4.9 collective-permute-start.34
  405.2 5.4 all-to-all-start.1
  460.9 3.1 convolution_convert_fusion.4
  464.0 3.1 convolution_convert_fusion.3
  498.2 6.6 fusion.56
  504.8 7.6 fusion.42
  557.8 5.1 collective-permute-start.49
  568.2 3.3 fusion.36
  586.3 5.2 collective-permute-done.52
  605.6 8.5 collective-permute-done.114
  614.1 11.4 %collective-permute-start.88 = (bf16[256,1728]{0,1:T(8,128)(2,1)}, bf16[256,1728]{0,1:T(8,128)(2,1)}, u32[]{:S(2)}, u32[]{:S(2)}) collective-permute-start(bf16[256,1728]{0,1:T(8,128)(2,1)} %get-tuple-element.302), channel_id=1, source_target_pairs={{0,4},{4,0},{8,12},{12,8},{1,5},{5,1},{9,13},{13,9},{2,6},{6,2},{1... | collective-permute-start | bytes 2654216 | tf_op jit(solution)/shard_map/ppermute | solution.py:86
  626.1 4.5 collective-permute-start.87
  651.7 3.1 convolution_convert_fusion.15
  662.2 4.6 collective-permute-start.124
  677.1 12.9 %collective-permute-start.64 = (bf16[256,1536]{1,0:T(8,128)(2,1)}, bf16[256,1536]{1,0:T(8,128)(2,1)}, u32[]{:S(2)}, u32[]{:S(2)}) collective-permute-start(bf16[256,1536]{1,0:T(8,128)(2,1)} %pad_maximum_fusion.16), channel_id=1, source_target_pairs={{0,4},{4,0},{8,12},{12,8},{1,5},{5,1},{9,13},{13,9},{2,6},{6,2},{1... | collective-permute-start | bytes 2359304 | tf_op jit(solution)/shard_map/ppermute | solution.py:86
  695.5 7.7 all-to-all-start.2
  715.6 3.1 convolution_convert_fusion.22
  718.7 3.1 convolution_convert_fusion.21
  721.8 3.1 convolution_convert_fusion.20
  756.9 6.8 collective-permute-done.69
  771.0 3.6 collective-permute-start.71
  778.2 3.5 collective-permute-done.90
  781.7 11.8 %collective-permute-done.91 = bf16[192,1728]{1,0:T(8,128)(2,1)S(1)} collective-permute-done((bf16[192,1728]{1,0:T(8,128)(2,1)S(1)}, bf16[192,1728]{1,0:T(8,128)(2,1)S(1)}, u32[]{:S(2)}, u32[]{:S(2)}) %collective-permute-start.91) | collective-permute-done | bytes 663584 | tf_op jit(solution)/shard_map/ppermute | solution.py:82
  793.4 3.6 collective-permute-start.62
  809.7 3.4 collective-permute-start.93
  813.4 4.6 collective-permute-done.81
  818.0 13.6 %collective-permute-done.82 = bf16[192,1728]{1,0:T(8,128)(2,1)S(1)} collective-permute-done((bf16[192,1728]{1,0:T(8,128)(2,1)S(1)}, bf16[192,1728]{1,0:T(8,128)(2,1)S(1)}, u32[]{:S(2)}, u32[]{:S(2)}) %collective-permute-start.82) | collective-permute-done | bytes 663584 | tf_op jit(solution)/shard_map/ppermute | solution.py:82
  831.6 3.6 collective-permute-done.83
  840.1 4.5 collective-permute-start.85
  (988 shorter events, 462.1 us)
Async XLA Ops:
  7.2 114.1 %all-gather.3.cloned.1.call-start = ((), (), s32[]{:S(2)}) async-start(), calls=%async_computation.3 | async-start | bytes 21491712 | tf_op jit(solution)/shard_map/all_gather | solution.py:247
  11.4 190.8 %all-gather.5.cloned.1.call-start = ((), (), s32[]{:S(2)}) async-start(), calls=%async_computation.4 | async-start | bytes 19869696 | tf_op jit(solution)/shard_map/all_gather | solution.py:248
  16.8 49.8 %all-to-all-start = ((bf16[32,24,1536]{2,1,0:T(8,128)(2,1)}), bf16[32,24,1536]{2,1,0:T(8,128)(2,1)S(1)}, u32[]{:S(2)}, u32[]{:S(2)}) async-start(bf16[32,24,1536]{2,1,0:T(8,128)(2,1)} %pad_maximum_fusion), calls=%async_computation | async-start | bytes 4718592 | tf_op jit(solution)/shard_map/all_to_all | solution.py:278
  129.3 81.0 %collective-permute-start.1 = (bf16[64,1536]{1,0:T(8,128)(2,1)}, bf16[64,1536]{1,0:T(8,128)(2,1)}, u32[]{:S(2)}, u32[]{:S(2)}) collective-permute-start(bf16[64,1536]{1,0:T(8,128)(2,1)} %get-tuple-element.252), channel_id=1, source_target_pairs={{0,3},{1,0},{2,1},{3,2},{4,7},{5,4},{6,5},{7,6},{8,11},{9,8},{10,9... | collective-permute-start | bytes 589832 | tf_op jit(solution)/shard_map/ppermute | solution.py:91
  131.8 78.5 %collective-permute-start.2 = (bf16[64,1536]{1,0:T(8,128)(2,1)}, bf16[64,1536]{1,0:T(8,128)(2,1)}, u32[]{:S(2)}, u32[]{:S(2)}) collective-permute-start(bf16[64,1536]{1,0:T(8,128)(2,1)} %get-tuple-element.254), channel_id=1, source_target_pairs={{0,2},{1,3},{2,0},{3,1},{4,6},{5,7},{6,4},{7,5},{8,10},{9,11},{10,... | collective-permute-start | bytes 589832 | tf_op jit(solution)/shard_map/ppermute | solution.py:91
  132.4 77.9 %collective-permute-start.3 = (bf16[64,1536]{1,0:T(8,128)(2,1)}, bf16[64,1536]{1,0:T(8,128)(2,1)}, u32[]{:S(2)}, u32[]{:S(2)}) collective-permute-start(bf16[64,1536]{1,0:T(8,128)(2,1)} %get-tuple-element.253), channel_id=1, source_target_pairs={{0,1},{1,2},{2,3},{3,0},{4,5},{5,6},{6,7},{7,4},{8,9},{9,10},{10,1... | collective-permute-start | bytes 589832 | tf_op jit(solution)/shard_map/ppermute | solution.py:91
  242.3 63.1 %collective-permute-start.72 = (bf16[256,1536]{1,0:T(8,128)(2,1)S(1)}, bf16[256,1536]{1,0:T(8,128)(2,1)S(1)}, u32[]{:S(2)}, u32[]{:S(2)}) collective-permute-start(bf16[256,1536]{1,0:T(8,128)(2,1)S(1)} %pad_maximum_fusion.10), channel_id=1, source_target_pairs={{0,4},{4,0},{8,12},{12,8},{1,5},{5,1},{9,13},{13,9},{2,6},{6,2},{1... | collective-permute-start | bytes 2359304 | tf_op jit(solution)/shard_map/ppermute | solution.py:86
  338.2 21.0 %collective-permute-start.24 = (bf16[64,1536]{1,0:T(8,128)(2,1)S(1)}, bf16[64,1536]{1,0:T(8,128)(2,1)S(1)}, u32[]{:S(2)}, u32[]{:S(2)}) collective-permute-start(bf16[64,1536]{1,0:T(8,128)(2,1)S(1)} %get-tuple-element.244), channel_id=1, source_target_pairs={{0,1},{1,2},{2,3},{3,0},{4,5},{5,6},{6,7},{7,4},{8,9},{9,10},{10,1... | collective-permute-start | bytes 589832 | tf_op jit(solution)/shard_map/ppermute | solution.py:91
  359.2 184.1 %collective-permute-start.104 = (bf16[256,384]{0,1:T(8,128)(2,1)}, bf16[256,384]{0,1:T(8,128)(2,1)}, u32[]{:S(2)}, u32[]{:S(2)}) collective-permute-start(bf16[256,384]{0,1:T(8,128)(2,1)} %bitcast.26), channel_id=1, source_target_pairs={{0,4},{4,0},{8,12},{12,8},{1,5},{5,1},{9,13},{13,9},{2,6},{6,2},{1... | collective-permute-start | bytes 589832 | tf_op jit(solution)/shard_map/ppermute | solution.py:86
  359.3 95.4 %collective-permute-start.127 = (bf16[256,1728]{0,1:T(8,128)(2,1)}, bf16[256,1728]{0,1:T(8,128)(2,1)}, u32[]{:S(2)}, u32[]{:S(2)}) collective-permute-start(bf16[256,1728]{0,1:T(8,128)(2,1)} %get-tuple-element.159), channel_id=1, source_target_pairs={{0,4},{4,0},{8,12},{12,8},{1,5},{5,1},{9,13},{13,9},{2,6},{6,2},{1... | collective-permute-start | bytes 2654216 | tf_op jit(solution)/shard_map/ppermute | solution.py:86
  374.3 21.3 %collective-permute-start.25 = (bf16[64,1536]{1,0:T(8,128)(2,1)}, bf16[64,1536]{1,0:T(8,128)(2,1)}, u32[]{:S(2)}, u32[]{:S(2)}) collective-permute-start(bf16[64,1536]{1,0:T(8,128)(2,1)} %get-tuple-element.282), channel_id=1, source_target_pairs={{0,1},{1,2},{2,3},{3,0},{4,5},{5,6},{6,7},{7,4},{8,9},{9,10},{10,1... | collective-permute-start | bytes 589832 | tf_op jit(solution)/shard_map/ppermute | solution.py:91
  374.7 25.7 %collective-permute-start.26 = (bf16[64,1536]{1,0:T(8,128)(2,1)}, bf16[64,1536]{1,0:T(8,128)(2,1)}, u32[]{:S(2)}, u32[]{:S(2)}) collective-permute-start(bf16[64,1536]{1,0:T(8,128)(2,1)} %get-tuple-element.282), channel_id=1, source_target_pairs={{0,2},{1,3},{2,0},{3,1},{4,6},{5,7},{6,4},{7,5},{8,10},{9,11},{10,... | collective-permute-start | bytes 589832 | tf_op jit(solution)/shard_map/ppermute | solution.py:91
  376.8 24.2 %collective-permute-start.27 = (bf16[64,1536]{1,0:T(8,128)(2,1)}, bf16[64,1536]{1,0:T(8,128)(2,1)}, u32[]{:S(2)}, u32[]{:S(2)}) collective-permute-start(bf16[64,1536]{1,0:T(8,128)(2,1)} %get-tuple-element.282), channel_id=1, source_target_pairs={{0,3},{1,0},{2,1},{3,2},{4,7},{5,4},{6,5},{7,6},{8,11},{9,8},{10,9... | collective-permute-start | bytes 589832 | tf_op jit(solution)/shard_map/ppermute | solution.py:91
  405.2 126.1 %all-to-all-start.1 = ((bf16[32,8,1536]{2,1,0:T(8,128)(2,1)}), bf16[32,8,1536]{2,1,0:T(8,128)(2,1)}, u32[]{:S(2)}, u32[]{:S(2)}) async-start(bf16[32,8,1536]{2,1,0:T(8,128)(2,1)} %gather_fusion.3), calls=%async_computation.1 | async-start | bytes 1572864 | tf_op jit(solution)/shard_map/all_to_all | solution.py:471
  427.1 40.0 %collective-permute-start.112 = (bf16[256,1728]{0,1:T(8,128)(2,1)}, bf16[256,1728]{0,1:T(8,128)(2,1)}, u32[]{:S(2)}, u32[]{:S(2)}) collective-permute-start(bf16[256,1728]{0,1:T(8,128)(2,1)} %copy-done.172), channel_id=1, source_target_pairs={{0,4},{4,0},{8,12},{12,8},{1,5},{5,1},{9,13},{13,9},{2,6},{6,2},{1... | collective-permute-start | bytes 2654216 | tf_op jit(solution)/shard_map/ppermute | solution.py:86
  428.9 51.6 %collective-permute-start.119 = (bf16[256,1728]{0,1:T(8,128)(2,1)}, bf16[256,1728]{0,1:T(8,128)(2,1)}, u32[]{:S(2)}, u32[]{:S(2)}) collective-permute-start(bf16[256,1728]{0,1:T(8,128)(2,1)} %copy-done.170), channel_id=1, source_target_pairs={{0,4},{4,0},{8,12},{12,8},{1,5},{5,1},{9,13},{13,9},{2,6},{6,2},{1... | collective-permute-start | bytes 2654216 | tf_op jit(solution)/shard_map/ppermute | solution.py:86
  448.1 89.2 %collective-permute-start.103 = (bf16[256,1536]{1,0:T(8,128)(2,1)}, bf16[256,1536]{1,0:T(8,128)(2,1)S(1)}, u32[]{:S(2)}, u32[]{:S(2)}) collective-permute-start(bf16[256,1536]{1,0:T(8,128)(2,1)} %pad_maximum_fusion.14), channel_id=1, source_target_pairs={{0,4},{4,0},{8,12},{12,8},{1,5},{5,1},{9,13},{13,9},{2,6},{6,2},{1... | collective-permute-start | bytes 2359304 | tf_op jit(solution)/shard_map/ppermute | solution.py:86
  454.6 38.3 %collective-permute-start.40 = (bf16[64,1536]{1,0:T(8,128)(2,1)S(1)}, bf16[64,1536]{1,0:T(8,128)(2,1)S(1)}, u32[]{:S(2)}, u32[]{:S(2)}) collective-permute-start(bf16[64,1536]{1,0:T(8,128)(2,1)S(1)} %get-tuple-element.126), channel_id=1, source_target_pairs={{0,1},{1,2},{2,3},{3,0},{4,5},{5,6},{6,7},{7,4},{8,9},{9,10},{10,1... | collective-permute-start | bytes 589832 | tf_op jit(solution)/shard_map/ppermute | solution.py:91
  467.1 27.3 %collective-permute-start.41 = (bf16[64,1536]{1,0:T(8,128)(2,1)S(1)}, bf16[64,1536]{1,0:T(8,128)(2,1)S(1)}, u32[]{:S(2)}, u32[]{:S(2)}) collective-permute-start(bf16[64,1536]{1,0:T(8,128)(2,1)S(1)} %get-tuple-element.126), channel_id=1, source_target_pairs={{0,2},{1,3},{2,0},{3,1},{4,6},{5,7},{6,4},{7,5},{8,10},{9,11},{10,... | collective-permute-start | bytes 589832 | tf_op jit(solution)/shard_map/ppermute | solution.py:91
  493.0 22.5 %collective-permute-start.97 = (bf16[192,640]{1,0:T(8,128)(2,1)S(1)}, bf16[192,640]{1,0:T(8,128)(2,1)S(1)}, u32[]{:S(2)}, u32[]{:S(2)}) collective-permute-start(bf16[192,640]{1,0:T(8,128)(2,1)S(1)} %convolution_convert_fusion.33), channel_id=1, source_target_pairs={{0,8},{4,12},{8,16},{12,20},{16,24},{20,28},{24,0},{28,4},{32,40},... | collective-permute-start | bytes 737288 | tf_op jit(solution)/shard_map/ppermute | solution.py:82
  494.4 21.1 %collective-permute-start.98 = (bf16[192,640]{1,0:T(8,128)(2,1)S(1)}, bf16[192,640]{1,0:T(8,128)(2,1)S(1)}, u32[]{:S(2)}, u32[]{:S(2)}) collective-permute-start(bf16[192,640]{1,0:T(8,128)(2,1)S(1)} %convolution_convert_fusion.32), channel_id=1, source_target_pairs={{0,16},{4,20},{8,24},{12,28},{16,0},{20,4},{24,8},{28,12},{32,48},... | collective-permute-start | bytes 737288 | tf_op jit(solution)/shard_map/ppermute | solution.py:82
  496.8 20.5 %collective-permute-start.99 = (bf16[192,640]{1,0:T(8,128)(2,1)S(1)}, bf16[192,640]{1,0:T(8,128)(2,1)S(1)}, u32[]{:S(2)}, u32[]{:S(2)}) collective-permute-start(bf16[192,640]{1,0:T(8,128)(2,1)S(1)} %convolution_convert_fusion.31), channel_id=1, source_target_pairs={{0,24},{4,28},{8,0},{12,4},{16,8},{20,12},{24,16},{28,20},{32,56},... | collective-permute-start | bytes 737288 | tf_op jit(solution)/shard_map/ppermute | solution.py:82
  534.0 59.4 %collective-permute-start.128 = (bf16[192,1728]{1,0:T(8,128)(2,1)}, bf16[192,1728]{1,0:T(8,128)(2,1)}, u32[]{:S(2)}, u32[]{:S(2)}) collective-permute-start(bf16[192,1728]{1,0:T(8,128)(2,1)} %convolution_convert_fusion.5), channel_id=1, source_target_pairs={{0,32},{4,36},{8,40},{12,44},{16,48},{20,52},{24,56},{28,60},{32,6... | collective-permute-start | bytes 1990664 | tf_op jit(solution)/shard_map/ppermute | solution.py:82
  534.0 63.4 %collective-permute-start.129 = (bf16[192,1728]{1,0:T(8,128)(2,1)}, bf16[192,1728]{1,0:T(8,128)(2,1)}, u32[]{:S(2)}, u32[]{:S(2)}) collective-permute-start(bf16[192,1728]{1,0:T(8,128)(2,1)} %convolution_convert_fusion.4), channel_id=1, source_target_pairs={{0,64},{4,68},{8,72},{12,76},{16,80},{20,84},{24,88},{28,92},{32,9... | collective-permute-start | bytes 1990664 | tf_op jit(solution)/shard_map/ppermute | solution.py:82
  591.4 22.7 %collective-permute-start.114 = (bf16[192,1728]{1,0:T(8,128)(2,1)}, bf16[192,1728]{1,0:T(8,128)(2,1)}, u32[]{:S(2)}, u32[]{:S(2)}) collective-permute-start(bf16[192,1728]{1,0:T(8,128)(2,1)} %convolution_convert_fusion.12), channel_id=1, source_target_pairs={{0,64},{4,68},{8,72},{12,76},{16,80},{20,84},{24,88},{28,92},{32,9... | collective-permute-start | bytes 1990664 | tf_op jit(solution)/shard_map/ppermute | solution.py:82
  593.4 32.7 %collective-permute-start.115 = (bf16[192,1728]{1,0:T(8,128)(2,1)}, bf16[192,1728]{1,0:T(8,128)(2,1)}, u32[]{:S(2)}, u32[]{:S(2)}) collective-permute-start(bf16[192,1728]{1,0:T(8,128)(2,1)} %convolution_convert_fusion.11), channel_id=1, source_target_pairs={{0,96},{4,100},{8,104},{12,108},{16,112},{20,116},{24,120},{28,124... | collective-permute-start | bytes 1990664 | tf_op jit(solution)/shard_map/ppermute | solution.py:82
  597.4 35.7 %collective-permute-start.120 = (bf16[192,1728]{1,0:T(8,128)(2,1)}, bf16[192,1728]{1,0:T(8,128)(2,1)S(1)}, u32[]{:S(2)}, u32[]{:S(2)}) collective-permute-start(bf16[192,1728]{1,0:T(8,128)(2,1)} %convolution_convert_fusion.9), channel_id=1, source_target_pairs={{0,8},{4,12},{8,16},{12,20},{16,24},{20,28},{24,0},{28,4},{32,40},... | collective-permute-start | bytes 1990664 | tf_op jit(solution)/shard_map/ppermute | solution.py:82
  598.4 34.8 %collective-permute-start.121 = (bf16[192,1728]{1,0:T(8,128)(2,1)}, bf16[192,1728]{1,0:T(8,128)(2,1)S(1)}, u32[]{:S(2)}, u32[]{:S(2)}) collective-permute-start(bf16[192,1728]{1,0:T(8,128)(2,1)} %convolution_convert_fusion.8), channel_id=1, source_target_pairs={{0,16},{4,20},{8,24},{12,28},{16,0},{20,4},{24,8},{28,12},{32,48},... | collective-permute-start | bytes 1990664 | tf_op jit(solution)/shard_map/ppermute | solution.py:82
  600.2 33.6 %collective-permute-start.122 = (bf16[192,1728]{1,0:T(8,128)(2,1)}, bf16[192,1728]{1,0:T(8,128)(2,1)S(1)}, u32[]{:S(2)}, u32[]{:S(2)}) collective-permute-start(bf16[192,1728]{1,0:T(8,128)(2,1)} %convolution_convert_fusion.7), channel_id=1, source_target_pairs={{0,24},{4,28},{8,0},{12,4},{16,8},{20,12},{24,16},{28,20},{32,56},... | collective-permute-start | bytes 1990664 | tf_op jit(solution)/shard_map/ppermute | solution.py:82
  614.1 27.5 %collective-permute-start.88 = (bf16[256,1728]{0,1:T(8,128)(2,1)}, bf16[256,1728]{0,1:T(8,128)(2,1)}, u32[]{:S(2)}, u32[]{:S(2)}) collective-permute-start(bf16[256,1728]{0,1:T(8,128)(2,1)} %get-tuple-element.302), channel_id=1, source_target_pairs={{0,4},{4,0},{8,12},{12,8},{1,5},{5,1},{9,13},{13,9},{2,6},{6,2},{1... | collective-permute-start | bytes 2654216 | tf_op jit(solution)/shard_map/ppermute | solution.py:86
  633.2 70.1 %collective-permute-start.73 = (bf16[256,1728]{0,1:T(8,128)(2,1)}, bf16[256,1728]{0,1:T(8,128)(2,1)}, u32[]{:S(2)}, u32[]{:S(2)}) collective-permute-start(bf16[256,1728]{0,1:T(8,128)(2,1)} %get-tuple-element.155), channel_id=1, source_target_pairs={{0,4},{4,0},{8,12},{12,8},{1,5},{5,1},{9,13},{13,9},{2,6},{6,2},{1... | collective-permute-start | bytes 2654216 | tf_op jit(solution)/shard_map/ppermute | solution.py:86
  633.3 82.3 %collective-permute-start.80 = (bf16[256,1728]{0,1:T(8,128)(2,1)}, bf16[256,1728]{0,1:T(8,128)(2,1)}, u32[]{:S(2)}, u32[]{:S(2)}) collective-permute-start(bf16[256,1728]{0,1:T(8,128)(2,1)} %get-tuple-element.156), channel_id=1, source_target_pairs={{0,4},{4,0},{8,12},{12,8},{1,5},{5,1},{9,13},{13,9},{2,6},{6,2},{1... | collective-permute-start | bytes 2654216 | tf_op jit(solution)/shard_map/ppermute | solution.py:86
  633.8 21.0 %collective-permute-start.131 = (bf16[48,1728]{1,0:T(8,128)(2,1)}, bf16[48,1728]{1,0:T(8,128)(2,1)}, u32[]{:S(2)}, u32[]{:S(2)}) collective-permute-start(bf16[48,1728]{1,0:T(8,128)(2,1)} %get-tuple-element.160), channel_id=1, source_target_pairs={{0,8},{4,12},{8,16},{12,20},{16,24},{20,28},{24,0},{28,4},{32,40},... | collective-permute-start | bytes 497672 | tf_op jit(solution)/shard_map/ppermute | solution.py:82
  677.1 59.2 %collective-permute-start.64 = (bf16[256,1536]{1,0:T(8,128)(2,1)}, bf16[256,1536]{1,0:T(8,128)(2,1)}, u32[]{:S(2)}, u32[]{:S(2)}) collective-permute-start(bf16[256,1536]{1,0:T(8,128)(2,1)} %pad_maximum_fusion.16), channel_id=1, source_target_pairs={{0,4},{4,0},{8,12},{12,8},{1,5},{5,1},{9,13},{13,9},{2,6},{6,2},{1... | collective-permute-start | bytes 2359304 | tf_op jit(solution)/shard_map/ppermute | solution.py:86
  690.0 38.0 %collective-permute-start.57 = (bf16[256,1152]{1,0:T(8,128)(2,1)S(1)}, bf16[256,1152]{1,0:T(8,128)(2,1)}, u32[]{:S(2)}, u32[]{:S(2)}) collective-permute-start(bf16[256,1152]{1,0:T(8,128)(2,1)S(1)} %pad_maximum_fusion.22), channel_id=1, source_target_pairs={{0,4},{4,0},{8,12},{12,8},{1,5},{5,1},{9,13},{13,9},{2,6},{6,2},{1... | collective-permute-start | bytes 1769480 | tf_op jit(solution)/shard_map/ppermute | solution.py:86
  690.8 85.9 %collective-permute-start.89 = (bf16[192,1728]{1,0:T(8,128)(2,1)}, bf16[192,1728]{1,0:T(8,128)(2,1)}, u32[]{:S(2)}, u32[]{:S(2)}) collective-permute-start(bf16[192,1728]{1,0:T(8,128)(2,1)} %convolution_convert_fusion.17), channel_id=1, source_target_pairs={{0,8},{4,12},{8,16},{12,20},{16,24},{20,28},{24,0},{28,4},{32,40},... | collective-permute-start | bytes 1990664 | tf_op jit(solution)/shard_map/ppermute | solution.py:82
  695.5 157.4 %all-to-all-start.2 = ((bf16[32,12,1536]{2,1,0:T(8,128)(2,1)}), bf16[32,12,1536]{2,1,0:T(8,128)(2,1)S(1)}, u32[]{:S(2)}, u32[]{:S(2)}) async-start(bf16[32,12,1536]{2,1,0:T(8,128)(2,1)} %pad_maximum_fusion.7), calls=%async_computation.2 | async-start | bytes 3145728 | tf_op jit(solution)/shard_map/all_to_all | solution.py:508
  730.3 35.1 %collective-permute-start.58 = (bf16[192,1152]{1,0:T(8,128)(2,1)}, bf16[192,1152]{1,0:T(8,128)(2,1)}, u32[]{:S(2)}, u32[]{:S(2)}) collective-permute-start(bf16[192,1152]{1,0:T(8,128)(2,1)} %convolution_convert_fusion.29), channel_id=1, source_target_pairs={{0,32},{4,36},{8,40},{12,44},{16,48},{20,52},{24,56},{28,60},{32,6... | collective-permute-start | bytes 1327112 | tf_op jit(solution)/shard_map/ppermute | solution.py:82
  765.4 28.1 %collective-permute-start.91 = (bf16[192,1728]{1,0:T(8,128)(2,1)S(1)}, bf16[192,1728]{1,0:T(8,128)(2,1)S(1)}, u32[]{:S(2)}, u32[]{:S(2)}) collective-permute-start(bf16[192,1728]{1,0:T(8,128)(2,1)S(1)} %copy-done.174), channel_id=1, source_target_pairs={{0,24},{4,28},{8,0},{12,4},{16,8},{20,12},{24,16},{28,20},{32,56},... | collective-permute-start | bytes 1990664 | tf_op jit(solution)/shard_map/ppermute | solution.py:82
  775.8 29.1 %collective-permute-start.74 = (bf16[192,1728]{1,0:T(8,128)(2,1)S(1)}, bf16[192,1728]{1,0:T(8,128)(2,1)S(1)}, u32[]{:S(2)}, u32[]{:S(2)}) collective-permute-start(bf16[192,1728]{1,0:T(8,128)(2,1)S(1)} %copy-done.181), channel_id=1, source_target_pairs={{0,32},{4,36},{8,40},{12,44},{16,48},{20,52},{24,56},{28,60},{32,6... | collective-permute-start | bytes 1990664 | tf_op jit(solution)/shard_map/ppermute | solution.py:82
  775.9 21.2 %collective-permute-start.61 = (bf16[48,1152]{1,0:T(8,128)(2,1)S(1)}, bf16[48,1152]{1,0:T(8,128)(2,1)S(1)}, u32[]{:S(2)}, u32[]{:S(2)}) collective-permute-start(bf16[48,1152]{1,0:T(8,128)(2,1)S(1)} %get-tuple-element.180), channel_id=1, source_target_pairs={{0,8},{4,12},{8,16},{12,20},{16,24},{20,28},{24,0},{28,4},{32,40},... | collective-permute-start | bytes 331784 | tf_op jit(solution)/shard_map/ppermute | solution.py:82
  776.7 32.0 %collective-permute-start.75 = (bf16[192,1728]{1,0:T(8,128)(2,1)S(1)}, bf16[192,1728]{1,0:T(8,128)(2,1)S(1)}, u32[]{:S(2)}, u32[]{:S(2)}) collective-permute-start(bf16[192,1728]{1,0:T(8,128)(2,1)S(1)} %copy-done.180), channel_id=1, source_target_pairs={{0,64},{4,68},{8,72},{12,76},{16,80},{20,84},{24,88},{28,92},{32,9... | collective-permute-start | bytes 1990664 | tf_op jit(solution)/shard_map/ppermute | solution.py:82
  781.7 28.1 %collective-permute-start.76 = (bf16[192,1728]{1,0:T(8,128)(2,1)S(1)}, bf16[192,1728]{1,0:T(8,128)(2,1)S(1)}, u32[]{:S(2)}, u32[]{:S(2)}) collective-permute-start(bf16[192,1728]{1,0:T(8,128)(2,1)S(1)} %copy-done.179), channel_id=1, source_target_pairs={{0,96},{4,100},{8,104},{12,108},{16,112},{20,116},{24,120},{28,124... | collective-permute-start | bytes 1990664 | tf_op jit(solution)/shard_map/ppermute | solution.py:82
  802.2 29.4 %collective-permute-start.82 = (bf16[192,1728]{1,0:T(8,128)(2,1)S(1)}, bf16[192,1728]{1,0:T(8,128)(2,1)S(1)}, u32[]{:S(2)}, u32[]{:S(2)}) collective-permute-start(bf16[192,1728]{1,0:T(8,128)(2,1)S(1)} %copy-done.177), channel_id=1, source_target_pairs={{0,16},{4,20},{8,24},{12,28},{16,0},{20,4},{24,8},{28,12},{32,48},... | collective-permute-start | bytes 1990664 | tf_op jit(solution)/shard_map/ppermute | solution.py:82
  804.9 30.4 %collective-permute-start.83 = (bf16[192,1728]{1,0:T(8,128)(2,1)S(1)}, bf16[192,1728]{1,0:T(8,128)(2,1)S(1)}, u32[]{:S(2)}, u32[]{:S(2)}) collective-permute-start(bf16[192,1728]{1,0:T(8,128)(2,1)S(1)} %copy-done.176), channel_id=1, source_target_pairs={{0,24},{4,28},{8,0},{12,4},{16,8},{20,12},{24,16},{28,20},{32,56},... | collective-permute-start | bytes 1990664 | tf_op jit(solution)/shard_map/ppermute | solution.py:82
  808.6 29.0 %collective-permute-start.92 = (bf16[48,1728]{1,0:T(8,128)(2,1)S(1)}, bf16[48,1728]{1,0:T(8,128)(2,1)S(1)}, u32[]{:S(2)}, u32[]{:S(2)}) collective-permute-start(bf16[48,1728]{1,0:T(8,128)(2,1)S(1)} %get-tuple-element.169), channel_id=1, source_target_pairs={{0,32},{4,36},{8,40},{12,44},{16,48},{20,52},{24,56},{28,60},{32,6... | collective-permute-start | bytes 497672 | tf_op jit(solution)/shard_map/ppermute | solution.py:82
  809.7 30.2 %collective-permute-start.93 = (bf16[48,1728]{1,0:T(8,128)(2,1)S(1)}, bf16[48,1728]{1,0:T(8,128)(2,1)S(1)}, u32[]{:S(2)}, u32[]{:S(2)}) collective-permute-start(bf16[48,1728]{1,0:T(8,128)(2,1)S(1)} %get-tuple-element.171), channel_id=1, source_target_pairs={{0,64},{4,68},{8,72},{12,76},{16,80},{20,84},{24,88},{28,92},{32,9... | collective-permute-start | bytes 497672 | tf_op jit(solution)/shard_map/ppermute | solution.py:82
  818.0 22.1 %collective-permute-start.94 = (bf16[48,1728]{1,0:T(8,128)(2,1)S(1)}, bf16[48,1728]{1,0:T(8,128)(2,1)S(1)}, u32[]{:S(2)}, u32[]{:S(2)}) collective-permute-start(bf16[48,1728]{1,0:T(8,128)(2,1)S(1)} %get-tuple-element.170), channel_id=1, source_target_pairs={{0,96},{4,100},{8,104},{12,108},{16,112},{20,116},{24,120},{28,124... | collective-permute-start | bytes 497672 | tf_op jit(solution)/shard_map/ppermute | solution.py:82
  (283 other events, 3299.5 us)
Sparse Core Ops, SparseCore 0:
  11.5 109.7 all-gather.2
  124.2 77.9 all-gather.4

commit v2 on v1

--- a/solution.py
+++ b/solution.py
@@ -1,7 +1,11 @@
+import functools
+
 import jax
 import jax.numpy as jnp
 from jax import lax
-from jax.sharding import PartitionSpec as P
+from jax.experimental import pallas as pl
+from jax.experimental.pallas import tpu as pltpu
+from jax.sharding import Mesh, PartitionSpec as P
 
 H = 24
 KVH = 8
@@ -11,9 +15,12 @@
 ROPE_BASE = 1000000.0
 NEGATIVE = -1e30
 
-TOKEN_AXES = ("fsdp", "ctx")
-RING = 4
-CORES = 2
+CHIP_AXES = ("x", "z_hi", "z_lo")
+TOKEN_AXES = CHIP_AXES + ("core",)
+GROUP_AXES = ("x", "z_hi")
+CTX_AXES = ("z_lo", "core")
+TILE = 256
+VMEM_LIMIT = 48 * 1024 * 1024
 F32 = jnp.float32
 BF16 = jnp.bfloat16
 
@@ -63,27 +70,18 @@
     return result
 
 
-def from_behind(block, axis, distance):
-    devices = range(lax.axis_size(axis))
+def from_behind(block, distance):
+    devices = range(lax.axis_size(CTX_AXES))
     route = [(i - distance, i) for i in devices if i - distance in devices]
-    return lax.ppermute(block, axis, route)
-
-
-def shift_chip(block, along_x, distance):
-    route = []
-    for x in range(RING):
-        for z in range(RING):
-            for core in range(CORES):
-                to_x = (x + distance) % RING if along_x else x
-                to_z = z if along_x else (z + distance) % RING
-                route.append(
-                    ((x * RING + z) * CORES + core, (to_x * RING + to_z) * CORES + core)
-                )
-    return lax.ppermute(block, TOKEN_AXES, route)
+    return lax.ppermute(block, CTX_AXES, route)
 
 
 def swap_ctx(block, mask):
-    return lax.ppermute(block, "ctx", [(i, i ^ mask) for i in range(lax.axis_size("ctx"))])
+    return lax.ppermute(block, CTX_AXES, [(i, i ^ mask) for i in range(lax.axis_size(CTX_AXES))])
+
+
+def swap_core(block):
+    return lax.ppermute(block, "core", [(0, 1), (1, 0)])
 
 
 def shift_tp(block, distance):
@@ -92,16 +90,21 @@
 
 
 def tp_gather(shard):
-    members = lax.axis_size("tp")
-    return jnp.concatenate([shard] + [shift_tp(shard, k) for k in range(1, members)], axis=0)
-
-
-def tp_reduce(partial):
-    members = lax.axis_size("tp")
-    rows = partial.shape[0] // members
-    total = partial[:rows].astype(F32)
-    for k in range(1, members):
-        total = total + shift_tp(partial[k * rows : (k + 1) * rows], -k).astype(F32)
+    return [shard] + [shift_tp(shard, k) for k in range(1, lax.axis_size("tp"))]
+
+
+def tp_chunks(partial):
+    rows = partial.shape[0] // lax.axis_size("tp")
+    return [
+        partial[k * rows : (k + 1) * rows].astype(F32 if k == 0 else BF16)
+        for k in range(lax.axis_size("tp"))
+    ]
+
+
+def tp_reduce(chunks):
+    total = chunks[0]
+    for k in range(1, len(chunks)):
+        total = total + shift_tp(chunks[k], -k).astype(F32)
     return total
 
 
@@ -126,70 +129,256 @@
     return lax.dot_general(left, right, (((1,), (1,)), ((), ())), preferred_element_type=F32)
 
 
-def pair(rows):
-    return jnp.concatenate([rows, swap_ctx(rows, 1)], axis=0)
-
-
-def block_order(x_first):
-    device = lax.axis_index(TOKEN_AXES)
-    core = device % CORES
-    z = device // CORES % RING
-    x = device // (CORES * RING)
-    outer, inner = jnp.meshgrid(jnp.arange(RING), jnp.arange(RING), indexing="ij")
-    step_x, step_z = (outer, inner) if x_first else (inner, outer)
-    return ((((x + step_x) % RING) * RING + (z + step_z) % RING) * CORES + core).reshape(-1)
-
-
-def left_blocks(paired, x_first):
-    tokens, width = paired.shape
-    shards = lax.axis_size(TOKEN_AXES)
-    columns = paired.T.reshape(shards, width // shards, tokens)
-    picked = jnp.take(columns, block_order(x_first), axis=0, mode="clip")
-    return picked.reshape(RING, -1, tokens)
-
-
-def reduce_gradient(left, right, x_first):
-    parts = [times(left[k], right).astype(BF16) for k in range(RING)]
-    rows = parts[0].shape[0] // RING
-    got = [parts[0]] + [shift_chip(parts[k], x_first, k) for k in range(1, RING)]
-    sums = [
-        sum(part[m * rows : (m + 1) * rows].astype(F32) for part in got) for m in range(RING)
+def assemble(chunk_refs, target):
+    rows = chunk_refs[0].shape[0]
+    for k, ref in enumerate(chunk_refs):
+        target[k * rows : (k + 1) * rows, :] = ref[...]
+
+
+def spread(total, chunk_refs):
+    rows = chunk_refs[0].shape[0]
+    for k, ref in enumerate(chunk_refs):
+        ref[...] = total[k * rows : (k + 1) * rows, :].astype(ref.dtype)
+
+
+def whole(shape):
+    return pl.BlockSpec(shape, lambda *_: (0,) * len(shape))
+
+
+def weight_specs(depth, steps):
+    return [
+        pl.BlockSpec((depth, 2 * TILE), lambda j: (0, j)),
+        pl.BlockSpec((depth, TILE), lambda j: (0, 2 * steps + j)),
     ]
-    total = sums[0]
-    for m in range(1, RING):
-        total = total + shift_chip(sums[m].astype(BF16), not x_first, m).astype(F32)
-    return total
-
-
-def ffn_forward(stream, gain, gateup, down_t):
-    hidden = down_t.shape[1]
-    normed = tp_gather(norm_rows(stream, gain).astype(BF16))
-    gate = times(normed, gateup[:, :hidden])
-    up = times(normed, gateup[:, hidden:])
-    active = (jax.nn.silu(gate) * up).astype(BF16)
-    result = stream + tp_reduce(times_t(active, down_t).astype(BF16))
-    return result, (normed, gate, up, active)
-
-
-def ffn_backward(stream, kept, gain, gateup, down_t, upward, back, down_x_first):
-    normed, gate, up, active = kept
-    d_active = times(back, down_t)
-    unused, pullback = jax.vjp(lambda a, b: jax.nn.silu(a) * b, gate, up)
-    d_gate, d_up = pullback(d_active)
-    d_gate = d_gate.astype(BF16)
-    d_up = d_up.astype(BF16)
-    d_both = jnp.concatenate([d_gate, d_up], axis=1)
-    d_normed = tp_reduce(times_t(d_both, gateup).astype(BF16))
-    unused, pullback = jax.vjp(norm_rows, stream, gain)
-    d_stream, d_gain = pullback(d_normed)
-    normed_pair = pair(normed)
-    back_pair = pair(back)
-    gate_grad = reduce_gradient(left_blocks(normed_pair, True), pair(d_gate), True)
-    up_grad = reduce_gradient(left_blocks(normed_pair, False), pair(d_up), False)
-    down_grad = reduce_gradient(
-        left_blocks(back_pair, down_x_first), pair(active), down_x_first
-    )
-    return upward + d_stream, d_gain, gate_grad, up_grad, down_grad
+
+
+def chunk_shapes(count, rows, width):
+    return [jax.ShapeDtypeStruct((rows, width), F32 if k == 0 else BF16) for k in range(count)]
+
+
+def ffn_forward_kernel(count, *refs):
+    x_refs, (gu_ref, dn_ref), outs = refs[:count], refs[count : count + 2], refs[count + 2 : -2]
+    x_all, total = refs[-2:]
+    step = pl.program_id(0)
+
+    @pl.when(step == 0)
+    def _():
+        assemble(x_refs, x_all)
+        total[...] = jnp.zeros_like(total)
+
+    both = times(x_all[...], gu_ref[...])
+    gate, up = both[:, :TILE], both[:, TILE:]
+    active = (gate * jax.nn.sigmoid(gate) * up).astype(BF16)
+    total[...] += times_t(active, dn_ref[...])
+
+    @pl.when(step == pl.num_programs(0) - 1)
+    def _():
+        spread(total[...], outs)
+
+
+def ffn_forward(chunks, pack, steps):
+    count, (rows, width) = len(chunks), chunks[0].shape
+    tokens = count * rows
+    return pl.pallas_call(
+        functools.partial(ffn_forward_kernel, count),
+        grid=(steps,),
+        in_specs=[whole((rows, width))] * count + weight_specs(width, steps),
+        out_specs=[whole((rows, width))] * count,
+        out_shape=chunk_shapes(count, rows, width),
+        scratch_shapes=[pltpu.VMEM((tokens, width), BF16), pltpu.VMEM((tokens, width), F32)],
+        compiler_params=pltpu.CompilerParams(vmem_limit_bytes=VMEM_LIMIT),
+        cost_estimate=pl.CostEstimate(
+            flops=2 * tokens * width * 3 * TILE * steps,
+            bytes_accessed=2 * width * 3 * TILE * steps,
+            transcendentals=tokens * TILE * steps,
+        ),
+        name="ffn_forward",
+    )(*chunks, pack, pack)
+
+
+def ffn_backward_kernel(count, forward, core_ref, *refs):
+    x_refs, b_refs = refs[:count], refs[count : 2 * count]
+    gu_ref, dn_ref = refs[2 * count : 2 * count + 2]
+    place = 2 * count + 2
+    back_outs = refs[place : place + count]
+    place += count
+    if forward:
+        outs = refs[place : place + count]
+        place += count
+    keep_ref, side_ref = refs[place : place + 2]
+    scratch = refs[place + 2 :]
+    x_all, b_all, d_total = scratch[:3]
+    step = pl.program_id(0)
+    width = x_all.shape[1]
+
+    @pl.when(step == 0)
+    def _():
+        assemble(x_refs, x_all)
+        assemble(b_refs, b_all)
+        side_ref[:, :width] = x_all[...]
+        side_ref[:, width : 2 * width] = b_all[...]
+        d_total[...] = jnp.zeros_like(d_total)
+        if forward:
+            scratch[3][...] = jnp.zeros_like(scratch[3])
+
+    both = times(x_all[...], gu_ref[...])
+    gate, up = both[:, :TILE], both[:, TILE:]
+    d_active = times(b_all[...], dn_ref[...])
+    sigmoid = jax.nn.sigmoid(gate)
+    silu = gate * sigmoid
+    active = (silu * up).astype(BF16)
+    if forward:
+        scratch[3][...] += times_t(active, dn_ref[...])
+    d_gate = (d_active * up * (sigmoid * (1.0 + gate * (1.0 - sigmoid)))).astype(BF16)
+    d_up = (d_active * silu).astype(BF16)
+    d_total[...] += times_t(jnp.concatenate([d_gate, d_up], axis=1), gu_ref[...])
+    first = core_ref[0] == 0
+    half = TILE // 2
+    low, high = active[:, :half], active[:, half:]
+    start = pl.multiple_of(2 * width + step * (TILE + half), half)
+
+    @pl.when(first)
+    def _():
+        keep_ref[:, :TILE] = d_gate
+        keep_ref[:, TILE:] = low
+        side_ref[:, pl.ds(start, TILE)] = d_up
+        side_ref[:, pl.ds(start + TILE, half)] = high
+
+    @pl.when(jnp.logical_not(first))
+    def _():
+        keep_ref[:, :TILE] = d_up
+        keep_ref[:, TILE:] = high
+        side_ref[:, pl.ds(start, TILE)] = d_gate
+        side_ref[:, pl.ds(start + TILE, half)] = low
+
+    @pl.when(step == pl.num_programs(0) - 1)
+    def _():
+        spread(d_total[...], back_outs)
+        if forward:
+            spread(scratch[3][...], outs)
+
+
+def ffn_backward(core, chunks, back_chunks, pack, steps, forward):
+    count, (rows, width) = len(chunks), chunks[0].shape
+    tokens = count * rows
+    block = TILE + TILE // 2
+    ways = 2 if forward else 1
+    side_width = 2 * width + steps * block
+    results = pl.pallas_call(
+        functools.partial(ffn_backward_kernel, count, forward),
+        grid=(steps,),
+        in_specs=[pl.BlockSpec(memory_space=pltpu.SMEM)]
+        + [whole((rows, width))] * (2 * count)
+        + weight_specs(width, steps),
+        out_specs=[whole((rows, width))] * (ways * count)
+        + [pl.BlockSpec((tokens, block), lambda j: (0, j)), whole((tokens, side_width))],
+        out_shape=chunk_shapes(count, rows, width) * ways
+        + [
+            jax.ShapeDtypeStruct((tokens, steps * block), BF16),
+            jax.ShapeDtypeStruct((tokens, side_width), BF16),
+        ],
+        scratch_shapes=[pltpu.VMEM((tokens, width), BF16)] * 2
+        + [pltpu.VMEM((tokens, width), F32)] * ways,
+        compiler_params=pltpu.CompilerParams(vmem_limit_bytes=VMEM_LIMIT),
+        cost_estimate=pl.CostEstimate(
+            flops=2 * tokens * width * (4 + ways) * TILE * steps,
+            bytes_accessed=2 * width * 3 * TILE * steps + 4 * tokens * side_width,
+            transcendentals=tokens * TILE * steps,
+        ),
+        name="ffn_both" if forward else "ffn_backward",
+    )(core, *chunks, *back_chunks, pack, pack)
+    return results[:count], results[count : ways * count], results[-2], results[-1]
+
+
+def gradient_kernel(cut, whole_steps, *refs):
+    one_own, one_other, two_own, two_other, own_ref, other_ref = refs[:6]
+    out_ref, one_t, two_t = refs[-3:]
+    tokens = one_own.shape[0]
+    step = pl.program_id(0)
+
+    @pl.when(step == 0)
+    def _():
+        one_t[:, :tokens] = one_own[...].T
+        one_t[:, tokens:] = one_other[...].T
+        two_t[:, :tokens] = two_own[...].T
+        two_t[:, tokens:] = two_other[...].T
+
+    right = jnp.concatenate([own_ref[...], other_ref[...]], axis=0)
+    if whole_steps:
+
+        @pl.when(step < whole_steps)
+        def _():
+            out_ref[...] = times(one_t[...], right).astype(BF16)
+
+        @pl.when(step >= whole_steps)
+        def _():
+            out_ref[...] = times(two_t[...], right).astype(BF16)
+
+    else:
+        out_ref[:, :cut] = times(one_t[...], right[:, :cut]).astype(BF16)
+        out_ref[:, cut:] = times(two_t[...], right[:, cut:]).astype(BF16)
+
+
+def gradient(lefts, own, other, other_start, block, steps, cut, whole_steps, width, out_width, out_start, target):
+    tokens = own.shape[0]
+
+    def left_spec(index):
+        return pl.BlockSpec((tokens, width), lambda j: (0, index))
+
+    in_specs = [left_spec(index) for unused, index in lefts] + [
+        pl.BlockSpec((tokens, block), lambda j: (0, j)),
+        pl.BlockSpec((tokens, block), lambda j: (0, other_start + j)),
+    ]
+    operands = [array for array, unused in lefts] + [own, other]
+    aliases = {}
+    if target is not None:
+        in_specs.append(pl.BlockSpec(memory_space=pl.ANY))
+        operands.append(target)
+        aliases = {len(operands) - 1: 0}
+    return pl.pallas_call(
+        functools.partial(gradient_kernel, cut, whole_steps),
+        grid=(steps,),
+        in_specs=in_specs,
+        out_specs=pl.BlockSpec((width, block), lambda j: (0, out_start + j)),
+        out_shape=jax.ShapeDtypeStruct((width, out_width), BF16),
+        scratch_shapes=[pltpu.VMEM((width, 2 * tokens), BF16)] * 2,
+        input_output_aliases=aliases,
+        compiler_params=pltpu.CompilerParams(vmem_limit_bytes=VMEM_LIMIT),
+        cost_estimate=pl.CostEstimate(
+            flops=4 * tokens * width * block * steps,
+            bytes_accessed=2 * width * block * steps,
+            transcendentals=0,
+        ),
+        name="weight_gradient",
+    )(*operands)
+
+
+def reduce_gradient(partial):
+    core = lax.axis_index("core")
+    summed = lax.psum_scatter(partial, CHIP_AXES, scatter_dimension=0, tiled=True)
+    rows = summed.shape[0] // 2
+    mine = lax.dynamic_slice_in_dim(summed, core * rows, rows, 0)
+    other = swap_core(lax.dynamic_slice_in_dim(summed, (1 - core) * rows, rows, 0))
+    first = core == 0
+    return jnp.where(first, mine, other).astype(F32), jnp.where(first, other, mine).astype(F32)
+
+
+def ffn_gradients(low, high, steps, hidden):
+    depth = low.shape[0]
+    low = low.reshape(depth, steps, -1)
+    high = high.reshape(depth, steps, -1)
+    gate = low[:, :, :TILE].reshape(depth, -1)[:, :hidden]
+    up = high[:, :, :TILE].reshape(depth, -1)[:, :hidden]
+    down = jnp.concatenate([low[:, :, TILE:], high[:, :, TILE:]], axis=2)
+    return jnp.stack([gate, up], axis=1), down.reshape(depth, -1)[:, :hidden].T
+
+
+def halves(proj, out):
+    first = lax.axis_index("core") == 0
+    half = (proj.shape[1] + out.shape[1]) // 2
+    late = jnp.concatenate([proj[:, half:], out], axis=1)
+    early = proj[:, :half]
+    return jnp.where(first, early, late), jnp.where(first, late, early)
 
 
 def body(
@@ -214,50 +403,43 @@
     second_down,
 ):
     shards = lax.axis_size(TOKEN_AXES)
-    contexts = lax.axis_size("ctx")
+    contexts = lax.axis_size(CTX_AXES)
     members = lax.axis_size("tp")
     row_count, width = hidden_in.shape
     piece_rows = row_count // shards
+    part_rows = piece_rows // members
     chunk = row_count // members
     device = lax.axis_index(TOKEN_AXES)
     own = lax.axis_index("tp")
+    core = lax.axis_index("core")
+    core_ref = core.reshape(1).astype(jnp.int32)
     depth = mixer_gain.shape[0]
     channels = mixer_output.shape[0]
     hidden = first_down.shape[0]
     heads_width = attend_output.shape[0]
+    steps = -(-hidden // TILE)
+    padded = steps * TILE
+    ffn_width = 3 * padded
+    block = TILE + TILE // 2
+
+    def pack_ffn(gateup, down):
+        wide = jnp.pad(gateup, ((0, 0), (0, 0), (0, padded - hidden)))
+        wide = wide.reshape(depth, 2, steps, TILE).transpose(0, 2, 1, 3).reshape(depth, -1)
+        return [wide, jnp.pad(down.T, ((0, 0), (0, padded - hidden)))]
 
     first_pack = jnp.concatenate(
-        [
-            mixer_project.reshape(depth, -1),
-            mixer_output.T,
-            first_gateup.reshape(depth, -1),
-            first_down.T,
-        ],
+        pack_ffn(first_gateup, first_down) + [mixer_project.reshape(depth, -1), mixer_output.T],
         axis=1,
     )
     second_pack = jnp.concatenate(
-        [
-            attend_project,
-            attend_output.T,
-            second_gateup.reshape(depth, -1),
-            second_down.T,
-        ],
-        axis=1,
+        pack_ffn(second_gateup, second_down) + [attend_project, attend_output.T], axis=1
     )
     first_all = lax.all_gather(first_pack, TOKEN_AXES, axis=0, tiled=True)
     second_all = lax.all_gather(second_pack, TOKEN_AXES, axis=0, tiled=True)
-    cut = 3 * channels
-    project_a = first_all[:, :cut]
-    output_a_t = first_all[:, cut : cut + channels]
-    cut = cut + channels
-    gateup_f = first_all[:, cut : cut + 2 * hidden]
-    down_f_t = first_all[:, cut + 2 * hidden :]
-    cut = attend_project.shape[1]
-    project_b = second_all[:, :cut]
-    output_b_t = second_all[:, cut : cut + heads_width]
-    cut = cut + heads_width
-    gateup_s = second_all[:, cut : cut + 2 * hidden]
-    down_s_t = second_all[:, cut + 2 * hidden :]
+    project_a = first_all[:, ffn_width : ffn_width + 3 * channels]
+    output_a_t = first_all[:, ffn_width + 3 * channels :]
+    project_b = second_all[:, ffn_width : ffn_width + attend_project.shape[1]]
+    output_b_t = second_all[:, ffn_width + attend_project.shape[1] :]
 
     piece_table = deal_order.reshape(shards, shards, piece_rows)[:, :, 0]
     anchor = piece_table // row_count
@@ -267,28 +449,43 @@
     gains_row = jnp.concatenate(
         [mixer_gain, first_gain, attend_gain, second_gain, jnp.zeros((width - 4 * depth,), BF16)]
     )
+
+    def my_part(rows):
+        parts = rows.reshape(shards, members, part_rows, width)
+        return lax.dynamic_index_in_dim(parts, own, 1, keepdims=False)[send_piece]
+
     outgoing = jnp.concatenate(
         [
-            hidden_in.reshape(shards, piece_rows, width)[send_piece],
-            cotangent.reshape(shards, piece_rows, width)[send_piece],
-            jnp.broadcast_to(gains_row, (shards, 8, width)),
+            my_part(hidden_in),
+            my_part(cotangent),
+            jnp.broadcast_to(gains_row, (shards, 1, width)),
         ],
         axis=1,
     )
     arrived = lax.all_to_all(outgoing, TOKEN_AXES, split_axis=0, concat_axis=0, tiled=True)
-    tokens = arrived[:, :piece_rows][my_anchor].reshape(row_count, width)
-    back_s = arrived[:, piece_rows : 2 * piece_rows][my_anchor].reshape(row_count, width)
     gains = (
-        arrived[:, 2 * piece_rows, : 4 * depth]
+        arrived[:, 2 * part_rows, : 4 * depth]
         .reshape(shards, 4, depth)
         .transpose(1, 0, 2)
         .reshape(4, width)
         .astype(F32)
     )
     gain_a, gain_f, gain_b, gain_s = gains[0], gains[1], gains[2], gains[3]
+    parts = arrived[:, : 2 * part_rows][my_anchor].reshape(2 * shards * part_rows, width)
+    parts = jnp.concatenate(tp_gather(parts)).reshape(members, shards, 2, part_rows, width)
+    member_slot = (own - jnp.arange(members)) % members
+    parts = jnp.stack(
+        [lax.dynamic_index_in_dim(parts, member_slot[t], 0, keepdims=False) for t in range(members)],
+        axis=2,
+    )
+    tokens = parts[:, 0].reshape(row_count, width)
+    back_s = parts[:, 1].reshape(row_count, width)
     stream0 = lax.dynamic_slice_in_dim(tokens, own * chunk, chunk, 0).astype(F32)
     upstream = lax.dynamic_slice_in_dim(back_s, own * chunk, chunk, 0).astype(F32)
-    back_s = reorder(back_s)
+    back_s_chunks = [
+        lax.dynamic_slice_in_dim(back_s, (own - k) % members * chunk, chunk, 0)
+        for k in range(members)
+    ]
 
     kernel_taps = mixer_kernel.shape[0]
     halo = kernel_taps - 1
@@ -298,10 +495,10 @@
     )
     offsets = reorder(jnp.arange(row_count))
     segment, places = locate(seq_lengths, device * row_count + offsets)
-    ctx = lax.axis_index("ctx")
+    ctx = lax.axis_index(CTX_AXES)
     group_rows = jnp.concatenate(
         [
-            (lax.axis_index("fsdp") * contexts + (ctx ^ mask)) * row_count + offsets
+            (lax.axis_index(GROUP_AXES) * contexts + (ctx ^ mask)) * row_count + offsets
             for mask in range(contexts)
         ]
     )
@@ -315,8 +512,9 @@
 
     kernel_local = lax.dynamic_slice_in_dim(mixer_kernel, own * channels, channels, 1).astype(F32)
     mixer_in = norm_rows(tokens.astype(F32), gain_a).astype(BF16)
+    mixer_in_other = swap_core(mixer_in)
     halo_pad = 16
-    halo_in = from_behind(mixer_in[row_count - halo_pad :], "ctx", 1)
+    halo_in = from_behind(mixer_in[row_count - halo_pad :], 1)
     proj_a = times(jnp.concatenate([halo_in, mixer_in]), project_a)
     proj_b_part = proj_a[:, :channels]
     proj_c_part = proj_a[halo_pad:, channels : 2 * channels]
@@ -324,8 +522,10 @@
     extended = (proj_b_part * proj_x_part)[halo_pad - halo :].astype(BF16).astype(F32)
     conv_out = shortconv(extended, kernel_local, halo_segment)
     gated_rows = reorder((proj_c_part * conv_out).astype(BF16))
-    stream1 = stream0 + tp_reduce(times_t(gated_rows, output_a_t).astype(BF16))
-    stream2, kept_first = ffn_forward(stream1, gain_f, gateup_f, down_f_t)
+    stream1 = stream0 + tp_reduce(tp_chunks(times_t(gated_rows, output_a_t)))
+
+    normed_f = tp_gather(norm_rows(stream1, gain_f).astype(BF16))
+    stream2 = stream1 + tp_reduce(ffn_forward(normed_f, first_all, steps))
 
     groups = H // KVH
     score_scale = HD ** (-0.5)
@@ -338,7 +538,7 @@
             rotate(norm_rows(key_in, gain_k), cosine, sine),
         )
 
-    attend_in = tp_gather(norm_rows(stream2, gain_b).astype(BF16))
+    attend_in = jnp.concatenate(tp_gather(norm_rows(stream2, gain_b).astype(BF16)))
     proj_b = times(attend_in, project_b).reshape(row_count, -1, groups + 2, HD)
     kv_heads = proj_b.shape[1]
     query_raw = proj_b[:, :, :groups]
@@ -373,13 +573,29 @@
         .astype(BF16)
         .reshape(row_count, -1)
     )
-    stream3 = stream2 + tp_reduce(times_t(attended, output_b_t).astype(BF16))
-    stream4, kept_second = ffn_forward(stream3, gain_s, gateup_s, down_s_t)
-
-    d_stream3, gain_s_grad, gate_s_grad, up_s_grad, down_s_grad = ffn_backward(
-        stream3, kept_second, gain_s, gateup_s, down_s_t, upstream, back_s, True
-    )
-    back_b = tp_gather(d_stream3.astype(BF16))
+    stream3 = stream2 + tp_reduce(tp_chunks(times_t(attended, output_b_t)))
+
+    normed_s = tp_gather(norm_rows(stream3, gain_s).astype(BF16))
+    d_chunks, out_chunks, keep, side = ffn_backward(
+        core_ref, normed_s, back_s_chunks, second_all, steps, True
+    )
+    unused, pullback = jax.vjp(norm_rows, stream3, gain_s)
+    d_stream, gain_s_grad = pullback(tp_reduce(d_chunks))
+    d_stream3 = upstream + d_stream
+    stream4 = stream3 + tp_reduce(out_chunks)
+    side_other = swap_core(side)
+    ffn_lefts = [(side, 0), (side_other, 0), (side, 1), (side_other, 1)]
+    ffn_cols = steps * block
+    side_start = 2 * width // block
+    second_grads = reduce_gradient(
+        gradient(
+            ffn_lefts, keep, side_other, side_start, block, steps, TILE, 0, width, ffn_cols, 0, None
+        )
+    )
+
+    back_b = jnp.concatenate(tp_gather(d_stream3.astype(BF16)))
+    back_b_other = swap_core(back_b)
+    attend_in_other = swap_core(attend_in)
     d_attended_b = times(back_b, output_b_t).astype(BF16).reshape(row_count, -1, groups, HD)
     scores_again = (
         jnp.einsum("tkgd,nkd->kgtn", query_b, key_all, preferred_element_type=F32) * score_scale
@@ -413,18 +629,64 @@
         .astype(BF16)
         .reshape(row_count, -1)
     )
-    d_attend_in = tp_reduce(times_t(d_proj_b, project_b).astype(BF16))
+    d_attend_in = tp_reduce(tp_chunks(times_t(d_proj_b, project_b)))
     unused, pullback = jax.vjp(norm_rows, stream2, gain_b)
     d_norm_b, gain_b_grad = pullback(d_attend_in)
     d_stream2 = d_stream3 + d_norm_b
-    project_b_grad = reduce_gradient(left_blocks(pair(attend_in), False), pair(d_proj_b), False)
-    output_b_grad = reduce_gradient(left_blocks(pair(back_b), False), pair(attended), False)
+    keep, send = halves(d_proj_b, attended)
+    first_core = core == 0
+    attend_cols = keep.shape[1]
+    small_tile = 2 * (heads_width + attend_project.shape[1]) // 16
+    third = gradient(
+        [
+            (attend_in, 0),
+            (attend_in_other, 0),
+            (jnp.where(first_core, attend_in, back_b), 0),
+            (jnp.where(first_core, attend_in_other, back_b_other), 0),
+        ],
+        keep,
+        swap_core(send),
+        0,
+        small_tile,
+        attend_cols // small_tile,
+        0,
+        (attend_project.shape[1] - attend_cols) // small_tile,
+        width,
+        ffn_cols + attend_cols,
+        ffn_cols // small_tile,
+        None,
+    )
 
     back_f = tp_gather(d_stream2.astype(BF16))
-    d_stream1, gain_f_grad, gate_f_grad, up_f_grad, down_f_grad = ffn_backward(
-        stream1, kept_first, gain_f, gateup_f, down_f_t, d_stream2, back_f, False
-    )
-    back_a = tp_gather(d_stream1.astype(BF16))
+    d_chunks, unused, keep, side = ffn_backward(
+        core_ref, normed_f, back_f, first_all, steps, False
+    )
+    unused, pullback = jax.vjp(norm_rows, stream1, gain_f)
+    d_stream, gain_f_grad = pullback(tp_reduce(d_chunks))
+    d_stream1 = d_stream2 + d_stream
+    side_other = swap_core(side)
+    ffn_lefts = [(side, 0), (side_other, 0), (side, 1), (side_other, 1)]
+    low, high = reduce_gradient(
+        gradient(
+            ffn_lefts,
+            keep,
+            side_other,
+            side_start,
+            block,
+            steps,
+            TILE,
+            0,
+            width,
+            ffn_cols + attend_cols,
+            0,
+            third,
+        )
+    )
+    first_grads = (low[:, :ffn_cols], high[:, :ffn_cols])
+    attend_grads = jnp.concatenate([low[:, ffn_cols:], high[:, ffn_cols:]], axis=1)
+
+    back_a = jnp.concatenate(tp_gather(d_stream1.astype(BF16)))
+    back_a_other = swap_core(back_a)
     d_gated = reorder(times(back_a, output_a_t))
     d_cgate = d_gated * conv_out
     d_conv = d_gated * proj_c_part
@@ -434,7 +696,7 @@
         kernel_local,
     )
     d_extended, kernel_grad = pullback(d_conv)
-    returned = from_behind(d_extended[:halo], "ctx", -1)
+    returned = from_behind(d_extended[:halo], -1)
     d_product = d_extended[halo:] + jnp.concatenate(
         [jnp.zeros((row_count - halo, channels), F32), returned]
     )
@@ -446,12 +708,34 @@
         ],
         axis=1,
     ).astype(BF16)
-    d_mixer_in = tp_reduce(times_t(reorder(d_proj_a), project_a).astype(BF16))
+    d_mixer_in = tp_reduce(tp_chunks(times_t(reorder(d_proj_a), project_a)))
     unused, pullback = jax.vjp(norm_rows, stream0, gain_a)
     d_norm_a, gain_a_grad = pullback(d_mixer_in)
     d_stream0 = d_stream1 + d_norm_a
-    project_a_grad = reduce_gradient(left_blocks(pair(mixer_in), True), pair(d_proj_a), True)
-    output_a_grad = reduce_gradient(left_blocks(pair(back_a), False), pair(gated_rows), False)
+    keep, send = halves(d_proj_a, gated_rows)
+    mixer_cols = keep.shape[1]
+    low, high = reduce_gradient(
+        gradient(
+            [
+                (mixer_in, 0),
+                (mixer_in_other, 0),
+                (jnp.where(first_core, mixer_in, back_a), 0),
+                (jnp.where(first_core, mixer_in_other, back_a_other), 0),
+            ],
+            keep,
+            swap_core(send),
+            0,
+            mixer_cols,
+            1,
+            3 * channels - mixer_cols,
+            0,
+            width,
+            mixer_cols,
+            0,
+            None,
+        )
+    )
+    mixer_grads = jnp.concatenate([low, high], axis=1)
 
     slot_for_anchor = jnp.sum(
         jnp.where(
@@ -467,7 +751,8 @@
     )
     pieces = shards // members
     slot_place = (own - slot_for_anchor // pieces) % members * pieces + slot_for_anchor % pieces
-    out_rows = tp_gather(stream4.astype(BF16)).reshape(shards, piece_rows, width)[slot_place]
+    out_rows = jnp.concatenate(tp_gather(stream4.astype(BF16)))
+    out_rows = out_rows.reshape(shards, piece_rows, width)[slot_place]
     out_home = lax.all_to_all(out_rows, TOKEN_AXES, split_axis=0, concat_axis=0, tiled=True)
     layer_out = out_home[dest_for_piece].reshape(row_count, width)
 
@@ -486,7 +771,9 @@
         ]
         + [jnp.zeros((width,), F32)] * 10
     )
-    last = tp_gather(jnp.concatenate([d_stream0.astype(BF16), small.astype(BF16)]))
+    last = jnp.concatenate(
+        tp_gather(jnp.concatenate([d_stream0.astype(BF16), small.astype(BF16)]))
+    )
     last = last.reshape(members, chunk + 16, width)
     grad_rows = last[:, :chunk].reshape(shards, piece_rows, width)[slot_place]
     smalls = last[:, chunk:].astype(F32)
@@ -520,28 +807,33 @@
     qgain_total = totals[kernel_end : kernel_end + HD]
     kgain_total = totals[kernel_end + HD : kernel_end + 2 * HD]
 
+    gateup_s_grad, down_s_grad = ffn_gradients(*second_grads, steps, hidden)
+    gateup_f_grad, down_f_grad = ffn_gradients(*first_grads, steps, hidden)
+    proj_cols = attend_project.shape[1]
     return (
         layer_out,
         input_gradient,
         gain_totals[0],
-        project_a_grad.reshape(depth, 3, channels),
+        mixer_grads[:, : 3 * channels].reshape(depth, 3, channels),
         kernel_total,
-        output_a_grad.T,
+        mixer_grads[:, 3 * channels :].T,
         gain_totals[1],
-        jnp.stack([gate_f_grad, up_f_grad], axis=1),
-        down_f_grad.T,
+        gateup_f_grad,
+        down_f_grad,
         gain_totals[2],
-        project_b_grad,
+        attend_grads[:, :proj_cols],
         qgain_total,
         kgain_total,
-        output_b_grad.T,
+        attend_grads[:, proj_cols:].T,
         gain_totals[3],
-        jnp.stack([gate_s_grad, up_s_grad], axis=1),
-        down_s_grad.T,
+        gateup_s_grad,
+        down_s_grad,
     )
 
 
 def solution(mesh):
+    names = TOKEN_AXES + ("tp",)
+    rings = mesh.shape["fsdp"] // 2, 2, mesh.shape["ctx"] // 2, 2, mesh.shape["tp"]
     tokens = P(TOKEN_AXES, None)
     rows = P(TOKEN_AXES)
     three = P(TOKEN_AXES, None, "tp")
@@ -549,7 +841,7 @@
     turned = P("tp", TOKEN_AXES)
     return jax.shard_map(
         body,
-        mesh=mesh,
+        mesh=Mesh(mesh.devices.reshape(rings), names),
         in_specs=(
             tokens, tokens, P(), P(),
             rows, three, P(), turned,

time: 878 us -> 701 us (0.80)
  matrix products: 188 us -> 37.1 us
  starting transfers between devices: 225 us -> 108 us
  waiting for transfers between devices: 251 us -> 338 us
  Pallas kernels: 0 us -> 72.8 us
  local copies, waits for them, and re-layouts: 112 us -> 64.8 us
  other arithmetic: 69.8 us -> 45.6 us
    dot_general x50 -> x4, matrix products: 144 us -> 10.3 us  [times(): lax.dot_general(left, right, (((1,), (0,)), ((), ())), preferred_element_...]
    ppermute x86 -> x19, starting transfers between devices: 148 us -> 17.3 us  [the longest x11 7.76 us: swap_core(): return lax.ppermute(block, 'core', [(0, 1), (1, 0)])]
    reduce_scatter x0 -> x3, waiting for transfers between devices: none -> 114 us  [reduce_gradient(): lax.psum_scatter(partial, CHIP_AXES, scatter_dimension=0, tiled=True)]
    pallas_call x0 -> x7, Pallas kernels: none -> 72.8 us  [the longest x4 31.4 us: gradient(): pl.pallas_call(functools.partial(gradient_kernel, cut, whole_steps), grid...]
    ppermute x48 -> x51, waiting for transfers between devices: 54.7 us -> 108 us  [shift_tp(): lax.ppermute(block, 'tp', [(i, (i + distance) % members) for i in range(m...]
    all_gather x1, waiting for transfers between devices: 69 us -> 16.1 us  [body(): second_all = lax.all_gather(second_pack, TOKEN_AXES, axis=0, tiled=True)]
    ppermute x86 -> x19, waiting for transfers between devices: 72.8 us -> 20 us  [the longest x6 10.1 us: swap_ctx(): lax.ppermute(block, CTX_AXES, [(i, i ^ mask) for i in range(lax.axis_size...]
    all_to_all x1, waiting for transfers between devices: 0.01 us -> 27.6 us  [body(): lax.all_to_all(jnp.concatenate([grad_rows, small_rows.reshape(shards, 4,...]
  transfers between devices with their start and end apart: 139 -> 78, of which waited for: 42 -> 45; matrix products, arithmetic and copies ran while one was open for 37% -> 12% of each run, Pallas kernels for 0% -> 6%
where the time goes in v2:
time: 701 us; the launch traced here: 692 us
  waiting for transfers between devices  338 us (48%)
  starting transfers between devices  108 us (15%)
  Pallas kernels  72.8 us (10%)
  local copies, waits for them, and re-layouts  64.8 us (9%)
  other arithmetic  45.6 us (7%)
  matrix products  37.1 us (5%)
  between operations  25.8 us (4%)
    reduce_scatter x3, waiting for transfers between devices, reduce_gradient(): lax.psum_scatter(partial, CHIP_AXES, scatter_dimension=0, tiled=True)  114 us
    ppermute x51, waiting for transfers between devices, shift_tp(): lax.ppermute(block, 'tp', [(i, (i + distance) % members) for i in range(m...  108 us
    ppermute x51, starting transfers between devices, shift_tp(): lax.ppermute(block, 'tp', [(i, (i + distance) % members) for i in range(m...  65.8 us
    pallas_call x4, Pallas kernels, gradient(): pl.pallas_call(functools.partial(gradient_kernel, cut, whole_steps), grid...  31.4 us
    pallas_call x2, Pallas kernels, ffn_backward(): pl.pallas_call(functools.partial(ffn_backward_kernel, count, forward), gr...  30.1 us
    all_to_all x1, waiting for transfers between devices, body(): lax.all_to_all(jnp.concatenate([grad_rows, small_rows.reshape(shards, 4,...  27.6 us
    all_gather x1, waiting for transfers between devices, body(): first_all = lax.all_gather(first_pack, TOKEN_AXES, axis=0, tiled=True)  21 us
    unnamed x332, local copies, waits for them, and re-layouts  19.6 us
  transfers between devices with their start and end apart: 78, of which 45 were waited for; matrix products, arithmetic and copies ran while one was open for 12% of the time, Pallas kernels for 6%

profile of v2, /device:TPU:1, one launch (start us, length us, event | category | flops | bytes accessed | tf_op | source)
XLA Modules:
  0.0 692.3 jit_solution(3861287965820185103)
XLA Ops:
  19.8 9.4 %all-to-all-start = ((bf16[32,5,1536]{2,1,0:T(8,128)(2,1)}), bf16[32,5,1536]{2,1,0:T(8,128)(2,1)S(1)}, u32[]{:S(2)}, u32[]{:S(2)}) async-start(bf16[32,5,1536]{2,1,0:T(8,128)(2,1)} %pad_maximum_fusion.4), calls=%async_computation | async-start | bytes 1572864 | tf_op jit(solution)/shard_map/all_to_all | solution.py:465
  34.2 15.4 %all-to-all-done = bf16[32,5,1536]{2,1,0:T(8,128)(2,1)S(1)} async-done(((bf16[32,5,1536]{2,1,0:T(8,128)(2,1)}), bf16[32,5,1536]{2,1,0:T(8,128)(2,1)S(1)}, u32[]{:S(2)}, u32[]{:S(2)}) %all-to-all-start) | async-done | bytes 491552 | tf_op jit(solution)/shard_map/all_to_all | solution.py:465
  65.3 5.0 collective-permute-done.2
  70.3 4.1 collective-permute-done
  84.3 21.0 %all-gather.3.cloned.1.call-done.refs_4_.refs_5_.refs_8_.refs_9_ = bf16[1536,6912]{1,0:T(8,128)(2,1)} async-done(((bf16[48,6912]{1,0:T(8,128)(2,1)}), bf16[1536,6912]{1,0:T(8,128)(2,1)}) %all-gather.3.cloned.1.call-update) | async-done | bytes 21233680 | tf_op jit(solution)/shard_map/all_gather | solution.py:437
  105.3 3.2 fusion.14
  110.4 3.1 fusion.147
  121.1 5.2 collective-permute-done.5
  134.8 5.9 collective-permute-done.8.refs_2_
  140.7 11.3 %ffn_forward.1 = (f32[64,1536]{1,0:T(8,128)S(1)}, bf16[64,1536]{1,0:T(8,128)(2,1)S(1)}, bf16[64,1536]{1,0:T(8,128)(2,1)S(1)}, bf16[64,1536]{1,0:T(8,128)(2,1)S(1)}) custom-call(bf16[64,1536]{1,0:T(8,128)(2,1)S(1)} %multiply_convert_fusion.4.refs_0_, bf16[64,1536]{1,0:T(8,128)(2,1)S(1)} %collective-permute-done.7.refs_1_, ...), custom_call_target="tpu_custom_call" | custom-call | flops 4227858432 | bytes 16515072 | tf_op jit(solution)/shard_map/ffn_forward/pallas_call | solution.py:182
  158.7 4.2 collective-permute-done.11
  164.9 3.6 collective-permute-start.15
  170.9 16.1 %all-gather.5.cloned.1.call-done.refs_8_.refs_9_ = bf16[1536,6400]{1,0:T(8,128)(2,1)} async-done(((bf16[48,6400]{1,0:T(8,128)(2,1)}), bf16[1536,6400]{1,0:T(8,128)(2,1)}) %all-gather.5.cloned.1.call-update) | async-done | bytes 19660816 | tf_op jit(solution)/shard_map/all_gather | solution.py:438
  204.6 3.1 fusion.148
  228.4 6.1 collective-permute-done.23.refs_2_
  234.5 14.9 %ffn_both.1 = (f32[64,1536]{1,0:T(8,128)S(1)}, bf16[64,1536]{1,0:T(8,128)(2,1)S(1)}, bf16[64,1536]{1,0:T(8,128)(2,1)S(1)}, bf16[64,1536]{1,0:T(8,128)(2,1)S(1)},...) custom-call(s32[1]{0:T(128)} %bitcast.38.core_ref, ...), custom_call_target="tpu_custom_call" | custom-call | flops 8455716864 | bytes 22413312 | tf_op jit(solution)/shard_map/ffn_both/pallas_call | solution.py:267
  256.2 4.8 collective-permute-done.32
  263.9 3.6 collective-permute-start.36
  269.0 3.2 collective-permute-done.36
  273.7 6.2 collective-permute-done.34
  284.1 4.9 fusion
  289.1 4.2 fusion.8
  293.2 4.5 fusion.2
  317.4 6.5 collective-permute-done.42
  324.4 7.8 %collective-permute-done.27 = bf16[64,1536]{1,0:T(8,128)(2,1)S(1)} collective-permute-done((bf16[64,1536]{1,0:T(8,128)(2,1)S(1)}, bf16[64,1536]{1,0:T(8,128)(2,1)S(1)}, u32[]{:S(2)}, u32[]{:S(2)}) %collective-permute-start.27) | collective-permute-done | bytes 196640 | tf_op jit(solution)/shard_map/ppermute | solution.py:89
  335.5 2.9 collective-permute-start.44
  340.6 6.0 collective-permute-done.44.refs_6_
  346.6 15.2 %ffn_backward.1 = (f32[64,1536]{1,0:T(8,128)S(1)}, bf16[64,1536]{1,0:T(8,128)(2,1)S(1)}, bf16[64,1536]{1,0:T(8,128)(2,1)S(1)}, bf16[64,1536]{1,0:T(8,128)(2,1)S(...) custom-call(s32[1]{0:T(128)} %bitcast.38.core_ref, bf16[64,1536]{1,0:T(8,128)(2,1)S(1)} %multiply_convert_fusion.4.refs_0_, ...), custom_call_target="tpu_custom_call" | custom-call | flops 7046430720 | bytes 22413312 | tf_op jit(solution)/shard_map/ffn_backward/pallas_call | solution.py:267
  363.1 3.0 collective-permute-start.47
  368.4 6.3 collective-permute-done.47
  380.4 6.2 collective-permute-done.51
  386.6 3.9 collective-permute-done.49
  394.9 2.9 collective-permute-start.52
  402.9 3.3 weight_gradient.4
  406.6 5.2 collective-permute-done.68.refs_1_.refs_3_.refs_5_
  414.8 11.2 %weight_gradient.7 = bf16[1536,2688]{1,0:T(8,128)(2,1)} custom-call(bf16[256,5760]{1,0:T(8,128)(2,1)S(1)} %copy-done, bf16[256,5760]{1,0:T(8,128)(2,1)} %copy-done.10, bf16[256,5760]{1,0:T(8,128)(2,1)S(1)} %copy-done, bf16[256,5760]{1,0:T(8,128)(2,1)} %copy-done.10, bf16[256,2688]{1,0:T(8,128)(2,1)S(1)} %copy-done.8, bf16[256,5760]{1,0:T(8,128)(2,1)} %copy-done.10), custom_call_target="tpu_custom_call" | custom-call | flops 4227858432 | bytes 8257536 | tf_op jit(solution)/shard_map/weight_gradient/pallas_call | solution.py:338
  428.0 2.9 pad_maximum_fusion.6
  437.9 5.8 weight_gradient.5.refs_6_
  443.7 11.2 %weight_gradient.6 = bf16[1536,3200]{1,0:T(8,128)(2,1)} custom-call(bf16[256,5760]{1,0:T(8,128)(2,1)S(1)} %copy-done.1, bf16[256,5760]{1,0:T(8,128)(2,1)} %collective-permute-done.63.refs_1_.refs_3_.refs_5_, bf16[256,5760]{1,0:T(8,128)(2,1)S(1)} %copy-done.1, ...), custom_call_target="tpu_custom_call", output_to_operand_aliasing={{}: (6, {})} | custom-call | flops 4227858432 | bytes 8257536 | tf_op jit(solution)/shard_map/weight_gradient/pallas_call | solution.py:338
  456.6 4.5 fusion.150
  466.7 9.7 %collective-permute-done.55 = bf16[64,1536]{1,0:T(8,128)(2,1)S(1)} collective-permute-done((bf16[64,1536]{1,0:T(8,128)(2,1)S(1)}, bf16[64,1536]{1,0:T(8,128)(2,1)S(1)}, u32[]{:S(2)}, u32[]{:S(2)}) %collective-permute-start.55) | collective-permute-done | bytes 196640 | tf_op jit(solution)/shard_map/ppermute | solution.py:89
  478.5 3.8 collective-permute-start.57
  484.9 10.7 %all-to-all-start.1 = ((bf16[32,8,1536]{2,1,0:T(8,128)(2,1)}), bf16[32,8,1536]{2,1,0:T(8,128)(2,1)S(1)}, u32[]{:S(2)}, u32[]{:S(2)}) async-start(bf16[32,8,1536]{2,1,0:T(8,128)(2,1)} %gather_fusion.3), calls=%async_computation.1 | async-start | bytes 1572864 | tf_op jit(solution)/shard_map/all_to_all | solution.py:756
  499.4 15.1 %all-to-all-done.1 = bf16[32,8,1536]{2,1,0:T(8,128)(2,1)S(1)} async-done(((bf16[32,8,1536]{2,1,0:T(8,128)(2,1)}), bf16[32,8,1536]{2,1,0:T(8,128)(2,1)S(1)}, u32[]{:S(2)}, u32[]{:S(2)}) %all-to-all-start.1) | async-done | bytes 786464 | tf_op jit(solution)/shard_map/all_to_all | solution.py:756
  514.5 5.0 all-to-all-start.2
  521.0 27.6 %all-to-all-done.2 = bf16[32,12,1536]{2,1,0:T(8,128)(2,1)S(1)} async-done(((bf16[32,12,1536]{2,1,0:T(8,128)(2,1)}), bf16[32,12,1536]{2,1,0:T(8,128)(2,1)S(1)}, u32[]{:S(2)}, u32[]{:S(2)}) %all-to-all-start.2) | async-done | bytes 1179680 | tf_op jit(solution)/shard_map/all_to_all | solution.py:795
  553.9 30.1 %reduce-scatter.8.cloned.1.call-done = bf16[96,2688]{1,0:T(8,128)(2,1)} async-done(((bf16[1536,2688]{1,0:T(8,128)(2,1)}), bf16[96,2688]{1,0:T(8,128)(2,1)}) %reduce-scatter.8.cloned.1.call-update) | async-done | bytes 516112 | tf_op jit(solution)/shard_map/reduce_scatter | solution.py:358
  591.1 84.3 %reduce-scatter.6.cloned.1.call-done = bf16[96,3200]{1,0:T(8,128)(2,1)} async-done(((bf16[1536,3200]{1,0:T(8,128)(2,1)}), bf16[96,3200]{1,0:T(8,128)(2,1)}) %reduce-scatter.6.cloned.1.call-update) | async-done | bytes 614416 | tf_op jit(solution)/shard_map/reduce_scatter | solution.py:358
  (735 shorter events, 212.4 us)
Async XLA Ops:
  7.2 98.1 %all-gather.3.cloned.1.call-start = ((), (), s32[]{:S(2)}) async-start(), calls=%async_computation.6 | async-start | bytes 21897216 | tf_op jit(solution)/shard_map/all_gather | solution.py:437
  11.2 175.8 %all-gather.5.cloned.1.call-start = ((), (), s32[]{:S(2)}) async-start(), calls=%async_computation.7 | async-start | bytes 20275200 | tf_op jit(solution)/shard_map/all_gather | solution.py:438
  19.8 29.8 %all-to-all-start = ((bf16[32,5,1536]{2,1,0:T(8,128)(2,1)}), bf16[32,5,1536]{2,1,0:T(8,128)(2,1)S(1)}, u32[]{:S(2)}, u32[]{:S(2)}) async-start(bf16[32,5,1536]{2,1,0:T(8,128)(2,1)} %pad_maximum_fusion.4), calls=%async_computation | async-start | bytes 1572864 | tf_op jit(solution)/shard_map/all_to_all | solution.py:465
  29.2 520.2 %reduce-scatter.4.cloned.1.call-start = ((), (), s32[]{:S(2)}) async-start(), calls=%async_computation.8 | async-start | bytes 2506752 | tf_op jit(solution)/shard_map/reduce_scatter | solution.py:358
  50.7 19.5 %collective-permute-start.2 = (bf16[128,1536]{1,0:T(8,128)(2,1)S(1)}, bf16[128,1536]{1,0:T(8,128)(2,1)S(1)}, u32[]{:S(2)}, u32[]{:S(2)}) collective-permute-start(bf16[128,1536]{1,0:T(8,128)(2,1)S(1)} %reshape.845), channel_id=1, source_target_pairs={{0,3},{1,0},{2,1},{3,2},{4,7},{5,4},{6,5},{7,6},{8,11},{9,8},{10,9... | collective-permute-start | bytes 1179656 | tf_op jit(solution)/shard_map/ppermute | solution.py:89
  53.3 17.0 %collective-permute-start.1 = (bf16[128,1536]{1,0:T(8,128)(2,1)S(1)}, bf16[128,1536]{1,0:T(8,128)(2,1)S(1)}, u32[]{:S(2)}, u32[]{:S(2)}) collective-permute-start(bf16[128,1536]{1,0:T(8,128)(2,1)S(1)} %reshape.845), channel_id=1, source_target_pairs={{0,2},{1,3},{2,0},{3,1},{4,6},{5,7},{6,4},{7,5},{8,10},{9,11},{10,... | collective-permute-start | bytes 1179656 | tf_op jit(solution)/shard_map/ppermute | solution.py:89
  53.8 20.5 %collective-permute-start = (bf16[128,1536]{1,0:T(8,128)(2,1)S(1)}, bf16[128,1536]{1,0:T(8,128)(2,1)S(1)}, u32[]{:S(2)}, u32[]{:S(2)}) collective-permute-start(bf16[128,1536]{1,0:T(8,128)(2,1)S(1)} %reshape.845), channel_id=1, source_target_pairs={{0,1},{1,2},{2,3},{3,0},{4,5},{5,6},{6,7},{7,4},{8,9},{9,10},{10,1... | collective-permute-start | bytes 1179656 | tf_op jit(solution)/shard_map/ppermute | solution.py:89
  114.8 11.4 %collective-permute-start.5 = (bf16[64,1536]{1,0:T(8,128)(2,1)S(1)}, bf16[64,1536]{1,0:T(8,128)(2,1)S(1)}, u32[]{:S(2)}, u32[]{:S(2)}) collective-permute-start(bf16[64,1536]{1,0:T(8,128)(2,1)S(1)} %get-tuple-element.241), channel_id=1, source_target_pairs={{0,2},{1,3},{2,0},{3,1},{4,6},{5,7},{6,4},{7,5},{8,10},{9,11},{10,... | collective-permute-start | bytes 589832 | tf_op jit(solution)/shard_map/ppermute | solution.py:89
  117.2 9.0 %collective-permute-start.4 = (bf16[64,1536]{1,0:T(8,128)(2,1)S(1)}, bf16[64,1536]{1,0:T(8,128)(2,1)S(1)}, u32[]{:S(2)}, u32[]{:S(2)}) collective-permute-start(bf16[64,1536]{1,0:T(8,128)(2,1)S(1)} %get-tuple-element.239), channel_id=1, source_target_pairs={{0,3},{1,0},{2,1},{3,2},{4,7},{5,4},{6,5},{7,6},{8,11},{9,8},{10,9... | collective-permute-start | bytes 589832 | tf_op jit(solution)/shard_map/ppermute | solution.py:89
  129.2 11.5 %collective-permute-start.8 = (bf16[64,1536]{1,0:T(8,128)(2,1)S(1)}, bf16[64,1536]{1,0:T(8,128)(2,1)S(1)}, u32[]{:S(2)}, u32[]{:S(2)}) collective-permute-start(bf16[64,1536]{1,0:T(8,128)(2,1)S(1)} %multiply_convert_fusion.4.refs_0_), channel_id=1, source_target_pairs={{0,2},{1,3},{2,0},{3,1},{4,6},{5,7},{6,4},{7,5},{8,10},{9,11},{10,... | collective-permute-start | bytes 589832 | tf_op jit(solution)/shard_map/ppermute | solution.py:89
  132.0 8.7 %collective-permute-start.9 = (bf16[64,1536]{1,0:T(8,128)(2,1)S(1)}, bf16[64,1536]{1,0:T(8,128)(2,1)S(1)}, u32[]{:S(2)}, u32[]{:S(2)}) collective-permute-start(bf16[64,1536]{1,0:T(8,128)(2,1)S(1)} %multiply_convert_fusion.4.refs_0_), channel_id=1, source_target_pairs={{0,3},{1,0},{2,1},{3,2},{4,7},{5,4},{6,5},{7,6},{8,11},{9,8},{10,9... | collective-permute-start | bytes 589832 | tf_op jit(solution)/shard_map/ppermute | solution.py:89
  153.8 9.2 %collective-permute-start.11 = (bf16[64,1536]{1,0:T(8,128)(2,1)S(1)}, bf16[64,1536]{1,0:T(8,128)(2,1)}, u32[]{:S(2)}, u32[]{:S(2)}) collective-permute-start(bf16[64,1536]{1,0:T(8,128)(2,1)S(1)} %get-tuple-element.39), channel_id=1, source_target_pairs={{0,2},{1,3},{2,0},{3,1},{4,6},{5,7},{6,4},{7,5},{8,10},{9,11},{10,... | collective-permute-start | bytes 589832 | tf_op jit(solution)/shard_map/ppermute | solution.py:89
  164.9 22.1 %collective-permute-start.15 = (bf16[64,1536]{1,0:T(8,128)(2,1)S(1)}, bf16[64,1536]{1,0:T(8,128)(2,1)S(1)}, u32[]{:S(2)}, u32[]{:S(2)}) collective-permute-start(bf16[64,1536]{1,0:T(8,128)(2,1)S(1)} %multiply_convert_fusion.3), channel_id=1, source_target_pairs={{0,3},{1,0},{2,1},{3,2},{4,7},{5,4},{6,5},{7,6},{8,11},{9,8},{10,9... | collective-permute-start | bytes 589832 | tf_op jit(solution)/shard_map/ppermute | solution.py:89
  168.4 18.6 %collective-permute-start.14 = (bf16[64,1536]{1,0:T(8,128)(2,1)S(1)}, bf16[64,1536]{1,0:T(8,128)(2,1)S(1)}, u32[]{:S(2)}, u32[]{:S(2)}) collective-permute-start(bf16[64,1536]{1,0:T(8,128)(2,1)S(1)} %multiply_convert_fusion.3), channel_id=1, source_target_pairs={{0,2},{1,3},{2,0},{3,1},{4,6},{5,7},{6,4},{7,5},{8,10},{9,11},{10,... | collective-permute-start | bytes 589832 | tf_op jit(solution)/shard_map/ppermute | solution.py:89
  170.0 17.1 %collective-permute-start.13 = (bf16[64,1536]{1,0:T(8,128)(2,1)S(1)}, bf16[64,1536]{1,0:T(8,128)(2,1)S(1)}, u32[]{:S(2)}, u32[]{:S(2)}) collective-permute-start(bf16[64,1536]{1,0:T(8,128)(2,1)S(1)} %multiply_convert_fusion.3), channel_id=1, source_target_pairs={{0,1},{1,2},{2,3},{3,0},{4,5},{5,6},{6,7},{7,4},{8,9},{9,10},{10,1... | collective-permute-start | bytes 589832 | tf_op jit(solution)/shard_map/ppermute | solution.py:89
  208.5 10.2 %collective-permute-start.21 = (bf16[64,1536]{1,0:T(8,128)(2,1)}, bf16[64,1536]{1,0:T(8,128)(2,1)}, u32[]{:S(2)}, u32[]{:S(2)}) collective-permute-start(bf16[64,1536]{1,0:T(8,128)(2,1)} %get-tuple-element.237), channel_id=1, source_target_pairs={{0,1},{1,2},{2,3},{3,0},{4,5},{5,6},{6,7},{7,4},{8,9},{9,10},{10,1... | collective-permute-start | bytes 589832 | tf_op jit(solution)/shard_map/ppermute | solution.py:89
  209.7 11.2 %collective-permute-start.20 = (bf16[64,1536]{1,0:T(8,128)(2,1)S(1)}, bf16[64,1536]{1,0:T(8,128)(2,1)}, u32[]{:S(2)}, u32[]{:S(2)}) collective-permute-start(bf16[64,1536]{1,0:T(8,128)(2,1)S(1)} %get-tuple-element.238), channel_id=1, source_target_pairs={{0,2},{1,3},{2,0},{3,1},{4,6},{5,7},{6,4},{7,5},{8,10},{9,11},{10,... | collective-permute-start | bytes 589832 | tf_op jit(solution)/shard_map/ppermute | solution.py:89
  212.2 8.7 %collective-permute-start.19 = (bf16[64,1536]{1,0:T(8,128)(2,1)S(1)}, bf16[64,1536]{1,0:T(8,128)(2,1)}, u32[]{:S(2)}, u32[]{:S(2)}) collective-permute-start(bf16[64,1536]{1,0:T(8,128)(2,1)S(1)} %get-tuple-element.236), channel_id=1, source_target_pairs={{0,3},{1,0},{2,1},{3,2},{4,7},{5,4},{6,5},{7,6},{8,11},{9,8},{10,9... | collective-permute-start | bytes 589832 | tf_op jit(solution)/shard_map/ppermute | solution.py:89
  223.9 10.6 %collective-permute-start.23 = (bf16[64,1536]{1,0:T(8,128)(2,1)S(1)}, bf16[64,1536]{1,0:T(8,128)(2,1)S(1)}, u32[]{:S(2)}, u32[]{:S(2)}) collective-permute-start(bf16[64,1536]{1,0:T(8,128)(2,1)S(1)} %multiply_convert_fusion.2.refs_0_), channel_id=1, source_target_pairs={{0,2},{1,3},{2,0},{3,1},{4,6},{5,7},{6,4},{7,5},{8,10},{9,11},{10,... | collective-permute-start | bytes 589832 | tf_op jit(solution)/shard_map/ppermute | solution.py:89
  251.9 9.1 %collective-permute-start.32 = (bf16[64,1536]{1,0:T(8,128)(2,1)S(1)}, bf16[64,1536]{1,0:T(8,128)(2,1)S(1)}, u32[]{:S(2)}, u32[]{:S(2)}) collective-permute-start(bf16[64,1536]{1,0:T(8,128)(2,1)S(1)} %get-tuple-element.47), channel_id=1, source_target_pairs={{0,2},{1,3},{2,0},{3,1},{4,6},{5,7},{6,4},{7,5},{8,10},{9,11},{10,... | collective-permute-start | bytes 589832 | tf_op jit(solution)/shard_map/ppermute | solution.py:89
  268.3 11.5 %collective-permute-start.34 = (bf16[64,1536]{1,0:T(8,128)(2,1)S(1)}, bf16[64,1536]{1,0:T(8,128)(2,1)S(1)}, u32[]{:S(2)}, u32[]{:S(2)}) collective-permute-start(bf16[64,1536]{1,0:T(8,128)(2,1)S(1)} %fusion.127), channel_id=1, source_target_pairs={{0,1},{1,2},{2,3},{3,0},{4,5},{5,6},{6,7},{7,4},{8,9},{9,10},{10,1... | collective-permute-start | bytes 589832 | tf_op jit(solution)/shard_map/ppermute | solution.py:89
  312.3 11.6 %collective-permute-start.42 = (bf16[64,1536]{1,0:T(8,128)(2,1)S(1)}, bf16[64,1536]{1,0:T(8,128)(2,1)S(1)}, u32[]{:S(2)}, u32[]{:S(2)}) collective-permute-start(bf16[64,1536]{1,0:T(8,128)(2,1)S(1)} %get-tuple-element.230), channel_id=1, source_target_pairs={{0,1},{1,2},{2,3},{3,0},{4,5},{5,6},{6,7},{7,4},{8,9},{9,10},{10,1... | collective-permute-start | bytes 589832 | tf_op jit(solution)/shard_map/ppermute | solution.py:89
  312.3 11.5 %collective-permute-start.41 = (bf16[64,1536]{1,0:T(8,128)(2,1)S(1)}, bf16[64,1536]{1,0:T(8,128)(2,1)S(1)}, u32[]{:S(2)}, u32[]{:S(2)}) collective-permute-start(bf16[64,1536]{1,0:T(8,128)(2,1)S(1)} %get-tuple-element.231), channel_id=1, source_target_pairs={{0,2},{1,3},{2,0},{3,1},{4,6},{5,7},{6,4},{7,5},{8,10},{9,11},{10,... | collective-permute-start | bytes 589832 | tf_op jit(solution)/shard_map/ppermute | solution.py:89
  313.1 11.0 %collective-permute-start.40 = (bf16[64,1536]{1,0:T(8,128)(2,1)S(1)}, bf16[64,1536]{1,0:T(8,128)(2,1)S(1)}, u32[]{:S(2)}, u32[]{:S(2)}) collective-permute-start(bf16[64,1536]{1,0:T(8,128)(2,1)S(1)} %get-tuple-element.229), channel_id=1, source_target_pairs={{0,3},{1,0},{2,1},{3,2},{4,7},{5,4},{6,5},{7,6},{8,11},{9,8},{10,9... | collective-permute-start | bytes 589832 | tf_op jit(solution)/shard_map/ppermute | solution.py:89
  315.0 17.3 %collective-permute-start.27 = (bf16[64,1536]{1,0:T(8,128)(2,1)S(1)}, bf16[64,1536]{1,0:T(8,128)(2,1)S(1)}, u32[]{:S(2)}, u32[]{:S(2)}) collective-permute-start(bf16[64,1536]{1,0:T(8,128)(2,1)S(1)} %get-tuple-element.44), channel_id=1, source_target_pairs={{0,1},{1,2},{2,3},{3,0},{4,5},{5,6},{6,7},{7,4},{8,9},{9,10},{10,1... | collective-permute-start | bytes 589832 | tf_op jit(solution)/shard_map/ppermute | solution.py:89
  315.6 16.7 %collective-permute-start.26 = (bf16[64,1536]{1,0:T(8,128)(2,1)S(1)}, bf16[64,1536]{1,0:T(8,128)(2,1)S(1)}, u32[]{:S(2)}, u32[]{:S(2)}) collective-permute-start(bf16[64,1536]{1,0:T(8,128)(2,1)S(1)} %get-tuple-element.43), channel_id=1, source_target_pairs={{0,2},{1,3},{2,0},{3,1},{4,6},{5,7},{6,4},{7,5},{8,10},{9,11},{10,... | collective-permute-start | bytes 589832 | tf_op jit(solution)/shard_map/ppermute | solution.py:89
  323.8 8.8 %collective-permute-start.25 = (bf16[64,1536]{1,0:T(8,128)(2,1)S(1)}, bf16[64,1536]{1,0:T(8,128)(2,1)S(1)}, u32[]{:S(2)}, u32[]{:S(2)}) collective-permute-start(bf16[64,1536]{1,0:T(8,128)(2,1)S(1)} %get-tuple-element.42), channel_id=1, source_target_pairs={{0,3},{1,0},{2,1},{3,2},{4,7},{5,4},{6,5},{7,6},{8,11},{9,8},{10,9... | collective-permute-start | bytes 589832 | tf_op jit(solution)/shard_map/ppermute | solution.py:89
  335.5 11.1 %collective-permute-start.44 = (bf16[64,1536]{1,0:T(8,128)(2,1)S(1)}, bf16[64,1536]{1,0:T(8,128)(2,1)S(1)}, u32[]{:S(2)}, u32[]{:S(2)}) collective-permute-start(bf16[64,1536]{1,0:T(8,128)(2,1)S(1)} %get-tuple-element.190.refs_4_), channel_id=1, source_target_pairs={{0,2},{1,3},{2,0},{3,1},{4,6},{5,7},{6,4},{7,5},{8,10},{9,11},{10,... | collective-permute-start | bytes 589832 | tf_op jit(solution)/shard_map/ppermute | solution.py:89
  338.3 8.3 %collective-permute-start.45 = (bf16[64,1536]{1,0:T(8,128)(2,1)S(1)}, bf16[64,1536]{1,0:T(8,128)(2,1)S(1)}, u32[]{:S(2)}, u32[]{:S(2)}) collective-permute-start(bf16[64,1536]{1,0:T(8,128)(2,1)S(1)} %get-tuple-element.190.refs_4_), channel_id=1, source_target_pairs={{0,3},{1,0},{2,1},{3,2},{4,7},{5,4},{6,5},{7,6},{8,11},{9,8},{10,9... | collective-permute-start | bytes 589832 | tf_op jit(solution)/shard_map/ppermute | solution.py:89
  363.1 11.6 %collective-permute-start.47 = (bf16[64,1536]{1,0:T(8,128)(2,1)S(1)}, bf16[64,1536]{1,0:T(8,128)(2,1)S(1)}, u32[]{:S(2)}, u32[]{:S(2)}) collective-permute-start(bf16[64,1536]{1,0:T(8,128)(2,1)S(1)} %get-tuple-element.51), channel_id=1, source_target_pairs={{0,2},{1,3},{2,0},{3,1},{4,6},{5,7},{6,4},{7,5},{8,10},{9,11},{10,... | collective-permute-start | bytes 589832 | tf_op jit(solution)/shard_map/ppermute | solution.py:89
  366.0 8.7 %collective-permute-start.46 = (bf16[64,1536]{1,0:T(8,128)(2,1)S(1)}, bf16[64,1536]{1,0:T(8,128)(2,1)S(1)}, u32[]{:S(2)}, u32[]{:S(2)}) collective-permute-start(bf16[64,1536]{1,0:T(8,128)(2,1)S(1)} %get-tuple-element.50), channel_id=1, source_target_pairs={{0,3},{1,0},{2,1},{3,2},{4,7},{5,4},{6,5},{7,6},{8,11},{9,8},{10,9... | collective-permute-start | bytes 589832 | tf_op jit(solution)/shard_map/ppermute | solution.py:89
  375.9 10.7 %collective-permute-start.51 = (bf16[64,1536]{1,0:T(8,128)(2,1)S(1)}, bf16[64,1536]{1,0:T(8,128)(2,1)S(1)}, u32[]{:S(2)}, u32[]{:S(2)}) collective-permute-start(bf16[64,1536]{1,0:T(8,128)(2,1)S(1)} %get-tuple-element.187), channel_id=1, source_target_pairs={{0,3},{1,0},{2,1},{3,2},{4,7},{5,4},{6,5},{7,6},{8,11},{9,8},{10,9... | collective-permute-start | bytes 589832 | tf_op jit(solution)/shard_map/ppermute | solution.py:89
  378.6 11.9 %collective-permute-start.49 = (bf16[64,1536]{1,0:T(8,128)(2,1)S(1)}, bf16[64,1536]{1,0:T(8,128)(2,1)S(1)}, u32[]{:S(2)}, u32[]{:S(2)}) collective-permute-start(bf16[64,1536]{1,0:T(8,128)(2,1)S(1)} %get-tuple-element.187), channel_id=1, source_target_pairs={{0,1},{1,2},{2,3},{3,0},{4,5},{5,6},{6,7},{7,4},{8,9},{9,10},{10,1... | collective-permute-start | bytes 589832 | tf_op jit(solution)/shard_map/ppermute | solution.py:89
  379.2 22.0 %collective-permute-start.59 = (bf16[256,1536]{1,0:T(8,128)(2,1)S(1)}, bf16[256,1536]{1,0:T(8,128)(2,1)S(1)}, u32[]{:S(2)}, u32[]{:S(2)}) collective-permute-start(bf16[256,1536]{1,0:T(8,128)(2,1)S(1)} %multiply_convert_fusion.refs_0_), channel_id=1, source_target_pairs={{0,4},{4,0},{1,5},{5,1},{2,6},{6,2},{3,7},{7,3},{8,12},{12,8},{9,1... | collective-permute-start | bytes 2359304 | tf_op jit(solution)/shard_map/ppermute | solution.py:84
  392.9 8.3 %collective-permute-start.60 = (bf16[256,1536]{1,0:T(8,128)(2,1)S(1)}, bf16[256,1536]{1,0:T(8,128)(2,1)S(1)}, u32[]{:S(2)}, u32[]{:S(2)}) collective-permute-start(bf16[256,1536]{1,0:T(8,128)(2,1)S(1)} %get-tuple-element.223), channel_id=1, source_target_pairs={{0,4},{4,0},{1,5},{5,1},{2,6},{6,2},{3,7},{7,3},{8,12},{12,8},{9,1... | collective-permute-start | bytes 2359304 | tf_op jit(solution)/shard_map/ppermute | solution.py:84
  406.3 177.7 %reduce-scatter.8.cloned.1.call-start = ((), (), s32[]{:S(2)}) async-start(), calls=%async_computation.10 | async-start | bytes 8773632 | tf_op jit(solution)/shard_map/reduce_scatter | solution.py:358
  426.0 249.4 %reduce-scatter.6.cloned.1.call-start = ((), (), s32[]{:S(2)}) async-start(), calls=%async_computation.9 | async-start | bytes 10444800 | tf_op jit(solution)/shard_map/reduce_scatter | solution.py:358
  427.8 15.9 %collective-permute-start.63 = (bf16[256,5760]{1,0:T(8,128)(2,1)S(1)}, bf16[256,5760]{1,0:T(8,128)(2,1)}, u32[]{:S(2)}, u32[]{:S(2)}) collective-permute-start(bf16[256,5760]{1,0:T(8,128)(2,1)S(1)} %copy-done.1), channel_id=1, source_target_pairs={{0,4},{4,0},{1,5},{5,1},{2,6},{6,2},{3,7},{7,3},{8,12},{12,8},{9,1... | collective-permute-start | bytes 8847368 | tf_op jit(solution)/shard_map/ppermute | solution.py:84
  461.1 15.3 %collective-permute-start.55 = (bf16[64,1536]{1,0:T(8,128)(2,1)S(1)}, bf16[64,1536]{1,0:T(8,128)(2,1)S(1)}, u32[]{:S(2)}, u32[]{:S(2)}) collective-permute-start(bf16[64,1536]{1,0:T(8,128)(2,1)S(1)} %get-tuple-element.226), channel_id=1, source_target_pairs={{0,1},{1,2},{2,3},{3,0},{4,5},{5,6},{6,7},{7,4},{8,9},{9,10},{10,1... | collective-permute-start | bytes 589832 | tf_op jit(solution)/shard_map/ppermute | solution.py:89
  461.2 15.4 %collective-permute-start.54 = (bf16[64,1536]{1,0:T(8,128)(2,1)S(1)}, bf16[64,1536]{1,0:T(8,128)(2,1)S(1)}, u32[]{:S(2)}, u32[]{:S(2)}) collective-permute-start(bf16[64,1536]{1,0:T(8,128)(2,1)S(1)} %get-tuple-element.227), channel_id=1, source_target_pairs={{0,2},{1,3},{2,0},{3,1},{4,6},{5,7},{6,4},{7,5},{8,10},{9,11},{10,... | collective-permute-start | bytes 589832 | tf_op jit(solution)/shard_map/ppermute | solution.py:89
  463.0 13.6 %collective-permute-start.53 = (bf16[64,1536]{1,0:T(8,128)(2,1)S(1)}, bf16[64,1536]{1,0:T(8,128)(2,1)S(1)}, u32[]{:S(2)}, u32[]{:S(2)}) collective-permute-start(bf16[64,1536]{1,0:T(8,128)(2,1)S(1)} %get-tuple-element.225), channel_id=1, source_target_pairs={{0,3},{1,0},{2,1},{3,2},{4,7},{5,4},{6,5},{7,6},{8,11},{9,8},{10,9... | collective-permute-start | bytes 589832 | tf_op jit(solution)/shard_map/ppermute | solution.py:89
  464.1 18.2 %collective-permute-start.30 = (bf16[64,1536]{1,0:T(8,128)(2,1)S(1)}, bf16[64,1536]{1,0:T(8,128)(2,1)S(1)}, u32[]{:S(2)}, u32[]{:S(2)}) collective-permute-start(bf16[64,1536]{1,0:T(8,128)(2,1)S(1)} %copy-done.50), channel_id=1, source_target_pairs={{0,3},{1,0},{2,1},{3,2},{4,7},{5,4},{6,5},{7,6},{8,11},{9,8},{10,9... | collective-permute-start | bytes 589832 | tf_op jit(solution)/shard_map/ppermute | solution.py:89
  464.8 17.5 %collective-permute-start.29 = (bf16[64,1536]{1,0:T(8,128)(2,1)S(1)}, bf16[64,1536]{1,0:T(8,128)(2,1)S(1)}, u32[]{:S(2)}, u32[]{:S(2)}) collective-permute-start(bf16[64,1536]{1,0:T(8,128)(2,1)S(1)} %copy-done.50), channel_id=1, source_target_pairs={{0,2},{1,3},{2,0},{3,1},{4,6},{5,7},{6,4},{7,5},{8,10},{9,11},{10,... | collective-permute-start | bytes 589832 | tf_op jit(solution)/shard_map/ppermute | solution.py:89
  478.4 17.3 %collective-permute-start.56 = (bf16[80,1536]{1,0:T(8,128)(2,1)S(1)}, bf16[80,1536]{1,0:T(8,128)(2,1)S(1)}, u32[]{:S(2)}, u32[]{:S(2)}) collective-permute-start(bf16[80,1536]{1,0:T(8,128)(2,1)S(1)} %concatenate.179), channel_id=1, source_target_pairs={{0,1},{1,2},{2,3},{3,0},{4,5},{5,6},{6,7},{7,4},{8,9},{9,10},{10,1... | collective-permute-start | bytes 737288 | tf_op jit(solution)/shard_map/ppermute | solution.py:89
  478.5 17.2 %collective-permute-start.57 = (bf16[80,1536]{1,0:T(8,128)(2,1)S(1)}, bf16[80,1536]{1,0:T(8,128)(2,1)S(1)}, u32[]{:S(2)}, u32[]{:S(2)}) collective-permute-start(bf16[80,1536]{1,0:T(8,128)(2,1)S(1)} %concatenate.179), channel_id=1, source_target_pairs={{0,2},{1,3},{2,0},{3,1},{4,6},{5,7},{6,4},{7,5},{8,10},{9,11},{10,... | collective-permute-start | bytes 737288 | tf_op jit(solution)/shard_map/ppermute | solution.py:89
  482.3 13.4 %collective-permute-start.58 = (bf16[80,1536]{1,0:T(8,128)(2,1)S(1)}, bf16[80,1536]{1,0:T(8,128)(2,1)S(1)}, u32[]{:S(2)}, u32[]{:S(2)}) collective-permute-start(bf16[80,1536]{1,0:T(8,128)(2,1)S(1)} %concatenate.179), channel_id=1, source_target_pairs={{0,3},{1,0},{2,1},{3,2},{4,7},{5,4},{6,5},{7,6},{8,11},{9,8},{10,9... | collective-permute-start | bytes 737288 | tf_op jit(solution)/shard_map/ppermute | solution.py:89
  484.9 29.5 %all-to-all-start.1 = ((bf16[32,8,1536]{2,1,0:T(8,128)(2,1)}), bf16[32,8,1536]{2,1,0:T(8,128)(2,1)S(1)}, u32[]{:S(2)}, u32[]{:S(2)}) async-start(bf16[32,8,1536]{2,1,0:T(8,128)(2,1)} %gather_fusion.3), calls=%async_computation.1 | async-start | bytes 1572864 | tf_op jit(solution)/shard_map/all_to_all | solution.py:756
  514.5 34.1 %all-to-all-start.2 = ((bf16[32,12,1536]{2,1,0:T(8,128)(2,1)}), bf16[32,12,1536]{2,1,0:T(8,128)(2,1)S(1)}, u32[]{:S(2)}, u32[]{:S(2)}) async-start(bf16[32,12,1536]{2,1,0:T(8,128)(2,1)} %pad_maximum_fusion.2), calls=%async_computation.2 | async-start | bytes 3145728 | tf_op jit(solution)/shard_map/all_to_all | solution.py:795
  (195 other events, 1889.4 us)
Sparse Core Ops, SparseCore 0:
  11.3 93.9 all-gather.2
  108.1 78.8 all-gather.4
  406.4 70.3 reduce-scatter.3
  480.1 103.8 reduce-scatter.7
  587.4 87.9 reduce-scatter.5

commit v3 on v2

--- a/solution.py
+++ b/solution.py
@@ -19,6 +19,8 @@
 TOKEN_AXES = CHIP_AXES + ("core",)
 GROUP_AXES = ("x", "z_hi")
 CTX_AXES = ("z_lo", "core")
+Z_AXES = ("z_hi", "z_lo")
+CORES = 2
 TILE = 256
 VMEM_LIMIT = 48 * 1024 * 1024
 F32 = jnp.float32
@@ -84,6 +86,11 @@
     return lax.ppermute(block, "core", [(0, 1), (1, 0)])
 
 
+def shift_ring(block, axis, distance):
+    ring = lax.axis_size(axis)
+    return lax.ppermute(block, axis, [(i, (i + distance) % ring) for i in range(ring)])
+
+
 def shift_tp(block, distance):
     members = lax.axis_size("tp")
     return lax.ppermute(block, "tp", [(i, (i + distance) % members) for i in range(members)])
@@ -127,6 +134,10 @@
 
 def times_t(left, right):
     return lax.dot_general(left, right, (((1,), (1,)), ((), ())), preferred_element_type=F32)
+
+
+def times_rows(left, right):
+    return lax.dot_general(left, right, (((0,), (0,)), ((), ())), preferred_element_type=F32)
 
 
 def assemble(chunk_refs, target):
@@ -292,31 +303,27 @@
 
 def gradient_kernel(cut, whole_steps, *refs):
     one_own, one_other, two_own, two_other, own_ref, other_ref = refs[:6]
-    out_ref, one_t, two_t = refs[-3:]
-    tokens = one_own.shape[0]
+    out_ref = refs[-1]
     step = pl.program_id(0)
 
-    @pl.when(step == 0)
-    def _():
-        one_t[:, :tokens] = one_own[...].T
-        one_t[:, tokens:] = one_other[...].T
-        two_t[:, :tokens] = two_own[...].T
-        two_t[:, tokens:] = two_other[...].T
-
-    right = jnp.concatenate([own_ref[...], other_ref[...]], axis=0)
+    def product(own_left, other_left, columns):
+        total = times_rows(own_left[...], own_ref[:, columns])
+        total += times_rows(other_left[...], other_ref[:, columns])
+        out_ref[:, columns] = total.astype(BF16)
+
     if whole_steps:
 
         @pl.when(step < whole_steps)
         def _():
-            out_ref[...] = times(one_t[...], right).astype(BF16)
+            product(one_own, one_other, slice(None))
 
         @pl.when(step >= whole_steps)
         def _():
-            out_ref[...] = times(two_t[...], right).astype(BF16)
+            product(two_own, two_other, slice(None))
 
     else:
-        out_ref[:, :cut] = times(one_t[...], right[:, :cut]).astype(BF16)
-        out_ref[:, cut:] = times(two_t[...], right[:, cut:]).astype(BF16)
+        product(one_own, one_other, slice(0, cut))
+        product(two_own, two_other, slice(cut, None))
 
 
 def gradient(lefts, own, other, other_start, block, steps, cut, whole_steps, width, out_width, out_start, target):
@@ -341,7 +348,6 @@
         in_specs=in_specs,
         out_specs=pl.BlockSpec((width, block), lambda j: (0, out_start + j)),
         out_shape=jax.ShapeDtypeStruct((width, out_width), BF16),
-        scratch_shapes=[pltpu.VMEM((width, 2 * tokens), BF16)] * 2,
         input_output_aliases=aliases,
         compiler_params=pltpu.CompilerParams(vmem_limit_bytes=VMEM_LIMIT),
         cost_estimate=pl.CostEstimate(
@@ -353,14 +359,53 @@
     )(*operands)
 
 
-def reduce_gradient(partial):
+def share_rows(summed):
     core = lax.axis_index("core")
-    summed = lax.psum_scatter(partial, CHIP_AXES, scatter_dimension=0, tiled=True)
     rows = summed.shape[0] // 2
     mine = lax.dynamic_slice_in_dim(summed, core * rows, rows, 0)
     other = swap_core(lax.dynamic_slice_in_dim(summed, (1 - core) * rows, rows, 0))
     first = core == 0
     return jnp.where(first, mine, other).astype(F32), jnp.where(first, other, mine).astype(F32)
+
+
+def reduce_gradient(partial):
+    return share_rows(lax.psum_scatter(partial, CHIP_AXES, scatter_dimension=0, tiled=True))
+
+
+def exchange_gradient(partial):
+    ring = lax.axis_size("x")
+    blocks = partial.reshape(ring, ring, -1, partial.shape[1])
+    half = partial.shape[1] // 2
+
+    def along(values, axis, dimension):
+        total = None
+        place = lax.axis_index(axis)
+        for k in range(ring):
+            block = lax.dynamic_index_in_dim(values, (place + k) % ring, dimension, False)
+            block = block if k == 0 else shift_ring(block.astype(BF16), axis, k)
+            total = block.astype(F32) if k == 0 else total + block.astype(F32)
+        return total
+
+    low = along(along(blocks[..., :half], "x", 0), Z_AXES, 0)
+    high = along(along(blocks[..., half:], Z_AXES, 1), "x", 0)
+    return share_rows(jnp.concatenate([low, high], axis=1).astype(BF16))
+
+
+def gather_pack(pack):
+    rows, columns = pack.shape
+    blocks = pack[None]
+    for axis in ("x", Z_AXES):
+        blocks = jnp.concatenate(
+            [blocks] + [shift_ring(blocks, axis, k) for k in range(1, lax.axis_size(axis))]
+        )
+    blocks = jnp.concatenate([blocks, swap_core(blocks)])
+    ring = lax.axis_size("x")
+    index = jnp.arange(blocks.shape[0])
+    step_core = (index % CORES - lax.axis_index("core")) % CORES
+    step_z = (lax.axis_index(Z_AXES) - index // CORES % ring) % ring
+    step_x = (lax.axis_index("x") - index // CORES // ring) % ring
+    place = (step_core * ring + step_z) * ring + step_x
+    return jnp.take(blocks, place, axis=0, mode="clip").reshape(-1, columns)
 
 
 def ffn_gradients(low, high, steps, hidden):
@@ -427,19 +472,18 @@
         wide = wide.reshape(depth, 2, steps, TILE).transpose(0, 2, 1, 3).reshape(depth, -1)
         return [wide, jnp.pad(down.T, ((0, 0), (0, padded - hidden)))]
 
+    mixer_pack = jnp.concatenate([mixer_project.reshape(depth, -1), mixer_output.T], axis=1)
     first_pack = jnp.concatenate(
-        pack_ffn(first_gateup, first_down) + [mixer_project.reshape(depth, -1), mixer_output.T],
-        axis=1,
-    )
-    second_pack = jnp.concatenate(
-        pack_ffn(second_gateup, second_down) + [attend_project, attend_output.T], axis=1
-    )
+        pack_ffn(first_gateup, first_down) + [attend_project, attend_output.T], axis=1
+    )
+    second_pack = jnp.concatenate(pack_ffn(second_gateup, second_down), axis=1)
     first_all = lax.all_gather(first_pack, TOKEN_AXES, axis=0, tiled=True)
     second_all = lax.all_gather(second_pack, TOKEN_AXES, axis=0, tiled=True)
-    project_a = first_all[:, ffn_width : ffn_width + 3 * channels]
-    output_a_t = first_all[:, ffn_width + 3 * channels :]
-    project_b = second_all[:, ffn_width : ffn_width + attend_project.shape[1]]
-    output_b_t = second_all[:, ffn_width + attend_project.shape[1] :]
+    mixer_all = gather_pack(mixer_pack)
+    project_a = mixer_all[:, : 3 * channels]
+    output_a_t = mixer_all[:, 3 * channels :]
+    project_b = first_all[:, ffn_width : ffn_width + attend_project.shape[1]]
+    output_b_t = first_all[:, ffn_width + attend_project.shape[1] :]
 
     piece_table = deal_order.reshape(shards, shards, piece_rows)[:, :, 0]
     anchor = piece_table // row_count
@@ -587,13 +631,14 @@
     ffn_lefts = [(side, 0), (side_other, 0), (side, 1), (side_other, 1)]
     ffn_cols = steps * block
     side_start = 2 * width // block
-    second_grads = reduce_gradient(
-        gradient(
-            ffn_lefts, keep, side_other, side_start, block, steps, TILE, 0, width, ffn_cols, 0, None
-        )
-    )
-
-    back_b = jnp.concatenate(tp_gather(d_stream3.astype(BF16)))
+    partial = gradient(
+        ffn_lefts, keep, side_other, side_start, block, steps, TILE, 0, width, ffn_cols, 0, None
+    )
+
+    back_b = tp_gather(d_stream3.astype(BF16))
+    back_b, partial = lax.optimization_barrier((back_b, partial))
+    second_grads = reduce_gradient(partial)
+    back_b = jnp.concatenate(back_b)
     back_b_other = swap_core(back_b)
     attend_in_other = swap_core(attend_in)
     d_attended_b = times(back_b, output_b_t).astype(BF16).reshape(row_count, -1, groups, HD)
@@ -657,7 +702,25 @@
         None,
     )
 
+    slot_for_anchor = jnp.sum(
+        jnp.where(
+            my_anchor[None, :] == jnp.arange(shards)[:, None], jnp.arange(shards)[None, :], 0
+        ),
+        axis=1,
+    )
+    dest_for_piece = jnp.sum(
+        jnp.where(
+            send_piece[None, :] == jnp.arange(shards)[:, None], jnp.arange(shards)[None, :], 0
+        ),
+        axis=1,
+    )
+    pieces = shards // members
+    slot_place = (own - slot_for_anchor // pieces) % members * pieces + slot_for_anchor % pieces
+    out_rows = jnp.concatenate(tp_gather(stream4.astype(BF16)))
+    out_rows = out_rows.reshape(shards, piece_rows, width)[slot_place]
+    out_home = lax.all_to_all(out_rows, TOKEN_AXES, split_axis=0, concat_axis=0, tiled=True)
     back_f = tp_gather(d_stream2.astype(BF16))
+    back_f, third = lax.optimization_barrier((back_f, third))
     d_chunks, unused, keep, side = ffn_backward(
         core_ref, normed_f, back_f, first_all, steps, False
     )
@@ -666,26 +729,27 @@
     d_stream1 = d_stream2 + d_stream
     side_other = swap_core(side)
     ffn_lefts = [(side, 0), (side_other, 0), (side, 1), (side_other, 1)]
-    low, high = reduce_gradient(
-        gradient(
-            ffn_lefts,
-            keep,
-            side_other,
-            side_start,
-            block,
-            steps,
-            TILE,
-            0,
-            width,
-            ffn_cols + attend_cols,
-            0,
-            third,
-        )
-    )
+    partial = gradient(
+        ffn_lefts,
+        keep,
+        side_other,
+        side_start,
+        block,
+        steps,
+        TILE,
+        0,
+        width,
+        ffn_cols + attend_cols,
+        0,
+        third,
+    )
+
+    back_a = tp_gather(d_stream1.astype(BF16))
+    back_a, partial, out_home = lax.optimization_barrier((back_a, partial, out_home))
+    low, high = reduce_gradient(partial)
     first_grads = (low[:, :ffn_cols], high[:, :ffn_cols])
     attend_grads = jnp.concatenate([low[:, ffn_cols:], high[:, ffn_cols:]], axis=1)
-
-    back_a = jnp.concatenate(tp_gather(d_stream1.astype(BF16)))
+    back_a = jnp.concatenate(back_a)
     back_a_other = swap_core(back_a)
     d_gated = reorder(times(back_a, output_a_t))
     d_cgate = d_gated * conv_out
@@ -714,7 +778,7 @@
     d_stream0 = d_stream1 + d_norm_a
     keep, send = halves(d_proj_a, gated_rows)
     mixer_cols = keep.shape[1]
-    low, high = reduce_gradient(
+    low, high = exchange_gradient(
         gradient(
             [
                 (mixer_in, 0),
@@ -736,25 +800,6 @@
         )
     )
     mixer_grads = jnp.concatenate([low, high], axis=1)
-
-    slot_for_anchor = jnp.sum(
-        jnp.where(
-            my_anchor[None, :] == jnp.arange(shards)[:, None], jnp.arange(shards)[None, :], 0
-        ),
-        axis=1,
-    )
-    dest_for_piece = jnp.sum(
-        jnp.where(
-            send_piece[None, :] == jnp.arange(shards)[:, None], jnp.arange(shards)[None, :], 0
-        ),
-        axis=1,
-    )
-    pieces = shards // members
-    slot_place = (own - slot_for_anchor // pieces) % members * pieces + slot_for_anchor % pieces
-    out_rows = jnp.concatenate(tp_gather(stream4.astype(BF16)))
-    out_rows = out_rows.reshape(shards, piece_rows, width)[slot_place]
-    out_home = lax.all_to_all(out_rows, TOKEN_AXES, split_axis=0, concat_axis=0, tiled=True)
-    layer_out = out_home[dest_for_piece].reshape(row_count, width)
 
     def row_of(values):
         flat = values.reshape(-1)
@@ -799,6 +844,7 @@
         concat_axis=0,
         tiled=True,
     )
+    layer_out = out_home[dest_for_piece].reshape(row_count, width)
     input_gradient = home[:, :piece_rows][dest_for_piece].reshape(row_count, width)
     totals = jnp.sum(home[:, piece_rows:].astype(F32), axis=0).reshape(-1)
     gain_totals = totals[: 4 * depth].reshape(4, depth)

time: 701 us -> 599 us (0.85)
  waiting for transfers between devices: 338 us -> 160 us
  local copies, waits for them, and re-layouts: 64.8 us -> 110 us
  starting transfers between devices: 108 us -> 134 us
  other arithmetic: 45.6 us -> 56.2 us
    reduce_scatter x3 -> x2, waiting for transfers between devices: 114 us -> 0.04 us  [reduce_gradient(): lax.psum_scatter(partial, CHIP_AXES, scatter_dimension=0, tiled=True)]
    ppermute x0 -> x18, waiting for transfers between devices: none -> 64.3 us  [shift_ring(): lax.ppermute(block, axis, [(i, (i + distance) % ring) for i in range(ring)])]
    ppermute x51, waiting for transfers between devices: 108 us -> 78 us  [shift_tp(): lax.ppermute(block, 'tp', [(i, (i + distance) % members) for i in range(m...]
    all_to_all x1, waiting for transfers between devices: 27.6 us -> 0.01 us  [body(): lax.all_to_all(jnp.concatenate([grad_rows, small_rows.reshape(shards, 4,...]
    ppermute x0 -> x18, starting transfers between devices: none -> 23.2 us  [shift_ring(): lax.ppermute(block, axis, [(i, (i + distance) % ring) for i in range(ring)])]
    all_gather x1, waiting for transfers between devices: 21 us -> 0.01 us  [body(): first_all = lax.all_gather(first_pack, TOKEN_AXES, axis=0, tiled=True)]
    all_gather x1, waiting for transfers between devices: 16.1 us -> 0.02 us  [body(): second_all = lax.all_gather(second_pack, TOKEN_AXES, axis=0, tiled=True)]
    all_to_all x1, waiting for transfers between devices: 15.4 us -> 0.01 us  [body(): lax.all_to_all(outgoing, TOKEN_AXES, split_axis=0, concat_axis=0, tiled=T...]
  transfers between devices with their start and end apart: 78 -> 96, of which waited for: 45 -> 41; matrix products, arithmetic and copies ran while one was open for 12% -> 31% of each run, Pallas kernels for 6% -> 9%
where the time goes in v3:
time: 599 us; the launch traced here: 588 us
  waiting for transfers between devices  160 us (27%)
  starting transfers between devices  134 us (22%)
  local copies, waits for them, and re-layouts  110 us (18%)
  Pallas kernels  69.1 us (12%)
  other arithmetic  56.2 us (9%)
  matrix products  32.7 us (5%)
  between operations  25.8 us (4%)
    ppermute x51, waiting for transfers between devices, shift_tp(): lax.ppermute(block, 'tp', [(i, (i + distance) % members) for i in range(m...  78 us
    ppermute x51, starting transfers between devices, shift_tp(): lax.ppermute(block, 'tp', [(i, (i + distance) % members) for i in range(m...  69.8 us
    ppermute x18, waiting for transfers between devices, shift_ring(): lax.ppermute(block, axis, [(i, (i + distance) % ring) for i in range(ring)])  64.3 us
    pallas_call x2, Pallas kernels, ffn_backward(): pl.pallas_call(functools.partial(ffn_backward_kernel, count, forward), gr...  30.4 us
    pallas_call x4, Pallas kernels, gradient(): pl.pallas_call(functools.partial(gradient_kernel, cut, whole_steps), grid...  27.7 us
    unnamed x333, local copies, waits for them, and re-layouts  25.5 us
    ppermute x18, starting transfers between devices, shift_ring(): lax.ppermute(block, axis, [(i, (i + distance) % ring) for i in range(ring)])  23.2 us
    ppermute x12, starting transfers between devices, swap_core(): return lax.ppermute(block, 'core', [(0, 1), (1, 0)])  15.3 us
  transfers between devices with their start and end apart: 96, of which 41 were waited for; matrix products, arithmetic and copies ran while one was open for 31% of the time, Pallas kernels for 9%

profile of v3, /device:TPU:1, one launch (start us, length us, event | category | flops | bytes accessed | tf_op | source)
XLA Modules:
  0.0 588.0 jit_solution(3547196462971727662)
XLA Ops:
  24.5 7.0 %all-to-all-start = ((bf16[32,5,1536]{2,1,0:T(8,128)(2,1)}), bf16[32,5,1536]{2,1,0:T(8,128)(2,1)S(1)}, u32[]{:S(2)}, u32[]{:S(2)}) async-start(bf16[32,5,1536]{2,1,0:T(8,128)(2,1)} %pad_maximum_fusion.4), calls=%async_computation | async-start | bytes 1572864 | tf_op jit(solution)/shard_map/all_to_all | solution.py:509
  59.6 9.1 %collective-permute-done.7 = bf16[4,48,1536]{2,1,0:T(8,128)(2,1)} collective-permute-done((bf16[4,48,1536]{2,1,0:T(8,128)(2,1)}, bf16[4,48,1536]{2,1,0:T(8,128)(2,1)}, u32[]{:S(2)}, u32[]{:S(2)}) %collective-permute-start.7) | collective-permute-done | bytes 589856 | tf_op jit(solution)/shard_map/ppermute | solution.py:91
  72.3 23.4 %collective-permute-done.8 = bf16[4,48,1536]{2,1,0:T(8,128)(2,1)} collective-permute-done((bf16[4,48,1536]{2,1,0:T(8,128)(2,1)}, bf16[4,48,1536]{2,1,0:T(8,128)(2,1)}, u32[]{:S(2)}, u32[]{:S(2)}) %collective-permute-start.8) | collective-permute-done | bytes 589856 | tf_op jit(solution)/shard_map/ppermute | solution.py:91
  99.0 2.9 collective-permute-start.10
  111.1 3.4 constant_dynamic-update-slice_fusion.7
  114.5 5.4 gather_fusion.3
  120.0 3.2 fusion.14
  135.9 5.2 collective-permute-done.12
  148.4 6.2 %collective-permute-done.15.refs_2_ = bf16[64,1536]{1,0:T(8,128)(2,1)S(1)} collective-permute-done((bf16[64,1536]{1,0:T(8,128)(2,1)S(1)}, bf16[64,1536]{1,0:T(8,128)(2,1)S(1)}, u32[]{:S(2)}, u32[]{:S(2)}) %collective-permute-start.15) | collective-permute-done | bytes 196640 | tf_op jit(solution)/shard_map/ppermute | solution.py:96
  154.6 10.9 %ffn_forward.1 = (f32[64,1536]{1,0:T(8,128)S(1)}, bf16[64,1536]{1,0:T(8,128)(2,1)S(1)}, bf16[64,1536]{1,0:T(8,128)(2,1)S(1)}, bf16[64,1536]{1,0:T(8,128)(2,1)S(1)}) custom-call(bf16[64,1536]{1,0:T(8,128)(2,1)S(1)} %multiply_convert_fusion.4.refs_0_, bf16[64,1536]{1,0:T(8,128)(2,1)S(1)} %collective-permute-done.14.refs_1_, ...), custom_call_target="tpu_custom_call" | custom-call | flops 4227858432 | bytes 16515072 | tf_op jit(solution)/shard_map/ffn_forward/pallas_call | solution.py:193
  172.4 5.2 collective-permute-done.18
  178.3 3.4 collective-permute-start.22
  185.8 2.9 collective-permute-done.21
  188.7 5.5 collective-permute-done.20
  200.1 3.4 collective-permute-done.25
  210.8 3.1 fusion.173
  219.1 6.3 %collective-permute-done.28 = bf16[64,1536]{1,0:T(8,128)(2,1)S(1)} collective-permute-done((bf16[64,1536]{1,0:T(8,128)(2,1)S(1)}, bf16[64,1536]{1,0:T(8,128)(2,1)S(1)}, u32[]{:S(2)}, u32[]{:S(2)}) %collective-permute-start.28) | collective-permute-done | bytes 196640 | tf_op jit(solution)/shard_map/ppermute | solution.py:96
  228.9 3.2 collective-permute-start.30
  235.0 5.8 collective-permute-done.30.refs_2_
  240.8 15.0 %ffn_both.1 = (f32[64,1536]{1,0:T(8,128)S(1)}, bf16[64,1536]{1,0:T(8,128)(2,1)S(1)}, bf16[64,1536]{1,0:T(8,128)(2,1)S(1)}, bf16[64,1536]{1,0:T(8,128)(2,1)S(1)},...) custom-call(s32[1]{0:T(128)} %bitcast.14.core_ref, ...), custom_call_target="tpu_custom_call" | custom-call | flops 8455716864 | bytes 22413312 | tf_op jit(solution)/shard_map/ffn_both/pallas_call | solution.py:278
  257.2 3.2 collective-permute-start.33
  261.9 3.0 collective-permute-done.34
  265.0 4.8 collective-permute-done.33
  273.4 4.8 collective-permute-done.59
  280.2 3.7 collective-permute-start.36
  285.6 10.4 %weight_gradient.4 = bf16[1536,2688]{1,0:T(8,128)(2,1)} custom-call(bf16[256,5760]{1,0:T(8,128)(2,1)S(1)} %copy-done, bf16[256,5760]{1,0:T(8,128)(2,1)} %copy-done.7, bf16[256,5760]{1,0:T(8,128)(2,1)S(1)} %copy-done, bf16[256,5760]{1,0:T(8,128)(2,1)} %copy-done.7, bf16[256,2688]{1,0:T(8,128)(2,1)S(1)} %get-tuple-element.62.refs_4_, bf16[256,5760]{1,0:T(8,128)(2,1)} %copy-done.7), custom_call_target="tpu_custom_call" | custom-call | flops 4227858432 | bytes 8257536 | tf_op jit(solution)/shard_map/weight_gradient/pallas_call | solution.py:345
  304.0 5.0 fusion
  321.9 5.2 collective-permute-done.40
  329.4 3.7 fusion.174
  342.6 4.3 collective-permute-start.50
  356.7 3.6 weight_gradient.5.refs_6_
  360.3 3.1 collective-permute-done.46.refs_6_
  363.4 15.4 %ffn_backward.1 = (f32[64,1536]{1,0:T(8,128)S(1)}, bf16[64,1536]{1,0:T(8,128)(2,1)}, bf16[64,1536]{1,0:T(8,128)(2,1)}, bf16[64,1536]{1,0:T(8,128)(2,1)}, bf16[25...) custom-call(s32[1]{0:T(128)} %bitcast.14.core_ref, bf16[64,1536]{1,0:T(8,128)(2,1)S(1)} %multiply_convert_fusion.4.refs_0_, ...), custom_call_target="tpu_custom_call" | custom-call | flops 7046430720 | bytes 22413312 | tf_op jit(solution)/shard_map/ffn_backward/pallas_call | solution.py:278
  392.4 4.3 collective-permute-start.51
  398.7 6.0 %all-to-all-start.1 = ((bf16[32,8,1536]{2,1,0:T(8,128)(2,1)}), bf16[32,8,1536]{2,1,0:T(8,128)(2,1)}, u32[]{:S(2)}, u32[]{:S(2)}) async-start(bf16[32,8,1536]{2,1,0:T(8,128)(2,1)} %gather_fusion.4), calls=%async_computation.1 | async-start | bytes 1572864 | tf_op jit(solution)/shard_map/all_to_all | solution.py:721
  411.6 3.1 collective-permute-start.55
  414.8 10.4 %weight_gradient.6 = bf16[1536,3200]{1,0:T(8,128)(2,1)} custom-call(bf16[256,5760]{1,0:T(8,128)(2,1)S(1)} %copy-done.1, bf16[256,5760]{1,0:T(8,128)(2,1)} %collective-permute-done.57.refs_1_.refs_3_.refs_5_, bf16[256,5760]{1,0:T(8,128)(2,1)S(1)} %copy-done.1, ...), custom_call_target="tpu_custom_call", output_to_operand_aliasing={{}: (6, {})} | custom-call | flops 4227858432 | bytes 8257536 | tf_op jit(solution)/shard_map/weight_gradient/pallas_call | solution.py:345
  434.8 3.3 collective-permute-done.64
  472.7 6.9 %collective-permute-done.68 = bf16[80,1536]{1,0:T(8,128)(2,1)S(1)} collective-permute-done((bf16[80,1536]{1,0:T(8,128)(2,1)}, bf16[80,1536]{1,0:T(8,128)(2,1)S(1)}, u32[]{:S(2)}, u32[]{:S(2)}) %collective-permute-start.68) | collective-permute-done | bytes 245792 | tf_op jit(solution)/shard_map/ppermute | solution.py:96
  480.6 8.4 %concatenate.203 = bf16[320,1536]{1,0:T(8,128)(2,1)} concatenate(bf16[64,1536]{1,0:T(8,128)(2,1)S(1)} %fusion.58, bf16[1,1536]{1,0:T(2,128)(2,1)} %reshape.1115, bf16[1,1536]{1,0:T(2,128)(2,1)} %reshape.1116, bf16[1,1536]{1,0:T(2,128)(2,1)} %reshape.1117, bf16[1,1536]{1,0:T(2,128)(2,1)S(1)} %reshape.1118, bf16[1,1536]{1,0:T(2,128)(2,1)} %stack.62, bf16[1,1536]{1,0:T(2,128)(2,1)} %stack.63, ...), dimensions={0} | concatenate | bytes 1966080 | tf_op jit(solution)/shard_map/concatenate | solution.py:819
  496.2 3.0 gather_fusion.6
  500.4 3.3 weight_gradient.7
  512.9 3.9 all-to-all-start.2
  520.2 3.6 collective-permute-done.76
  523.8 3.3 collective-permute-done.74
  529.4 12.9 %collective-permute-done.82 = bf16[4,96,384]{2,1,0:T(8,128)(2,1)S(1)} collective-permute-done((bf16[4,96,384]{2,1,0:T(8,128)(2,1)S(1)}, bf16[4,96,384]{2,1,0:T(8,128)(2,1)S(1)}, u32[]{:S(2)}, u32[]{:S(2)}) %collective-permute-start.82) | collective-permute-done | bytes 294944 | tf_op jit(solution)/shard_map/ppermute | solution.py:91
  545.3 5.3 collective-permute-done.80
  554.5 3.4 collective-permute-done.84
  (790 shorter events, 280.1 us)
Async XLA Ops:
  7.2 147.4 %all-gather.3.cloned.1.call-start = ((), (), s32[]{:S(2)}) async-start(), calls=%async_computation.5 | async-start | bytes 20275200 | tf_op jit(solution)/shard_map/all_gather | solution.py:480
  10.3 222.3 %all-gather.5.cloned.1.call-start = ((), (), s32[]{:S(2)}) async-start(), calls=%async_computation.6 | async-start | bytes 17031168 | tf_op jit(solution)/shard_map/all_gather | solution.py:481
  13.0 33.2 %collective-permute-start.4 = (bf16[1,48,1536]{2,1,0:T(8,128)(2,1)}, bf16[1,48,1536]{2,1,0:T(8,128)(2,1)S(1)}, u32[]{:S(2)}, u32[]{:S(2)}) collective-permute-start(bf16[1,48,1536]{2,1,0:T(8,128)(2,1)} %maximum_bitcast_fusion.1), channel_id=1, source_target_pairs={{0,32},{32,64},{64,96},{96,0},{1,33},{33,65},{65,97},{97,1},{2,34}... | collective-permute-start | bytes 442376 | tf_op jit(solution)/shard_map/ppermute | solution.py:91
  15.1 31.1 %collective-permute-start.5 = (bf16[1,48,1536]{2,1,0:T(8,128)(2,1)}, bf16[1,48,1536]{2,1,0:T(8,128)(2,1)S(1)}, u32[]{:S(2)}, u32[]{:S(2)}) collective-permute-start(bf16[1,48,1536]{2,1,0:T(8,128)(2,1)} %maximum_bitcast_fusion.1), channel_id=1, source_target_pairs={{0,64},{32,96},{64,0},{96,32},{1,65},{33,97},{65,1},{97,33},{2,66}... | collective-permute-start | bytes 442376 | tf_op jit(solution)/shard_map/ppermute | solution.py:91
  17.5 28.7 %collective-permute-start.6 = (bf16[1,48,1536]{2,1,0:T(8,128)(2,1)}, bf16[1,48,1536]{2,1,0:T(8,128)(2,1)S(1)}, u32[]{:S(2)}, u32[]{:S(2)}) collective-permute-start(bf16[1,48,1536]{2,1,0:T(8,128)(2,1)} %maximum_bitcast_fusion.1), channel_id=1, source_target_pairs={{0,96},{32,0},{64,32},{96,64},{1,97},{33,1},{65,33},{97,65},{2,98}... | collective-permute-start | bytes 442376 | tf_op jit(solution)/shard_map/ppermute | solution.py:91
  24.5 30.7 %all-to-all-start = ((bf16[32,5,1536]{2,1,0:T(8,128)(2,1)}), bf16[32,5,1536]{2,1,0:T(8,128)(2,1)S(1)}, u32[]{:S(2)}, u32[]{:S(2)}) async-start(bf16[32,5,1536]{2,1,0:T(8,128)(2,1)} %pad_maximum_fusion.4), calls=%async_computation | async-start | bytes 1572864 | tf_op jit(solution)/shard_map/all_to_all | solution.py:509
  31.5 533.7 %reduce-scatter.5.cloned.1.call-start = ((), (), s32[]{:S(2)}) async-start(), calls=%async_computation.8 | async-start | bytes 8773632 | tf_op jit(solution)/shard_map/reduce_scatter | solution.py:372
  48.0 20.7 %collective-permute-start.7 = (bf16[4,48,1536]{2,1,0:T(8,128)(2,1)}, bf16[4,48,1536]{2,1,0:T(8,128)(2,1)}, u32[]{:S(2)}, u32[]{:S(2)}) collective-permute-start(bf16[4,48,1536]{2,1,0:T(8,128)(2,1)} %pad_maximum_fusion.8), channel_id=1, source_target_pairs={{0,8},{8,16},{16,24},{24,0},{1,9},{9,17},{17,25},{25,1},{2,10},{10... | collective-permute-start | bytes 1769480 | tf_op jit(solution)/shard_map/ppermute | solution.py:91
  49.4 46.3 %collective-permute-start.8 = (bf16[4,48,1536]{2,1,0:T(8,128)(2,1)}, bf16[4,48,1536]{2,1,0:T(8,128)(2,1)}, u32[]{:S(2)}, u32[]{:S(2)}) collective-permute-start(bf16[4,48,1536]{2,1,0:T(8,128)(2,1)} %pad_maximum_fusion.8), channel_id=1, source_target_pairs={{0,16},{8,24},{16,0},{24,8},{1,17},{9,25},{17,1},{25,9},{2,18},{10... | collective-permute-start | bytes 1769480 | tf_op jit(solution)/shard_map/ppermute | solution.py:91
  51.8 46.1 %collective-permute-start.9 = (bf16[4,48,1536]{2,1,0:T(8,128)(2,1)}, bf16[4,48,1536]{2,1,0:T(8,128)(2,1)S(1)}, u32[]{:S(2)}, u32[]{:S(2)}) collective-permute-start(bf16[4,48,1536]{2,1,0:T(8,128)(2,1)} %pad_maximum_fusion.8), channel_id=1, source_target_pairs={{0,24},{8,0},{16,8},{24,16},{1,25},{9,1},{17,9},{25,17},{2,26},{10... | collective-permute-start | bytes 1769480 | tf_op jit(solution)/shard_map/ppermute | solution.py:91
  56.3 46.5 %collective-permute-start.2 = (bf16[128,1536]{1,0:T(8,128)(2,1)S(1)}, bf16[128,1536]{1,0:T(8,128)(2,1)S(1)}, u32[]{:S(2)}, u32[]{:S(2)}) collective-permute-start(bf16[128,1536]{1,0:T(8,128)(2,1)S(1)} %reshape.1094), channel_id=1, source_target_pairs={{0,3},{1,0},{2,1},{3,2},{4,7},{5,4},{6,5},{7,6},{8,11},{9,8},{10,9... | collective-permute-start | bytes 1179656 | tf_op jit(solution)/shard_map/ppermute | solution.py:96
  59.1 43.8 %collective-permute-start.1 = (bf16[128,1536]{1,0:T(8,128)(2,1)S(1)}, bf16[128,1536]{1,0:T(8,128)(2,1)S(1)}, u32[]{:S(2)}, u32[]{:S(2)}) collective-permute-start(bf16[128,1536]{1,0:T(8,128)(2,1)S(1)} %reshape.1094), channel_id=1, source_target_pairs={{0,2},{1,3},{2,0},{3,1},{4,6},{5,7},{6,4},{7,5},{8,10},{9,11},{10,... | collective-permute-start | bytes 1179656 | tf_op jit(solution)/shard_map/ppermute | solution.py:96
  68.7 34.1 %collective-permute-start = (bf16[128,1536]{1,0:T(8,128)(2,1)S(1)}, bf16[128,1536]{1,0:T(8,128)(2,1)}, u32[]{:S(2)}, u32[]{:S(2)}) collective-permute-start(bf16[128,1536]{1,0:T(8,128)(2,1)S(1)} %reshape.1094), channel_id=1, source_target_pairs={{0,1},{1,2},{2,3},{3,0},{4,5},{5,6},{6,7},{7,4},{8,9},{9,10},{10,1... | collective-permute-start | bytes 1179656 | tf_op jit(solution)/shard_map/ppermute | solution.py:96
  255.8 28.1 %collective-permute-start.38 = (bf16[256,5760]{1,0:T(8,128)(2,1)}, bf16[256,5760]{1,0:T(8,128)(2,1)S(1)}, u32[]{:S(2)}, u32[]{:S(2)}) collective-permute-start(bf16[256,5760]{1,0:T(8,128)(2,1)} %get-tuple-element.61.refs_0_.refs_2_), channel_id=1, source_target_pairs={{0,4},{4,0},{1,5},{5,1},{2,6},{6,2},{3,7},{7,3},{8,12},{12,8},{9,1... | collective-permute-start | bytes 8847368 | tf_op jit(solution)/shard_map/ppermute | solution.py:86
  260.5 12.9 %collective-permute-start.60 = (bf16[64,1536]{1,0:T(8,128)(2,1)S(1)}, bf16[64,1536]{1,0:T(8,128)(2,1)S(1)}, u32[]{:S(2)}, u32[]{:S(2)}) collective-permute-start(bf16[64,1536]{1,0:T(8,128)(2,1)S(1)} %get-tuple-element.81), channel_id=1, source_target_pairs={{0,1},{1,2},{2,3},{3,0},{4,5},{5,6},{6,7},{7,4},{8,9},{9,10},{10,1... | collective-permute-start | bytes 589832 | tf_op jit(solution)/shard_map/ppermute | solution.py:96
  265.0 13.2 %collective-permute-start.59 = (bf16[64,1536]{1,0:T(8,128)(2,1)S(1)}, bf16[64,1536]{1,0:T(8,128)(2,1)S(1)}, u32[]{:S(2)}, u32[]{:S(2)}) collective-permute-start(bf16[64,1536]{1,0:T(8,128)(2,1)S(1)} %get-tuple-element.80), channel_id=1, source_target_pairs={{0,2},{1,3},{2,0},{3,1},{4,6},{5,7},{6,4},{7,5},{8,10},{9,11},{10,... | collective-permute-start | bytes 589832 | tf_op jit(solution)/shard_map/ppermute | solution.py:96
  280.0 16.0 %collective-permute-start.35 = (bf16[64,1536]{1,0:T(8,128)(2,1)S(1)}, bf16[64,1536]{1,0:T(8,128)(2,1)S(1)}, u32[]{:S(2)}, u32[]{:S(2)}) collective-permute-start(bf16[64,1536]{1,0:T(8,128)(2,1)S(1)} %get-tuple-element.63), channel_id=1, source_target_pairs={{0,1},{1,2},{2,3},{3,0},{4,5},{5,6},{6,7},{7,4},{8,9},{9,10},{10,1... | collective-permute-start | bytes 589832 | tf_op jit(solution)/shard_map/ppermute | solution.py:96
  280.2 15.8 %collective-permute-start.36 = (bf16[64,1536]{1,0:T(8,128)(2,1)S(1)}, bf16[64,1536]{1,0:T(8,128)(2,1)S(1)}, u32[]{:S(2)}, u32[]{:S(2)}) collective-permute-start(bf16[64,1536]{1,0:T(8,128)(2,1)S(1)} %get-tuple-element.63), channel_id=1, source_target_pairs={{0,2},{1,3},{2,0},{3,1},{4,6},{5,7},{6,4},{7,5},{8,10},{9,11},{10,... | collective-permute-start | bytes 589832 | tf_op jit(solution)/shard_map/ppermute | solution.py:96
  300.5 54.9 %collective-permute-start.49 = (bf16[256,1536]{1,0:T(8,128)(2,1)}, bf16[256,1536]{1,0:T(8,128)(2,1)}, u32[]{:S(2)}, u32[]{:S(2)}) collective-permute-start(bf16[256,1536]{1,0:T(8,128)(2,1)} %constant_dynamic-update-slice_fusion.15), channel_id=1, source_target_pairs={{0,4},{4,0},{1,5},{5,1},{2,6},{6,2},{3,7},{7,3},{8,12},{12,8},{9,1... | collective-permute-start | bytes 2359304 | tf_op jit(solution)/shard_map/ppermute | solution.py:86
  313.5 13.6 %collective-permute-start.40 = (bf16[256,256]{0,1:T(8,128)(2,1)S(1)}, bf16[256,256]{0,1:T(8,128)(2,1)S(1)}, u32[]{:S(2)}, u32[]{:S(2)}) collective-permute-start(bf16[256,256]{0,1:T(8,128)(2,1)S(1)} %get-tuple-element.284), channel_id=1, source_target_pairs={{0,8},{4,12},{8,0},{12,4},{1,9},{5,13},{9,1},{13,5},{2,10},{6,14},... | collective-permute-start | bytes 393224 | tf_op jit(solution)/shard_map/ppermute | solution.py:82
  317.1 37.7 %collective-permute-start.48 = (bf16[256,1536]{1,0:T(8,128)(2,1)S(1)}, bf16[256,1536]{1,0:T(8,128)(2,1)S(1)}, u32[]{:S(2)}, u32[]{:S(2)}) collective-permute-start(bf16[256,1536]{1,0:T(8,128)(2,1)S(1)} %get-tuple-element.248.refs_0_), channel_id=1, source_target_pairs={{0,4},{4,0},{1,5},{5,1},{2,6},{6,2},{3,7},{7,3},{8,12},{12,8},{9,1... | collective-permute-start | bytes 2359304 | tf_op jit(solution)/shard_map/ppermute | solution.py:86
  342.6 14.1 %collective-permute-start.50 = (bf16[256,512]{1,0:T(8,128)(2,1)S(1)}, bf16[256,512]{1,0:T(8,128)(2,1)S(1)}, u32[]{:S(2)}, u32[]{:S(2)}) collective-permute-start(bf16[256,512]{1,0:T(8,128)(2,1)S(1)} %get-tuple-element.280), channel_id=1, source_target_pairs={{0,4},{4,0},{1,5},{5,1},{2,6},{6,2},{3,7},{7,3},{8,12},{12,8},{9,1... | collective-permute-start | bytes 786440 | tf_op jit(solution)/shard_map/ppermute | solution.py:86
  380.0 34.8 %collective-permute-start.57 = (bf16[256,5760]{1,0:T(8,128)(2,1)}, bf16[256,5760]{1,0:T(8,128)(2,1)}, u32[]{:S(2)}, u32[]{:S(2)}) collective-permute-start(bf16[256,5760]{1,0:T(8,128)(2,1)} %get-tuple-element.75.refs_0_.refs_2_), channel_id=1, source_target_pairs={{0,4},{4,0},{1,5},{5,1},{2,6},{6,2},{3,7},{7,3},{8,12},{12,8},{9,1... | collective-permute-start | bytes 8847368 | tf_op jit(solution)/shard_map/ppermute | solution.py:86
  385.3 19.5 %collective-permute-start.53 = (bf16[64,1536]{1,0:T(8,128)(2,1)}, bf16[64,1536]{1,0:T(8,128)(2,1)S(1)}, u32[]{:S(2)}, u32[]{:S(2)}) collective-permute-start(bf16[64,1536]{1,0:T(8,128)(2,1)} %get-tuple-element.74), channel_id=1, source_target_pairs={{0,1},{1,2},{2,3},{3,0},{4,5},{5,6},{6,7},{7,4},{8,9},{9,10},{10,1... | collective-permute-start | bytes 589832 | tf_op jit(solution)/shard_map/ppermute | solution.py:96
  389.2 15.9 %collective-permute-start.52 = (bf16[64,1536]{1,0:T(8,128)(2,1)}, bf16[64,1536]{1,0:T(8,128)(2,1)}, u32[]{:S(2)}, u32[]{:S(2)}) collective-permute-start(bf16[64,1536]{1,0:T(8,128)(2,1)} %get-tuple-element.73), channel_id=1, source_target_pairs={{0,2},{1,3},{2,0},{3,1},{4,6},{5,7},{6,4},{7,5},{8,10},{9,11},{10,... | collective-permute-start | bytes 589832 | tf_op jit(solution)/shard_map/ppermute | solution.py:96
  392.4 13.5 %collective-permute-start.51 = (bf16[64,1536]{1,0:T(8,128)(2,1)}, bf16[64,1536]{1,0:T(8,128)(2,1)}, u32[]{:S(2)}, u32[]{:S(2)}) collective-permute-start(bf16[64,1536]{1,0:T(8,128)(2,1)} %get-tuple-element.72), channel_id=1, source_target_pairs={{0,3},{1,0},{2,1},{3,2},{4,7},{5,4},{6,5},{7,6},{8,11},{9,8},{10,9... | collective-permute-start | bytes 589832 | tf_op jit(solution)/shard_map/ppermute | solution.py:96
  398.7 26.5 %all-to-all-start.1 = ((bf16[32,8,1536]{2,1,0:T(8,128)(2,1)}), bf16[32,8,1536]{2,1,0:T(8,128)(2,1)}, u32[]{:S(2)}, u32[]{:S(2)}) async-start(bf16[32,8,1536]{2,1,0:T(8,128)(2,1)} %gather_fusion.4), calls=%async_computation.1 | async-start | bytes 1572864 | tf_op jit(solution)/shard_map/all_to_all | solution.py:721
  404.7 167.8 %reduce-scatter.3.cloned.1.call-start = ((), (), s32[]{:S(2)}) async-start(), calls=%async_computation.7 | async-start | bytes 10444800 | tf_op jit(solution)/shard_map/reduce_scatter | solution.py:372
  410.5 14.8 %collective-permute-start.54 = (bf16[64,1536]{1,0:T(8,128)(2,1)S(1)}, bf16[64,1536]{1,0:T(8,128)(2,1)S(1)}, u32[]{:S(2)}, u32[]{:S(2)}) collective-permute-start(bf16[64,1536]{1,0:T(8,128)(2,1)S(1)} %get-tuple-element.83), channel_id=1, source_target_pairs={{0,1},{1,2},{2,3},{3,0},{4,5},{5,6},{6,7},{7,4},{8,9},{9,10},{10,1... | collective-permute-start | bytes 589832 | tf_op jit(solution)/shard_map/ppermute | solution.py:96
  411.6 13.6 %collective-permute-start.55 = (bf16[64,1536]{1,0:T(8,128)(2,1)S(1)}, bf16[64,1536]{1,0:T(8,128)(2,1)S(1)}, u32[]{:S(2)}, u32[]{:S(2)}) collective-permute-start(bf16[64,1536]{1,0:T(8,128)(2,1)S(1)} %get-tuple-element.83), channel_id=1, source_target_pairs={{0,2},{1,3},{2,0},{3,1},{4,6},{5,7},{6,4},{7,5},{8,10},{9,11},{10,... | collective-permute-start | bytes 589832 | tf_op jit(solution)/shard_map/ppermute | solution.py:96
  426.4 72.7 %collective-permute-start.71 = (bf16[256,1536]{1,0:T(8,128)(2,1)S(1)}, bf16[256,1536]{1,0:T(8,128)(2,1)S(1)}, u32[]{:S(2)}, u32[]{:S(2)}) collective-permute-start(bf16[256,1536]{1,0:T(8,128)(2,1)S(1)} %copy-done.3), channel_id=1, source_target_pairs={{0,4},{4,0},{1,5},{5,1},{2,6},{6,2},{3,7},{7,3},{8,12},{12,8},{9,1... | collective-permute-start | bytes 2359304 | tf_op jit(solution)/shard_map/ppermute | solution.py:86
  441.6 17.3 %collective-permute-start.67 = (bf16[64,1536]{1,0:T(8,128)(2,1)}, bf16[64,1536]{1,0:T(8,128)(2,1)S(1)}, u32[]{:S(2)}, u32[]{:S(2)}) collective-permute-start(bf16[64,1536]{1,0:T(8,128)(2,1)} %get-tuple-element.244), channel_id=1, source_target_pairs={{0,1},{1,2},{2,3},{3,0},{4,5},{5,6},{6,7},{7,4},{8,9},{9,10},{10,1... | collective-permute-start | bytes 589832 | tf_op jit(solution)/shard_map/ppermute | solution.py:96
  443.5 15.4 %collective-permute-start.66 = (bf16[64,1536]{1,0:T(8,128)(2,1)}, bf16[64,1536]{1,0:T(8,128)(2,1)S(1)}, u32[]{:S(2)}, u32[]{:S(2)}) collective-permute-start(bf16[64,1536]{1,0:T(8,128)(2,1)} %get-tuple-element.245), channel_id=1, source_target_pairs={{0,2},{1,3},{2,0},{3,1},{4,6},{5,7},{6,4},{7,5},{8,10},{9,11},{10,... | collective-permute-start | bytes 589832 | tf_op jit(solution)/shard_map/ppermute | solution.py:96
  443.9 15.1 %collective-permute-start.65 = (bf16[64,1536]{1,0:T(8,128)(2,1)S(1)}, bf16[64,1536]{1,0:T(8,128)(2,1)}, u32[]{:S(2)}, u32[]{:S(2)}) collective-permute-start(bf16[64,1536]{1,0:T(8,128)(2,1)S(1)} %get-tuple-element.243), channel_id=1, source_target_pairs={{0,3},{1,0},{2,1},{3,2},{4,7},{5,4},{6,5},{7,6},{8,11},{9,8},{10,9... | collective-permute-start | bytes 589832 | tf_op jit(solution)/shard_map/ppermute | solution.py:96
  466.1 13.6 %collective-permute-start.68 = (bf16[80,1536]{1,0:T(8,128)(2,1)}, bf16[80,1536]{1,0:T(8,128)(2,1)S(1)}, u32[]{:S(2)}, u32[]{:S(2)}) collective-permute-start(bf16[80,1536]{1,0:T(8,128)(2,1)} %concatenate.202), channel_id=1, source_target_pairs={{0,1},{1,2},{2,3},{3,0},{4,5},{5,6},{6,7},{7,4},{8,9},{9,10},{10,1... | collective-permute-start | bytes 737288 | tf_op jit(solution)/shard_map/ppermute | solution.py:96
  466.1 14.3 %collective-permute-start.69 = (bf16[80,1536]{1,0:T(8,128)(2,1)}, bf16[80,1536]{1,0:T(8,128)(2,1)}, u32[]{:S(2)}, u32[]{:S(2)}) collective-permute-start(bf16[80,1536]{1,0:T(8,128)(2,1)} %concatenate.202), channel_id=1, source_target_pairs={{0,2},{1,3},{2,0},{3,1},{4,6},{5,7},{6,4},{7,5},{8,10},{9,11},{10,... | collective-permute-start | bytes 737288 | tf_op jit(solution)/shard_map/ppermute | solution.py:96
  468.0 12.6 %collective-permute-start.70 = (bf16[80,1536]{1,0:T(8,128)(2,1)}, bf16[80,1536]{1,0:T(8,128)(2,1)}, u32[]{:S(2)}, u32[]{:S(2)}) collective-permute-start(bf16[80,1536]{1,0:T(8,128)(2,1)} %concatenate.202), channel_id=1, source_target_pairs={{0,3},{1,0},{2,1},{3,2},{4,7},{5,4},{6,5},{7,6},{8,11},{9,8},{10,9... | collective-permute-start | bytes 737288 | tf_op jit(solution)/shard_map/ppermute | solution.py:96
  470.6 28.6 %collective-permute-start.72 = (bf16[256,1536]{1,0:T(8,128)(2,1)}, bf16[256,1536]{1,0:T(8,128)(2,1)}, u32[]{:S(2)}, u32[]{:S(2)}) collective-permute-start(bf16[256,1536]{1,0:T(8,128)(2,1)} %copy-done.34), channel_id=1, source_target_pairs={{0,4},{4,0},{1,5},{5,1},{2,6},{6,2},{3,7},{7,3},{8,12},{12,8},{9,1... | collective-permute-start | bytes 2359304 | tf_op jit(solution)/shard_map/ppermute | solution.py:86
  480.4 20.0 %collective-permute-start.73 = (bf16[256,768]{1,0:T(8,128)(2,1)}, bf16[256,768]{1,0:T(8,128)(2,1)S(1)}, u32[]{:S(2)}, u32[]{:S(2)}) collective-permute-start(bf16[256,768]{1,0:T(8,128)(2,1)} %get-tuple-element.241), channel_id=1, source_target_pairs={{0,4},{4,0},{1,5},{5,1},{2,6},{6,2},{3,7},{7,3},{8,12},{12,8},{9,1... | collective-permute-start | bytes 1179656 | tf_op jit(solution)/shard_map/ppermute | solution.py:86
  507.6 16.2 %collective-permute-start.76 = (bf16[4,96,384]{2,1,0:T(8,128)(2,1)}, bf16[4,96,384]{2,1,0:T(8,128)(2,1)}, u32[]{:S(2)}, u32[]{:S(2)}) collective-permute-start(bf16[4,96,384]{2,1,0:T(8,128)(2,1)} %get-tuple-element.237), channel_id=1, source_target_pairs={{0,96},{32,0},{64,32},{96,64},{1,97},{33,1},{65,33},{97,65},{2,98}... | collective-permute-start | bytes 884744 | tf_op jit(solution)/shard_map/ppermute | solution.py:91
  510.4 13.4 %collective-permute-start.75 = (bf16[4,96,384]{2,1,0:T(8,128)(2,1)S(1)}, bf16[4,96,384]{2,1,0:T(8,128)(2,1)}, u32[]{:S(2)}, u32[]{:S(2)}) collective-permute-start(bf16[4,96,384]{2,1,0:T(8,128)(2,1)S(1)} %get-tuple-element.238), channel_id=1, source_target_pairs={{0,64},{32,96},{64,0},{96,32},{1,65},{33,97},{65,1},{97,33},{2,66}... | collective-permute-start | bytes 884744 | tf_op jit(solution)/shard_map/ppermute | solution.py:91
  510.9 16.2 %collective-permute-start.74 = (bf16[4,96,384]{2,1,0:T(8,128)(2,1)S(1)}, bf16[4,96,384]{2,1,0:T(8,128)(2,1)}, u32[]{:S(2)}, u32[]{:S(2)}) collective-permute-start(bf16[4,96,384]{2,1,0:T(8,128)(2,1)S(1)} %get-tuple-element.236), channel_id=1, source_target_pairs={{0,32},{32,64},{64,96},{96,0},{1,33},{33,65},{65,97},{97,1},{2,34}... | collective-permute-start | bytes 884744 | tf_op jit(solution)/shard_map/ppermute | solution.py:91
  512.9 52.1 %all-to-all-start.2 = ((bf16[32,12,1536]{2,1,0:T(8,128)(2,1)}), bf16[32,12,1536]{2,1,0:T(8,128)(2,1)S(1)}, u32[]{:S(2)}, u32[]{:S(2)}) async-start(bf16[32,12,1536]{2,1,0:T(8,128)(2,1)} %pad_maximum_fusion.2), calls=%async_computation.2 | async-start | bytes 3145728 | tf_op jit(solution)/shard_map/all_to_all | solution.py:840
  516.9 25.3 %collective-permute-start.82 = (bf16[4,96,384]{2,1,0:T(8,128)(2,1)S(1)}, bf16[4,96,384]{2,1,0:T(8,128)(2,1)S(1)}, u32[]{:S(2)}, u32[]{:S(2)}) collective-permute-start(bf16[4,96,384]{2,1,0:T(8,128)(2,1)S(1)} %get-tuple-element.235), channel_id=1, source_target_pairs={{0,24},{8,0},{16,8},{24,16},{1,25},{9,1},{17,9},{25,17},{2,26},{10... | collective-permute-start | bytes 884744 | tf_op jit(solution)/shard_map/ppermute | solution.py:91
  519.6 25.7 %collective-permute-start.81 = (bf16[4,96,384]{2,1,0:T(8,128)(2,1)S(1)}, bf16[4,96,384]{2,1,0:T(8,128)(2,1)S(1)}, u32[]{:S(2)}, u32[]{:S(2)}) collective-permute-start(bf16[4,96,384]{2,1,0:T(8,128)(2,1)S(1)} %get-tuple-element.234), channel_id=1, source_target_pairs={{0,16},{8,24},{16,0},{24,8},{1,17},{9,25},{17,1},{25,9},{2,18},{10... | collective-permute-start | bytes 884744 | tf_op jit(solution)/shard_map/ppermute | solution.py:91
  523.8 26.8 %collective-permute-start.80 = (bf16[4,96,384]{2,1,0:T(8,128)(2,1)S(1)}, bf16[4,96,384]{2,1,0:T(8,128)(2,1)S(1)}, u32[]{:S(2)}, u32[]{:S(2)}) collective-permute-start(bf16[4,96,384]{2,1,0:T(8,128)(2,1)S(1)} %get-tuple-element.233), channel_id=1, source_target_pairs={{0,8},{8,16},{16,24},{24,0},{1,9},{9,17},{17,25},{25,1},{2,10},{10... | collective-permute-start | bytes 884744 | tf_op jit(solution)/shard_map/ppermute | solution.py:91
  528.5 24.8 %collective-permute-start.79 = (bf16[96,384]{1,0:T(8,128)(2,1)S(1)}, bf16[96,384]{1,0:T(8,128)(2,1)S(1)}, u32[]{:S(2)}, u32[]{:S(2)}) collective-permute-start(bf16[96,384]{1,0:T(8,128)(2,1)S(1)} %get-tuple-element.268), channel_id=1, source_target_pairs={{0,24},{8,0},{16,8},{24,16},{1,25},{9,1},{17,9},{25,17},{2,26},{10... | collective-permute-start | bytes 221192 | tf_op jit(solution)/shard_map/ppermute | solution.py:91
  528.6 25.5 %collective-permute-start.78 = (bf16[96,384]{1,0:T(8,128)(2,1)S(1)}, bf16[96,384]{1,0:T(8,128)(2,1)S(1)}, u32[]{:S(2)}, u32[]{:S(2)}) collective-permute-start(bf16[96,384]{1,0:T(8,128)(2,1)S(1)} %get-tuple-element.269), channel_id=1, source_target_pairs={{0,16},{8,24},{16,0},{24,8},{1,17},{9,25},{17,1},{25,9},{2,18},{10... | collective-permute-start | bytes 221192 | tf_op jit(solution)/shard_map/ppermute | solution.py:91
  (206 other events, 2170.0 us)
Sparse Core Ops, SparseCore 0:
  10.9 108.8 all-gather.2
  122.7 73.4 all-gather.4
  296.2 85.0 reduce-scatter.4
  425.4 86.7 reduce-scatter.2

commit v4 on v3

--- a/solution.py
+++ b/solution.py
@@ -115,17 +115,8 @@
     return total
 
 
-def reorder(rows):
-    members = lax.axis_size("tp")
-    own = lax.axis_index("tp")
-    chunk = rows.shape[0] // members
-    return jnp.concatenate(
-        [
-            lax.dynamic_slice_in_dim(rows, (own - k) % members * chunk, chunk, 0)
-            for k in range(members)
-        ],
-        axis=0,
-    )
+def arrange(order, rows):
+    return times(order, rows).astype(BF16)
 
 
 def times(left, right):
@@ -389,23 +380,6 @@
     low = along(along(blocks[..., :half], "x", 0), Z_AXES, 0)
     high = along(along(blocks[..., half:], Z_AXES, 1), "x", 0)
     return share_rows(jnp.concatenate([low, high], axis=1).astype(BF16))
-
-
-def gather_pack(pack):
-    rows, columns = pack.shape
-    blocks = pack[None]
-    for axis in ("x", Z_AXES):
-        blocks = jnp.concatenate(
-            [blocks] + [shift_ring(blocks, axis, k) for k in range(1, lax.axis_size(axis))]
-        )
-    blocks = jnp.concatenate([blocks, swap_core(blocks)])
-    ring = lax.axis_size("x")
-    index = jnp.arange(blocks.shape[0])
-    step_core = (index % CORES - lax.axis_index("core")) % CORES
-    step_z = (lax.axis_index(Z_AXES) - index // CORES % ring) % ring
-    step_x = (lax.axis_index("x") - index // CORES // ring) % ring
-    place = (step_core * ring + step_z) * ring + step_x
-    return jnp.take(blocks, place, axis=0, mode="clip").reshape(-1, columns)
 
 
 def ffn_gradients(low, high, steps, hidden):
@@ -473,13 +447,13 @@
         return [wide, jnp.pad(down.T, ((0, 0), (0, padded - hidden)))]
 
     mixer_pack = jnp.concatenate([mixer_project.reshape(depth, -1), mixer_output.T], axis=1)
+    mixer_all = lax.all_gather(mixer_pack, TOKEN_AXES, axis=0, tiled=True)
     first_pack = jnp.concatenate(
         pack_ffn(first_gateup, first_down) + [attend_project, attend_output.T], axis=1
     )
     second_pack = jnp.concatenate(pack_ffn(second_gateup, second_down), axis=1)
     first_all = lax.all_gather(first_pack, TOKEN_AXES, axis=0, tiled=True)
     second_all = lax.all_gather(second_pack, TOKEN_AXES, axis=0, tiled=True)
-    mixer_all = gather_pack(mixer_pack)
     project_a = mixer_all[:, : 3 * channels]
     output_a_t = mixer_all[:, 3 * channels :]
     project_b = first_all[:, ffn_width : ffn_width + attend_project.shape[1]]
@@ -515,21 +489,22 @@
         .astype(F32)
     )
     gain_a, gain_f, gain_b, gain_s = gains[0], gains[1], gains[2], gains[3]
-    parts = arrived[:, : 2 * part_rows][my_anchor].reshape(2 * shards * part_rows, width)
-    parts = jnp.concatenate(tp_gather(parts)).reshape(members, shards, 2, part_rows, width)
-    member_slot = (own - jnp.arange(members)) % members
-    parts = jnp.stack(
-        [lax.dynamic_index_in_dim(parts, member_slot[t], 0, keepdims=False) for t in range(members)],
-        axis=2,
-    )
-    tokens = parts[:, 0].reshape(row_count, width)
-    back_s = parts[:, 1].reshape(row_count, width)
-    stream0 = lax.dynamic_slice_in_dim(tokens, own * chunk, chunk, 0).astype(F32)
-    upstream = lax.dynamic_slice_in_dim(back_s, own * chunk, chunk, 0).astype(F32)
-    back_s_chunks = [
-        lax.dynamic_slice_in_dim(back_s, (own - k) % members * chunk, chunk, 0)
-        for k in range(members)
-    ]
+    parts = arrived[:, : 2 * part_rows][my_anchor]
+    own_tokens = parts[:, :part_rows].reshape(chunk, width)
+    own_back = parts[:, part_rows:].reshape(chunk, width)
+    stream0 = own_tokens.astype(F32)
+    upstream = own_back.astype(F32)
+    both = tp_gather(jnp.concatenate([own_tokens, own_back]))
+    back_s_chunks = [slot[chunk:] for slot in both]
+
+    gathered = jnp.arange(row_count)
+    member_of = (own - gathered // chunk) % members
+    offsets = (
+        gathered % chunk // part_rows * piece_rows + member_of * part_rows + gathered % part_rows
+    )
+    to_gathered = (offsets[:, None] == gathered[None, :]).astype(BF16)
+    to_dealt = (offsets[None, :] == gathered[:, None]).astype(BF16)
+    tokens = times(to_dealt, jnp.concatenate([slot[:chunk] for slot in both]))
 
     kernel_taps = mixer_kernel.shape[0]
     halo = kernel_taps - 1
@@ -537,7 +512,6 @@
     halo_segment, unused = locate(
         seq_lengths, local_rows[0] - halo + jnp.arange(row_count + halo)
     )
-    offsets = reorder(jnp.arange(row_count))
     segment, places = locate(seq_lengths, device * row_count + offsets)
     ctx = lax.axis_index(CTX_AXES)
     group_rows = jnp.concatenate(
@@ -555,7 +529,7 @@
     sine = jnp.sin(angles)
 
     kernel_local = lax.dynamic_slice_in_dim(mixer_kernel, own * channels, channels, 1).astype(F32)
-    mixer_in = norm_rows(tokens.astype(F32), gain_a).astype(BF16)
+    mixer_in = norm_rows(tokens, gain_a).astype(BF16)
     mixer_in_other = swap_core(mixer_in)
     halo_pad = 16
     halo_in = from_behind(mixer_in[row_count - halo_pad :], 1)
@@ -565,8 +539,9 @@
     proj_x_part = proj_a[:, 2 * channels :]
     extended = (proj_b_part * proj_x_part)[halo_pad - halo :].astype(BF16).astype(F32)
     conv_out = shortconv(extended, kernel_local, halo_segment)
-    gated_rows = reorder((proj_c_part * conv_out).astype(BF16))
-    stream1 = stream0 + tp_reduce(tp_chunks(times_t(gated_rows, output_a_t)))
+    gated_rows = (proj_c_part * conv_out).astype(BF16)
+    gated_parts = arrange(to_gathered, gated_rows)
+    stream1 = stream0 + tp_reduce(tp_chunks(times_t(gated_parts, output_a_t)))
 
     normed_f = tp_gather(norm_rows(stream1, gain_f).astype(BF16))
     stream2 = stream1 + tp_reduce(ffn_forward(normed_f, first_all, steps))
@@ -702,31 +677,11 @@
         None,
     )
 
-    slot_for_anchor = jnp.sum(
-        jnp.where(
-            my_anchor[None, :] == jnp.arange(shards)[:, None], jnp.arange(shards)[None, :], 0
-        ),
-        axis=1,
-    )
-    dest_for_piece = jnp.sum(
-        jnp.where(
-            send_piece[None, :] == jnp.arange(shards)[:, None], jnp.arange(shards)[None, :], 0
-        ),
-        axis=1,
-    )
-    pieces = shards // members
-    slot_place = (own - slot_for_anchor // pieces) % members * pieces + slot_for_anchor % pieces
-    out_rows = jnp.concatenate(tp_gather(stream4.astype(BF16)))
-    out_rows = out_rows.reshape(shards, piece_rows, width)[slot_place]
-    out_home = lax.all_to_all(out_rows, TOKEN_AXES, split_axis=0, concat_axis=0, tiled=True)
     back_f = tp_gather(d_stream2.astype(BF16))
-    back_f, third = lax.optimization_barrier((back_f, third))
+    back_f, third, stream4 = lax.optimization_barrier((back_f, third, stream4))
     d_chunks, unused, keep, side = ffn_backward(
         core_ref, normed_f, back_f, first_all, steps, False
     )
-    unused, pullback = jax.vjp(norm_rows, stream1, gain_f)
-    d_stream, gain_f_grad = pullback(tp_reduce(d_chunks))
-    d_stream1 = d_stream2 + d_stream
     side_other = swap_core(side)
     ffn_lefts = [(side, 0), (side_other, 0), (side, 1), (side_other, 1)]
     partial = gradient(
@@ -744,14 +699,18 @@
         third,
     )
 
+    d_normed, partial = lax.optimization_barrier((tp_reduce(d_chunks), partial))
+    unused, pullback = jax.vjp(norm_rows, stream1, gain_f)
+    d_stream, gain_f_grad = pullback(d_normed)
+    d_stream1 = d_stream2 + d_stream
+
     back_a = tp_gather(d_stream1.astype(BF16))
-    back_a, partial, out_home = lax.optimization_barrier((back_a, partial, out_home))
     low, high = reduce_gradient(partial)
     first_grads = (low[:, :ffn_cols], high[:, :ffn_cols])
     attend_grads = jnp.concatenate([low[:, ffn_cols:], high[:, ffn_cols:]], axis=1)
-    back_a = jnp.concatenate(back_a)
+    back_a = arrange(to_dealt, jnp.concatenate(back_a))
     back_a_other = swap_core(back_a)
-    d_gated = reorder(times(back_a, output_a_t))
+    d_gated = times(back_a, output_a_t)
     d_cgate = d_gated * conv_out
     d_conv = d_gated * proj_c_part
     unused, pullback = jax.vjp(
@@ -772,86 +731,107 @@
         ],
         axis=1,
     ).astype(BF16)
-    d_mixer_in = tp_reduce(tp_chunks(times_t(reorder(d_proj_a), project_a)))
+    d_chunks = tp_chunks(times_t(arrange(to_gathered, d_proj_a), project_a))
+    keep, send = halves(d_proj_a, gated_rows)
+    mixer_cols = keep.shape[1]
+    partial = gradient(
+        [
+            (mixer_in, 0),
+            (mixer_in_other, 0),
+            (jnp.where(first_core, mixer_in, back_a), 0),
+            (jnp.where(first_core, mixer_in_other, back_a_other), 0),
+        ],
+        keep,
+        swap_core(send),
+        0,
+        mixer_cols,
+        1,
+        3 * channels - mixer_cols,
+        0,
+        width,
+        mixer_cols,
+        0,
+        None,
+    )
+    d_mixer_in, partial = lax.optimization_barrier((tp_reduce(d_chunks), partial))
     unused, pullback = jax.vjp(norm_rows, stream0, gain_a)
     d_norm_a, gain_a_grad = pullback(d_mixer_in)
     d_stream0 = d_stream1 + d_norm_a
-    keep, send = halves(d_proj_a, gated_rows)
-    mixer_cols = keep.shape[1]
-    low, high = exchange_gradient(
-        gradient(
-            [
-                (mixer_in, 0),
-                (mixer_in_other, 0),
-                (jnp.where(first_core, mixer_in, back_a), 0),
-                (jnp.where(first_core, mixer_in_other, back_a_other), 0),
-            ],
-            keep,
-            swap_core(send),
-            0,
-            mixer_cols,
-            1,
-            3 * channels - mixer_cols,
-            0,
-            width,
-            mixer_cols,
-            0,
-            None,
-        )
-    )
+    low, high = exchange_gradient(partial)
     mixer_grads = jnp.concatenate([low, high], axis=1)
 
-    def row_of(values):
-        flat = values.reshape(-1)
-        return jnp.concatenate([flat, jnp.zeros((width - flat.shape[0],), F32)])
-
-    small = jnp.stack(
-        [
-            gain_a_grad,
-            gain_f_grad,
-            gain_b_grad,
-            gain_s_grad,
-            row_of(jnp.concatenate([qgain_grad, kgain_grad])),
-            row_of(kernel_grad),
-        ]
-        + [jnp.zeros((width,), F32)] * 10
-    )
-    last = jnp.concatenate(
-        tp_gather(jnp.concatenate([d_stream0.astype(BF16), small.astype(BF16)]))
-    )
-    last = last.reshape(members, chunk + 16, width)
-    grad_rows = last[:, :chunk].reshape(shards, piece_rows, width)[slot_place]
-    smalls = last[:, chunk:].astype(F32)
-    summed = jnp.sum(smalls[:, :5], axis=0)
-    gain_sums = summed[:4].reshape(4, shards, depth).transpose(1, 0, 2).reshape(shards, 4 * depth)
-    head_sums = summed[4, : 2 * HD]
-    kernel_rows = reorder(smalls[:, 5, : kernel_taps * channels])
-    kernel_rows = kernel_rows.reshape(members, kernel_taps, channels).transpose(1, 0, 2)
-    shared = jnp.concatenate([kernel_rows.reshape(-1), head_sums])
-    fill = 4 * width - 4 * depth - shared.shape[0]
-    small_rows = jnp.concatenate(
-        [
-            gain_sums,
+    slot_for_anchor = jnp.sum(
+        jnp.where(
+            my_anchor[None, :] == jnp.arange(shards)[:, None], jnp.arange(shards)[None, :], 0
+        ),
+        axis=1,
+    )
+    gain_rows = jnp.concatenate(
+        [
+            grad.reshape(shards, depth)
+            for grad in (gain_f_grad, gain_b_grad, gain_s_grad, gain_a_grad)
+        ],
+        axis=1,
+    )
+    kernel_cols = kernel_taps * channels
+    shared = jnp.concatenate([kernel_grad.reshape(-1), qgain_grad, kgain_grad])
+    fill = width - shared.shape[0] - 4 * depth
+    small_row = jnp.concatenate(
+        [
             jnp.broadcast_to(shared, (shards, shared.shape[0])),
-            jnp.zeros((shards, fill), F32),
+            jnp.pad(gain_rows, ((0, 0), (0, fill))),
         ],
         axis=1,
     ).astype(BF16)
+
+    def by_anchor(rows):
+        return rows.astype(BF16).reshape(shards, part_rows, width)[slot_for_anchor]
+
     home = lax.all_to_all(
-        jnp.concatenate([grad_rows, small_rows.reshape(shards, 4, width)], axis=1),
+        jnp.concatenate(
+            [by_anchor(d_stream0), by_anchor(stream4), small_row[:, None]], axis=1
+        ),
         TOKEN_AXES,
         split_axis=0,
         concat_axis=0,
         tiled=True,
     )
-    layer_out = out_home[dest_for_piece].reshape(row_count, width)
-    input_gradient = home[:, :piece_rows][dest_for_piece].reshape(row_count, width)
-    totals = jnp.sum(home[:, piece_rows:].astype(F32), axis=0).reshape(-1)
-    gain_totals = totals[: 4 * depth].reshape(4, depth)
-    kernel_end = 4 * depth + kernel_taps * width
-    kernel_total = totals[4 * depth : kernel_end].reshape(kernel_taps, width)
-    qgain_total = totals[kernel_end : kernel_end + HD]
-    kgain_total = totals[kernel_end + HD : kernel_end + 2 * HD]
+    small_sum = jnp.sum(home[:, 2 * part_rows].astype(F32), axis=0)
+    small_high = small_sum.astype(BF16)
+    small_low = (small_sum - small_high.astype(F32)).astype(BF16)
+    last = tp_gather(
+        jnp.concatenate(
+            [
+                home[:, :part_rows].reshape(chunk, width),
+                home[:, part_rows : 2 * part_rows].reshape(chunk, width),
+                jnp.pad(jnp.stack([small_high, small_low]), ((0, 6), (0, 0))),
+            ]
+        )
+    )
+    home_rows = (
+        jnp.repeat(jnp.tile(send_piece, members), part_rows) * piece_rows
+        + member_of * part_rows
+        + gathered % part_rows
+    )
+    to_arrival = (home_rows[None, :] == gathered[:, None]).astype(BF16)
+    input_gradient = arrange(to_arrival, jnp.concatenate([slot[:chunk] for slot in last]))
+    layer_out = arrange(to_arrival, jnp.concatenate([slot[chunk : 2 * chunk] for slot in last]))
+    smalls = [
+        slot[2 * chunk].astype(F32) + slot[2 * chunk + 1].astype(F32) for slot in last
+    ]
+    totals = sum(smalls)
+    kernel_rows = jnp.stack([small[:kernel_cols].reshape(kernel_taps, channels) for small in smalls])
+    kernel_total = jnp.concatenate(
+        [
+            lax.dynamic_index_in_dim(kernel_rows, (own - member) % members, 0, keepdims=False)
+            for member in range(members)
+        ],
+        axis=1,
+    )
+    qgain_total = totals[kernel_cols : kernel_cols + HD]
+    kgain_total = totals[kernel_cols + HD : kernel_cols + 2 * HD]
+    gain_start = kernel_cols + 2 * HD
+    gain_totals = totals[gain_start : gain_start + 4 * depth].reshape(4, depth)
 
     gateup_s_grad, down_s_grad = ffn_gradients(*second_grads, steps, hidden)
     gateup_f_grad, down_f_grad = ffn_gradients(*first_grads, steps, hidden)
@@ -859,19 +839,19 @@
     return (
         layer_out,
         input_gradient,
-        gain_totals[0],
+        gain_totals[3],
         mixer_grads[:, : 3 * channels].reshape(depth, 3, channels),
         kernel_total,
         mixer_grads[:, 3 * channels :].T,
-        gain_totals[1],
+        gain_totals[0],
         gateup_f_grad,
         down_f_grad,
-        gain_totals[2],
+        gain_totals[1],
         attend_grads[:, :proj_cols],
         qgain_total,
         kgain_total,
         attend_grads[:, proj_cols:].T,
-        gain_totals[3],
+        gain_totals[2],
         gateup_s_grad,
         down_s_grad,
     )

time: 599 us -> 597 us (level)
  waiting for transfers between devices: 160 us -> 229 us
  local copies, waits for them, and re-layouts: 110 us -> 74.1 us
  starting transfers between devices: 134 us -> 109 us
  matrix products: 32.7 us -> 43.8 us
  other arithmetic: 56.2 us -> 46.6 us
  between operations: 25.8 us -> 18 us
    ppermute x51 -> x48, waiting for transfers between devices: 78 us -> 131 us  [shift_tp(): lax.ppermute(block, 'tp', [(i, (i + distance) % members) for i in range(m...]
    all_gather x1, waiting for transfers between devices: 0.01 us -> 37.6 us  [body(): first_all = lax.all_gather(first_pack, TOKEN_AXES, axis=0, tiled=True)]
    ppermute x18 -> x12, waiting for transfers between devices: 64.3 us -> 27.5 us  [shift_ring(): lax.ppermute(block, axis, [(i, (i + distance) % ring) for i in range(ring)])]
    concatenate x12 -> x4, local copies, waits for them, and re-layouts: 21.5 us -> 3.97 us  [the longest x1 2.7 us: body(): shared = jnp.concatenate([kernel_grad.reshape(-1), qgain_grad, kgain_grad])]
    ppermute x51 -> x48, starting transfers between devices: 69.8 us -> 56.8 us  [shift_tp(): lax.ppermute(block, 'tp', [(i, (i + distance) % members) for i in range(m...]
    all_to_all x1, waiting for transfers between devices: 0.01 us -> 11 us  [body(): lax.all_to_all(outgoing, TOKEN_AXES, split_axis=0, concat_axis=0, tiled=T...]
    gather x6 -> x3, local copies, waits for them, and re-layouts: 14.8 us -> 4.24 us  [the longest x2 3.36 us: by_anchor(): return rows.astype(BF16).reshape(shards, part_rows, width)[slot_for_anchor]]
    ppermute x18 -> x12, starting transfers between devices: 23.2 us -> 16.4 us  [shift_ring(): lax.ppermute(block, axis, [(i, (i + distance) % ring) for i in range(ring)])]
  transfers between devices with their start and end apart: 96 -> 86, of which waited for: 41 -> 48; matrix products, arithmetic and copies ran while one was open for 31% -> 23% of each run, Pallas kernels for 9% -> 9%
where the time goes in v4:
time: 597 us; the launch traced here: 588 us
  waiting for transfers between devices  229 us (38%)
  starting transfers between devices  109 us (18%)
  local copies, waits for them, and re-layouts  74.1 us (12%)
  Pallas kernels  68.3 us (11%)
  other arithmetic  46.6 us (8%)
  matrix products  43.8 us (7%)
  between operations  18 us (3%)
    ppermute x48, waiting for transfers between devices, shift_tp(): lax.ppermute(block, 'tp', [(i, (i + distance) % members) for i in range(m...  131 us
    ppermute x48, starting transfers between devices, shift_tp(): lax.ppermute(block, 'tp', [(i, (i + distance) % members) for i in range(m...  56.8 us
    all_gather x1, waiting for transfers between devices, body(): first_all = lax.all_gather(first_pack, TOKEN_AXES, axis=0, tiled=True)  37.6 us
    unnamed x343, local copies, waits for them, and re-layouts  30.6 us
    pallas_call x2, Pallas kernels, ffn_backward(): pl.pallas_call(functools.partial(ffn_backward_kernel, count, forward), gr...  30.2 us
    pallas_call x4, Pallas kernels, gradient(): pl.pallas_call(functools.partial(gradient_kernel, cut, whole_steps), grid...  27.7 us
    ppermute x12, waiting for transfers between devices, shift_ring(): lax.ppermute(block, axis, [(i, (i + distance) % ring) for i in range(ring)])  27.5 us
    ppermute x6, waiting for transfers between devices, swap_ctx(): lax.ppermute(block, CTX_AXES, [(i, i ^ mask) for i in range(lax.axis_size...  18.9 us
  transfers between devices with their start and end apart: 86, of which 48 were waited for; matrix products, arithmetic and copies ran while one was open for 23% of the time, Pallas kernels for 9%

profile of v4, /device:TPU:1, one launch (start us, length us, event | category | flops | bytes accessed | tf_op | source)
XLA Modules:
  0.0 587.9 jit_solution(13274074129377976126)
XLA Ops:
  21.2 9.4 %all-to-all-start = ((bf16[32,5,1536]{2,1,0:T(8,128)(2,1)}), bf16[32,5,1536]{2,1,0:T(8,128)(2,1)S(1)}, u32[]{:S(2)}, u32[]{:S(2)}) async-start(bf16[32,5,1536]{2,1,0:T(8,128)(2,1)} %pad_maximum_fusion.1), calls=%async_computation | async-start | bytes 1572864 | tf_op jit(solution)/shard_map/all_to_all | solution.py:483
  34.1 11.0 %all-to-all-done = bf16[32,5,1536]{2,1,0:T(8,128)(2,1)S(1)} async-done(((bf16[32,5,1536]{2,1,0:T(8,128)(2,1)}), bf16[32,5,1536]{2,1,0:T(8,128)(2,1)S(1)}, u32[]{:S(2)}, u32[]{:S(2)}) %all-to-all-start) | async-done | bytes 491552 | tf_op jit(solution)/shard_map/all_to_all | solution.py:483
  52.3 13.9 %collective-permute-done.2 = bf16[128,1536]{1,0:T(8,128)(2,1)S(1)} collective-permute-done((bf16[128,1536]{1,0:T(8,128)(2,1)S(1)}, bf16[128,1536]{1,0:T(8,128)(2,1)S(1)}, u32[]{:S(2)}, u32[]{:S(2)}) %collective-permute-start.2) | collective-permute-done | bytes 393248 | tf_op jit(solution)/shard_map/ppermute | solution.py:96
  66.3 5.0 collective-permute-done
  75.8 3.2 fusion.14
  81.1 3.0 fusion.225
  90.7 7.2 %collective-permute-done.6 = bf16[64,1536]{1,0:T(8,128)(2,1)} collective-permute-done((bf16[64,1536]{1,0:T(8,128)(2,1)}, bf16[64,1536]{1,0:T(8,128)(2,1)}, u32[]{:S(2)}, u32[]{:S(2)}) %collective-permute-start.6) | collective-permute-done | bytes 196640 | tf_op jit(solution)/shard_map/ppermute | solution.py:96
  106.0 5.3 collective-permute-done.8.refs_2_
  111.6 37.6 %all-gather.6.cloned.1.call-done.refs_4_.refs_5_.refs_8_.refs_9_ = bf16[1536,6400]{1,0:T(8,128)(2,1)} async-done(((bf16[48,6400]{1,0:T(8,128)(2,1)}), bf16[1536,6400]{1,0:T(8,128)(2,1)}) %all-gather.6.cloned.1.call-update) | async-done | bytes 19660816 | tf_op jit(solution)/shard_map/all_gather | solution.py:455
  149.2 10.4 %ffn_forward.1 = (f32[64,1536]{1,0:T(8,128)S(1)}, bf16[64,1536]{1,0:T(8,128)(2,1)S(1)}, bf16[64,1536]{1,0:T(8,128)(2,1)S(1)}, bf16[64,1536]{1,0:T(8,128)(2,1)S(1)}) custom-call(bf16[64,1536]{1,0:T(8,128)(2,1)S(1)} %multiply_convert_fusion.4.refs_0_, bf16[64,1536]{1,0:T(8,128)(2,1)S(1)} %collective-permute-done.7.refs_1_, ...), custom_call_target="tpu_custom_call" | custom-call | flops 4227858432 | bytes 16515072 | tf_op jit(solution)/shard_map/ffn_forward/pallas_call | solution.py:184
  167.3 5.1 collective-permute-done.11
  177.5 6.9 %collective-permute-done.15 = bf16[64,1536]{1,0:T(8,128)(2,1)S(1)} collective-permute-done((bf16[64,1536]{1,0:T(8,128)(2,1)S(1)}, bf16[64,1536]{1,0:T(8,128)(2,1)S(1)}, u32[]{:S(2)}, u32[]{:S(2)}) %collective-permute-start.15) | collective-permute-done | bytes 196640 | tf_op jit(solution)/shard_map/ppermute | solution.py:96
  184.4 4.5 collective-permute-done.13
  195.7 5.7 collective-permute-done.18
  201.4 5.4 collective-permute-done.17
  212.6 3.2 fusion.226
  218.7 8.7 %collective-permute-done.21 = bf16[64,1536]{1,0:T(8,128)(2,1)S(1)} collective-permute-done((bf16[64,1536]{1,0:T(8,128)(2,1)S(1)}, bf16[64,1536]{1,0:T(8,128)(2,1)S(1)}, u32[]{:S(2)}, u32[]{:S(2)}) %collective-permute-start.21) | collective-permute-done | bytes 196640 | tf_op jit(solution)/shard_map/ppermute | solution.py:96
  230.5 3.0 collective-permute-start.23
  235.8 6.0 %collective-permute-done.23.refs_2_ = bf16[64,1536]{1,0:T(8,128)(2,1)S(1)} collective-permute-done((bf16[64,1536]{1,0:T(8,128)(2,1)S(1)}, bf16[64,1536]{1,0:T(8,128)(2,1)S(1)}, u32[]{:S(2)}, u32[]{:S(2)}) %collective-permute-start.23) | collective-permute-done | bytes 196640 | tf_op jit(solution)/shard_map/ppermute | solution.py:96
  245.0 15.0 %ffn_both.1 = (f32[64,1536]{1,0:T(8,128)S(1)}, bf16[64,1536]{1,0:T(8,128)(2,1)S(1)}, bf16[64,1536]{1,0:T(8,128)(2,1)S(1)}, bf16[64,1536]{1,0:T(8,128)(2,1)S(1)},...) custom-call(s32[1]{0:T(128)} %bitcast.6.core_ref, ...), custom_call_target="tpu_custom_call" | custom-call | flops 8455716864 | bytes 22413312 | tf_op jit(solution)/shard_map/ffn_both/pallas_call | solution.py:269
  266.5 5.4 collective-permute-done.27
  271.8 3.7 collective-permute-done.26
  277.6 3.0 collective-permute-start.29
  282.7 10.4 %weight_gradient.4 = bf16[1536,2688]{1,0:T(8,128)(2,1)} custom-call(bf16[256,5760]{1,0:T(8,128)(2,1)S(1)} %copy-done, bf16[256,5760]{1,0:T(8,128)(2,1)} %copy-done.21, bf16[256,5760]{1,0:T(8,128)(2,1)S(1)} %copy-done, bf16[256,5760]{1,0:T(8,128)(2,1)} %copy-done.21, bf16[256,2688]{1,0:T(8,128)(2,1)S(1)} %get-tuple-element.61.refs_4_, ...), custom_call_target="tpu_custom_call" | custom-call | flops 4227858432 | bytes 8257536 | tf_op jit(solution)/shard_map/weight_gradient/pallas_call | solution.py:336
  298.8 3.0 collective-permute-done.46
  317.0 7.4 %fusion = (f32[2,3,256]{2,1,0:T(4,128)S(1)}, f32[2,1024,256,3]{2,1,3,0:T(8,128)}) fusion(f32[2,1024,256,3]{2,1,3,0:T(8,128)} %copy-done.20, f32[2,3,256]{2,1,0:T(4,128)S(1)} %log_add_fusion, pred[256,1024]{0,1:T(8,128)(4,1)S(1)} %compare_and_fusion, bf16[1024,2,64,1]{0,2,3,1:T(8,128)(2,1)S(1)} %bitcast.265, bf16[256,2,3,64]{0,3,2,1:T(8,128)(2,1)S(1)} %bitcast.271), kind=kOutput, calls=%fused_computation.7 | convolution fusion | flops 209189376 | bytes 13316096 | tf_op jit(solution)/shard_map/tkgd,nkd->kgtn/dot_general | solution.py:624
  324.4 4.9 fusion.2
  337.5 3.1 collective-permute-done.34
  340.7 4.6 collective-permute-done.33
  347.6 3.6 fusion.227
  373.2 3.6 weight_gradient.5.refs_6_
  376.9 3.4 collective-permute-done.39.refs_6_
  380.3 15.3 %ffn_backward.1 = (f32[64,1536]{1,0:T(8,128)S(1)}, bf16[64,1536]{1,0:T(8,128)(2,1)S(1)}, bf16[64,1536]{1,0:T(8,128)(2,1)S(1)}, bf16[64,1536]{1,0:T(8,128)(2,1)S(...) custom-call(s32[1]{0:T(128)} %bitcast.6.core_ref, bf16[64,1536]{1,0:T(8,128)(2,1)S(1)} %multiply_convert_fusion.4.refs_0_, ...), custom_call_target="tpu_custom_call" | custom-call | flops 7046430720 | bytes 22413312 | tf_op jit(solution)/shard_map/ffn_backward/pallas_call | solution.py:269
  400.5 4.4 collective-permute-done.49
  404.9 4.5 collective-permute-done.48
  413.0 10.4 %weight_gradient.6 = bf16[1536,3200]{1,0:T(8,128)(2,1)} custom-call(bf16[256,5760]{1,0:T(8,128)(2,1)S(1)} %copy-done.1, bf16[256,5760]{1,0:T(8,128)(2,1)} %copy-done.22, bf16[256,5760]{1,0:T(8,128)(2,1)S(1)} %copy-done.1, bf16[256,5760]{1,0:T(8,128)(2,1)} %copy-done.22, ...), custom_call_target="tpu_custom_call", output_to_operand_aliasing={{}: (6, {})} | custom-call | flops 4227858432 | bytes 8257536 | tf_op jit(solution)/shard_map/weight_gradient/pallas_call | solution.py:336
  425.6 3.0 collective-permute-start.53
  437.9 3.2 collective-permute-done.51
  452.0 4.9 fusion.228
  468.3 3.1 collective-permute-done.57
  474.6 3.3 weight_gradient.7
  488.2 5.0 all-to-all-start.1
  498.8 3.1 collective-permute-done.64
  505.7 7.0 %collective-permute-done.72 = bf16[4,96,384]{2,1,0:T(8,128)(2,1)S(1)} collective-permute-done((bf16[4,96,384]{2,1,0:T(8,128)(2,1)S(1)}, bf16[4,96,384]{2,1,0:T(8,128)(2,1)S(1)}, u32[]{:S(2)}, u32[]{:S(2)}) %collective-permute-start.72) | collective-permute-done | bytes 294944 | tf_op jit(solution)/shard_map/ppermute | solution.py:91
  514.2 11.4 %collective-permute-done.70 = bf16[4,96,384]{2,1,0:T(8,128)(2,1)S(1)} collective-permute-done((bf16[4,96,384]{2,1,0:T(8,128)(2,1)S(1)}, bf16[4,96,384]{2,1,0:T(8,128)(2,1)S(1)}, u32[]{:S(2)}, u32[]{:S(2)}) %collective-permute-start.70) | collective-permute-done | bytes 294944 | tf_op jit(solution)/shard_map/ppermute | solution.py:91
  542.2 7.2 %collective-permute-done.63 = bf16[136,1536]{1,0:T(8,128)(2,1)S(1)} collective-permute-done((bf16[136,1536]{1,0:T(8,128)(2,1)S(1)}, bf16[136,1536]{1,0:T(8,128)(2,1)S(1)}, u32[]{:S(2)}, u32[]{:S(2)}) %collective-permute-start.63) | collective-permute-done | bytes 417824 | tf_op jit(solution)/shard_map/ppermute | solution.py:96
  549.5 3.6 collective-permute-done.62
  553.1 9.9 %collective-permute-done.61 = bf16[136,1536]{1,0:T(8,128)(2,1)S(1)} collective-permute-done((bf16[136,1536]{1,0:T(8,128)(2,1)S(1)}, bf16[136,1536]{1,0:T(8,128)(2,1)S(1)}, u32[]{:S(2)}, u32[]{:S(2)}) %collective-permute-start.61) | collective-permute-done | bytes 417824 | tf_op jit(solution)/shard_map/ppermute | solution.py:96
  (756 shorter events, 245.0 us)
Async XLA Ops:
  7.2 68.6 %all-gather.4.cloned.1.call-start = ((), (), s32[]{:S(2)}) async-start(), calls=%async_computation.4 | async-start | bytes 4866048 | tf_op jit(solution)/shard_map/all_gather | solution.py:450
  9.6 139.6 %all-gather.6.cloned.1.call-start = ((), (), s32[]{:S(2)}) async-start(), calls=%async_computation.5 | async-start | bytes 20275200 | tf_op jit(solution)/shard_map/all_gather | solution.py:455
  12.7 220.8 %all-gather.8.cloned.1.call-start = ((), (), s32[]{:S(2)}) async-start(), calls=%async_computation.6 | async-start | bytes 17031168 | tf_op jit(solution)/shard_map/all_gather | solution.py:456
  21.2 23.9 %all-to-all-start = ((bf16[32,5,1536]{2,1,0:T(8,128)(2,1)}), bf16[32,5,1536]{2,1,0:T(8,128)(2,1)S(1)}, u32[]{:S(2)}, u32[]{:S(2)}) async-start(bf16[32,5,1536]{2,1,0:T(8,128)(2,1)} %pad_maximum_fusion.1), calls=%async_computation | async-start | bytes 1572864 | tf_op jit(solution)/shard_map/all_to_all | solution.py:483
  30.7 535.1 %reduce-scatter.5.cloned.1.call-start = ((), (), s32[]{:S(2)}) async-start(), calls=%async_computation.8 | async-start | bytes 8773632 | tf_op jit(solution)/shard_map/reduce_scatter | solution.py:363
  46.7 19.4 %collective-permute-start.2 = (bf16[128,1536]{1,0:T(8,128)(2,1)S(1)}, bf16[128,1536]{1,0:T(8,128)(2,1)S(1)}, u32[]{:S(2)}, u32[]{:S(2)}) collective-permute-start(bf16[128,1536]{1,0:T(8,128)(2,1)S(1)} %constant_dynamic-update-slice_fusion), channel_id=1, source_target_pairs={{0,3},{1,0},{2,1},{3,2},{4,7},{5,4},{6,5},{7,6},{8,11},{9,8},{10,9... | collective-permute-start | bytes 1179656 | tf_op jit(solution)/shard_map/ppermute | solution.py:96
  50.3 16.0 %collective-permute-start.1 = (bf16[128,1536]{1,0:T(8,128)(2,1)S(1)}, bf16[128,1536]{1,0:T(8,128)(2,1)S(1)}, u32[]{:S(2)}, u32[]{:S(2)}) collective-permute-start(bf16[128,1536]{1,0:T(8,128)(2,1)S(1)} %constant_dynamic-update-slice_fusion), channel_id=1, source_target_pairs={{0,2},{1,3},{2,0},{3,1},{4,6},{5,7},{6,4},{7,5},{8,10},{9,11},{10,... | collective-permute-start | bytes 1179656 | tf_op jit(solution)/shard_map/ppermute | solution.py:96
  50.6 20.7 %collective-permute-start = (bf16[128,1536]{1,0:T(8,128)(2,1)S(1)}, bf16[128,1536]{1,0:T(8,128)(2,1)S(1)}, u32[]{:S(2)}, u32[]{:S(2)}) collective-permute-start(bf16[128,1536]{1,0:T(8,128)(2,1)S(1)} %constant_dynamic-update-slice_fusion), channel_id=1, source_target_pairs={{0,1},{1,2},{2,3},{3,0},{4,5},{5,6},{6,7},{7,4},{8,9},{9,10},{10,1... | collective-permute-start | bytes 1179656 | tf_op jit(solution)/shard_map/ppermute | solution.py:96
  85.9 11.9 %collective-permute-start.6 = (bf16[64,1536]{1,0:T(8,128)(2,1)}, bf16[64,1536]{1,0:T(8,128)(2,1)}, u32[]{:S(2)}, u32[]{:S(2)}) collective-permute-start(bf16[64,1536]{1,0:T(8,128)(2,1)} %get-tuple-element.213), channel_id=1, source_target_pairs={{0,1},{1,2},{2,3},{3,0},{4,5},{5,6},{6,7},{7,4},{8,9},{9,10},{10,1... | collective-permute-start | bytes 589832 | tf_op jit(solution)/shard_map/ppermute | solution.py:96
  85.9 11.9 %collective-permute-start.5 = (bf16[64,1536]{1,0:T(8,128)(2,1)}, bf16[64,1536]{1,0:T(8,128)(2,1)}, u32[]{:S(2)}, u32[]{:S(2)}) collective-permute-start(bf16[64,1536]{1,0:T(8,128)(2,1)} %get-tuple-element.214), channel_id=1, source_target_pairs={{0,2},{1,3},{2,0},{3,1},{4,6},{5,7},{6,4},{7,5},{8,10},{9,11},{10,... | collective-permute-start | bytes 589832 | tf_op jit(solution)/shard_map/ppermute | solution.py:96
  160.9 11.4 %collective-permute-start.11 = (bf16[64,1536]{1,0:T(8,128)(2,1)S(1)}, bf16[64,1536]{1,0:T(8,128)(2,1)S(1)}, u32[]{:S(2)}, u32[]{:S(2)}) collective-permute-start(bf16[64,1536]{1,0:T(8,128)(2,1)S(1)} %get-tuple-element.54), channel_id=1, source_target_pairs={{0,2},{1,3},{2,0},{3,1},{4,6},{5,7},{6,4},{7,5},{8,10},{9,11},{10,... | collective-permute-start | bytes 589832 | tf_op jit(solution)/shard_map/ppermute | solution.py:96
  176.7 12.2 %collective-permute-start.13 = (bf16[64,1536]{1,0:T(8,128)(2,1)S(1)}, bf16[64,1536]{1,0:T(8,128)(2,1)S(1)}, u32[]{:S(2)}, u32[]{:S(2)}) collective-permute-start(bf16[64,1536]{1,0:T(8,128)(2,1)S(1)} %multiply_convert_fusion.3), channel_id=1, source_target_pairs={{0,1},{1,2},{2,3},{3,0},{4,5},{5,6},{6,7},{7,4},{8,9},{9,10},{10,1... | collective-permute-start | bytes 589832 | tf_op jit(solution)/shard_map/ppermute | solution.py:96
  193.4 13.4 %collective-permute-start.17 = (bf16[256,256]{0,1:T(8,128)(2,1)S(1)}, bf16[256,256]{0,1:T(8,128)(2,1)S(1)}, u32[]{:S(2)}, u32[]{:S(2)}) collective-permute-start(bf16[256,256]{0,1:T(8,128)(2,1)S(1)} %pad_maximum_fusion.16), channel_id=1, source_target_pairs={{0,8},{4,12},{8,0},{12,4},{1,9},{5,13},{9,1},{13,5},{2,10},{6,14},... | collective-permute-start | bytes 393224 | tf_op jit(solution)/shard_map/ppermute | solution.py:82
  194.3 12.5 %collective-permute-start.16 = (bf16[256,256]{0,1:T(8,128)(2,1)S(1)}, bf16[256,256]{0,1:T(8,128)(2,1)S(1)}, u32[]{:S(2)}, u32[]{:S(2)}) collective-permute-start(bf16[256,256]{0,1:T(8,128)(2,1)S(1)} %pad_maximum_fusion.16), channel_id=1, source_target_pairs={{0,4},{4,0},{8,12},{12,8},{1,5},{5,1},{9,13},{13,9},{2,6},{6,2},{1... | collective-permute-start | bytes 393224 | tf_op jit(solution)/shard_map/ppermute | solution.py:82
  215.8 11.5 %collective-permute-start.21 = (bf16[64,1536]{1,0:T(8,128)(2,1)S(1)}, bf16[64,1536]{1,0:T(8,128)(2,1)S(1)}, u32[]{:S(2)}, u32[]{:S(2)}) collective-permute-start(bf16[64,1536]{1,0:T(8,128)(2,1)S(1)} %get-tuple-element.210), channel_id=1, source_target_pairs={{0,1},{1,2},{2,3},{3,0},{4,5},{5,6},{6,7},{7,4},{8,9},{9,10},{10,1... | collective-permute-start | bytes 589832 | tf_op jit(solution)/shard_map/ppermute | solution.py:96
  215.9 11.4 %collective-permute-start.20 = (bf16[64,1536]{1,0:T(8,128)(2,1)S(1)}, bf16[64,1536]{1,0:T(8,128)(2,1)}, u32[]{:S(2)}, u32[]{:S(2)}) collective-permute-start(bf16[64,1536]{1,0:T(8,128)(2,1)S(1)} %get-tuple-element.211), channel_id=1, source_target_pairs={{0,2},{1,3},{2,0},{3,1},{4,6},{5,7},{6,4},{7,5},{8,10},{9,11},{10,... | collective-permute-start | bytes 589832 | tf_op jit(solution)/shard_map/ppermute | solution.py:96
  262.1 19.0 %collective-permute-start.31 = (bf16[256,5760]{1,0:T(8,128)(2,1)}, bf16[256,5760]{1,0:T(8,128)(2,1)S(1)}, u32[]{:S(2)}, u32[]{:S(2)}) collective-permute-start(bf16[256,5760]{1,0:T(8,128)(2,1)} %get-tuple-element.60.refs_0_.refs_2_), channel_id=1, source_target_pairs={{0,4},{4,0},{1,5},{5,1},{2,6},{6,2},{3,7},{7,3},{8,12},{12,8},{9,1... | collective-permute-start | bytes 8847368 | tf_op jit(solution)/shard_map/ppermute | solution.py:86
  263.8 11.7 %collective-permute-start.26 = (bf16[64,1536]{1,0:T(8,128)(2,1)S(1)}, bf16[64,1536]{1,0:T(8,128)(2,1)S(1)}, u32[]{:S(2)}, u32[]{:S(2)}) collective-permute-start(bf16[64,1536]{1,0:T(8,128)(2,1)S(1)} %get-tuple-element.58), channel_id=1, source_target_pairs={{0,2},{1,3},{2,0},{3,1},{4,6},{5,7},{6,4},{7,5},{8,10},{9,11},{10,... | collective-permute-start | bytes 589832 | tf_op jit(solution)/shard_map/ppermute | solution.py:96
  277.0 16.2 %collective-permute-start.28 = (bf16[64,1536]{1,0:T(8,128)(2,1)S(1)}, bf16[64,1536]{1,0:T(8,128)(2,1)}, u32[]{:S(2)}, u32[]{:S(2)}) collective-permute-start(bf16[64,1536]{1,0:T(8,128)(2,1)S(1)} %fusion.192), channel_id=1, source_target_pairs={{0,1},{1,2},{2,3},{3,0},{4,5},{5,6},{6,7},{7,4},{8,9},{9,10},{10,1... | collective-permute-start | bytes 589832 | tf_op jit(solution)/shard_map/ppermute | solution.py:96
  277.6 15.6 %collective-permute-start.29 = (bf16[64,1536]{1,0:T(8,128)(2,1)S(1)}, bf16[64,1536]{1,0:T(8,128)(2,1)}, u32[]{:S(2)}, u32[]{:S(2)}) collective-permute-start(bf16[64,1536]{1,0:T(8,128)(2,1)S(1)} %fusion.192), channel_id=1, source_target_pairs={{0,2},{1,3},{2,0},{3,1},{4,6},{5,7},{6,4},{7,5},{8,10},{9,11},{10,... | collective-permute-start | bytes 589832 | tf_op jit(solution)/shard_map/ppermute | solution.py:96
  280.7 12.6 %collective-permute-start.30 = (bf16[64,1536]{1,0:T(8,128)(2,1)S(1)}, bf16[64,1536]{1,0:T(8,128)(2,1)}, u32[]{:S(2)}, u32[]{:S(2)}) collective-permute-start(bf16[64,1536]{1,0:T(8,128)(2,1)S(1)} %fusion.192), channel_id=1, source_target_pairs={{0,3},{1,0},{2,1},{3,2},{4,7},{5,4},{6,5},{7,6},{8,11},{9,8},{10,9... | collective-permute-start | bytes 589832 | tf_op jit(solution)/shard_map/ppermute | solution.py:96
  293.3 278.9 %reduce-scatter.3.cloned.1.call-start = ((), (), s32[]{:S(2)}) async-start(), calls=%async_computation.7 | async-start | bytes 10444800 | tf_op jit(solution)/shard_map/reduce_scatter | solution.py:363
  312.2 59.7 %collective-permute-start.42 = (bf16[256,1536]{1,0:T(8,128)(2,1)}, bf16[256,1536]{1,0:T(8,128)(2,1)}, u32[]{:S(2)}, u32[]{:S(2)}) collective-permute-start(bf16[256,1536]{1,0:T(8,128)(2,1)} %constant_dynamic-update-slice_fusion.2), channel_id=1, source_target_pairs={{0,4},{4,0},{1,5},{5,1},{2,6},{6,2},{3,7},{7,3},{8,12},{12,8},{9,1... | collective-permute-start | bytes 2359304 | tf_op jit(solution)/shard_map/ppermute | solution.py:86
  332.2 13.1 %collective-permute-start.33 = (bf16[256,256]{0,1:T(8,128)(2,1)S(1)}, bf16[256,256]{0,1:T(8,128)(2,1)S(1)}, u32[]{:S(2)}, u32[]{:S(2)}) collective-permute-start(bf16[256,256]{0,1:T(8,128)(2,1)S(1)} %get-tuple-element.227), channel_id=1, source_target_pairs={{0,8},{4,12},{8,0},{12,4},{1,9},{5,13},{9,1},{13,5},{2,10},{6,14},... | collective-permute-start | bytes 393224 | tf_op jit(solution)/shard_map/ppermute | solution.py:82
  333.3 12.0 %collective-permute-start.32 = (bf16[256,256]{0,1:T(8,128)(2,1)S(1)}, bf16[256,256]{0,1:T(8,128)(2,1)S(1)}, u32[]{:S(2)}, u32[]{:S(2)}) collective-permute-start(bf16[256,256]{0,1:T(8,128)(2,1)S(1)} %get-tuple-element.225), channel_id=1, source_target_pairs={{0,4},{4,0},{8,12},{12,8},{1,5},{5,1},{9,13},{13,9},{2,6},{6,2},{1... | collective-permute-start | bytes 393224 | tf_op jit(solution)/shard_map/ppermute | solution.py:82
  335.6 36.4 %collective-permute-start.41 = (bf16[256,1536]{1,0:T(8,128)(2,1)S(1)}, bf16[256,1536]{1,0:T(8,128)(2,1)S(1)}, u32[]{:S(2)}, u32[]{:S(2)}) collective-permute-start(bf16[256,1536]{1,0:T(8,128)(2,1)S(1)} %get-tuple-element.205.refs_0_), channel_id=1, source_target_pairs={{0,4},{4,0},{1,5},{5,1},{2,6},{6,2},{3,7},{7,3},{8,12},{12,8},{9,1... | collective-permute-start | bytes 2359304 | tf_op jit(solution)/shard_map/ppermute | solution.py:86
  360.3 12.9 %collective-permute-start.43 = (bf16[256,512]{1,0:T(8,128)(2,1)S(1)}, bf16[256,512]{1,0:T(8,128)(2,1)S(1)}, u32[]{:S(2)}, u32[]{:S(2)}) collective-permute-start(bf16[256,512]{1,0:T(8,128)(2,1)S(1)} %get-tuple-element.223), channel_id=1, source_target_pairs={{0,4},{4,0},{1,5},{5,1},{2,6},{6,2},{3,7},{7,3},{8,12},{12,8},{9,1... | collective-permute-start | bytes 786440 | tf_op jit(solution)/shard_map/ppermute | solution.py:86
  395.6 14.0 %collective-permute-start.50 = (bf16[256,5760]{1,0:T(8,128)(2,1)}, bf16[256,5760]{1,0:T(8,128)(2,1)S(1)}, u32[]{:S(2)}, u32[]{:S(2)}) collective-permute-start(bf16[256,5760]{1,0:T(8,128)(2,1)} %get-tuple-element.78.refs_0_.refs_2_), channel_id=1, source_target_pairs={{0,4},{4,0},{1,5},{5,1},{2,6},{6,2},{3,7},{7,3},{8,12},{12,8},{9,1... | collective-permute-start | bytes 8847368 | tf_op jit(solution)/shard_map/ppermute | solution.py:86
  397.7 11.7 %collective-permute-start.48 = (bf16[64,1536]{1,0:T(8,128)(2,1)S(1)}, bf16[64,1536]{1,0:T(8,128)(2,1)S(1)}, u32[]{:S(2)}, u32[]{:S(2)}) collective-permute-start(bf16[64,1536]{1,0:T(8,128)(2,1)S(1)} %get-tuple-element.76), channel_id=1, source_target_pairs={{0,2},{1,3},{2,0},{3,1},{4,6},{5,7},{6,4},{7,5},{8,10},{9,11},{10,... | collective-permute-start | bytes 589832 | tf_op jit(solution)/shard_map/ppermute | solution.py:96
  428.8 12.2 %collective-permute-start.51 = (bf16[64,1536]{1,0:T(8,128)(2,1)S(1)}, bf16[64,1536]{1,0:T(8,128)(2,1)}, u32[]{:S(2)}, u32[]{:S(2)}) collective-permute-start(bf16[64,1536]{1,0:T(8,128)(2,1)S(1)} %get-tuple-element.167), channel_id=1, source_target_pairs={{0,1},{1,2},{2,3},{3,0},{4,5},{5,6},{6,7},{7,4},{8,9},{9,10},{10,1... | collective-permute-start | bytes 589832 | tf_op jit(solution)/shard_map/ppermute | solution.py:96
  430.1 43.1 %collective-permute-start.58 = (bf16[256,1536]{1,0:T(8,128)(2,1)S(1)}, bf16[256,1536]{1,0:T(8,128)(2,1)S(1)}, u32[]{:S(2)}, u32[]{:S(2)}) collective-permute-start(bf16[256,1536]{1,0:T(8,128)(2,1)S(1)} %multiply_convert_fusion.refs_0_), channel_id=1, source_target_pairs={{0,4},{4,0},{1,5},{5,1},{2,6},{6,2},{3,7},{7,3},{8,12},{12,8},{9,1... | collective-permute-start | bytes 2359304 | tf_op jit(solution)/shard_map/ppermute | solution.py:86
  449.3 24.0 %collective-permute-start.59 = (bf16[256,1536]{1,0:T(8,128)(2,1)}, bf16[256,1536]{1,0:T(8,128)(2,1)}, u32[]{:S(2)}, u32[]{:S(2)}) collective-permute-start(bf16[256,1536]{1,0:T(8,128)(2,1)} %get-tuple-element.291), channel_id=1, source_target_pairs={{0,4},{4,0},{1,5},{5,1},{2,6},{6,2},{3,7},{7,3},{8,12},{12,8},{9,1... | collective-permute-start | bytes 2359304 | tf_op jit(solution)/shard_map/ppermute | solution.py:86
  458.9 12.6 %collective-permute-start.57 = (bf16[64,1536]{1,0:T(8,128)(2,1)}, bf16[64,1536]{1,0:T(8,128)(2,1)}, u32[]{:S(2)}, u32[]{:S(2)}) collective-permute-start(bf16[64,1536]{1,0:T(8,128)(2,1)} %get-tuple-element.202), channel_id=1, source_target_pairs={{0,1},{1,2},{2,3},{3,0},{4,5},{5,6},{6,7},{7,4},{8,9},{9,10},{10,1... | collective-permute-start | bytes 589832 | tf_op jit(solution)/shard_map/ppermute | solution.py:96
  458.9 13.1 %collective-permute-start.56 = (bf16[64,1536]{1,0:T(8,128)(2,1)}, bf16[64,1536]{1,0:T(8,128)(2,1)}, u32[]{:S(2)}, u32[]{:S(2)}) collective-permute-start(bf16[64,1536]{1,0:T(8,128)(2,1)} %get-tuple-element.203), channel_id=1, source_target_pairs={{0,2},{1,3},{2,0},{3,1},{4,6},{5,7},{6,4},{7,5},{8,10},{9,11},{10,... | collective-permute-start | bytes 589832 | tf_op jit(solution)/shard_map/ppermute | solution.py:96
  460.3 11.7 %collective-permute-start.55 = (bf16[64,1536]{1,0:T(8,128)(2,1)}, bf16[64,1536]{1,0:T(8,128)(2,1)}, u32[]{:S(2)}, u32[]{:S(2)}) collective-permute-start(bf16[64,1536]{1,0:T(8,128)(2,1)} %get-tuple-element.201), channel_id=1, source_target_pairs={{0,3},{1,0},{2,1},{3,2},{4,7},{5,4},{6,5},{7,6},{8,11},{9,8},{10,9... | collective-permute-start | bytes 589832 | tf_op jit(solution)/shard_map/ppermute | solution.py:96
  482.9 13.7 %collective-permute-start.66 = (bf16[4,96,384]{2,1,0:T(8,128)(2,1)S(1)}, bf16[4,96,384]{2,1,0:T(8,128)(2,1)}, u32[]{:S(2)}, u32[]{:S(2)}) collective-permute-start(bf16[4,96,384]{2,1,0:T(8,128)(2,1)S(1)} %get-tuple-element.193), channel_id=1, source_target_pairs={{0,96},{32,0},{64,32},{96,64},{1,97},{33,1},{65,33},{97,65},{2,98}... | collective-permute-start | bytes 884744 | tf_op jit(solution)/shard_map/ppermute | solution.py:91
  485.0 13.8 %collective-permute-start.65 = (bf16[4,96,384]{2,1,0:T(8,128)(2,1)S(1)}, bf16[4,96,384]{2,1,0:T(8,128)(2,1)}, u32[]{:S(2)}, u32[]{:S(2)}) collective-permute-start(bf16[4,96,384]{2,1,0:T(8,128)(2,1)S(1)} %get-tuple-element.194), channel_id=1, source_target_pairs={{0,64},{32,96},{64,0},{96,32},{1,65},{33,97},{65,1},{97,33},{2,66}... | collective-permute-start | bytes 884744 | tf_op jit(solution)/shard_map/ppermute | solution.py:91
  486.1 15.8 %collective-permute-start.64 = (bf16[4,96,384]{2,1,0:T(8,128)(2,1)S(1)}, bf16[4,96,384]{2,1,0:T(8,128)(2,1)}, u32[]{:S(2)}, u32[]{:S(2)}) collective-permute-start(bf16[4,96,384]{2,1,0:T(8,128)(2,1)S(1)} %get-tuple-element.192), channel_id=1, source_target_pairs={{0,32},{32,64},{64,96},{96,0},{1,33},{33,65},{65,97},{97,1},{2,34}... | collective-permute-start | bytes 884744 | tf_op jit(solution)/shard_map/ppermute | solution.py:91
  488.2 48.9 %all-to-all-start.1 = ((bf16[32,5,1536]{2,1,0:T(8,128)(2,1)}), bf16[32,5,1536]{2,1,0:T(8,128)(2,1)S(1)}, u32[]{:S(2)}, u32[]{:S(2)}) async-start(bf16[32,5,1536]{2,1,0:T(8,128)(2,1)} %maximum_maximum_fusion), calls=%async_computation.1 | async-start | bytes 1572864 | tf_op jit(solution)/shard_map/all_to_all | solution.py:790
  493.4 19.2 %collective-permute-start.72 = (bf16[4,96,384]{2,1,0:T(8,128)(2,1)S(1)}, bf16[4,96,384]{2,1,0:T(8,128)(2,1)S(1)}, u32[]{:S(2)}, u32[]{:S(2)}) collective-permute-start(bf16[4,96,384]{2,1,0:T(8,128)(2,1)S(1)} %get-tuple-element.191), channel_id=1, source_target_pairs={{0,24},{8,0},{16,8},{24,16},{1,25},{9,1},{17,9},{25,17},{2,26},{10... | collective-permute-start | bytes 884744 | tf_op jit(solution)/shard_map/ppermute | solution.py:91
  496.1 18.1 %collective-permute-start.71 = (bf16[4,96,384]{2,1,0:T(8,128)(2,1)S(1)}, bf16[4,96,384]{2,1,0:T(8,128)(2,1)S(1)}, u32[]{:S(2)}, u32[]{:S(2)}) collective-permute-start(bf16[4,96,384]{2,1,0:T(8,128)(2,1)S(1)} %get-tuple-element.190), channel_id=1, source_target_pairs={{0,16},{8,24},{16,0},{24,8},{1,17},{9,25},{17,1},{25,9},{2,18},{10... | collective-permute-start | bytes 884744 | tf_op jit(solution)/shard_map/ppermute | solution.py:91
  496.6 28.9 %collective-permute-start.70 = (bf16[4,96,384]{2,1,0:T(8,128)(2,1)S(1)}, bf16[4,96,384]{2,1,0:T(8,128)(2,1)S(1)}, u32[]{:S(2)}, u32[]{:S(2)}) collective-permute-start(bf16[4,96,384]{2,1,0:T(8,128)(2,1)S(1)} %get-tuple-element.189), channel_id=1, source_target_pairs={{0,8},{8,16},{16,24},{24,0},{1,9},{9,17},{17,25},{25,1},{2,10},{10... | collective-permute-start | bytes 884744 | tf_op jit(solution)/shard_map/ppermute | solution.py:91
  503.3 25.2 %collective-permute-start.69 = (bf16[96,384]{1,0:T(8,128)(2,1)S(1)}, bf16[96,384]{1,0:T(8,128)(2,1)S(1)}, u32[]{:S(2)}, u32[]{:S(2)}) collective-permute-start(bf16[96,384]{1,0:T(8,128)(2,1)S(1)} %get-tuple-element.221), channel_id=1, source_target_pairs={{0,24},{8,0},{16,8},{24,16},{1,25},{9,1},{17,9},{25,17},{2,26},{10... | collective-permute-start | bytes 221192 | tf_op jit(solution)/shard_map/ppermute | solution.py:91
  504.8 24.5 %collective-permute-start.68 = (bf16[96,384]{1,0:T(8,128)(2,1)S(1)}, bf16[96,384]{1,0:T(8,128)(2,1)S(1)}, u32[]{:S(2)}, u32[]{:S(2)}) collective-permute-start(bf16[96,384]{1,0:T(8,128)(2,1)S(1)} %get-tuple-element.222), channel_id=1, source_target_pairs={{0,16},{8,24},{16,0},{24,8},{1,17},{9,25},{17,1},{25,9},{2,18},{10... | collective-permute-start | bytes 221192 | tf_op jit(solution)/shard_map/ppermute | solution.py:91
  512.6 16.9 %collective-permute-start.67 = (bf16[96,384]{1,0:T(8,128)(2,1)S(1)}, bf16[96,384]{1,0:T(8,128)(2,1)S(1)}, u32[]{:S(2)}, u32[]{:S(2)}) collective-permute-start(bf16[96,384]{1,0:T(8,128)(2,1)S(1)} %get-tuple-element.220), channel_id=1, source_target_pairs={{0,8},{8,16},{16,24},{24,0},{1,9},{9,17},{17,25},{25,1},{2,10},{10... | collective-permute-start | bytes 221192 | tf_op jit(solution)/shard_map/ppermute | solution.py:91
  538.0 11.5 %collective-permute-start.63 = (bf16[136,1536]{1,0:T(8,128)(2,1)S(1)}, bf16[136,1536]{1,0:T(8,128)(2,1)S(1)}, u32[]{:S(2)}, u32[]{:S(2)}) collective-permute-start(bf16[136,1536]{1,0:T(8,128)(2,1)S(1)} %pad_maximum_fusion.6), channel_id=1, source_target_pairs={{0,3},{1,0},{2,1},{3,2},{4,7},{5,4},{6,5},{7,6},{8,11},{9,8},{10,9... | collective-permute-start | bytes 1253384 | tf_op jit(solution)/shard_map/ppermute | solution.py:96
  541.0 12.1 %collective-permute-start.62 = (bf16[136,1536]{1,0:T(8,128)(2,1)S(1)}, bf16[136,1536]{1,0:T(8,128)(2,1)S(1)}, u32[]{:S(2)}, u32[]{:S(2)}) collective-permute-start(bf16[136,1536]{1,0:T(8,128)(2,1)S(1)} %pad_maximum_fusion.6), channel_id=1, source_target_pairs={{0,2},{1,3},{2,0},{3,1},{4,6},{5,7},{6,4},{7,5},{8,10},{9,11},{10,... | collective-permute-start | bytes 1253384 | tf_op jit(solution)/shard_map/ppermute | solution.py:96
  541.6 21.4 %collective-permute-start.61 = (bf16[136,1536]{1,0:T(8,128)(2,1)S(1)}, bf16[136,1536]{1,0:T(8,128)(2,1)S(1)}, u32[]{:S(2)}, u32[]{:S(2)}) collective-permute-start(bf16[136,1536]{1,0:T(8,128)(2,1)S(1)} %pad_maximum_fusion.6), channel_id=1, source_target_pairs={{0,1},{1,2},{2,3},{3,0},{4,5},{5,6},{6,7},{7,4},{8,9},{9,10},{10,1... | collective-permute-start | bytes 1253384 | tf_op jit(solution)/shard_map/ppermute | solution.py:96
  (205 other events, 2137.2 us)
Sparse Core Ops, SparseCore 0:
  10.8 56.8 all-gather.3
  70.5 78.6 all-gather.5
  152.0 75.3 all-gather.7
  293.4 86.7 reduce-scatter.4
  423.6 109.8 reduce-scatter.2

commit v5 on v4

--- a/solution.py
+++ b/solution.py
@@ -217,8 +217,9 @@
     def _():
         assemble(x_refs, x_all)
         assemble(b_refs, b_all)
-        side_ref[:, :width] = x_all[...]
-        side_ref[:, width : 2 * width] = b_all[...]
+        if forward:
+            side_ref[:, :width] = x_all[...]
+            side_ref[:, width : 2 * width] = b_all[...]
         d_total[...] = jnp.zeros_like(d_total)
         if forward:
             scratch[3][...] = jnp.zeros_like(scratch[3])
@@ -237,7 +238,8 @@
     first = core_ref[0] == 0
     half = TILE // 2
     low, high = active[:, :half], active[:, half:]
-    start = pl.multiple_of(2 * width + step * (TILE + half), half)
+    start = (2 * width if forward else 0) + step * (TILE + half)
+    start = pl.multiple_of(start, half)
 
     @pl.when(first)
     def _():
@@ -265,7 +267,7 @@
     tokens = count * rows
     block = TILE + TILE // 2
     ways = 2 if forward else 1
-    side_width = 2 * width + steps * block
+    side_width = (2 * width if forward else 0) + steps * block
     results = pl.pallas_call(
         functools.partial(ffn_backward_kernel, count, forward),
         grid=(steps,),
@@ -363,23 +365,62 @@
     return share_rows(lax.psum_scatter(partial, CHIP_AXES, scatter_dimension=0, tiled=True))
 
 
-def exchange_gradient(partial):
+def along(values, axis, dimension):
+    ring = lax.axis_size(axis)
+    place = lax.axis_index(axis)
+    total = None
+    for k in range(ring):
+        block = lax.dynamic_index_in_dim(values, (place + k) % ring, dimension, False)
+        block = block if k == 0 else shift_ring(block.astype(BF16), axis, k)
+        total = block.astype(F32) if k == 0 else total + block.astype(F32)
+    return total
+
+
+def exchange_first(partial):
     ring = lax.axis_size("x")
     blocks = partial.reshape(ring, ring, -1, partial.shape[1])
     half = partial.shape[1] // 2
-
-    def along(values, axis, dimension):
-        total = None
-        place = lax.axis_index(axis)
-        for k in range(ring):
-            block = lax.dynamic_index_in_dim(values, (place + k) % ring, dimension, False)
-            block = block if k == 0 else shift_ring(block.astype(BF16), axis, k)
-            total = block.astype(F32) if k == 0 else total + block.astype(F32)
-        return total
-
-    low = along(along(blocks[..., :half], "x", 0), Z_AXES, 0)
-    high = along(along(blocks[..., half:], Z_AXES, 1), "x", 0)
-    return share_rows(jnp.concatenate([low, high], axis=1).astype(BF16))
+    return along(blocks[..., :half], "x", 0), along(blocks[..., half:], Z_AXES, 1)
+
+
+def exchange_second(low, high):
+    total = jnp.concatenate([along(low, Z_AXES, 0), along(high, "x", 0)], axis=1)
+    return share_rows(total.astype(BF16))
+
+
+def gather_pack(pack):
+    rows, columns = pack.shape
+    half = columns // 2
+    ring = lax.axis_size("x")
+    x, z, core = lax.axis_index("x"), lax.axis_index(Z_AXES), lax.axis_index("core")
+
+    def fill(shape, parts):
+        result = jnp.zeros(shape, pack.dtype)
+        for part, place in parts:
+            result = lax.dynamic_update_slice(result, part, place)
+        return result
+
+    low, high = pack[:, :half], pack[:, half:]
+    low_parts = [(shift_ring(low, "x", k)[None] if k else low[None], k) for k in range(ring)]
+    high_parts = [(shift_ring(high, Z_AXES, k)[None] if k else high[None], k) for k in range(ring)]
+    low = fill((ring, rows, half), [(v, ((x - k) % ring, 0, 0)) for v, k in low_parts])
+    high = fill((ring, rows, half), [(v, ((z - k) % ring, 0, 0)) for v, k in high_parts])
+    parts = []
+    for k in range(ring):
+        part = shift_ring(low, Z_AXES, k) if k else low
+        parts.append((part[:, None], (0, (z - k) % ring, 0, 0)))
+        part = shift_ring(high, "x", k) if k else high
+        parts.append((part[None], ((x - k) % ring, 0, 0, half)))
+    plane = fill((ring, ring, rows, columns), parts)
+    other = swap_core(plane)
+    both = fill(
+        (ring, ring, CORES, rows, columns),
+        [
+            (plane[:, :, None], (0, 0, core, 0, 0)),
+            (other[:, :, None], (0, 0, 1 - core, 0, 0)),
+        ],
+    )
+    return both.reshape(-1, columns)
 
 
 def ffn_gradients(low, high, steps, hidden):
@@ -447,12 +488,12 @@
         return [wide, jnp.pad(down.T, ((0, 0), (0, padded - hidden)))]
 
     mixer_pack = jnp.concatenate([mixer_project.reshape(depth, -1), mixer_output.T], axis=1)
-    mixer_all = lax.all_gather(mixer_pack, TOKEN_AXES, axis=0, tiled=True)
     first_pack = jnp.concatenate(
         pack_ffn(first_gateup, first_down) + [attend_project, attend_output.T], axis=1
     )
     second_pack = jnp.concatenate(pack_ffn(second_gateup, second_down), axis=1)
     first_all = lax.all_gather(first_pack, TOKEN_AXES, axis=0, tiled=True)
+    mixer_all = gather_pack(mixer_pack)
     second_all = lax.all_gather(second_pack, TOKEN_AXES, axis=0, tiled=True)
     project_a = mixer_all[:, : 3 * channels]
     output_a_t = mixer_all[:, 3 * channels :]
@@ -601,7 +642,7 @@
     unused, pullback = jax.vjp(norm_rows, stream3, gain_s)
     d_stream, gain_s_grad = pullback(tp_reduce(d_chunks))
     d_stream3 = upstream + d_stream
-    stream4 = stream3 + tp_reduce(out_chunks)
+    out_others = [shift_tp(out_chunks[k], -k) for k in range(1, members)]
     side_other = swap_core(side)
     ffn_lefts = [(side, 0), (side_other, 0), (side, 1), (side_other, 1)]
     ffn_cols = steps * block
@@ -678,17 +719,21 @@
     )
 
     back_f = tp_gather(d_stream2.astype(BF16))
-    back_f, third, stream4 = lax.optimization_barrier((back_f, third, stream4))
+    back_f, third = lax.optimization_barrier((back_f, third))
+    left_x, left_b = jnp.concatenate(normed_f), jnp.concatenate(back_f)
+    ffn_lefts = [(left_x, 0), (swap_core(left_x), 0), (left_b, 0), (swap_core(left_b), 0)]
     d_chunks, unused, keep, side = ffn_backward(
         core_ref, normed_f, back_f, first_all, steps, False
     )
-    side_other = swap_core(side)
-    ffn_lefts = [(side, 0), (side_other, 0), (side, 1), (side_other, 1)]
+    d_chunks, out_others = lax.optimization_barrier((d_chunks, out_others))
+    stream4 = stream3 + out_chunks[0]
+    for part in out_others:
+        stream4 = stream4 + part.astype(F32)
     partial = gradient(
         ffn_lefts,
         keep,
-        side_other,
-        side_start,
+        swap_core(side),
+        0,
         block,
         steps,
         TILE,
@@ -757,8 +802,7 @@
     unused, pullback = jax.vjp(norm_rows, stream0, gain_a)
     d_norm_a, gain_a_grad = pullback(d_mixer_in)
     d_stream0 = d_stream1 + d_norm_a
-    low, high = exchange_gradient(partial)
-    mixer_grads = jnp.concatenate([low, high], axis=1)
+    mixer_partial = exchange_first(partial)
 
     slot_for_anchor = jnp.sum(
         jnp.where(
@@ -808,6 +852,8 @@
             ]
         )
     )
+    last, mixer_partial = lax.optimization_barrier((last, mixer_partial))
+    mixer_grads = jnp.concatenate(exchange_second(*mixer_partial), axis=1)
     home_rows = (
         jnp.repeat(jnp.tile(send_piece, members), part_rows) * piece_rows
         + member_of * part_rows

time: 597 us -> 585 us (0.980)
  waiting for transfers between devices: 229 us -> 171 us
  starting transfers between devices: 109 us -> 139 us
  other arithmetic: 46.6 us -> 56.9 us
    all_gather x1, waiting for transfers between devices: 37.6 us -> 0.01 us  [body(): first_all = lax.all_gather(first_pack, TOKEN_AXES, axis=0, tiled=True)]
    ppermute x12 -> x24, starting transfers between devices: 16.4 us -> 34.1 us  [shift_ring(): lax.ppermute(block, axis, [(i, (i + distance) % ring) for i in range(ring)])]
    dynamic_update_slice x0 -> x17, local copies, waits for them, and re-layouts: none -> 15.5 us  [fill(): result = lax.dynamic_update_slice(result, part, place)]
    ppermute x48, waiting for transfers between devices: 131 us -> 117 us  [shift_tp(): lax.ppermute(block, 'tp', [(i, (i + distance) % members) for i in range(m...]
    unnamed x343 -> x354, local copies, waits for them, and re-layouts: 30.6 us -> 18.6 us
    ppermute x11 -> x14, starting transfers between devices: 11.1 us -> 22.4 us  [swap_core(): return lax.ppermute(block, 'core', [(0, 1), (1, 0)])]
    all_to_all x1, waiting for transfers between devices: 11 us -> 0.01 us  [body(): lax.all_to_all(outgoing, TOKEN_AXES, split_axis=0, concat_axis=0, tiled=T...]
    all_to_all x1, waiting for transfers between devices: 0.01 us -> 10.7 us  [body(): lax.all_to_all(jnp.concatenate([by_anchor(d_stream0), by_anchor(stream4),...]
  transfers between devices with their start and end apart: 86 -> 100, of which waited for: 48 -> 46; matrix products, arithmetic and copies ran while one was open for 23% -> 28% of each run, Pallas kernels for 9% -> 9%
where the time goes in v5:
time: 585 us; the launch traced here: 574 us
  waiting for transfers between devices  171 us (29%)
  starting transfers between devices  139 us (24%)
  local copies, waits for them, and re-layouts  79.2 us (14%)
  Pallas kernels  66.3 us (11%)
  other arithmetic  56.9 us (10%)
  matrix products  44.3 us (8%)
  between operations  18.5 us (3%)
    ppermute x48, waiting for transfers between devices, shift_tp(): lax.ppermute(block, 'tp', [(i, (i + distance) % members) for i in range(m...  117 us
    ppermute x48, starting transfers between devices, shift_tp(): lax.ppermute(block, 'tp', [(i, (i + distance) % members) for i in range(m...  60.2 us
    ppermute x24, starting transfers between devices, shift_ring(): lax.ppermute(block, axis, [(i, (i + distance) % ring) for i in range(ring)])  34.1 us
    pallas_call x2, Pallas kernels, ffn_backward(): pl.pallas_call(functools.partial(ffn_backward_kernel, count, forward), gr...  28.6 us
    pallas_call x4, Pallas kernels, gradient(): pl.pallas_call(functools.partial(gradient_kernel, cut, whole_steps), grid...  27.1 us
    ppermute x24, waiting for transfers between devices, shift_ring(): lax.ppermute(block, axis, [(i, (i + distance) % ring) for i in range(ring)])  24.9 us
    ppermute x14, starting transfers between devices, swap_core(): return lax.ppermute(block, 'core', [(0, 1), (1, 0)])  22.4 us
    unnamed x354, local copies, waits for them, and re-layouts  18.6 us
  transfers between devices with their start and end apart: 100, of which 46 were waited for; matrix products, arithmetic and copies ran while one was open for 28% of the time, Pallas kernels for 9%

profile of v5, /device:TPU:1, one launch (start us, length us, event | category | flops | bytes accessed | tf_op | source)
XLA Modules:
  0.0 574.5 jit_solution(13748386567366326519)
XLA Ops:
  20.4 3.3 collective-permute-start.8
  29.5 5.6 all-to-all-start
  60.0 4.6 collective-permute-done.12
  65.4 5.7 collective-permute-done.13
  73.6 5.9 %collective-permute-start.16 = (bf16[4,4,48,1536]{3,2,1,0:T(8,128)(2,1)}, bf16[4,4,48,1536]{3,2,1,0:T(8,128)(2,1)}, u32[]{:S(2)}, u32[]{:S(2)}) collective-permute-start(bf16[4,4,48,1536]{3,2,1,0:T(8,128)(2,1)} %bitcast_dynamic-update-slice_fusion.6), channel_id=1, source_target_pairs={{0,4},{4,0},{1,5},{5,1},{2,6},{6,2},{3,7},{7,3},{8,12},{12,8},{9,1... | collective-permute-start | bytes 7077896 | tf_op jit(solution)/shard_map/ppermute | solution.py:86
  87.1 3.4 bitcast_dynamic-update-slice_fusion
  92.4 8.9 %collective-permute-done.2 = bf16[128,1536]{1,0:T(8,128)(2,1)S(1)} collective-permute-done((bf16[128,1536]{1,0:T(8,128)(2,1)S(1)}, bf16[128,1536]{1,0:T(8,128)(2,1)S(1)}, u32[]{:S(2)}, u32[]{:S(2)}) %collective-permute-start.2) | collective-permute-done | bytes 393248 | tf_op jit(solution)/shard_map/ppermute | solution.py:96
  102.3 8.8 %collective-permute-done = bf16[128,1536]{1,0:T(8,128)(2,1)S(1)} collective-permute-done((bf16[128,1536]{1,0:T(8,128)(2,1)S(1)}, bf16[128,1536]{1,0:T(8,128)(2,1)S(1)}, u32[]{:S(2)}, u32[]{:S(2)}) %collective-permute-start) | collective-permute-done | bytes 393248 | tf_op jit(solution)/shard_map/ppermute | solution.py:96
  111.8 4.2 collective-permute-start.3
  116.0 3.3 bitcast_dynamic-update-slice_fusion.1
  119.3 3.4 fusion.14
  134.4 6.0 %collective-permute-done.19 = bf16[64,1536]{1,0:T(8,128)(2,1)S(1)} collective-permute-done((bf16[64,1536]{1,0:T(8,128)(2,1)}, bf16[64,1536]{1,0:T(8,128)(2,1)S(1)}, u32[]{:S(2)}, u32[]{:S(2)}) %collective-permute-start.19) | collective-permute-done | bytes 196640 | tf_op jit(solution)/shard_map/ppermute | solution.py:96
  143.0 3.5 collective-permute-start.21
  147.0 3.8 collective-permute-done.20.refs_1_
  150.9 4.4 collective-permute-done.21.refs_2_
  155.4 10.6 %ffn_forward.1 = (f32[64,1536]{1,0:T(8,128)S(1)}, bf16[64,1536]{1,0:T(8,128)(2,1)S(1)}, bf16[64,1536]{1,0:T(8,128)(2,1)S(1)}, bf16[64,1536]{1,0:T(8,128)(2,1)S(1)}) custom-call(bf16[64,1536]{1,0:T(8,128)(2,1)S(1)} %multiply_convert_fusion.4.refs_0_, bf16[64,1536]{1,0:T(8,128)(2,1)S(1)} %collective-permute-done.20.refs_1_, ...), custom_call_target="tpu_custom_call" | custom-call | flops 4227858432 | bytes 16515072 | tf_op jit(solution)/shard_map/ffn_forward/pallas_call | solution.py:184
  166.6 4.2 collective-permute-start.24
  173.9 6.5 %collective-permute-done.24 = bf16[64,1536]{1,0:T(8,128)(2,1)} collective-permute-done((bf16[64,1536]{1,0:T(8,128)(2,1)S(1)}, bf16[64,1536]{1,0:T(8,128)(2,1)}, u32[]{:S(2)}, u32[]{:S(2)}) %collective-permute-start.24) | collective-permute-done | bytes 196640 | tf_op jit(solution)/shard_map/ppermute | solution.py:96
  192.0 5.0 collective-permute-done.26
  202.8 3.5 collective-permute-done.31
  220.4 8.0 %collective-permute-done.34 = bf16[64,1536]{1,0:T(8,128)(2,1)S(1)} collective-permute-done((bf16[64,1536]{1,0:T(8,128)(2,1)S(1)}, bf16[64,1536]{1,0:T(8,128)(2,1)S(1)}, u32[]{:S(2)}, u32[]{:S(2)}) %collective-permute-start.34) | collective-permute-done | bytes 196640 | tf_op jit(solution)/shard_map/ppermute | solution.py:96
  237.4 6.0 %collective-permute-done.36.refs_2_ = bf16[64,1536]{1,0:T(8,128)(2,1)S(1)} collective-permute-done((bf16[64,1536]{1,0:T(8,128)(2,1)S(1)}, bf16[64,1536]{1,0:T(8,128)(2,1)S(1)}, u32[]{:S(2)}, u32[]{:S(2)}) %collective-permute-start.36) | collective-permute-done | bytes 196640 | tf_op jit(solution)/shard_map/ppermute | solution.py:96
  243.4 15.0 %ffn_both.1 = (f32[64,1536]{1,0:T(8,128)S(1)}, bf16[64,1536]{1,0:T(8,128)(2,1)S(1)}, bf16[64,1536]{1,0:T(8,128)(2,1)S(1)}, bf16[64,1536]{1,0:T(8,128)(2,1)S(1)},...) custom-call(s32[1]{0:T(128)} %bitcast.6.core_ref, ...), custom_call_target="tpu_custom_call" | custom-call | flops 8455716864 | bytes 22413312 | tf_op jit(solution)/shard_map/ffn_both/pallas_call | solution.py:271
  264.2 4.6 collective-permute-done.40
  268.8 4.6 collective-permute-done.39
  275.2 3.5 collective-permute-start.42
  280.3 10.4 %weight_gradient.4 = bf16[1536,2688]{1,0:T(8,128)(2,1)} custom-call(bf16[256,5760]{1,0:T(8,128)(2,1)S(1)} %copy-done, bf16[256,5760]{1,0:T(8,128)(2,1)} %copy-done.16, bf16[256,5760]{1,0:T(8,128)(2,1)S(1)} %copy-done, bf16[256,5760]{1,0:T(8,128)(2,1)} %copy-done.16, bf16[256,2688]{1,0:T(8,128)(2,1)S(1)} %get-tuple-element.73.refs_4_, ...), custom_call_target="tpu_custom_call" | custom-call | flops 4227858432 | bytes 8257536 | tf_op jit(solution)/shard_map/weight_gradient/pallas_call | solution.py:338
  299.9 7.3 %fusion = (f32[2,3,256]{2,1,0:T(4,128)S(1)}, f32[2,1024,256,3]{2,1,3,0:T(8,128)}) fusion(f32[2,1024,256,3]{2,1,3,0:T(8,128)} %copy-done.15, f32[2,3,256]{2,1,0:T(4,128)S(1)} %copy-done.89, pred[256,1024]{0,1:T(8,128)(4,1)S(1)} %copy-done.29, bf16[1024,2,64,1]{0,2,3,1:T(8,128)(2,1)S(1)} %bitcast.326, bf16[256,2,3,64]{0,3,2,1:T(8,128)(2,1)S(1)} %bitcast.332), kind=kOutput, calls=%fused_computation.7 | convolution fusion | flops 209189376 | bytes 13316096 | tf_op jit(solution)/shard_map/tkgd,nkd->kgtn/dot_general | solution.py:665
  307.3 4.6 fusion.2
  323.3 4.9 collective-permute-done.46
  330.5 3.6 fusion.216
  343.7 4.3 collective-permute-start.54
  357.4 3.6 weight_gradient.5.refs_6_
  363.7 13.6 %ffn_backward.1 = (f32[64,1536]{1,0:T(8,128)S(1)}, bf16[64,1536]{1,0:T(8,128)(2,1)S(1)}, bf16[64,1536]{1,0:T(8,128)(2,1)S(1)}, bf16[64,1536]{1,0:T(8,128)(2,1)S(...) custom-call(s32[1]{0:T(128)} %bitcast.6.core_ref, bf16[64,1536]{1,0:T(8,128)(2,1)S(1)} %multiply_convert_fusion.4.refs_0_, ...), custom_call_target="tpu_custom_call" | custom-call | flops 7046430720 | bytes 19267584 | tf_op jit(solution)/shard_map/ffn_backward/pallas_call | solution.py:271
  385.7 3.8 collective-permute-done.61
  391.5 9.8 %weight_gradient.6 = bf16[1536,3200]{1,0:T(8,128)(2,1)} custom-call(bf16[256,1536]{1,0:T(8,128)(2,1)S(1)} %pad_maximum_fusion.3.refs_0_, bf16[256,1536]{1,0:T(8,128)(2,1)} %collective-permute-done.63.refs_1_, bf16[256,1536]{1,0:T(8,128)(2,1)S(1)} %constant_dynamic-update-slice_fusion.6.refs_2_, ...), custom_call_target="tpu_custom_call", output_to_operand_aliasing={{}: (6, {})} | custom-call | flops 4227858432 | bytes 8257536 | tf_op jit(solution)/shard_map/weight_gradient/pallas_call | solution.py:338
  418.1 5.0 collective-permute-done.68
  423.2 4.1 collective-permute-done.66
  438.4 4.9 fusion.217
  449.8 6.8 %collective-permute-done.72 = bf16[64,1536]{1,0:T(8,128)(2,1)} collective-permute-done((bf16[64,1536]{1,0:T(8,128)(2,1)}, bf16[64,1536]{1,0:T(8,128)(2,1)}, u32[]{:S(2)}, u32[]{:S(2)}) %collective-permute-start.72) | collective-permute-done | bytes 196640 | tf_op jit(solution)/shard_map/ppermute | solution.py:96
  460.2 3.3 weight_gradient.7
  470.1 4.4 all-to-all-start.1
  482.4 10.7 %all-to-all-done.1 = bf16[32,5,1536]{2,1,0:T(8,128)(2,1)} async-done(((bf16[32,5,1536]{2,1,0:T(8,128)(2,1)}), bf16[32,5,1536]{2,1,0:T(8,128)(2,1)}, u32[]{:S(2)}, u32[]{:S(2)}) %all-to-all-start.1) | async-done | bytes 491552 | tf_op jit(solution)/shard_map/all_to_all | solution.py:834
  496.5 3.3 collective-permute-done.81
  501.9 6.3 %collective-permute-done.79 = bf16[4,96,384]{2,1,0:T(8,128)(2,1)} collective-permute-done((bf16[4,96,384]{2,1,0:T(8,128)(2,1)S(1)}, bf16[4,96,384]{2,1,0:T(8,128)(2,1)}, u32[]{:S(2)}, u32[]{:S(2)}) %collective-permute-start.79) | collective-permute-done | bytes 294944 | tf_op jit(solution)/shard_map/ppermute | solution.py:91
  513.8 9.6 %collective-permute-done.77 = bf16[136,1536]{1,0:T(8,128)(2,1)S(1)} collective-permute-done((bf16[136,1536]{1,0:T(8,128)(2,1)S(1)}, bf16[136,1536]{1,0:T(8,128)(2,1)S(1)}, u32[]{:S(2)}, u32[]{:S(2)}) %collective-permute-start.77) | collective-permute-done | bytes 417824 | tf_op jit(solution)/shard_map/ppermute | solution.py:96
  523.4 6.4 %collective-permute-done.78 = bf16[136,1536]{1,0:T(8,128)(2,1)S(1)} collective-permute-done((bf16[136,1536]{1,0:T(8,128)(2,1)S(1)}, bf16[136,1536]{1,0:T(8,128)(2,1)S(1)}, u32[]{:S(2)}, u32[]{:S(2)}) %collective-permute-start.78) | collective-permute-done | bytes 417824 | tf_op jit(solution)/shard_map/ppermute | solution.py:96
  547.0 4.3 collective-permute-start.91
  (815 shorter events, 274.5 us)
Async XLA Ops:
  7.2 148.2 %all-gather.3.cloned.1.call-start = ((), (), s32[]{:S(2)}) async-start(), calls=%async_computation.4 | async-start | bytes 20275200 | tf_op jit(solution)/shard_map/all_gather | solution.py:495
  10.3 224.8 %all-gather.5.cloned.1.call-start = ((), (), s32[]{:S(2)}) async-start(), calls=%async_computation.5 | async-start | bytes 17031168 | tf_op jit(solution)/shard_map/all_gather | solution.py:497
  12.3 29.8 %collective-permute-start.4 = (bf16[48,768]{1,0:T(8,128)(2,1)S(1)}, bf16[48,768]{1,0:T(8,128)(2,1)}, u32[]{:S(2)}, u32[]{:S(2)}) collective-permute-start(bf16[48,768]{1,0:T(8,128)(2,1)S(1)} %slice.585), channel_id=1, source_target_pairs={{0,32},{32,64},{64,96},{96,0},{1,33},{33,65},{65,97},{97,1},{2,34}... | collective-permute-start | bytes 221192 | tf_op jit(solution)/shard_map/ppermute | solution.py:91
  14.4 31.3 %collective-permute-start.5 = (bf16[48,768]{1,0:T(8,128)(2,1)S(1)}, bf16[48,768]{1,0:T(8,128)(2,1)S(1)}, u32[]{:S(2)}, u32[]{:S(2)}) collective-permute-start(bf16[48,768]{1,0:T(8,128)(2,1)S(1)} %slice.585), channel_id=1, source_target_pairs={{0,64},{32,96},{64,0},{96,32},{1,65},{33,97},{65,1},{97,33},{2,66}... | collective-permute-start | bytes 221192 | tf_op jit(solution)/shard_map/ppermute | solution.py:91
  16.9 28.8 %collective-permute-start.6 = (bf16[48,768]{1,0:T(8,128)(2,1)S(1)}, bf16[48,768]{1,0:T(8,128)(2,1)S(1)}, u32[]{:S(2)}, u32[]{:S(2)}) collective-permute-start(bf16[48,768]{1,0:T(8,128)(2,1)S(1)} %slice.585), channel_id=1, source_target_pairs={{0,96},{32,0},{64,32},{96,64},{1,97},{33,1},{65,33},{97,65},{2,98}... | collective-permute-start | bytes 221192 | tf_op jit(solution)/shard_map/ppermute | solution.py:91
  18.7 28.8 %collective-permute-start.7 = (bf16[48,768]{1,0:T(8,128)(2,1)}, bf16[48,768]{1,0:T(8,128)(2,1)}, u32[]{:S(2)}, u32[]{:S(2)}) collective-permute-start(bf16[48,768]{1,0:T(8,128)(2,1)} %get-tuple-element.207), channel_id=1, source_target_pairs={{0,8},{8,16},{16,24},{24,0},{1,9},{9,17},{17,25},{25,1},{2,10},{10... | collective-permute-start | bytes 221192 | tf_op jit(solution)/shard_map/ppermute | solution.py:91
  20.4 28.1 %collective-permute-start.8 = (bf16[48,768]{1,0:T(8,128)(2,1)}, bf16[48,768]{1,0:T(8,128)(2,1)}, u32[]{:S(2)}, u32[]{:S(2)}) collective-permute-start(bf16[48,768]{1,0:T(8,128)(2,1)} %get-tuple-element.207), channel_id=1, source_target_pairs={{0,16},{8,24},{16,0},{24,8},{1,17},{9,25},{17,1},{25,9},{2,18},{10... | collective-permute-start | bytes 221192 | tf_op jit(solution)/shard_map/ppermute | solution.py:91
  29.5 50.0 %all-to-all-start = ((bf16[32,5,1536]{2,1,0:T(8,128)(2,1)}), bf16[32,5,1536]{2,1,0:T(8,128)(2,1)S(1)}, u32[]{:S(2)}, u32[]{:S(2)}) async-start(bf16[32,5,1536]{2,1,0:T(8,128)(2,1)} %pad_maximum_fusion.1), calls=%async_computation | async-start | bytes 1572864 | tf_op jit(solution)/shard_map/all_to_all | solution.py:524
  35.1 517.1 %reduce-scatter.5.cloned.1.call-start = ((), (), s32[]{:S(2)}) async-start(), calls=%async_computation.7 | async-start | bytes 8773632 | tf_op jit(solution)/shard_map/reduce_scatter | solution.py:365
  45.7 11.9 %collective-permute-start.10 = (bf16[4,48,768]{2,1,0:T(8,128)(2,1)S(1)}, bf16[4,48,768]{2,1,0:T(8,128)(2,1)S(1)}, u32[]{:S(2)}, u32[]{:S(2)}) collective-permute-start(bf16[4,48,768]{2,1,0:T(8,128)(2,1)S(1)} %bitcast_dynamic-update-slice_fusion.14), channel_id=1, source_target_pairs={{0,8},{8,16},{16,24},{24,0},{1,9},{9,17},{17,25},{25,1},{2,10},{10... | collective-permute-start | bytes 884744 | tf_op jit(solution)/shard_map/ppermute | solution.py:91
  45.8 18.8 %collective-permute-start.12 = (bf16[4,48,768]{2,1,0:T(8,128)(2,1)S(1)}, bf16[4,48,768]{2,1,0:T(8,128)(2,1)S(1)}, u32[]{:S(2)}, u32[]{:S(2)}) collective-permute-start(bf16[4,48,768]{2,1,0:T(8,128)(2,1)S(1)} %bitcast_dynamic-update-slice_fusion.14), channel_id=1, source_target_pairs={{0,16},{8,24},{16,0},{24,8},{1,17},{9,25},{17,1},{25,9},{2,18},{10... | collective-permute-start | bytes 884744 | tf_op jit(solution)/shard_map/ppermute | solution.py:91
  50.7 20.5 %collective-permute-start.13 = (bf16[4,48,768]{2,1,0:T(8,128)(2,1)S(1)}, bf16[4,48,768]{2,1,0:T(8,128)(2,1)S(1)}, u32[]{:S(2)}, u32[]{:S(2)}) collective-permute-start(bf16[4,48,768]{2,1,0:T(8,128)(2,1)S(1)} %bitcast_dynamic-update-slice_fusion.10), channel_id=1, source_target_pairs={{0,64},{32,96},{64,0},{96,32},{1,65},{33,97},{65,1},{97,33},{2,66}... | collective-permute-start | bytes 884744 | tf_op jit(solution)/shard_map/ppermute | solution.py:91
  53.2 18.8 %collective-permute-start.14 = (bf16[4,48,768]{2,1,0:T(8,128)(2,1)S(1)}, bf16[4,48,768]{2,1,0:T(8,128)(2,1)S(1)}, u32[]{:S(2)}, u32[]{:S(2)}) collective-permute-start(bf16[4,48,768]{2,1,0:T(8,128)(2,1)S(1)} %bitcast_dynamic-update-slice_fusion.14), channel_id=1, source_target_pairs={{0,24},{8,0},{16,8},{24,16},{1,25},{9,1},{17,9},{25,17},{2,26},{10... | collective-permute-start | bytes 884744 | tf_op jit(solution)/shard_map/ppermute | solution.py:91
  57.6 15.2 %collective-permute-start.15 = (bf16[4,48,768]{2,1,0:T(8,128)(2,1)S(1)}, bf16[4,48,768]{2,1,0:T(8,128)(2,1)S(1)}, u32[]{:S(2)}, u32[]{:S(2)}) collective-permute-start(bf16[4,48,768]{2,1,0:T(8,128)(2,1)S(1)} %bitcast_dynamic-update-slice_fusion.10), channel_id=1, source_target_pairs={{0,96},{32,0},{64,32},{96,64},{1,97},{33,1},{65,33},{97,65},{2,98}... | collective-permute-start | bytes 884744 | tf_op jit(solution)/shard_map/ppermute | solution.py:91
  73.6 42.4 %collective-permute-start.16 = (bf16[4,4,48,1536]{3,2,1,0:T(8,128)(2,1)}, bf16[4,4,48,1536]{3,2,1,0:T(8,128)(2,1)}, u32[]{:S(2)}, u32[]{:S(2)}) collective-permute-start(bf16[4,4,48,1536]{3,2,1,0:T(8,128)(2,1)} %bitcast_dynamic-update-slice_fusion.6), channel_id=1, source_target_pairs={{0,4},{4,0},{1,5},{5,1},{2,6},{6,2},{3,7},{7,3},{8,12},{12,8},{9,1... | collective-permute-start | bytes 7077896 | tf_op jit(solution)/shard_map/ppermute | solution.py:86
  81.4 19.9 %collective-permute-start.2 = (bf16[128,1536]{1,0:T(8,128)(2,1)S(1)}, bf16[128,1536]{1,0:T(8,128)(2,1)S(1)}, u32[]{:S(2)}, u32[]{:S(2)}) collective-permute-start(bf16[128,1536]{1,0:T(8,128)(2,1)S(1)} %constant_dynamic-update-slice_fusion), channel_id=1, source_target_pairs={{0,3},{1,0},{2,1},{3,2},{4,7},{5,4},{6,5},{7,6},{8,11},{9,8},{10,9... | collective-permute-start | bytes 1179656 | tf_op jit(solution)/shard_map/ppermute | solution.py:96
  90.6 20.5 %collective-permute-start = (bf16[128,1536]{1,0:T(8,128)(2,1)S(1)}, bf16[128,1536]{1,0:T(8,128)(2,1)S(1)}, u32[]{:S(2)}, u32[]{:S(2)}) collective-permute-start(bf16[128,1536]{1,0:T(8,128)(2,1)S(1)} %constant_dynamic-update-slice_fusion), channel_id=1, source_target_pairs={{0,1},{1,2},{2,3},{3,0},{4,5},{5,6},{6,7},{7,4},{8,9},{9,10},{10,1... | collective-permute-start | bytes 1179656 | tf_op jit(solution)/shard_map/ppermute | solution.py:96
  143.0 12.3 %collective-permute-start.21 = (bf16[64,1536]{1,0:T(8,128)(2,1)S(1)}, bf16[64,1536]{1,0:T(8,128)(2,1)S(1)}, u32[]{:S(2)}, u32[]{:S(2)}) collective-permute-start(bf16[64,1536]{1,0:T(8,128)(2,1)S(1)} %multiply_convert_fusion.4.refs_0_), channel_id=1, source_target_pairs={{0,2},{1,3},{2,0},{3,1},{4,6},{5,7},{6,4},{7,5},{8,10},{9,11},{10,... | collective-permute-start | bytes 589832 | tf_op jit(solution)/shard_map/ppermute | solution.py:96
  166.6 13.8 %collective-permute-start.24 = (bf16[64,1536]{1,0:T(8,128)(2,1)S(1)}, bf16[64,1536]{1,0:T(8,128)(2,1)}, u32[]{:S(2)}, u32[]{:S(2)}) collective-permute-start(bf16[64,1536]{1,0:T(8,128)(2,1)S(1)} %get-tuple-element.66), channel_id=1, source_target_pairs={{0,2},{1,3},{2,0},{3,1},{4,6},{5,7},{6,4},{7,5},{8,10},{9,11},{10,... | collective-permute-start | bytes 589832 | tf_op jit(solution)/shard_map/ppermute | solution.py:96
  184.7 12.3 %collective-permute-start.26 = (bf16[64,1536]{1,0:T(8,128)(2,1)S(1)}, bf16[64,1536]{1,0:T(8,128)(2,1)S(1)}, u32[]{:S(2)}, u32[]{:S(2)}) collective-permute-start(bf16[64,1536]{1,0:T(8,128)(2,1)S(1)} %multiply_convert_fusion.3), channel_id=1, source_target_pairs={{0,1},{1,2},{2,3},{3,0},{4,5},{5,6},{6,7},{7,4},{8,9},{9,10},{10,1... | collective-permute-start | bytes 589832 | tf_op jit(solution)/shard_map/ppermute | solution.py:96
  259.2 19.5 %collective-permute-start.44 = (bf16[256,5760]{1,0:T(8,128)(2,1)}, bf16[256,5760]{1,0:T(8,128)(2,1)S(1)}, u32[]{:S(2)}, u32[]{:S(2)}) collective-permute-start(bf16[256,5760]{1,0:T(8,128)(2,1)} %get-tuple-element.72.refs_0_.refs_2_), channel_id=1, source_target_pairs={{0,4},{4,0},{1,5},{5,1},{2,6},{6,2},{3,7},{7,3},{8,12},{12,8},{9,1... | collective-permute-start | bytes 8847368 | tf_op jit(solution)/shard_map/ppermute | solution.py:86
  261.2 12.2 %collective-permute-start.39 = (bf16[64,1536]{1,0:T(8,128)(2,1)S(1)}, bf16[64,1536]{1,0:T(8,128)(2,1)S(1)}, u32[]{:S(2)}, u32[]{:S(2)}) collective-permute-start(bf16[64,1536]{1,0:T(8,128)(2,1)S(1)} %get-tuple-element.70), channel_id=1, source_target_pairs={{0,2},{1,3},{2,0},{3,1},{4,6},{5,7},{6,4},{7,5},{8,10},{9,11},{10,... | collective-permute-start | bytes 589832 | tf_op jit(solution)/shard_map/ppermute | solution.py:96
  274.4 16.3 %collective-permute-start.41 = (bf16[64,1536]{1,0:T(8,128)(2,1)S(1)}, bf16[64,1536]{1,0:T(8,128)(2,1)S(1)}, u32[]{:S(2)}, u32[]{:S(2)}) collective-permute-start(bf16[64,1536]{1,0:T(8,128)(2,1)S(1)} %fusion.188), channel_id=1, source_target_pairs={{0,1},{1,2},{2,3},{3,0},{4,5},{5,6},{6,7},{7,4},{8,9},{9,10},{10,1... | collective-permute-start | bytes 589832 | tf_op jit(solution)/shard_map/ppermute | solution.py:96
  275.2 15.5 %collective-permute-start.42 = (bf16[64,1536]{1,0:T(8,128)(2,1)S(1)}, bf16[64,1536]{1,0:T(8,128)(2,1)S(1)}, u32[]{:S(2)}, u32[]{:S(2)}) collective-permute-start(bf16[64,1536]{1,0:T(8,128)(2,1)S(1)} %fusion.188), channel_id=1, source_target_pairs={{0,2},{1,3},{2,0},{3,1},{4,6},{5,7},{6,4},{7,5},{8,10},{9,11},{10,... | collective-permute-start | bytes 589832 | tf_op jit(solution)/shard_map/ppermute | solution.py:96
  278.7 12.1 %collective-permute-start.43 = (bf16[64,1536]{1,0:T(8,128)(2,1)S(1)}, bf16[64,1536]{1,0:T(8,128)(2,1)S(1)}, u32[]{:S(2)}, u32[]{:S(2)}) collective-permute-start(bf16[64,1536]{1,0:T(8,128)(2,1)S(1)} %fusion.188), channel_id=1, source_target_pairs={{0,3},{1,0},{2,1},{3,2},{4,7},{5,4},{6,5},{7,6},{8,11},{9,8},{10,9... | collective-permute-start | bytes 589832 | tf_op jit(solution)/shard_map/ppermute | solution.py:96
  290.8 268.0 %reduce-scatter.3.cloned.1.call-start = ((), (), s32[]{:S(2)}) async-start(), calls=%async_computation.6 | async-start | bytes 10444800 | tf_op jit(solution)/shard_map/reduce_scatter | solution.py:365
  290.9 100.6 %collective-permute-start.63 = (bf16[256,1536]{1,0:T(8,128)(2,1)S(1)}, bf16[256,1536]{1,0:T(8,128)(2,1)}, u32[]{:S(2)}, u32[]{:S(2)}) collective-permute-start(bf16[256,1536]{1,0:T(8,128)(2,1)S(1)} %pad_maximum_fusion.3.refs_0_), channel_id=1, source_target_pairs={{0,4},{4,0},{1,5},{5,1},{2,6},{6,2},{3,7},{7,3},{8,12},{12,8},{9,1... | collective-permute-start | bytes 2359304 | tf_op jit(solution)/shard_map/ppermute | solution.py:86
  297.0 58.0 %collective-permute-start.55 = (bf16[256,1536]{1,0:T(8,128)(2,1)}, bf16[256,1536]{1,0:T(8,128)(2,1)}, u32[]{:S(2)}, u32[]{:S(2)}) collective-permute-start(bf16[256,1536]{1,0:T(8,128)(2,1)} %constant_dynamic-update-slice_fusion.2), channel_id=1, source_target_pairs={{0,4},{4,0},{1,5},{5,1},{2,6},{6,2},{3,7},{7,3},{8,12},{12,8},{9,1... | collective-permute-start | bytes 2359304 | tf_op jit(solution)/shard_map/ppermute | solution.py:86
  314.6 13.6 %collective-permute-start.46 = (bf16[256,256]{0,1:T(8,128)(2,1)S(1)}, bf16[256,256]{0,1:T(8,128)(2,1)S(1)}, u32[]{:S(2)}, u32[]{:S(2)}) collective-permute-start(bf16[256,256]{0,1:T(8,128)(2,1)S(1)} %get-tuple-element.252), channel_id=1, source_target_pairs={{0,8},{4,12},{8,0},{12,4},{1,9},{5,13},{9,1},{13,5},{2,10},{6,14},... | collective-permute-start | bytes 393224 | tf_op jit(solution)/shard_map/ppermute | solution.py:82
  316.1 12.1 %collective-permute-start.45 = (bf16[256,256]{0,1:T(8,128)(2,1)S(1)}, bf16[256,256]{0,1:T(8,128)(2,1)S(1)}, u32[]{:S(2)}, u32[]{:S(2)}) collective-permute-start(bf16[256,256]{0,1:T(8,128)(2,1)S(1)} %get-tuple-element.250), channel_id=1, source_target_pairs={{0,4},{4,0},{8,12},{12,8},{1,5},{5,1},{9,13},{13,9},{2,6},{6,2},{1... | collective-permute-start | bytes 393224 | tf_op jit(solution)/shard_map/ppermute | solution.py:82
  356.6 20.6 %collective-permute-start.57 = (bf16[64,1536]{1,0:T(8,128)(2,1)S(1)}, bf16[64,1536]{1,0:T(8,128)(2,1)S(1)}, u32[]{:S(2)}, u32[]{:S(2)}) collective-permute-start(bf16[64,1536]{1,0:T(8,128)(2,1)S(1)} %copy-done.14), channel_id=1, source_target_pairs={{0,3},{1,0},{2,1},{3,2},{4,7},{5,4},{6,5},{7,6},{8,11},{9,8},{10,9... | collective-permute-start | bytes 589832 | tf_op jit(solution)/shard_map/ppermute | solution.py:96
  361.1 16.2 %collective-permute-start.58 = (bf16[64,1536]{1,0:T(8,128)(2,1)S(1)}, bf16[64,1536]{1,0:T(8,128)(2,1)S(1)}, u32[]{:S(2)}, u32[]{:S(2)}) collective-permute-start(bf16[64,1536]{1,0:T(8,128)(2,1)S(1)} %copy-done.12), channel_id=1, source_target_pairs={{0,2},{1,3},{2,0},{3,1},{4,6},{5,7},{6,4},{7,5},{8,10},{9,11},{10,... | collective-permute-start | bytes 589832 | tf_op jit(solution)/shard_map/ppermute | solution.py:96
  363.7 13.7 %collective-permute-start.59 = (bf16[64,1536]{1,0:T(8,128)(2,1)S(1)}, bf16[64,1536]{1,0:T(8,128)(2,1)S(1)}, u32[]{:S(2)}, u32[]{:S(2)}) collective-permute-start(bf16[64,1536]{1,0:T(8,128)(2,1)S(1)} %copy-done.10), channel_id=1, source_target_pairs={{0,1},{1,2},{2,3},{3,0},{4,5},{5,6},{6,7},{7,4},{8,9},{9,10},{10,1... | collective-permute-start | bytes 589832 | tf_op jit(solution)/shard_map/ppermute | solution.py:96
  379.4 12.1 %collective-permute-start.65 = (bf16[256,2688]{1,0:T(8,128)(2,1)S(1)}, bf16[256,2688]{1,0:T(8,128)(2,1)S(1)}, u32[]{:S(2)}, u32[]{:S(2)}) collective-permute-start(bf16[256,2688]{1,0:T(8,128)(2,1)S(1)} %get-tuple-element.94), channel_id=1, source_target_pairs={{0,4},{4,0},{1,5},{5,1},{2,6},{6,2},{3,7},{7,3},{8,12},{12,8},{9,1... | collective-permute-start | bytes 4128776 | tf_op jit(solution)/shard_map/ppermute | solution.py:86
  405.2 53.6 %collective-permute-start.73 = (bf16[256,1536]{1,0:T(8,128)(2,1)S(1)}, bf16[256,1536]{1,0:T(8,128)(2,1)S(1)}, u32[]{:S(2)}, u32[]{:S(2)}) collective-permute-start(bf16[256,1536]{1,0:T(8,128)(2,1)S(1)} %multiply_convert_fusion.refs_0_), channel_id=1, source_target_pairs={{0,4},{4,0},{1,5},{5,1},{2,6},{6,2},{3,7},{7,3},{8,12},{12,8},{9,1... | collective-permute-start | bytes 2359304 | tf_op jit(solution)/shard_map/ppermute | solution.py:86
  414.9 12.4 %collective-permute-start.66 = (bf16[64,1536]{1,0:T(8,128)(2,1)}, bf16[64,1536]{1,0:T(8,128)(2,1)}, u32[]{:S(2)}, u32[]{:S(2)}) collective-permute-start(bf16[64,1536]{1,0:T(8,128)(2,1)} %get-tuple-element.190), channel_id=1, source_target_pairs={{0,1},{1,2},{2,3},{3,0},{4,5},{5,6},{6,7},{7,4},{8,9},{9,10},{10,1... | collective-permute-start | bytes 589832 | tf_op jit(solution)/shard_map/ppermute | solution.py:96
  435.4 23.5 %collective-permute-start.74 = (bf16[256,1536]{1,0:T(8,128)(2,1)}, bf16[256,1536]{1,0:T(8,128)(2,1)}, u32[]{:S(2)}, u32[]{:S(2)}) collective-permute-start(bf16[256,1536]{1,0:T(8,128)(2,1)} %get-tuple-element.316), channel_id=1, source_target_pairs={{0,4},{4,0},{1,5},{5,1},{2,6},{6,2},{3,7},{7,3},{8,12},{12,8},{9,1... | collective-permute-start | bytes 2359304 | tf_op jit(solution)/shard_map/ppermute | solution.py:86
  470.1 23.0 %all-to-all-start.1 = ((bf16[32,5,1536]{2,1,0:T(8,128)(2,1)}), bf16[32,5,1536]{2,1,0:T(8,128)(2,1)}, u32[]{:S(2)}, u32[]{:S(2)}) async-start(bf16[32,5,1536]{2,1,0:T(8,128)(2,1)} %maximum_maximum_fusion), calls=%async_computation.1 | async-start | bytes 1572864 | tf_op jit(solution)/shard_map/all_to_all | solution.py:834
  475.9 23.9 %collective-permute-start.81 = (bf16[4,96,384]{2,1,0:T(8,128)(2,1)S(1)}, bf16[4,96,384]{2,1,0:T(8,128)(2,1)S(1)}, u32[]{:S(2)}, u32[]{:S(2)}) collective-permute-start(bf16[4,96,384]{2,1,0:T(8,128)(2,1)S(1)} %get-tuple-element.218), channel_id=1, source_target_pairs={{0,96},{32,0},{64,32},{96,64},{1,97},{33,1},{65,33},{97,65},{2,98}... | collective-permute-start | bytes 884744 | tf_op jit(solution)/shard_map/ppermute | solution.py:91
  477.4 23.9 %collective-permute-start.80 = (bf16[4,96,384]{2,1,0:T(8,128)(2,1)S(1)}, bf16[4,96,384]{2,1,0:T(8,128)(2,1)}, u32[]{:S(2)}, u32[]{:S(2)}) collective-permute-start(bf16[4,96,384]{2,1,0:T(8,128)(2,1)S(1)} %get-tuple-element.219), channel_id=1, source_target_pairs={{0,64},{32,96},{64,0},{96,32},{1,65},{33,97},{65,1},{97,33},{2,66}... | collective-permute-start | bytes 884744 | tf_op jit(solution)/shard_map/ppermute | solution.py:91
  477.9 30.3 %collective-permute-start.79 = (bf16[4,96,384]{2,1,0:T(8,128)(2,1)S(1)}, bf16[4,96,384]{2,1,0:T(8,128)(2,1)}, u32[]{:S(2)}, u32[]{:S(2)}) collective-permute-start(bf16[4,96,384]{2,1,0:T(8,128)(2,1)S(1)} %get-tuple-element.217), channel_id=1, source_target_pairs={{0,32},{32,64},{64,96},{96,0},{1,33},{33,65},{65,97},{97,1},{2,34}... | collective-permute-start | bytes 884744 | tf_op jit(solution)/shard_map/ppermute | solution.py:91
  479.4 29.0 %collective-permute-start.84 = (bf16[4,96,384]{2,1,0:T(8,128)(2,1)}, bf16[4,96,384]{2,1,0:T(8,128)(2,1)}, u32[]{:S(2)}, u32[]{:S(2)}) collective-permute-start(bf16[4,96,384]{2,1,0:T(8,128)(2,1)} %get-tuple-element.216), channel_id=1, source_target_pairs={{0,24},{8,0},{16,8},{24,16},{1,25},{9,1},{17,9},{25,17},{2,26},{10... | collective-permute-start | bytes 884744 | tf_op jit(solution)/shard_map/ppermute | solution.py:91
  481.9 30.7 %collective-permute-start.83 = (bf16[4,96,384]{2,1,0:T(8,128)(2,1)}, bf16[4,96,384]{2,1,0:T(8,128)(2,1)}, u32[]{:S(2)}, u32[]{:S(2)}) collective-permute-start(bf16[4,96,384]{2,1,0:T(8,128)(2,1)} %get-tuple-element.215), channel_id=1, source_target_pairs={{0,16},{8,24},{16,0},{24,8},{1,17},{9,25},{17,1},{25,9},{2,18},{10... | collective-permute-start | bytes 884744 | tf_op jit(solution)/shard_map/ppermute | solution.py:91
  499.8 12.7 %collective-permute-start.82 = (bf16[4,96,384]{2,1,0:T(8,128)(2,1)S(1)}, bf16[4,96,384]{2,1,0:T(8,128)(2,1)S(1)}, u32[]{:S(2)}, u32[]{:S(2)}) collective-permute-start(bf16[4,96,384]{2,1,0:T(8,128)(2,1)S(1)} %get-tuple-element.214), channel_id=1, source_target_pairs={{0,8},{8,16},{16,24},{24,0},{1,9},{9,17},{17,25},{25,1},{2,10},{10... | collective-permute-start | bytes 884744 | tf_op jit(solution)/shard_map/ppermute | solution.py:91
  501.3 12.4 %collective-permute-start.76 = (bf16[136,1536]{1,0:T(8,128)(2,1)S(1)}, bf16[136,1536]{1,0:T(8,128)(2,1)S(1)}, u32[]{:S(2)}, u32[]{:S(2)}) collective-permute-start(bf16[136,1536]{1,0:T(8,128)(2,1)S(1)} %pad_maximum_fusion.7), channel_id=1, source_target_pairs={{0,1},{1,2},{2,3},{3,0},{4,5},{5,6},{6,7},{7,4},{8,9},{9,10},{10,1... | collective-permute-start | bytes 1253384 | tf_op jit(solution)/shard_map/ppermute | solution.py:96
  508.2 15.1 %collective-permute-start.77 = (bf16[136,1536]{1,0:T(8,128)(2,1)S(1)}, bf16[136,1536]{1,0:T(8,128)(2,1)S(1)}, u32[]{:S(2)}, u32[]{:S(2)}) collective-permute-start(bf16[136,1536]{1,0:T(8,128)(2,1)S(1)} %pad_maximum_fusion.7), channel_id=1, source_target_pairs={{0,2},{1,3},{2,0},{3,1},{4,6},{5,7},{6,4},{7,5},{8,10},{9,11},{10,... | collective-permute-start | bytes 1253384 | tf_op jit(solution)/shard_map/ppermute | solution.py:96
  508.4 21.4 %collective-permute-start.78 = (bf16[136,1536]{1,0:T(8,128)(2,1)S(1)}, bf16[136,1536]{1,0:T(8,128)(2,1)S(1)}, u32[]{:S(2)}, u32[]{:S(2)}) collective-permute-start(bf16[136,1536]{1,0:T(8,128)(2,1)S(1)} %pad_maximum_fusion.7), channel_id=1, source_target_pairs={{0,3},{1,0},{2,1},{3,2},{4,7},{5,4},{6,5},{7,6},{8,11},{9,8},{10,9... | collective-permute-start | bytes 1253384 | tf_op jit(solution)/shard_map/ppermute | solution.py:96
  529.8 12.7 %collective-permute-start.87 = (bf16[96,384]{1,0:T(8,128)(2,1)S(1)}, bf16[96,384]{1,0:T(8,128)(2,1)S(1)}, u32[]{:S(2)}, u32[]{:S(2)}) collective-permute-start(bf16[96,384]{1,0:T(8,128)(2,1)S(1)} %get-tuple-element.246), channel_id=1, source_target_pairs={{0,24},{8,0},{16,8},{24,16},{1,25},{9,1},{17,9},{25,17},{2,26},{10... | collective-permute-start | bytes 221192 | tf_op jit(solution)/shard_map/ppermute | solution.py:91
  (221 other events, 2555.7 us)
Sparse Core Ops, SparseCore 0:
  10.9 97.1 all-gather.2
  110.9 72.5 all-gather.4
  290.9 83.6 reduce-scatter.4
  401.5 107.3 reduce-scatter.2

commit v6 on v5

--- a/solution.py
+++ b/solution.py
@@ -365,46 +365,46 @@
     return share_rows(lax.psum_scatter(partial, CHIP_AXES, scatter_dimension=0, tiled=True))
 
 
-def along(values, axis, dimension):
+def along(blocks, axis):
     ring = lax.axis_size(axis)
     place = lax.axis_index(axis)
-    total = None
-    for k in range(ring):
-        block = lax.dynamic_index_in_dim(values, (place + k) % ring, dimension, False)
-        block = block if k == 0 else shift_ring(block.astype(BF16), axis, k)
-        total = block.astype(F32) if k == 0 else total + block.astype(F32)
+    return [lax.dynamic_index_in_dim(blocks, place, 0, False)] + [
+        shift_ring(lax.dynamic_index_in_dim(blocks, (place + k) % ring, 0, False), axis, k)
+        for k in range(1, ring)
+    ]
+
+
+def add_parts(parts):
+    total = parts[0].astype(F32)
+    for part in parts[1:]:
+        total = total + part.astype(F32)
     return total
 
 
-def exchange_first(partial):
-    ring = lax.axis_size("x")
-    blocks = partial.reshape(ring, ring, -1, partial.shape[1])
-    half = partial.shape[1] // 2
-    return along(blocks[..., :half], "x", 0), along(blocks[..., half:], Z_AXES, 1)
-
-
-def exchange_second(low, high):
-    total = jnp.concatenate([along(low, Z_AXES, 0), along(high, "x", 0)], axis=1)
-    return share_rows(total.astype(BF16))
-
-
-def gather_pack(pack):
+def fill(shape, parts):
+    result = jnp.zeros(shape, BF16)
+    for part, place in parts:
+        result = lax.dynamic_update_slice(result, part, place)
+    return result
+
+
+def gather_first(pack):
     rows, columns = pack.shape
     half = columns // 2
     ring = lax.axis_size("x")
-    x, z, core = lax.axis_index("x"), lax.axis_index(Z_AXES), lax.axis_index("core")
-
-    def fill(shape, parts):
-        result = jnp.zeros(shape, pack.dtype)
-        for part, place in parts:
-            result = lax.dynamic_update_slice(result, part, place)
-        return result
-
+    x, z = lax.axis_index("x"), lax.axis_index(Z_AXES)
     low, high = pack[:, :half], pack[:, half:]
     low_parts = [(shift_ring(low, "x", k)[None] if k else low[None], k) for k in range(ring)]
     high_parts = [(shift_ring(high, Z_AXES, k)[None] if k else high[None], k) for k in range(ring)]
     low = fill((ring, rows, half), [(v, ((x - k) % ring, 0, 0)) for v, k in low_parts])
     high = fill((ring, rows, half), [(v, ((z - k) % ring, 0, 0)) for v, k in high_parts])
+    return low, high
+
+
+def gather_second(low, high):
+    ring, rows, half = low.shape
+    columns = 2 * half
+    x, z, core = lax.axis_index("x"), lax.axis_index(Z_AXES), lax.axis_index("core")
     parts = []
     for k in range(ring):
         part = shift_ring(low, Z_AXES, k) if k else low
@@ -493,10 +493,7 @@
     )
     second_pack = jnp.concatenate(pack_ffn(second_gateup, second_down), axis=1)
     first_all = lax.all_gather(first_pack, TOKEN_AXES, axis=0, tiled=True)
-    mixer_all = gather_pack(mixer_pack)
     second_all = lax.all_gather(second_pack, TOKEN_AXES, axis=0, tiled=True)
-    project_a = mixer_all[:, : 3 * channels]
-    output_a_t = mixer_all[:, 3 * channels :]
     project_b = first_all[:, ffn_width : ffn_width + attend_project.shape[1]]
     output_b_t = first_all[:, ffn_width + attend_project.shape[1] :]
 
@@ -521,6 +518,8 @@
         ],
         axis=1,
     )
+    outgoing, mixer_pack = lax.optimization_barrier((outgoing, mixer_pack))
+    mixer_low, mixer_high = gather_first(mixer_pack)
     arrived = lax.all_to_all(outgoing, TOKEN_AXES, split_axis=0, concat_axis=0, tiled=True)
     gains = (
         arrived[:, 2 * part_rows, : 4 * depth]
@@ -536,6 +535,10 @@
     stream0 = own_tokens.astype(F32)
     upstream = own_back.astype(F32)
     both = tp_gather(jnp.concatenate([own_tokens, own_back]))
+    both, mixer_low, mixer_high = lax.optimization_barrier((both, mixer_low, mixer_high))
+    mixer_all = gather_second(mixer_low, mixer_high)
+    project_a = mixer_all[:, : 3 * channels]
+    output_a_t = mixer_all[:, 3 * channels :]
     back_s_chunks = [slot[chunk:] for slot in both]
 
     gathered = jnp.arange(row_count)
@@ -744,12 +747,12 @@
         third,
     )
 
-    d_normed, partial = lax.optimization_barrier((tp_reduce(d_chunks), partial))
     unused, pullback = jax.vjp(norm_rows, stream1, gain_f)
-    d_stream, gain_f_grad = pullback(d_normed)
+    d_stream, gain_f_grad = pullback(tp_reduce(d_chunks))
     d_stream1 = d_stream2 + d_stream
 
     back_a = tp_gather(d_stream1.astype(BF16))
+    back_a, partial = lax.optimization_barrier((back_a, partial))
     low, high = reduce_gradient(partial)
     first_grads = (low[:, :ffn_cols], high[:, :ffn_cols])
     attend_grads = jnp.concatenate([low[:, ffn_cols:], high[:, ffn_cols:]], axis=1)
@@ -798,11 +801,11 @@
         0,
         None,
     )
-    d_mixer_in, partial = lax.optimization_barrier((tp_reduce(d_chunks), partial))
+    second_grads = ffn_gradients(*second_grads, steps, hidden)
+    d_mixer_in, second_grads = lax.optimization_barrier((tp_reduce(d_chunks), second_grads))
     unused, pullback = jax.vjp(norm_rows, stream0, gain_a)
     d_norm_a, gain_a_grad = pullback(d_mixer_in)
     d_stream0 = d_stream1 + d_norm_a
-    mixer_partial = exchange_first(partial)
 
     slot_for_anchor = jnp.sum(
         jnp.where(
@@ -840,6 +843,9 @@
         concat_axis=0,
         tiled=True,
     )
+    home, partial = lax.optimization_barrier((home, partial))
+    ring = lax.axis_size("x")
+    mixer_parts = along(partial.reshape(ring, -1, mixer_cols), "x")
     small_sum = jnp.sum(home[:, 2 * part_rows].astype(F32), axis=0)
     small_high = small_sum.astype(BF16)
     small_low = (small_sum - small_high.astype(F32)).astype(BF16)
@@ -852,8 +858,12 @@
             ]
         )
     )
-    last, mixer_partial = lax.optimization_barrier((last, mixer_partial))
-    mixer_grads = jnp.concatenate(exchange_second(*mixer_partial), axis=1)
+    last, mixer_parts = lax.optimization_barrier((last, mixer_parts))
+    mixer_parts = add_parts(mixer_parts).astype(BF16).reshape(ring, -1, mixer_cols)
+    mixer_parts = along(mixer_parts, Z_AXES)
+    first_grads = ffn_gradients(*first_grads, steps, hidden)
+    mixer_parts, first_grads = lax.optimization_barrier((mixer_parts, first_grads))
+    mixer_grads = jnp.concatenate(share_rows(add_parts(mixer_parts).astype(BF16)), axis=1)
     home_rows = (
         jnp.repeat(jnp.tile(send_piece, members), part_rows) * piece_rows
         + member_of * part_rows
@@ -879,8 +889,8 @@
     gain_start = kernel_cols + 2 * HD
     gain_totals = totals[gain_start : gain_start + 4 * depth].reshape(4, depth)
 
-    gateup_s_grad, down_s_grad = ffn_gradients(*second_grads, steps, hidden)
-    gateup_f_grad, down_f_grad = ffn_gradients(*first_grads, steps, hidden)
+    gateup_s_grad, down_s_grad = second_grads
+    gateup_f_grad, down_f_grad = first_grads
     proj_cols = attend_project.shape[1]
     return (
         layer_out,

time: 585 us -> 562 us (0.961)
  waiting for transfers between devices: 171 us -> 149 us
  starting transfers between devices: 139 us -> 147 us
    ppermute x48, waiting for transfers between devices: 117 us -> 88.4 us  [shift_tp(): lax.ppermute(block, 'tp', [(i, (i + distance) % members) for i in range(m...]
    dynamic_update_slice x17 -> x18, local copies, waits for them, and re-layouts: 15.5 us -> 1.74 us  [fill(): result = lax.dynamic_update_slice(result, part, place)]
    ppermute x48, starting transfers between devices: 60.2 us -> 72.9 us  [shift_tp(): lax.ppermute(block, 'tp', [(i, (i + distance) % members) for i in range(m...]
    ppermute x24 -> x18, starting transfers between devices: 34.1 us -> 30 us  [shift_ring(): lax.ppermute(block, axis, [(i, (i + distance) % ring) for i in range(ring)])]
    ppermute x24 -> x18, waiting for transfers between devices: 24.9 us -> 28.1 us  [shift_ring(): lax.ppermute(block, axis, [(i, (i + distance) % ring) for i in range(ring)])]
    unnamed x354 -> x352, local copies, waits for them, and re-layouts: 18.6 us -> 18.4 us
  transfers between devices with their start and end apart: 100 -> 94, of which waited for: 46 -> 38; matrix products, arithmetic and copies ran while one was open for 28% -> 28% of each run, Pallas kernels for 9% -> 9%
where the time goes in v6:
time: 562 us; the launch traced here: 552 us
  waiting for transfers between devices  149 us (27%)
  starting transfers between devices  147 us (26%)
  local copies, waits for them, and re-layouts  73.7 us (13%)
  Pallas kernels  66.5 us (12%)
  other arithmetic  56.1 us (10%)
  matrix products  41.9 us (7%)
  between operations  18.1 us (3%)
    ppermute x48, waiting for transfers between devices, shift_tp(): lax.ppermute(block, 'tp', [(i, (i + distance) % members) for i in range(m...  88.4 us
    ppermute x48, starting transfers between devices, shift_tp(): lax.ppermute(block, 'tp', [(i, (i + distance) % members) for i in range(m...  72.9 us
    ppermute x18, starting transfers between devices, shift_ring(): lax.ppermute(block, axis, [(i, (i + distance) % ring) for i in range(ring)])  30 us
    pallas_call x2, Pallas kernels, ffn_backward(): pl.pallas_call(functools.partial(ffn_backward_kernel, count, forward), gr...  28.5 us
    ppermute x18, waiting for transfers between devices, shift_ring(): lax.ppermute(block, axis, [(i, (i + distance) % ring) for i in range(ring)])  28.1 us
    pallas_call x4, Pallas kernels, gradient(): pl.pallas_call(functools.partial(gradient_kernel, cut, whole_steps), grid...  27.3 us
    ppermute x14, starting transfers between devices, swap_core(): return lax.ppermute(block, 'core', [(0, 1), (1, 0)])  22.1 us
    unnamed x352, local copies, waits for them, and re-layouts  18.4 us
  transfers between devices with their start and end apart: 94, of which 38 were waited for; matrix products, arithmetic and copies ran while one was open for 28% of the time, Pallas kernels for 9%

profile of v6, /device:TPU:1, one launch (start us, length us, event | category | flops | bytes accessed | tf_op | source)
XLA Modules:
  0.0 552.3 jit_solution(15658576633233327005)
XLA Ops:
  26.1 3.3 collective-permute-start.7
  29.4 5.6 %all-to-all-start = ((bf16[32,5,1536]{2,1,0:T(8,128)(2,1)}), bf16[32,5,1536]{2,1,0:T(8,128)(2,1)S(1)}, u32[]{:S(2)}, u32[]{:S(2)}) async-start(bf16[32,5,1536]{2,1,0:T(8,128)(2,1)} %pad_maximum_fusion.1), calls=%async_computation | async-start | bytes 1572864 | tf_op jit(solution)/shard_map/all_to_all | solution.py:523
  46.0 4.4 all-to-all-done
  59.3 4.6 collective-permute-done
  63.9 9.4 %collective-permute-done.1 = bf16[128,1536]{1,0:T(8,128)(2,1)S(1)} collective-permute-done((bf16[128,1536]{1,0:T(8,128)(2,1)S(1)}, bf16[128,1536]{1,0:T(8,128)(2,1)S(1)}, u32[]{:S(2)}, u32[]{:S(2)}) %collective-permute-start.1) | collective-permute-done | bytes 393248 | tf_op jit(solution)/shard_map/ppermute | solution.py:96
  73.5 2.8 collective-permute-start.12
  80.8 8.7 %collective-permute-done.10 = bf16[4,48,768]{2,1,0:T(8,128)(2,1)S(1)} collective-permute-done((bf16[4,48,768]{2,1,0:T(8,128)(2,1)S(1)}, bf16[4,48,768]{2,1,0:T(8,128)(2,1)S(1)}, u32[]{:S(2)}, u32[]{:S(2)}) %collective-permute-start.10) | collective-permute-done | bytes 294944 | tf_op jit(solution)/shard_map/ppermute | solution.py:91
  92.5 9.7 %collective-permute-done.12 = bf16[4,48,768]{2,1,0:T(8,128)(2,1)S(1)} collective-permute-done((bf16[4,48,768]{2,1,0:T(8,128)(2,1)S(1)}, bf16[4,48,768]{2,1,0:T(8,128)(2,1)S(1)}, u32[]{:S(2)}, u32[]{:S(2)}) %collective-permute-start.12) | collective-permute-done | bytes 294944 | tf_op jit(solution)/shard_map/ppermute | solution.py:91
  117.3 3.0 fusion.196
  129.7 5.3 collective-permute-done.18
  138.2 2.8 collective-permute-start.21
  143.6 6.1 %collective-permute-done.21.refs_2_ = bf16[64,1536]{1,0:T(8,128)(2,1)S(1)} collective-permute-done((bf16[64,1536]{1,0:T(8,128)(2,1)S(1)}, bf16[64,1536]{1,0:T(8,128)(2,1)S(1)}, u32[]{:S(2)}, u32[]{:S(2)}) %collective-permute-start.21) | collective-permute-done | bytes 196640 | tf_op jit(solution)/shard_map/ppermute | solution.py:96
  149.8 10.7 %ffn_forward.1 = (f32[64,1536]{1,0:T(8,128)S(1)}, bf16[64,1536]{1,0:T(8,128)(2,1)S(1)}, bf16[64,1536]{1,0:T(8,128)(2,1)S(1)}, bf16[64,1536]{1,0:T(8,128)(2,1)S(1)}) custom-call(bf16[64,1536]{1,0:T(8,128)(2,1)S(1)} %multiply_convert_fusion.4.refs_0_, bf16[64,1536]{1,0:T(8,128)(2,1)S(1)} %collective-permute-done.20.refs_1_, ...), custom_call_target="tpu_custom_call" | custom-call | flops 4227858432 | bytes 16515072 | tf_op jit(solution)/shard_map/ffn_forward/pallas_call | solution.py:184
  167.5 5.9 %collective-permute-done.24 = bf16[64,1536]{1,0:T(8,128)(2,1)} collective-permute-done((bf16[64,1536]{1,0:T(8,128)(2,1)S(1)}, bf16[64,1536]{1,0:T(8,128)(2,1)}, u32[]{:S(2)}, u32[]{:S(2)}) %collective-permute-start.24) | collective-permute-done | bytes 196640 | tf_op jit(solution)/shard_map/ppermute | solution.py:96
  178.3 8.6 %collective-permute-start.26 = (bf16[64,1536]{1,0:T(8,128)(2,1)S(1)}, bf16[64,1536]{1,0:T(8,128)(2,1)S(1)}, u32[]{:S(2)}, u32[]{:S(2)}) collective-permute-start(bf16[64,1536]{1,0:T(8,128)(2,1)S(1)} %multiply_convert_fusion.3), channel_id=1, source_target_pairs={{0,1},{1,2},{2,3},{3,0},{4,5},{5,6},{6,7},{7,4},{8,9},{9,10},{10,1... | collective-permute-start | bytes 589832 | tf_op jit(solution)/shard_map/ppermute | solution.py:96
  187.2 6.1 %collective-permute-done.26 = bf16[64,1536]{1,0:T(8,128)(2,1)S(1)} collective-permute-done((bf16[64,1536]{1,0:T(8,128)(2,1)S(1)}, bf16[64,1536]{1,0:T(8,128)(2,1)S(1)}, u32[]{:S(2)}, u32[]{:S(2)}) %collective-permute-start.26) | collective-permute-done | bytes 196640 | tf_op jit(solution)/shard_map/ppermute | solution.py:96
  196.7 3.3 collective-permute-start.31
  200.9 3.4 collective-permute-done.31
  204.3 2.8 collective-permute-done.30
  212.9 3.1 fusion.197
  219.6 8.2 %collective-permute-done.34 = bf16[64,1536]{1,0:T(8,128)(2,1)S(1)} collective-permute-done((bf16[64,1536]{1,0:T(8,128)(2,1)S(1)}, bf16[64,1536]{1,0:T(8,128)(2,1)S(1)}, u32[]{:S(2)}, u32[]{:S(2)}) %collective-permute-start.34) | collective-permute-done | bytes 196640 | tf_op jit(solution)/shard_map/ppermute | solution.py:96
  231.3 2.9 collective-permute-start.36
  236.5 6.0 %collective-permute-done.36.refs_2_ = bf16[64,1536]{1,0:T(8,128)(2,1)S(1)} collective-permute-done((bf16[64,1536]{1,0:T(8,128)(2,1)S(1)}, bf16[64,1536]{1,0:T(8,128)(2,1)S(1)}, u32[]{:S(2)}, u32[]{:S(2)}) %collective-permute-start.36) | collective-permute-done | bytes 196640 | tf_op jit(solution)/shard_map/ppermute | solution.py:96
  242.6 15.0 %ffn_both.1 = (f32[64,1536]{1,0:T(8,128)S(1)}, bf16[64,1536]{1,0:T(8,128)(2,1)S(1)}, bf16[64,1536]{1,0:T(8,128)(2,1)S(1)}, bf16[64,1536]{1,0:T(8,128)(2,1)S(1)},...) custom-call(s32[1]{0:T(128)} %bitcast.7.core_ref, ...), custom_call_target="tpu_custom_call" | custom-call | flops 8455716864 | bytes 22413312 | tf_op jit(solution)/shard_map/ffn_both/pallas_call | solution.py:271
  260.5 2.9 collective-permute-start.39
  263.5 4.6 collective-permute-done.40
  268.1 4.6 collective-permute-done.39
  274.4 3.4 collective-permute-start.42
  279.5 10.4 %weight_gradient.4 = bf16[1536,2688]{1,0:T(8,128)(2,1)} custom-call(bf16[256,5760]{1,0:T(8,128)(2,1)S(1)} %copy-done, bf16[256,5760]{1,0:T(8,128)(2,1)} %copy-done.14, bf16[256,5760]{1,0:T(8,128)(2,1)S(1)} %copy-done, bf16[256,5760]{1,0:T(8,128)(2,1)} %copy-done.14, bf16[256,2688]{1,0:T(8,128)(2,1)S(1)} %get-tuple-element.103.refs_4_, ...), custom_call_target="tpu_custom_call" | custom-call | flops 4227858432 | bytes 8257536 | tf_op jit(solution)/shard_map/weight_gradient/pallas_call | solution.py:338
  298.7 7.3 %fusion = (f32[2,3,256]{2,1,0:T(4,128)S(1)}, f32[2,1024,256,3]{2,1,3,0:T(8,128)}) fusion(f32[2,1024,256,3]{2,1,3,0:T(8,128)} %copy-done.13, f32[2,3,256]{2,1,0:T(4,128)S(1)} %copy-done.89, pred[256,1024]{0,1:T(8,128)(4,1)S(1)} %copy-done.28, bf16[1024,2,64,1]{0,2,3,1:T(8,128)(2,1)S(1)} %bitcast.291, bf16[256,2,3,64]{0,3,2,1:T(8,128)(2,1)S(1)} %bitcast.297), kind=kOutput, calls=%fused_computation.7 | convolution fusion | flops 209189376 | bytes 13316096 | tf_op jit(solution)/shard_map/tkgd,nkd->kgtn/dot_general | solution.py:668
  306.1 4.6 fusion.2
  319.1 3.0 collective-permute-done.47
  322.1 4.4 collective-permute-done.46
  328.9 3.6 fusion.198
  342.0 4.4 collective-permute-start.54
  355.0 3.7 weight_gradient.5.refs_6_
  360.9 13.5 %ffn_backward.1 = (f32[64,1536]{1,0:T(8,128)S(1)}, bf16[64,1536]{1,0:T(8,128)(2,1)S(1)}, bf16[64,1536]{1,0:T(8,128)(2,1)S(1)}, bf16[64,1536]{1,0:T(8,128)(2,1)S(...) custom-call(s32[1]{0:T(128)} %bitcast.7.core_ref, bf16[64,1536]{1,0:T(8,128)(2,1)S(1)} %multiply_convert_fusion.4.refs_0_, ...), custom_call_target="tpu_custom_call" | custom-call | flops 7046430720 | bytes 19267584 | tf_op jit(solution)/shard_map/ffn_backward/pallas_call | solution.py:271
  379.3 3.0 collective-permute-start.68
  392.2 9.9 %weight_gradient.6 = bf16[1536,3200]{1,0:T(8,128)(2,1)} custom-call(bf16[256,1536]{1,0:T(8,128)(2,1)S(1)} %pad_maximum_fusion.3.refs_0_, bf16[256,1536]{1,0:T(8,128)(2,1)} %collective-permute-done.66.refs_1_, bf16[256,1536]{1,0:T(8,128)(2,1)S(1)} %constant_dynamic-update-slice_fusion.6.refs_2_, ...), custom_call_target="tpu_custom_call", output_to_operand_aliasing={{}: (6, {})} | custom-call | flops 4227858432 | bytes 8257536 | tf_op jit(solution)/shard_map/weight_gradient/pallas_call | solution.py:338
  421.6 4.9 fusion.199
  435.1 4.6 collective-permute-done.72
  462.9 5.2 all-to-all-start.1
  469.3 3.3 weight_gradient.7
  472.6 11.2 %all-to-all-done.1 = bf16[32,5,1536]{2,1,0:T(8,128)(2,1)} async-done(((bf16[32,5,1536]{2,1,0:T(8,128)(2,1)}), bf16[32,5,1536]{2,1,0:T(8,128)(2,1)}, u32[]{:S(2)}, u32[]{:S(2)}) %all-to-all-start.1) | async-done | bytes 491552 | tf_op jit(solution)/shard_map/all_to_all | solution.py:837
  496.4 3.4 collective-permute-done.77
  502.9 6.8 %collective-permute-done.78 = bf16[136,1536]{1,0:T(8,128)(2,1)S(1)} collective-permute-done((bf16[136,1536]{1,0:T(8,128)(2,1)S(1)}, bf16[136,1536]{1,0:T(8,128)(2,1)S(1)}, u32[]{:S(2)}, u32[]{:S(2)}) %collective-permute-start.78) | collective-permute-done | bytes 417824 | tf_op jit(solution)/shard_map/ppermute | solution.py:96
  509.7 5.3 collective-permute-done.79
  529.3 3.0 collective-permute-start.84
  (800 shorter events, 261.2 us)
Async XLA Ops:
  7.2 142.6 %all-gather.3.cloned.1.call-start = ((), (), s32[]{:S(2)}) async-start(), calls=%async_computation.4 | async-start | bytes 20275200 | tf_op jit(solution)/shard_map/all_gather | solution.py:495
  10.3 224.0 %all-gather.5.cloned.1.call-start = ((), (), s32[]{:S(2)}) async-start(), calls=%async_computation.5 | async-start | bytes 17031168 | tf_op jit(solution)/shard_map/all_gather | solution.py:496
  18.8 24.4 %collective-permute-start.3 = (bf16[48,768]{1,0:T(8,128)(2,1)S(1)}, bf16[48,768]{1,0:T(8,128)(2,1)S(1)}, u32[]{:S(2)}, u32[]{:S(2)}) collective-permute-start(bf16[48,768]{1,0:T(8,128)(2,1)S(1)} %get-tuple-element.325), channel_id=1, source_target_pairs={{0,32},{32,64},{64,96},{96,0},{1,33},{33,65},{65,97},{97,1},{2,34}... | collective-permute-start | bytes 221192 | tf_op jit(solution)/shard_map/ppermute | solution.py:91
  20.9 25.0 %collective-permute-start.4 = (bf16[48,768]{1,0:T(8,128)(2,1)S(1)}, bf16[48,768]{1,0:T(8,128)(2,1)S(1)}, u32[]{:S(2)}, u32[]{:S(2)}) collective-permute-start(bf16[48,768]{1,0:T(8,128)(2,1)S(1)} %get-tuple-element.325), channel_id=1, source_target_pairs={{0,64},{32,96},{64,0},{96,32},{1,65},{33,97},{65,1},{97,33},{2,66}... | collective-permute-start | bytes 221192 | tf_op jit(solution)/shard_map/ppermute | solution.py:91
  23.3 22.5 %collective-permute-start.5 = (bf16[48,768]{1,0:T(8,128)(2,1)S(1)}, bf16[48,768]{1,0:T(8,128)(2,1)S(1)}, u32[]{:S(2)}, u32[]{:S(2)}) collective-permute-start(bf16[48,768]{1,0:T(8,128)(2,1)S(1)} %get-tuple-element.325), channel_id=1, source_target_pairs={{0,96},{32,0},{64,32},{96,64},{1,97},{33,1},{65,33},{97,65},{2,98}... | collective-permute-start | bytes 221192 | tf_op jit(solution)/shard_map/ppermute | solution.py:91
  24.5 21.4 %collective-permute-start.6 = (bf16[48,768]{1,0:T(8,128)(2,1)}, bf16[48,768]{1,0:T(8,128)(2,1)S(1)}, u32[]{:S(2)}, u32[]{:S(2)}) collective-permute-start(bf16[48,768]{1,0:T(8,128)(2,1)} %get-tuple-element.324), channel_id=1, source_target_pairs={{0,8},{8,16},{16,24},{24,0},{1,9},{9,17},{17,25},{25,1},{2,10},{10... | collective-permute-start | bytes 221192 | tf_op jit(solution)/shard_map/ppermute | solution.py:91
  26.1 19.8 %collective-permute-start.7 = (bf16[48,768]{1,0:T(8,128)(2,1)}, bf16[48,768]{1,0:T(8,128)(2,1)S(1)}, u32[]{:S(2)}, u32[]{:S(2)}) collective-permute-start(bf16[48,768]{1,0:T(8,128)(2,1)} %get-tuple-element.324), channel_id=1, source_target_pairs={{0,16},{8,24},{16,0},{24,8},{1,17},{9,25},{17,1},{25,9},{2,18},{10... | collective-permute-start | bytes 221192 | tf_op jit(solution)/shard_map/ppermute | solution.py:91
  29.4 21.0 %all-to-all-start = ((bf16[32,5,1536]{2,1,0:T(8,128)(2,1)}), bf16[32,5,1536]{2,1,0:T(8,128)(2,1)S(1)}, u32[]{:S(2)}, u32[]{:S(2)}) async-start(bf16[32,5,1536]{2,1,0:T(8,128)(2,1)} %pad_maximum_fusion.1), calls=%async_computation | async-start | bytes 1572864 | tf_op jit(solution)/shard_map/all_to_all | solution.py:523
  35.1 398.9 %reduce-scatter.3.cloned.1.call-start = ((), (), s32[]{:S(2)}) async-start(), calls=%async_computation.6 | async-start | bytes 8773632 | tf_op jit(solution)/shard_map/reduce_scatter | solution.py:365
  43.2 14.2 %collective-permute-start.8 = (bf16[48,768]{1,0:T(8,128)(2,1)}, bf16[48,768]{1,0:T(8,128)(2,1)}, u32[]{:S(2)}, u32[]{:S(2)}) collective-permute-start(bf16[48,768]{1,0:T(8,128)(2,1)} %get-tuple-element.324), channel_id=1, source_target_pairs={{0,24},{8,0},{16,8},{24,16},{1,25},{9,1},{17,9},{25,17},{2,26},{10... | collective-permute-start | bytes 221192 | tf_op jit(solution)/shard_map/ppermute | solution.py:91
  53.6 19.6 %collective-permute-start.1 = (bf16[128,1536]{1,0:T(8,128)(2,1)S(1)}, bf16[128,1536]{1,0:T(8,128)(2,1)S(1)}, u32[]{:S(2)}, u32[]{:S(2)}) collective-permute-start(bf16[128,1536]{1,0:T(8,128)(2,1)S(1)} %constant_dynamic-update-slice_fusion), channel_id=1, source_target_pairs={{0,2},{1,3},{2,0},{3,1},{4,6},{5,7},{6,4},{7,5},{8,10},{9,11},{10,... | collective-permute-start | bytes 1179656 | tf_op jit(solution)/shard_map/ppermute | solution.py:96
  56.2 17.1 %collective-permute-start.2 = (bf16[128,1536]{1,0:T(8,128)(2,1)S(1)}, bf16[128,1536]{1,0:T(8,128)(2,1)S(1)}, u32[]{:S(2)}, u32[]{:S(2)}) collective-permute-start(bf16[128,1536]{1,0:T(8,128)(2,1)S(1)} %constant_dynamic-update-slice_fusion), channel_id=1, source_target_pairs={{0,3},{1,0},{2,1},{3,2},{4,7},{5,4},{6,5},{7,6},{8,11},{9,8},{10,9... | collective-permute-start | bytes 1179656 | tf_op jit(solution)/shard_map/ppermute | solution.py:96
  73.3 16.2 %collective-permute-start.10 = (bf16[4,48,768]{2,1,0:T(8,128)(2,1)S(1)}, bf16[4,48,768]{2,1,0:T(8,128)(2,1)S(1)}, u32[]{:S(2)}, u32[]{:S(2)}) collective-permute-start(bf16[4,48,768]{2,1,0:T(8,128)(2,1)S(1)} %bitcast_dynamic-update-slice_fusion.14), channel_id=1, source_target_pairs={{0,8},{8,16},{16,24},{24,0},{1,9},{9,17},{17,25},{25,1},{2,10},{10... | collective-permute-start | bytes 884744 | tf_op jit(solution)/shard_map/ppermute | solution.py:91
  73.5 28.7 %collective-permute-start.12 = (bf16[4,48,768]{2,1,0:T(8,128)(2,1)S(1)}, bf16[4,48,768]{2,1,0:T(8,128)(2,1)S(1)}, u32[]{:S(2)}, u32[]{:S(2)}) collective-permute-start(bf16[4,48,768]{2,1,0:T(8,128)(2,1)S(1)} %bitcast_dynamic-update-slice_fusion.14), channel_id=1, source_target_pairs={{0,16},{8,24},{16,0},{24,8},{1,17},{9,25},{17,1},{25,9},{2,18},{10... | collective-permute-start | bytes 884744 | tf_op jit(solution)/shard_map/ppermute | solution.py:91
  76.3 16.2 %collective-permute-start.11 = (bf16[4,48,768]{2,1,0:T(8,128)(2,1)S(1)}, bf16[4,48,768]{2,1,0:T(8,128)(2,1)S(1)}, u32[]{:S(2)}, u32[]{:S(2)}) collective-permute-start(bf16[4,48,768]{2,1,0:T(8,128)(2,1)S(1)} %bitcast_dynamic-update-slice_fusion.10), channel_id=1, source_target_pairs={{0,32},{32,64},{64,96},{96,0},{1,33},{33,65},{65,97},{97,1},{2,34}... | collective-permute-start | bytes 884744 | tf_op jit(solution)/shard_map/ppermute | solution.py:91
  76.7 27.4 %collective-permute-start.13 = (bf16[4,48,768]{2,1,0:T(8,128)(2,1)S(1)}, bf16[4,48,768]{2,1,0:T(8,128)(2,1)S(1)}, u32[]{:S(2)}, u32[]{:S(2)}) collective-permute-start(bf16[4,48,768]{2,1,0:T(8,128)(2,1)S(1)} %bitcast_dynamic-update-slice_fusion.10), channel_id=1, source_target_pairs={{0,64},{32,96},{64,0},{96,32},{1,65},{33,97},{65,1},{97,33},{2,66}... | collective-permute-start | bytes 884744 | tf_op jit(solution)/shard_map/ppermute | solution.py:91
  78.4 25.7 %collective-permute-start.14 = (bf16[4,48,768]{2,1,0:T(8,128)(2,1)S(1)}, bf16[4,48,768]{2,1,0:T(8,128)(2,1)S(1)}, u32[]{:S(2)}, u32[]{:S(2)}) collective-permute-start(bf16[4,48,768]{2,1,0:T(8,128)(2,1)S(1)} %bitcast_dynamic-update-slice_fusion.14), channel_id=1, source_target_pairs={{0,24},{8,0},{16,8},{24,16},{1,25},{9,1},{17,9},{25,17},{2,26},{10... | collective-permute-start | bytes 884744 | tf_op jit(solution)/shard_map/ppermute | solution.py:91
  89.5 15.9 %collective-permute-start.15 = (bf16[4,48,768]{2,1,0:T(8,128)(2,1)S(1)}, bf16[4,48,768]{2,1,0:T(8,128)(2,1)S(1)}, u32[]{:S(2)}, u32[]{:S(2)}) collective-permute-start(bf16[4,48,768]{2,1,0:T(8,128)(2,1)S(1)} %bitcast_dynamic-update-slice_fusion.10), channel_id=1, source_target_pairs={{0,96},{32,0},{64,32},{96,64},{1,97},{33,1},{65,33},{97,65},{2,98}... | collective-permute-start | bytes 884744 | tf_op jit(solution)/shard_map/ppermute | solution.py:91
  174.9 12.2 %collective-permute-start.28 = (bf16[64,1536]{1,0:T(8,128)(2,1)S(1)}, bf16[64,1536]{1,0:T(8,128)(2,1)S(1)}, u32[]{:S(2)}, u32[]{:S(2)}) collective-permute-start(bf16[64,1536]{1,0:T(8,128)(2,1)S(1)} %multiply_convert_fusion.3), channel_id=1, source_target_pairs={{0,3},{1,0},{2,1},{3,2},{4,7},{5,4},{6,5},{7,6},{8,11},{9,8},{10,9... | collective-permute-start | bytes 589832 | tf_op jit(solution)/shard_map/ppermute | solution.py:96
  178.3 15.0 %collective-permute-start.26 = (bf16[64,1536]{1,0:T(8,128)(2,1)S(1)}, bf16[64,1536]{1,0:T(8,128)(2,1)S(1)}, u32[]{:S(2)}, u32[]{:S(2)}) collective-permute-start(bf16[64,1536]{1,0:T(8,128)(2,1)S(1)} %multiply_convert_fusion.3), channel_id=1, source_target_pairs={{0,1},{1,2},{2,3},{3,0},{4,5},{5,6},{6,7},{7,4},{8,9},{9,10},{10,1... | collective-permute-start | bytes 589832 | tf_op jit(solution)/shard_map/ppermute | solution.py:96
  216.1 11.7 %collective-permute-start.34 = (bf16[64,1536]{1,0:T(8,128)(2,1)S(1)}, bf16[64,1536]{1,0:T(8,128)(2,1)S(1)}, u32[]{:S(2)}, u32[]{:S(2)}) collective-permute-start(bf16[64,1536]{1,0:T(8,128)(2,1)S(1)} %get-tuple-element.274), channel_id=1, source_target_pairs={{0,1},{1,2},{2,3},{3,0},{4,5},{5,6},{6,7},{7,4},{8,9},{9,10},{10,1... | collective-permute-start | bytes 589832 | tf_op jit(solution)/shard_map/ppermute | solution.py:96
  216.3 11.8 %collective-permute-start.32 = (bf16[64,1536]{1,0:T(8,128)(2,1)S(1)}, bf16[64,1536]{1,0:T(8,128)(2,1)}, u32[]{:S(2)}, u32[]{:S(2)}) collective-permute-start(bf16[64,1536]{1,0:T(8,128)(2,1)S(1)} %get-tuple-element.273), channel_id=1, source_target_pairs={{0,3},{1,0},{2,1},{3,2},{4,7},{5,4},{6,5},{7,6},{8,11},{9,8},{10,9... | collective-permute-start | bytes 589832 | tf_op jit(solution)/shard_map/ppermute | solution.py:96
  258.4 19.5 %collective-permute-start.44 = (bf16[256,5760]{1,0:T(8,128)(2,1)}, bf16[256,5760]{1,0:T(8,128)(2,1)S(1)}, u32[]{:S(2)}, u32[]{:S(2)}) collective-permute-start(bf16[256,5760]{1,0:T(8,128)(2,1)} %get-tuple-element.102.refs_0_.refs_2_), channel_id=1, source_target_pairs={{0,4},{4,0},{1,5},{5,1},{2,6},{6,2},{3,7},{7,3},{8,12},{12,8},{9,1... | collective-permute-start | bytes 8847368 | tf_op jit(solution)/shard_map/ppermute | solution.py:86
  260.5 12.1 %collective-permute-start.39 = (bf16[64,1536]{1,0:T(8,128)(2,1)S(1)}, bf16[64,1536]{1,0:T(8,128)(2,1)S(1)}, u32[]{:S(2)}, u32[]{:S(2)}) collective-permute-start(bf16[64,1536]{1,0:T(8,128)(2,1)S(1)} %get-tuple-element.100), channel_id=1, source_target_pairs={{0,2},{1,3},{2,0},{3,1},{4,6},{5,7},{6,4},{7,5},{8,10},{9,11},{10,... | collective-permute-start | bytes 589832 | tf_op jit(solution)/shard_map/ppermute | solution.py:96
  273.6 16.4 %collective-permute-start.41 = (bf16[64,1536]{1,0:T(8,128)(2,1)S(1)}, bf16[64,1536]{1,0:T(8,128)(2,1)S(1)}, u32[]{:S(2)}, u32[]{:S(2)}) collective-permute-start(bf16[64,1536]{1,0:T(8,128)(2,1)S(1)} %fusion.169), channel_id=1, source_target_pairs={{0,1},{1,2},{2,3},{3,0},{4,5},{5,6},{6,7},{7,4},{8,9},{9,10},{10,1... | collective-permute-start | bytes 589832 | tf_op jit(solution)/shard_map/ppermute | solution.py:96
  274.4 15.6 %collective-permute-start.42 = (bf16[64,1536]{1,0:T(8,128)(2,1)S(1)}, bf16[64,1536]{1,0:T(8,128)(2,1)S(1)}, u32[]{:S(2)}, u32[]{:S(2)}) collective-permute-start(bf16[64,1536]{1,0:T(8,128)(2,1)S(1)} %fusion.169), channel_id=1, source_target_pairs={{0,2},{1,3},{2,0},{3,1},{4,6},{5,7},{6,4},{7,5},{8,10},{9,11},{10,... | collective-permute-start | bytes 589832 | tf_op jit(solution)/shard_map/ppermute | solution.py:96
  277.9 12.1 %collective-permute-start.43 = (bf16[64,1536]{1,0:T(8,128)(2,1)S(1)}, bf16[64,1536]{1,0:T(8,128)(2,1)S(1)}, u32[]{:S(2)}, u32[]{:S(2)}) collective-permute-start(bf16[64,1536]{1,0:T(8,128)(2,1)S(1)} %fusion.169), channel_id=1, source_target_pairs={{0,3},{1,0},{2,1},{3,2},{4,7},{5,4},{6,5},{7,6},{8,11},{9,8},{10,9... | collective-permute-start | bytes 589832 | tf_op jit(solution)/shard_map/ppermute | solution.py:96
  290.1 236.1 %reduce-scatter.5.cloned.1.call-start = ((), (), s32[]{:S(2)}) async-start(), calls=%async_computation.7 | async-start | bytes 10444800 | tf_op jit(solution)/shard_map/reduce_scatter | solution.py:365
  290.2 101.6 %collective-permute-start.66 = (bf16[256,1536]{1,0:T(8,128)(2,1)S(1)}, bf16[256,1536]{1,0:T(8,128)(2,1)}, u32[]{:S(2)}, u32[]{:S(2)}) collective-permute-start(bf16[256,1536]{1,0:T(8,128)(2,1)S(1)} %pad_maximum_fusion.3.refs_0_), channel_id=1, source_target_pairs={{0,4},{4,0},{1,5},{5,1},{2,6},{6,2},{3,7},{7,3},{8,12},{12,8},{9,1... | collective-permute-start | bytes 2359304 | tf_op jit(solution)/shard_map/ppermute | solution.py:86
  295.5 56.8 %collective-permute-start.55 = (bf16[256,1536]{1,0:T(8,128)(2,1)}, bf16[256,1536]{1,0:T(8,128)(2,1)}, u32[]{:S(2)}, u32[]{:S(2)}) collective-permute-start(bf16[256,1536]{1,0:T(8,128)(2,1)} %constant_dynamic-update-slice_fusion.2), channel_id=1, source_target_pairs={{0,4},{4,0},{1,5},{5,1},{2,6},{6,2},{3,7},{7,3},{8,12},{12,8},{9,1... | collective-permute-start | bytes 2359304 | tf_op jit(solution)/shard_map/ppermute | solution.py:86
  313.7 12.8 %collective-permute-start.46 = (bf16[256,256]{0,1:T(8,128)(2,1)S(1)}, bf16[256,256]{0,1:T(8,128)(2,1)S(1)}, u32[]{:S(2)}, u32[]{:S(2)}) collective-permute-start(bf16[256,256]{0,1:T(8,128)(2,1)S(1)} %get-tuple-element.289), channel_id=1, source_target_pairs={{0,8},{4,12},{8,0},{12,4},{1,9},{5,13},{9,1},{13,5},{2,10},{6,14},... | collective-permute-start | bytes 393224 | tf_op jit(solution)/shard_map/ppermute | solution.py:82
  314.4 12.2 %collective-permute-start.45 = (bf16[256,256]{0,1:T(8,128)(2,1)S(1)}, bf16[256,256]{0,1:T(8,128)(2,1)S(1)}, u32[]{:S(2)}, u32[]{:S(2)}) collective-permute-start(bf16[256,256]{0,1:T(8,128)(2,1)S(1)} %get-tuple-element.287), channel_id=1, source_target_pairs={{0,4},{4,0},{8,12},{12,8},{1,5},{5,1},{9,13},{13,9},{2,6},{6,2},{1... | collective-permute-start | bytes 393224 | tf_op jit(solution)/shard_map/ppermute | solution.py:82
  354.2 20.2 %collective-permute-start.57 = (bf16[64,1536]{1,0:T(8,128)(2,1)S(1)}, bf16[64,1536]{1,0:T(8,128)(2,1)S(1)}, u32[]{:S(2)}, u32[]{:S(2)}) collective-permute-start(bf16[64,1536]{1,0:T(8,128)(2,1)S(1)} %copy-done.12), channel_id=1, source_target_pairs={{0,3},{1,0},{2,1},{3,2},{4,7},{5,4},{6,5},{7,6},{8,11},{9,8},{10,9... | collective-permute-start | bytes 589832 | tf_op jit(solution)/shard_map/ppermute | solution.py:96
  358.7 15.8 %collective-permute-start.58 = (bf16[64,1536]{1,0:T(8,128)(2,1)S(1)}, bf16[64,1536]{1,0:T(8,128)(2,1)S(1)}, u32[]{:S(2)}, u32[]{:S(2)}) collective-permute-start(bf16[64,1536]{1,0:T(8,128)(2,1)S(1)} %copy-done.10), channel_id=1, source_target_pairs={{0,2},{1,3},{2,0},{3,1},{4,6},{5,7},{6,4},{7,5},{8,10},{9,11},{10,... | collective-permute-start | bytes 589832 | tf_op jit(solution)/shard_map/ppermute | solution.py:96
  360.7 13.8 %collective-permute-start.59 = (bf16[64,1536]{1,0:T(8,128)(2,1)S(1)}, bf16[64,1536]{1,0:T(8,128)(2,1)S(1)}, u32[]{:S(2)}, u32[]{:S(2)}) collective-permute-start(bf16[64,1536]{1,0:T(8,128)(2,1)S(1)} %copy-done.8), channel_id=1, source_target_pairs={{0,1},{1,2},{2,3},{3,0},{4,5},{5,6},{6,7},{7,4},{8,9},{9,10},{10,1... | collective-permute-start | bytes 589832 | tf_op jit(solution)/shard_map/ppermute | solution.py:96
  379.3 12.9 %collective-permute-start.68 = (bf16[256,2688]{1,0:T(8,128)(2,1)S(1)}, bf16[256,2688]{1,0:T(8,128)(2,1)S(1)}, u32[]{:S(2)}, u32[]{:S(2)}) collective-permute-start(bf16[256,2688]{1,0:T(8,128)(2,1)S(1)} %get-tuple-element.124), channel_id=1, source_target_pairs={{0,4},{4,0},{1,5},{5,1},{2,6},{6,2},{3,7},{7,3},{8,12},{12,8},{9,1... | collective-permute-start | bytes 4128776 | tf_op jit(solution)/shard_map/ppermute | solution.py:86
  388.4 13.7 %collective-permute-start.63 = (bf16[64,1536]{1,0:T(8,128)(2,1)S(1)}, bf16[64,1536]{1,0:T(8,128)(2,1)}, u32[]{:S(2)}, u32[]{:S(2)}) collective-permute-start(bf16[64,1536]{1,0:T(8,128)(2,1)S(1)} %get-tuple-element.126), channel_id=1, source_target_pairs={{0,1},{1,2},{2,3},{3,0},{4,5},{5,6},{6,7},{7,4},{8,9},{9,10},{10,1... | collective-permute-start | bytes 589832 | tf_op jit(solution)/shard_map/ppermute | solution.py:96
  389.6 12.5 %collective-permute-start.64 = (bf16[64,1536]{1,0:T(8,128)(2,1)S(1)}, bf16[64,1536]{1,0:T(8,128)(2,1)}, u32[]{:S(2)}, u32[]{:S(2)}) collective-permute-start(bf16[64,1536]{1,0:T(8,128)(2,1)S(1)} %get-tuple-element.126), channel_id=1, source_target_pairs={{0,2},{1,3},{2,0},{3,1},{4,6},{5,7},{6,4},{7,5},{8,10},{9,11},{10,... | collective-permute-start | bytes 589832 | tf_op jit(solution)/shard_map/ppermute | solution.py:96
  404.0 64.0 %collective-permute-start.74 = (bf16[256,1536]{1,0:T(8,128)(2,1)S(1)}, bf16[256,1536]{1,0:T(8,128)(2,1)S(1)}, u32[]{:S(2)}, u32[]{:S(2)}) collective-permute-start(bf16[256,1536]{1,0:T(8,128)(2,1)S(1)} %multiply_convert_fusion.refs_0_), channel_id=1, source_target_pairs={{0,4},{4,0},{1,5},{5,1},{2,6},{6,2},{3,7},{7,3},{8,12},{12,8},{9,1... | collective-permute-start | bytes 2359304 | tf_op jit(solution)/shard_map/ppermute | solution.py:86
  412.4 55.6 %collective-permute-start.75 = (bf16[256,1536]{1,0:T(8,128)(2,1)}, bf16[256,1536]{1,0:T(8,128)(2,1)}, u32[]{:S(2)}, u32[]{:S(2)}) collective-permute-start(bf16[256,1536]{1,0:T(8,128)(2,1)} %get-tuple-element.357), channel_id=1, source_target_pairs={{0,4},{4,0},{1,5},{5,1},{2,6},{6,2},{3,7},{7,3},{8,12},{12,8},{9,1... | collective-permute-start | bytes 2359304 | tf_op jit(solution)/shard_map/ppermute | solution.py:86
  439.7 29.6 %collective-permute-start.76 = (bf16[256,768]{1,0:T(8,128)(2,1)}, bf16[256,768]{1,0:T(8,128)(2,1)S(1)}, u32[]{:S(2)}, u32[]{:S(2)}) collective-permute-start(bf16[256,768]{1,0:T(8,128)(2,1)} %get-tuple-element.263), channel_id=1, source_target_pairs={{0,4},{4,0},{1,5},{5,1},{2,6},{6,2},{3,7},{7,3},{8,12},{12,8},{9,1... | collective-permute-start | bytes 1179656 | tf_op jit(solution)/shard_map/ppermute | solution.py:86
  462.9 20.9 %all-to-all-start.1 = ((bf16[32,5,1536]{2,1,0:T(8,128)(2,1)}), bf16[32,5,1536]{2,1,0:T(8,128)(2,1)}, u32[]{:S(2)}, u32[]{:S(2)}) async-start(bf16[32,5,1536]{2,1,0:T(8,128)(2,1)} %maximum_maximum_fusion), calls=%async_computation.2 | async-start | bytes 1572864 | tf_op jit(solution)/shard_map/all_to_all | solution.py:837
  487.2 12.6 %collective-permute-start.77 = (bf16[136,1536]{1,0:T(8,128)(2,1)S(1)}, bf16[136,1536]{1,0:T(8,128)(2,1)}, u32[]{:S(2)}, u32[]{:S(2)}) collective-permute-start(bf16[136,1536]{1,0:T(8,128)(2,1)S(1)} %pad_maximum_fusion.7), channel_id=1, source_target_pairs={{0,1},{1,2},{2,3},{3,0},{4,5},{5,6},{6,7},{7,4},{8,9},{9,10},{10,1... | collective-permute-start | bytes 1253384 | tf_op jit(solution)/shard_map/ppermute | solution.py:96
  489.7 25.3 %collective-permute-start.80 = (bf16[384,768]{1,0:T(8,128)(2,1)}, bf16[384,768]{1,0:T(8,128)(2,1)S(1)}, u32[]{:S(2)}, u32[]{:S(2)}) collective-permute-start(bf16[384,768]{1,0:T(8,128)(2,1)} %get-tuple-element.253), channel_id=1, source_target_pairs={{0,32},{32,64},{64,96},{96,0},{1,33},{33,65},{65,97},{97,1},{2,34}... | collective-permute-start | bytes 1769480 | tf_op jit(solution)/shard_map/ppermute | solution.py:91
  489.7 27.8 %collective-permute-start.81 = (bf16[384,768]{1,0:T(8,128)(2,1)}, bf16[384,768]{1,0:T(8,128)(2,1)S(1)}, u32[]{:S(2)}, u32[]{:S(2)}) collective-permute-start(bf16[384,768]{1,0:T(8,128)(2,1)} %get-tuple-element.252), channel_id=1, source_target_pairs={{0,64},{32,96},{64,0},{96,32},{1,65},{33,97},{65,1},{97,33},{2,66}... | collective-permute-start | bytes 1769480 | tf_op jit(solution)/shard_map/ppermute | solution.py:91
  491.6 27.1 %collective-permute-start.82 = (bf16[384,768]{1,0:T(8,128)(2,1)}, bf16[384,768]{1,0:T(8,128)(2,1)S(1)}, u32[]{:S(2)}, u32[]{:S(2)}) collective-permute-start(bf16[384,768]{1,0:T(8,128)(2,1)} %get-tuple-element.251), channel_id=1, source_target_pairs={{0,96},{32,0},{64,32},{96,64},{1,97},{33,1},{65,33},{97,65},{2,98}... | collective-permute-start | bytes 1769480 | tf_op jit(solution)/shard_map/ppermute | solution.py:91
  493.6 16.1 %collective-permute-start.78 = (bf16[136,1536]{1,0:T(8,128)(2,1)S(1)}, bf16[136,1536]{1,0:T(8,128)(2,1)S(1)}, u32[]{:S(2)}, u32[]{:S(2)}) collective-permute-start(bf16[136,1536]{1,0:T(8,128)(2,1)S(1)} %pad_maximum_fusion.7), channel_id=1, source_target_pairs={{0,2},{1,3},{2,0},{3,1},{4,6},{5,7},{6,4},{7,5},{8,10},{9,11},{10,... | collective-permute-start | bytes 1253384 | tf_op jit(solution)/shard_map/ppermute | solution.py:96
  499.8 15.2 %collective-permute-start.79 = (bf16[136,1536]{1,0:T(8,128)(2,1)S(1)}, bf16[136,1536]{1,0:T(8,128)(2,1)}, u32[]{:S(2)}, u32[]{:S(2)}) collective-permute-start(bf16[136,1536]{1,0:T(8,128)(2,1)S(1)} %pad_maximum_fusion.7), channel_id=1, source_target_pairs={{0,3},{1,0},{2,1},{3,2},{4,7},{5,4},{6,5},{7,6},{8,11},{9,8},{10,9... | collective-permute-start | bytes 1253384 | tf_op jit(solution)/shard_map/ppermute | solution.py:96
  (217 other events, 2279.3 us)
Sparse Core Ops, SparseCore 0:
  10.9 105.9 all-gather.2
  119.7 71.3 all-gather.4
  290.2 84.1 reduce-scatter.2
  402.3 90.1 reduce-scatter.4

commit v7 on v6

--- a/solution.py
+++ b/solution.py
@@ -238,22 +238,25 @@
     first = core_ref[0] == 0
     half = TILE // 2
     low, high = active[:, :half], active[:, half:]
-    start = (2 * width if forward else 0) + step * (TILE + half)
-    start = pl.multiple_of(start, half)
+    offset = 2 * width if forward else 0
+    wide = pl.multiple_of(step * TILE, TILE)
+    narrow = pl.multiple_of(pl.num_programs(0) * TILE + step * half, half)
+    side_wide = pl.multiple_of(offset + wide, TILE)
+    side_narrow = pl.multiple_of(offset + narrow, half)
 
     @pl.when(first)
     def _():
-        keep_ref[:, :TILE] = d_gate
-        keep_ref[:, TILE:] = low
-        side_ref[:, pl.ds(start, TILE)] = d_up
-        side_ref[:, pl.ds(start + TILE, half)] = high
+        keep_ref[:, pl.ds(wide, TILE)] = d_gate
+        keep_ref[:, pl.ds(narrow, half)] = low
+        side_ref[:, pl.ds(side_wide, TILE)] = d_up
+        side_ref[:, pl.ds(side_narrow, half)] = high
 
     @pl.when(jnp.logical_not(first))
     def _():
-        keep_ref[:, :TILE] = d_up
-        keep_ref[:, TILE:] = high
-        side_ref[:, pl.ds(start, TILE)] = d_gate
-        side_ref[:, pl.ds(start + TILE, half)] = low
+        keep_ref[:, pl.ds(wide, TILE)] = d_up
+        keep_ref[:, pl.ds(narrow, half)] = high
+        side_ref[:, pl.ds(side_wide, TILE)] = d_gate
+        side_ref[:, pl.ds(side_narrow, half)] = low
 
     @pl.when(step == pl.num_programs(0) - 1)
     def _():
@@ -275,7 +278,7 @@
         + [whole((rows, width))] * (2 * count)
         + weight_specs(width, steps),
         out_specs=[whole((rows, width))] * (ways * count)
-        + [pl.BlockSpec((tokens, block), lambda j: (0, j)), whole((tokens, side_width))],
+        + [whole((tokens, steps * block)), whole((tokens, side_width))],
         out_shape=chunk_shapes(count, rows, width) * ways
         + [
             jax.ShapeDtypeStruct((tokens, steps * block), BF16),
@@ -294,7 +297,7 @@
     return results[:count], results[count : ways * count], results[-2], results[-1]
 
 
-def gradient_kernel(cut, whole_steps, *refs):
+def gradient_kernel(edge, cut, *refs):
     one_own, one_other, two_own, two_other, own_ref, other_ref = refs[:6]
     out_ref = refs[-1]
     step = pl.program_id(0)
@@ -304,23 +307,25 @@
         total += times_rows(other_left[...], other_ref[:, columns])
         out_ref[:, columns] = total.astype(BF16)
 
-    if whole_steps:
-
-        @pl.when(step < whole_steps)
+    @pl.when(step < edge)
+    def _():
+        product(one_own, one_other, slice(None))
+
+    @pl.when(step > edge if cut else step >= edge)
+    def _():
+        product(two_own, two_other, slice(None))
+
+    if cut:
+
+        @pl.when(step == edge)
         def _():
-            product(one_own, one_other, slice(None))
-
-        @pl.when(step >= whole_steps)
-        def _():
-            product(two_own, two_other, slice(None))
-
-    else:
-        product(one_own, one_other, slice(0, cut))
-        product(two_own, two_other, slice(cut, None))
-
-
-def gradient(lefts, own, other, other_start, block, steps, cut, whole_steps, width, out_width, out_start, target):
+            product(one_own, one_other, slice(0, cut))
+            product(two_own, two_other, slice(cut, None))
+
+
+def gradient(lefts, own, other, other_start, block, steps, columns, width, out_width, out_start, target):
     tokens = own.shape[0]
+    edge, cut = divmod(columns, block)
 
     def left_spec(index):
         return pl.BlockSpec((tokens, width), lambda j: (0, index))
@@ -336,7 +341,7 @@
         operands.append(target)
         aliases = {len(operands) - 1: 0}
     return pl.pallas_call(
-        functools.partial(gradient_kernel, cut, whole_steps),
+        functools.partial(gradient_kernel, edge, cut),
         grid=(steps,),
         in_specs=in_specs,
         out_specs=pl.BlockSpec((width, block), lambda j: (0, out_start + j)),
@@ -361,8 +366,8 @@
     return jnp.where(first, mine, other).astype(F32), jnp.where(first, other, mine).astype(F32)
 
 
-def reduce_gradient(partial):
-    return share_rows(lax.psum_scatter(partial, CHIP_AXES, scatter_dimension=0, tiled=True))
+def sum_chips(partial):
+    return lax.psum_scatter(partial, CHIP_AXES, scatter_dimension=0, tiled=True)
 
 
 def along(blocks, axis):
@@ -425,12 +430,12 @@
 
 def ffn_gradients(low, high, steps, hidden):
     depth = low.shape[0]
-    low = low.reshape(depth, steps, -1)
-    high = high.reshape(depth, steps, -1)
-    gate = low[:, :, :TILE].reshape(depth, -1)[:, :hidden]
-    up = high[:, :, :TILE].reshape(depth, -1)[:, :hidden]
-    down = jnp.concatenate([low[:, :, TILE:], high[:, :, TILE:]], axis=2)
-    return jnp.stack([gate, up], axis=1), down.reshape(depth, -1)[:, :hidden].T
+    padded = steps * TILE
+    gateup = jnp.stack([low[:, :hidden], high[:, :hidden]], axis=1)
+    down = jnp.concatenate(
+        [part[:, padded:].reshape(depth, steps, TILE // 2) for part in (low, high)], axis=2
+    )
+    return gateup, down.reshape(depth, padded)[:, :hidden].T
 
 
 def halves(proj, out):
@@ -518,9 +523,9 @@
         ],
         axis=1,
     )
-    outgoing, mixer_pack = lax.optimization_barrier((outgoing, mixer_pack))
+    arrived = lax.all_to_all(outgoing, TOKEN_AXES, split_axis=0, concat_axis=0, tiled=True)
+    arrived, mixer_pack = lax.optimization_barrier((arrived, mixer_pack))
     mixer_low, mixer_high = gather_first(mixer_pack)
-    arrived = lax.all_to_all(outgoing, TOKEN_AXES, split_axis=0, concat_axis=0, tiled=True)
     gains = (
         arrived[:, 2 * part_rows, : 4 * depth]
         .reshape(shards, 4, depth)
@@ -615,8 +620,10 @@
         ],
         axis=1,
     )
+    key_value_z = swap_ctx(key_value, 2)
+    key_value_core = swap_core(jnp.concatenate([key_value, key_value_z]))
     key_value_all = jnp.concatenate(
-        [key_value] + [swap_ctx(key_value, mask) for mask in range(1, contexts)], axis=0
+        [key_value, key_value_core[:row_count], key_value_z, key_value_core[row_count:]]
     )
     key_all = key_value_all[:, : kv_heads * HD].reshape(-1, kv_heads, HD)
     value_all = key_value_all[:, kv_heads * HD :].reshape(-1, kv_heads, HD)
@@ -651,12 +658,12 @@
     ffn_cols = steps * block
     side_start = 2 * width // block
     partial = gradient(
-        ffn_lefts, keep, side_other, side_start, block, steps, TILE, 0, width, ffn_cols, 0, None
+        ffn_lefts, keep, side_other, side_start, block, steps, padded, width, ffn_cols, 0, None
     )
 
     back_b = tp_gather(d_stream3.astype(BF16))
     back_b, partial = lax.optimization_barrier((back_b, partial))
-    second_grads = reduce_gradient(partial)
+    second_grads = share_rows(sum_chips(partial))
     back_b = jnp.concatenate(back_b)
     back_b_other = swap_core(back_b)
     attend_in_other = swap_core(attend_in)
@@ -680,10 +687,11 @@
     d_key_value = jnp.concatenate(
         [d_keys.reshape(-1, kv_heads * HD), d_values.reshape(-1, kv_heads * HD)], axis=1
     )
-    d_local = d_key_value[:row_count]
-    for mask in range(1, contexts):
-        part = d_key_value[mask * row_count : (mask + 1) * row_count].astype(BF16)
-        d_local = d_local + swap_ctx(part, mask).astype(F32)
+    d_slots = d_key_value.reshape(contexts, row_count, -1)
+    d_others = jnp.concatenate([d_slots[1], d_slots[3]]).astype(BF16)
+    d_others = swap_core(d_others).astype(F32)
+    d_far = (d_slots[2] + d_others[row_count:]).astype(BF16)
+    d_local = d_slots[0] + d_others[:row_count] + swap_ctx(d_far, 2).astype(F32)
     d_key_local = d_local[:, : kv_heads * HD].reshape(row_count, kv_heads, HD)
     d_value_local = d_local[:, kv_heads * HD :].reshape(row_count, kv_heads, HD)
     unused, pullback = jax.vjp(qk_maps, query_raw, key_raw, qgain_f, kgain_f)
@@ -713,8 +721,7 @@
         0,
         small_tile,
         attend_cols // small_tile,
-        0,
-        (attend_project.shape[1] - attend_cols) // small_tile,
+        attend_project.shape[1] - attend_cols,
         width,
         ffn_cols + attend_cols,
         ffn_cols // small_tile,
@@ -739,8 +746,7 @@
         0,
         block,
         steps,
-        TILE,
-        0,
+        padded,
         width,
         ffn_cols + attend_cols,
         0,
@@ -753,9 +759,7 @@
 
     back_a = tp_gather(d_stream1.astype(BF16))
     back_a, partial = lax.optimization_barrier((back_a, partial))
-    low, high = reduce_gradient(partial)
-    first_grads = (low[:, :ffn_cols], high[:, :ffn_cols])
-    attend_grads = jnp.concatenate([low[:, ffn_cols:], high[:, ffn_cols:]], axis=1)
+    first_sums = sum_chips(partial)
     back_a = arrange(to_dealt, jnp.concatenate(back_a))
     back_a_other = swap_core(back_a)
     d_gated = times(back_a, output_a_t)
@@ -795,14 +799,28 @@
         mixer_cols,
         1,
         3 * channels - mixer_cols,
-        0,
         width,
         mixer_cols,
         0,
         None,
     )
-    second_grads = ffn_gradients(*second_grads, steps, hidden)
-    d_mixer_in, second_grads = lax.optimization_barrier((tp_reduce(d_chunks), second_grads))
+    kernel_cols = kernel_taps * channels
+    gain_start = kernel_cols + 2 * HD
+    shared = jnp.concatenate([kernel_grad.reshape(-1), qgain_grad, kgain_grad])
+    early_gains = [
+        grad.reshape(shards, depth) for grad in (gain_f_grad, gain_b_grad, gain_s_grad)
+    ]
+    early_row = jnp.concatenate(
+        [
+            jnp.broadcast_to(shared, (shards, gain_start)),
+            jnp.pad(
+                jnp.concatenate(early_gains, axis=1),
+                ((0, 0), (0, width - gain_start - 3 * depth)),
+            ),
+        ],
+        axis=1,
+    )
+    d_mixer_in, early_row = lax.optimization_barrier((tp_reduce(d_chunks), early_row))
     unused, pullback = jax.vjp(norm_rows, stream0, gain_a)
     d_norm_a, gain_a_grad = pullback(d_mixer_in)
     d_stream0 = d_stream1 + d_norm_a
@@ -813,56 +831,59 @@
         ),
         axis=1,
     )
-    gain_rows = jnp.concatenate(
-        [
-            grad.reshape(shards, depth)
-            for grad in (gain_f_grad, gain_b_grad, gain_s_grad, gain_a_grad)
-        ],
-        axis=1,
-    )
-    kernel_cols = kernel_taps * channels
-    shared = jnp.concatenate([kernel_grad.reshape(-1), qgain_grad, kgain_grad])
-    fill = width - shared.shape[0] - 4 * depth
-    small_row = jnp.concatenate(
-        [
-            jnp.broadcast_to(shared, (shards, shared.shape[0])),
-            jnp.pad(gain_rows, ((0, 0), (0, fill))),
-        ],
-        axis=1,
-    ).astype(BF16)
-
-    def by_anchor(rows):
-        return rows.astype(BF16).reshape(shards, part_rows, width)[slot_for_anchor]
-
+    late_start = gain_start + 3 * depth
+    late_row = jnp.pad(
+        gain_a_grad.reshape(shards, depth), ((0, 0), (late_start, width - late_start - depth))
+    )
+    leaving = jnp.concatenate(
+        [d_stream0.astype(BF16), stream4.astype(BF16), (early_row + late_row).astype(BF16)]
+    )
+    line = jnp.arange(shards * piece_rows)
+    target, item = line // piece_rows, line % piece_rows
+    source = jnp.where(
+        item < 2 * part_rows,
+        item // part_rows * chunk
+        + jnp.repeat(slot_for_anchor, piece_rows) * part_rows
+        + item % part_rows,
+        jnp.where(item == 2 * part_rows, 2 * chunk + target, -1),
+    )
+    to_leaving = (source[:, None] == jnp.arange(leaving.shape[0])[None, :]).astype(BF16)
+    leaving = arrange(to_leaving, leaving)
+    leaving, partial = lax.optimization_barrier((leaving, partial))
     home = lax.all_to_all(
-        jnp.concatenate(
-            [by_anchor(d_stream0), by_anchor(stream4), small_row[:, None]], axis=1
-        ),
+        leaving.reshape(shards, piece_rows, width),
         TOKEN_AXES,
         split_axis=0,
         concat_axis=0,
         tiled=True,
     )
-    home, partial = lax.optimization_barrier((home, partial))
     ring = lax.axis_size("x")
     mixer_parts = along(partial.reshape(ring, -1, mixer_cols), "x")
-    small_sum = jnp.sum(home[:, 2 * part_rows].astype(F32), axis=0)
-    small_high = small_sum.astype(BF16)
-    small_low = (small_sum - small_high.astype(F32)).astype(BF16)
-    last = tp_gather(
-        jnp.concatenate(
-            [
-                home[:, :part_rows].reshape(chunk, width),
-                home[:, part_rows : 2 * part_rows].reshape(chunk, width),
-                jnp.pad(jnp.stack([small_high, small_low]), ((0, 6), (0, 0))),
-            ]
-        )
-    )
-    last, mixer_parts = lax.optimization_barrier((last, mixer_parts))
+    second_grads = ffn_gradients(*second_grads, steps, hidden)
+    home, mixer_parts, second_grads = lax.optimization_barrier((home, mixer_parts, second_grads))
+    place = jnp.arange(2 * chunk + 8)
+    small_line = (place == 2 * chunk) | (place == 2 * chunk + 1)
+    wanted = (
+        place % chunk // part_rows * piece_rows
+        + place // chunk * part_rows
+        + place % part_rows
+    )
+    to_payload = jnp.where(
+        (place < 2 * chunk)[:, None],
+        wanted[:, None] == line[None, :],
+        small_line[:, None] & (item == 2 * part_rows)[None, :],
+    ).astype(BF16)
+    payload = times(to_payload, home.reshape(shards * piece_rows, width))
+    rounded = payload.astype(BF16).astype(F32)
+    payload = jnp.where((place == 2 * chunk + 1)[:, None], payload - rounded, payload)
+    last = tp_gather(payload.astype(BF16))
     mixer_parts = add_parts(mixer_parts).astype(BF16).reshape(ring, -1, mixer_cols)
+    last[1], mixer_parts = lax.optimization_barrier((last[1], mixer_parts))
     mixer_parts = along(mixer_parts, Z_AXES)
-    first_grads = ffn_gradients(*first_grads, steps, hidden)
-    mixer_parts, first_grads = lax.optimization_barrier((mixer_parts, first_grads))
+    last, first_sums = lax.optimization_barrier((last, first_sums))
+    low, high = share_rows(first_sums)
+    first_grads = ffn_gradients(low[:, :ffn_cols], high[:, :ffn_cols], steps, hidden)
+    attend_grads = jnp.concatenate([low[:, ffn_cols:], high[:, ffn_cols:]], axis=1)
     mixer_grads = jnp.concatenate(share_rows(add_parts(mixer_parts).astype(BF16)), axis=1)
     home_rows = (
         jnp.repeat(jnp.tile(send_piece, members), part_rows) * piece_rows
@@ -886,7 +907,6 @@
     )
     qgain_total = totals[kernel_cols : kernel_cols + HD]
     kgain_total = totals[kernel_cols + HD : kernel_cols + 2 * HD]
-    gain_start = kernel_cols + 2 * HD
     gain_totals = totals[gain_start : gain_start + 4 * depth].reshape(4, depth)
 
     gateup_s_grad, down_s_grad = second_grads

time: 562 us -> 590 us (1.050)
  waiting for transfers between devices: 149 us -> 194 us
  local copies, waits for them, and re-layouts: 73.7 us -> 59.2 us
  starting transfers between devices: 147 us -> 140 us
    ppermute x18, waiting for transfers between devices: 28.1 us -> 83.1 us  [shift_ring(): lax.ppermute(block, axis, [(i, (i + distance) % ring) for i in range(ring)])]
    all_to_all x1, waiting for transfers between devices: 11.2 us -> 0.01 us  [body(): lax.all_to_all(leaving.reshape(shards, piece_rows, width), TOKEN_AXES, sp...]
    ppermute x18, starting transfers between devices: 30 us -> 20 us  [shift_ring(): lax.ppermute(block, axis, [(i, (i + distance) % ring) for i in range(ring)])]
    all_to_all x1, waiting for transfers between devices: 4.42 us -> 12.3 us  [body(): lax.all_to_all(outgoing, TOKEN_AXES, split_axis=0, concat_axis=0, tiled=T...]
    ppermute x14 -> x16, starting transfers between devices: 22.1 us -> 26.6 us  [swap_core(): return lax.ppermute(block, 'core', [(0, 1), (1, 0)])]
    dot_general x8 -> x10, matrix products: 13.8 us -> 18.1 us  [times(): lax.dot_general(left, right, (((1,), (0,)), ((), ())), preferred_element_...]
    ppermute x6 -> x2, waiting for transfers between devices: 13.7 us -> 11.2 us  [swap_ctx(): lax.ppermute(block, CTX_AXES, [(i, i ^ mask) for i in range(lax.axis_size...]
    unnamed x352 -> x350, local copies, waits for them, and re-layouts: 18.4 us -> 19.5 us
  transfers between devices with their start and end apart: 94 -> 92, of which waited for: 38 -> 42; matrix products, arithmetic and copies ran while one was open for 28% -> 24% of each run, Pallas kernels for 9% -> 9%
where the time goes in v7:
time: 590 us; the launch traced here: 580 us
  waiting for transfers between devices  194 us (33%)
  starting transfers between devices  140 us (24%)
  Pallas kernels  67.2 us (11%)
  local copies, waits for them, and re-layouts  59.2 us (10%)
  other arithmetic  54.6 us (9%)
  matrix products  46.4 us (8%)
  between operations  18.2 us (3%)
    ppermute x48, waiting for transfers between devices, shift_tp(): lax.ppermute(block, 'tp', [(i, (i + distance) % members) for i in range(m...  83.8 us
    ppermute x18, waiting for transfers between devices, shift_ring(): lax.ppermute(block, axis, [(i, (i + distance) % ring) for i in range(ring)])  83.1 us
    ppermute x48, starting transfers between devices, shift_tp(): lax.ppermute(block, 'tp', [(i, (i + distance) % members) for i in range(m...  71 us
    pallas_call x2, Pallas kernels, ffn_backward(): pl.pallas_call(functools.partial(ffn_backward_kernel, count, forward), gr...  28.4 us
    pallas_call x4, Pallas kernels, gradient(): pl.pallas_call(functools.partial(gradient_kernel, edge, cut), grid=(steps...  28.1 us
    ppermute x16, starting transfers between devices, swap_core(): return lax.ppermute(block, 'core', [(0, 1), (1, 0)])  26.6 us
    ppermute x18, starting transfers between devices, shift_ring(): lax.ppermute(block, axis, [(i, (i + distance) % ring) for i in range(ring)])  20 us
    unnamed x350, local copies, waits for them, and re-layouts  19.5 us
  transfers between devices with their start and end apart: 92, of which 42 were waited for; matrix products, arithmetic and copies ran while one was open for 24% of the time, Pallas kernels for 9%

profile of v7, /device:TPU:1, one launch (start us, length us, event | category | flops | bytes accessed | tf_op | source)
XLA Modules:
  0.0 579.6 jit_solution(13477605265701390053)
XLA Ops:
  18.7 9.4 %all-to-all-start = ((bf16[32,5,1536]{2,1,0:T(8,128)(2,1)}), bf16[32,5,1536]{2,1,0:T(8,128)(2,1)S(1)}, u32[]{:S(2)}, u32[]{:S(2)}) async-start(bf16[32,5,1536]{2,1,0:T(8,128)(2,1)} %pad_maximum_fusion.1), calls=%async_computation | async-start | bytes 1572864 | tf_op jit(solution)/shard_map/all_to_all | solution.py:526
  36.1 12.3 %all-to-all-done = bf16[32,5,1536]{2,1,0:T(8,128)(2,1)S(1)} async-done(((bf16[32,5,1536]{2,1,0:T(8,128)(2,1)}), bf16[32,5,1536]{2,1,0:T(8,128)(2,1)S(1)}, u32[]{:S(2)}, u32[]{:S(2)}) %all-to-all-start) | async-done | bytes 491552 | tf_op jit(solution)/shard_map/all_to_all | solution.py:526
  58.9 4.5 collective-permute-done.3
  71.4 4.7 collective-permute-done.7
  83.8 9.0 %collective-permute-done.10 = bf16[4,48,768]{2,1,0:T(8,128)(2,1)S(1)} collective-permute-done((bf16[4,48,768]{2,1,0:T(8,128)(2,1)S(1)}, bf16[4,48,768]{2,1,0:T(8,128)(2,1)S(1)}, u32[]{:S(2)}, u32[]{:S(2)}) %collective-permute-start.10) | collective-permute-done | bytes 294944 | tf_op jit(solution)/shard_map/ppermute | solution.py:91
  94.9 9.9 %collective-permute-done.12 = bf16[4,48,768]{2,1,0:T(8,128)(2,1)S(1)} collective-permute-done((bf16[4,48,768]{2,1,0:T(8,128)(2,1)S(1)}, bf16[4,48,768]{2,1,0:T(8,128)(2,1)S(1)}, u32[]{:S(2)}, u32[]{:S(2)}) %collective-permute-start.12) | collective-permute-done | bytes 294944 | tf_op jit(solution)/shard_map/ppermute | solution.py:91
  104.8 2.9 collective-permute-done.13
  108.8 4.4 collective-permute-start.16
  113.9 3.0 collective-permute-start.9
  122.2 3.0 fusion.217
  131.8 4.1 collective-permute-done.19
  142.2 3.0 collective-permute-start.21
  148.3 5.4 collective-permute-done.21.refs_2_
  153.7 10.6 %ffn_forward.1 = (f32[64,1536]{1,0:T(8,128)S(1)}, bf16[64,1536]{1,0:T(8,128)(2,1)S(1)}, bf16[64,1536]{1,0:T(8,128)(2,1)S(1)}, bf16[64,1536]{1,0:T(8,128)(2,1)S(1)}) custom-call(bf16[64,1536]{1,0:T(8,128)(2,1)S(1)} %multiply_convert_fusion.4.refs_0_, bf16[64,1536]{1,0:T(8,128)(2,1)S(1)} %collective-permute-done.20.refs_1_, ...), custom_call_target="tpu_custom_call" | custom-call | flops 4227858432 | bytes 16515072 | tf_op jit(solution)/shard_map/ffn_forward/pallas_call | solution.py:184
  165.4 3.4 collective-permute-start.24
  171.6 6.1 %collective-permute-done.24 = bf16[64,1536]{1,0:T(8,128)(2,1)} collective-permute-done((bf16[64,1536]{1,0:T(8,128)(2,1)S(1)}, bf16[64,1536]{1,0:T(8,128)(2,1)}, u32[]{:S(2)}, u32[]{:S(2)}) %collective-permute-start.24) | collective-permute-done | bytes 196640 | tf_op jit(solution)/shard_map/ppermute | solution.py:96
  182.6 9.2 %collective-permute-start.26 = (bf16[64,1536]{1,0:T(8,128)(2,1)S(1)}, bf16[64,1536]{1,0:T(8,128)(2,1)S(1)}, u32[]{:S(2)}, u32[]{:S(2)}) collective-permute-start(bf16[64,1536]{1,0:T(8,128)(2,1)S(1)} %multiply_convert_fusion.3), channel_id=1, source_target_pairs={{0,1},{1,2},{2,3},{3,0},{4,5},{5,6},{6,7},{7,4},{8,9},{9,10},{10,1... | collective-permute-start | bytes 589832 | tf_op jit(solution)/shard_map/ppermute | solution.py:96
  192.1 5.7 collective-permute-done.26
  201.4 3.7 collective-permute-done.29
  205.1 3.1 collective-permute-start.30
  215.2 3.1 fusion.218
  223.1 7.0 %collective-permute-done.33 = bf16[64,1536]{1,0:T(8,128)(2,1)S(1)} collective-permute-done((bf16[64,1536]{1,0:T(8,128)(2,1)S(1)}, bf16[64,1536]{1,0:T(8,128)(2,1)S(1)}, u32[]{:S(2)}, u32[]{:S(2)}) %collective-permute-start.33) | collective-permute-done | bytes 196640 | tf_op jit(solution)/shard_map/ppermute | solution.py:96
  240.2 5.8 collective-permute-done.35.refs_2_
  246.0 15.0 %ffn_both.1 = (f32[64,1536]{1,0:T(8,128)S(1)}, bf16[64,1536]{1,0:T(8,128)(2,1)S(1)}, bf16[64,1536]{1,0:T(8,128)(2,1)S(1)}, bf16[64,1536]{1,0:T(8,128)(2,1)S(1)},...) custom-call(s32[1]{0:T(128)} %bitcast.8.core_ref, ...), custom_call_target="tpu_custom_call" | custom-call | flops 8455716864 | bytes 22413312 | tf_op jit(solution)/shard_map/ffn_both/pallas_call | solution.py:274
  266.8 3.9 collective-permute-done.39
  270.8 4.6 collective-permute-done.38
  282.6 10.4 %weight_gradient.4 = bf16[1536,2688]{1,0:T(8,128)(2,1)} custom-call(bf16[256,5760]{1,0:T(8,128)(2,1)S(1)} %copy-done, bf16[256,5760]{1,0:T(8,128)(2,1)} %copy-done.14, bf16[256,5760]{1,0:T(8,128)(2,1)S(1)} %copy-done, bf16[256,5760]{1,0:T(8,128)(2,1)} %copy-done.14, bf16[256,2688]{1,0:T(8,128)(2,1)S(1)} %get-tuple-element.102.refs_4_, ...), custom_call_target="tpu_custom_call" | custom-call | flops 4227858432 | bytes 8257536 | tf_op jit(solution)/shard_map/weight_gradient/pallas_call | solution.py:343
  301.6 7.4 %fusion = (f32[2,3,256]{2,1,0:T(4,128)S(1)}, f32[2,1024,256,3]{2,1,3,0:T(8,128)}) fusion(f32[2,1024,256,3]{2,1,3,0:T(8,128)} %copy-done.13, f32[2,3,256]{2,1,0:T(4,128)S(1)} %copy-done.83, pred[256,1024]{0,1:T(8,128)(4,1)S(1)} %copy-done.27, bf16[1024,2,64,1]{0,2,3,1:T(8,128)(2,1)S(1)} %bitcast.279, bf16[256,2,3,64]{0,3,2,1:T(8,128)(2,1)S(1)} %bitcast.292), kind=kOutput, calls=%fused_computation.5 | convolution fusion | flops 209189376 | bytes 13316096 | tf_op jit(solution)/shard_map/tkgd,nkd->kgtn/dot_general | solution.py:675
  309.0 4.6 fusion.2
  320.9 7.5 %collective-permute-done.45 = bf16[256,256]{0,1:T(8,128)(2,1)S(1)} collective-permute-done((bf16[256,256]{0,1:T(8,128)(2,1)S(1)}, bf16[256,256]{0,1:T(8,128)(2,1)S(1)}, u32[]{:S(2)}, u32[]{:S(2)}) %collective-permute-start.45) | collective-permute-done | bytes 131104 | tf_op jit(solution)/shard_map/ppermute | solution.py:82
  330.7 3.6 fusion.219
  343.8 4.4 collective-permute-start.52
  356.8 3.6 weight_gradient.5.refs_6_
  363.3 13.5 %ffn_backward.1 = (f32[64,1536]{1,0:T(8,128)S(1)}, bf16[64,1536]{1,0:T(8,128)(2,1)S(1)}, bf16[64,1536]{1,0:T(8,128)(2,1)S(1)}, bf16[64,1536]{1,0:T(8,128)(2,1)S(...) custom-call(s32[1]{0:T(128)} %bitcast.8.core_ref, bf16[64,1536]{1,0:T(8,128)(2,1)S(1)} %multiply_convert_fusion.4.refs_0_, ...), custom_call_target="tpu_custom_call" | custom-call | flops 7046430720 | bytes 19267584 | tf_op jit(solution)/shard_map/ffn_backward/pallas_call | solution.py:274
  381.0 3.0 collective-permute-start.66
  384.1 3.0 collective-permute-start.65
  394.0 9.8 %weight_gradient.6 = bf16[1536,3200]{1,0:T(8,128)(2,1)} custom-call(bf16[256,1536]{1,0:T(8,128)(2,1)S(1)} %pad_maximum_fusion.3.refs_0_, bf16[256,1536]{1,0:T(8,128)(2,1)} %collective-permute-done.64.refs_1_, bf16[256,1536]{1,0:T(8,128)(2,1)S(1)} %constant_dynamic-update-slice_fusion.6.refs_2_, ...), custom_call_target="tpu_custom_call", output_to_operand_aliasing={{}: (6, {})} | custom-call | flops 4227858432 | bytes 8257536 | tf_op jit(solution)/shard_map/weight_gradient/pallas_call | solution.py:343
  416.2 3.0 multiply_reduce_fusion.8
  426.0 5.2 fusion.220
  437.9 5.6 collective-permute-done.70
  454.7 4.3 weight_gradient.7
  459.0 6.6 %all-to-all-start.1 = ((bf16[32,8,1536]{2,1,0:T(8,128)(2,1)}), bf16[32,8,1536]{2,1,0:T(8,128)(2,1)S(1)}, u32[]{:S(2)}, u32[]{:S(2)}) async-start(bf16[32,8,1536]{2,1,0:T(8,128)(2,1)} %bitcast.291), calls=%async_computation.1 | async-start | bytes 1572864 | tf_op jit(solution)/shard_map/all_to_all | solution.py:853
  475.7 18.3 %collective-permute-done.74 = bf16[384,768]{1,0:T(8,128)(2,1)} collective-permute-done((bf16[384,768]{1,0:T(8,128)(2,1)}, bf16[384,768]{1,0:T(8,128)(2,1)}, u32[]{:S(2)}, u32[]{:S(2)}) %collective-permute-start.74) | collective-permute-done | bytes 589856 | tf_op jit(solution)/shard_map/ppermute | solution.py:91
  494.0 19.1 %collective-permute-done.75 = bf16[384,768]{1,0:T(8,128)(2,1)} collective-permute-done((bf16[384,768]{1,0:T(8,128)(2,1)}, bf16[384,768]{1,0:T(8,128)(2,1)}, u32[]{:S(2)}, u32[]{:S(2)}) %collective-permute-start.75) | collective-permute-done | bytes 589856 | tf_op jit(solution)/shard_map/ppermute | solution.py:91
  516.6 8.3 %collective-permute-done.78 = bf16[136,1536]{1,0:T(8,128)(2,1)S(1)} collective-permute-done((bf16[136,1536]{1,0:T(8,128)(2,1)S(1)}, bf16[136,1536]{1,0:T(8,128)(2,1)S(1)}, u32[]{:S(2)}, u32[]{:S(2)}) %collective-permute-start.78) | collective-permute-done | bytes 417824 | tf_op jit(solution)/shard_map/ppermute | solution.py:96
  533.1 3.6 collective-permute-done.81
  543.9 7.6 %collective-permute-done.79 = bf16[136,1536]{1,0:T(8,128)(2,1)S(1)} collective-permute-done((bf16[136,1536]{1,0:T(8,128)(2,1)S(1)}, bf16[136,1536]{1,0:T(8,128)(2,1)S(1)}, u32[]{:S(2)}, u32[]{:S(2)}) %collective-permute-start.79) | collective-permute-done | bytes 417824 | tf_op jit(solution)/shard_map/ppermute | solution.py:96
  551.5 7.6 %collective-permute-done.80 = bf16[136,1536]{1,0:T(8,128)(2,1)S(1)} collective-permute-done((bf16[136,1536]{1,0:T(8,128)(2,1)S(1)}, bf16[136,1536]{1,0:T(8,128)(2,1)S(1)}, u32[]{:S(2)}, u32[]{:S(2)}) %collective-permute-start.80) | collective-permute-done | bytes 417824 | tf_op jit(solution)/shard_map/ppermute | solution.py:96
  (782 shorter events, 244.8 us)
Async XLA Ops:
  7.2 146.5 %all-gather.3.cloned.1.call-start = ((), (), s32[]{:S(2)}) async-start(), calls=%async_computation.4 | async-start | bytes 20275200 | tf_op jit(solution)/shard_map/all_gather | solution.py:500
  10.3 226.9 %all-gather.5.cloned.1.call-start = ((), (), s32[]{:S(2)}) async-start(), calls=%async_computation.5 | async-start | bytes 17031168 | tf_op jit(solution)/shard_map/all_gather | solution.py:501
  18.7 29.7 %all-to-all-start = ((bf16[32,5,1536]{2,1,0:T(8,128)(2,1)}), bf16[32,5,1536]{2,1,0:T(8,128)(2,1)S(1)}, u32[]{:S(2)}, u32[]{:S(2)}) async-start(bf16[32,5,1536]{2,1,0:T(8,128)(2,1)} %pad_maximum_fusion.1), calls=%async_computation | async-start | bytes 1572864 | tf_op jit(solution)/shard_map/all_to_all | solution.py:526
  28.2 424.8 %reduce-scatter.3.cloned.1.call-start = ((), (), s32[]{:S(2)}) async-start(), calls=%async_computation.6 | async-start | bytes 8773632 | tf_op jit(solution)/shard_map/reduce_scatter | solution.py:370
  50.3 26.8 %collective-permute-start = (bf16[128,1536]{1,0:T(8,128)(2,1)S(1)}, bf16[128,1536]{1,0:T(8,128)(2,1)S(1)}, u32[]{:S(2)}, u32[]{:S(2)}) collective-permute-start(bf16[128,1536]{1,0:T(8,128)(2,1)S(1)} %constant_dynamic-update-slice_fusion), channel_id=1, source_target_pairs={{0,1},{1,2},{2,3},{3,0},{4,5},{5,6},{6,7},{7,4},{8,9},{9,10},{10,1... | collective-permute-start | bytes 1179656 | tf_op jit(solution)/shard_map/ppermute | solution.py:96
  51.6 25.6 %collective-permute-start.1 = (bf16[128,1536]{1,0:T(8,128)(2,1)S(1)}, bf16[128,1536]{1,0:T(8,128)(2,1)S(1)}, u32[]{:S(2)}, u32[]{:S(2)}) collective-permute-start(bf16[128,1536]{1,0:T(8,128)(2,1)S(1)} %constant_dynamic-update-slice_fusion), channel_id=1, source_target_pairs={{0,2},{1,3},{2,0},{3,1},{4,6},{5,7},{6,4},{7,5},{8,10},{9,11},{10,... | collective-permute-start | bytes 1179656 | tf_op jit(solution)/shard_map/ppermute | solution.py:96
  54.0 23.1 %collective-permute-start.2 = (bf16[128,1536]{1,0:T(8,128)(2,1)S(1)}, bf16[128,1536]{1,0:T(8,128)(2,1)S(1)}, u32[]{:S(2)}, u32[]{:S(2)}) collective-permute-start(bf16[128,1536]{1,0:T(8,128)(2,1)S(1)} %constant_dynamic-update-slice_fusion), channel_id=1, source_target_pairs={{0,3},{1,0},{2,1},{3,2},{4,7},{5,4},{6,5},{7,6},{8,11},{9,8},{10,9... | collective-permute-start | bytes 1179656 | tf_op jit(solution)/shard_map/ppermute | solution.py:96
  77.2 15.6 %collective-permute-start.10 = (bf16[4,48,768]{2,1,0:T(8,128)(2,1)S(1)}, bf16[4,48,768]{2,1,0:T(8,128)(2,1)S(1)}, u32[]{:S(2)}, u32[]{:S(2)}) collective-permute-start(bf16[4,48,768]{2,1,0:T(8,128)(2,1)S(1)} %bitcast_dynamic-update-slice_fusion.14), channel_id=1, source_target_pairs={{0,8},{8,16},{16,24},{24,0},{1,9},{9,17},{17,25},{25,1},{2,10},{10... | collective-permute-start | bytes 884744 | tf_op jit(solution)/shard_map/ppermute | solution.py:91
  77.5 27.3 %collective-permute-start.12 = (bf16[4,48,768]{2,1,0:T(8,128)(2,1)S(1)}, bf16[4,48,768]{2,1,0:T(8,128)(2,1)S(1)}, u32[]{:S(2)}, u32[]{:S(2)}) collective-permute-start(bf16[4,48,768]{2,1,0:T(8,128)(2,1)S(1)} %bitcast_dynamic-update-slice_fusion.14), channel_id=1, source_target_pairs={{0,16},{8,24},{16,0},{24,8},{1,17},{9,25},{17,1},{25,9},{2,18},{10... | collective-permute-start | bytes 884744 | tf_op jit(solution)/shard_map/ppermute | solution.py:91
  79.8 15.0 %collective-permute-start.11 = (bf16[4,48,768]{2,1,0:T(8,128)(2,1)S(1)}, bf16[4,48,768]{2,1,0:T(8,128)(2,1)S(1)}, u32[]{:S(2)}, u32[]{:S(2)}) collective-permute-start(bf16[4,48,768]{2,1,0:T(8,128)(2,1)S(1)} %bitcast_dynamic-update-slice_fusion.10), channel_id=1, source_target_pairs={{0,32},{32,64},{64,96},{96,0},{1,33},{33,65},{65,97},{97,1},{2,34}... | collective-permute-start | bytes 884744 | tf_op jit(solution)/shard_map/ppermute | solution.py:91
  81.5 26.3 %collective-permute-start.13 = (bf16[4,48,768]{2,1,0:T(8,128)(2,1)S(1)}, bf16[4,48,768]{2,1,0:T(8,128)(2,1)S(1)}, u32[]{:S(2)}, u32[]{:S(2)}) collective-permute-start(bf16[4,48,768]{2,1,0:T(8,128)(2,1)S(1)} %bitcast_dynamic-update-slice_fusion.10), channel_id=1, source_target_pairs={{0,64},{32,96},{64,0},{96,32},{1,65},{33,97},{65,1},{97,33},{2,66}... | collective-permute-start | bytes 884744 | tf_op jit(solution)/shard_map/ppermute | solution.py:91
  82.7 25.1 %collective-permute-start.14 = (bf16[4,48,768]{2,1,0:T(8,128)(2,1)S(1)}, bf16[4,48,768]{2,1,0:T(8,128)(2,1)S(1)}, u32[]{:S(2)}, u32[]{:S(2)}) collective-permute-start(bf16[4,48,768]{2,1,0:T(8,128)(2,1)S(1)} %bitcast_dynamic-update-slice_fusion.14), channel_id=1, source_target_pairs={{0,24},{8,0},{16,8},{24,16},{1,25},{9,1},{17,9},{25,17},{2,26},{10... | collective-permute-start | bytes 884744 | tf_op jit(solution)/shard_map/ppermute | solution.py:91
  92.8 16.0 %collective-permute-start.15 = (bf16[4,48,768]{2,1,0:T(8,128)(2,1)S(1)}, bf16[4,48,768]{2,1,0:T(8,128)(2,1)S(1)}, u32[]{:S(2)}, u32[]{:S(2)}) collective-permute-start(bf16[4,48,768]{2,1,0:T(8,128)(2,1)S(1)} %bitcast_dynamic-update-slice_fusion.10), channel_id=1, source_target_pairs={{0,96},{32,0},{64,32},{96,64},{1,97},{33,1},{65,33},{97,65},{2,98}... | collective-permute-start | bytes 884744 | tf_op jit(solution)/shard_map/ppermute | solution.py:91
  127.2 11.5 %collective-permute-start.18 = (bf16[64,1536]{1,0:T(8,128)(2,1)}, bf16[64,1536]{1,0:T(8,128)(2,1)}, u32[]{:S(2)}, u32[]{:S(2)}) collective-permute-start(bf16[64,1536]{1,0:T(8,128)(2,1)} %get-tuple-element.291), channel_id=1, source_target_pairs={{0,2},{1,3},{2,0},{3,1},{4,6},{5,7},{6,4},{7,5},{8,10},{9,11},{10,... | collective-permute-start | bytes 589832 | tf_op jit(solution)/shard_map/ppermute | solution.py:96
  142.2 11.5 %collective-permute-start.21 = (bf16[64,1536]{1,0:T(8,128)(2,1)S(1)}, bf16[64,1536]{1,0:T(8,128)(2,1)S(1)}, u32[]{:S(2)}, u32[]{:S(2)}) collective-permute-start(bf16[64,1536]{1,0:T(8,128)(2,1)S(1)} %multiply_convert_fusion.4.refs_0_), channel_id=1, source_target_pairs={{0,2},{1,3},{2,0},{3,1},{4,6},{5,7},{6,4},{7,5},{8,10},{9,11},{10,... | collective-permute-start | bytes 589832 | tf_op jit(solution)/shard_map/ppermute | solution.py:96
  165.4 12.2 %collective-permute-start.24 = (bf16[64,1536]{1,0:T(8,128)(2,1)S(1)}, bf16[64,1536]{1,0:T(8,128)(2,1)}, u32[]{:S(2)}, u32[]{:S(2)}) collective-permute-start(bf16[64,1536]{1,0:T(8,128)(2,1)S(1)} %get-tuple-element.95), channel_id=1, source_target_pairs={{0,2},{1,3},{2,0},{3,1},{4,6},{5,7},{6,4},{7,5},{8,10},{9,11},{10,... | collective-permute-start | bytes 589832 | tf_op jit(solution)/shard_map/ppermute | solution.py:96
  179.9 12.2 %collective-permute-start.28 = (bf16[64,1536]{1,0:T(8,128)(2,1)S(1)}, bf16[64,1536]{1,0:T(8,128)(2,1)S(1)}, u32[]{:S(2)}, u32[]{:S(2)}) collective-permute-start(bf16[64,1536]{1,0:T(8,128)(2,1)S(1)} %multiply_convert_fusion.3), channel_id=1, source_target_pairs={{0,3},{1,0},{2,1},{3,2},{4,7},{5,4},{6,5},{7,6},{8,11},{9,8},{10,9... | collective-permute-start | bytes 589832 | tf_op jit(solution)/shard_map/ppermute | solution.py:96
  182.6 15.2 %collective-permute-start.26 = (bf16[64,1536]{1,0:T(8,128)(2,1)S(1)}, bf16[64,1536]{1,0:T(8,128)(2,1)S(1)}, u32[]{:S(2)}, u32[]{:S(2)}) collective-permute-start(bf16[64,1536]{1,0:T(8,128)(2,1)S(1)} %multiply_convert_fusion.3), channel_id=1, source_target_pairs={{0,1},{1,2},{2,3},{3,0},{4,5},{5,6},{6,7},{7,4},{8,9},{9,10},{10,1... | collective-permute-start | bytes 589832 | tf_op jit(solution)/shard_map/ppermute | solution.py:96
  218.4 11.7 %collective-permute-start.33 = (bf16[64,1536]{1,0:T(8,128)(2,1)S(1)}, bf16[64,1536]{1,0:T(8,128)(2,1)S(1)}, u32[]{:S(2)}, u32[]{:S(2)}) collective-permute-start(bf16[64,1536]{1,0:T(8,128)(2,1)S(1)} %get-tuple-element.287), channel_id=1, source_target_pairs={{0,1},{1,2},{2,3},{3,0},{4,5},{5,6},{6,7},{7,4},{8,9},{9,10},{10,1... | collective-permute-start | bytes 589832 | tf_op jit(solution)/shard_map/ppermute | solution.py:96
  218.5 11.6 %collective-permute-start.32 = (bf16[64,1536]{1,0:T(8,128)(2,1)S(1)}, bf16[64,1536]{1,0:T(8,128)(2,1)}, u32[]{:S(2)}, u32[]{:S(2)}) collective-permute-start(bf16[64,1536]{1,0:T(8,128)(2,1)S(1)} %get-tuple-element.288), channel_id=1, source_target_pairs={{0,2},{1,3},{2,0},{3,1},{4,6},{5,7},{6,4},{7,5},{8,10},{9,11},{10,... | collective-permute-start | bytes 589832 | tf_op jit(solution)/shard_map/ppermute | solution.py:96
  234.8 11.1 %collective-permute-start.35 = (bf16[64,1536]{1,0:T(8,128)(2,1)S(1)}, bf16[64,1536]{1,0:T(8,128)(2,1)S(1)}, u32[]{:S(2)}, u32[]{:S(2)}) collective-permute-start(bf16[64,1536]{1,0:T(8,128)(2,1)S(1)} %multiply_convert_fusion.2.refs_0_), channel_id=1, source_target_pairs={{0,2},{1,3},{2,0},{3,1},{4,6},{5,7},{6,4},{7,5},{8,10},{9,11},{10,... | collective-permute-start | bytes 589832 | tf_op jit(solution)/shard_map/ppermute | solution.py:96
  261.7 19.2 %collective-permute-start.43 = (bf16[256,5760]{1,0:T(8,128)(2,1)}, bf16[256,5760]{1,0:T(8,128)(2,1)S(1)}, u32[]{:S(2)}, u32[]{:S(2)}) collective-permute-start(bf16[256,5760]{1,0:T(8,128)(2,1)} %get-tuple-element.101.refs_0_.refs_2_), channel_id=1, source_target_pairs={{0,4},{4,0},{1,5},{5,1},{2,6},{6,2},{3,7},{7,3},{8,12},{12,8},{9,1... | collective-permute-start | bytes 8847368 | tf_op jit(solution)/shard_map/ppermute | solution.py:86
  263.7 11.6 %collective-permute-start.38 = (bf16[64,1536]{1,0:T(8,128)(2,1)S(1)}, bf16[64,1536]{1,0:T(8,128)(2,1)S(1)}, u32[]{:S(2)}, u32[]{:S(2)}) collective-permute-start(bf16[64,1536]{1,0:T(8,128)(2,1)S(1)} %get-tuple-element.99), channel_id=1, source_target_pairs={{0,2},{1,3},{2,0},{3,1},{4,6},{5,7},{6,4},{7,5},{8,10},{9,11},{10,... | collective-permute-start | bytes 589832 | tf_op jit(solution)/shard_map/ppermute | solution.py:96
  276.7 16.4 %collective-permute-start.40 = (bf16[64,1536]{1,0:T(8,128)(2,1)S(1)}, bf16[64,1536]{1,0:T(8,128)(2,1)S(1)}, u32[]{:S(2)}, u32[]{:S(2)}) collective-permute-start(bf16[64,1536]{1,0:T(8,128)(2,1)S(1)} %fusion.190), channel_id=1, source_target_pairs={{0,1},{1,2},{2,3},{3,0},{4,5},{5,6},{6,7},{7,4},{8,9},{9,10},{10,1... | collective-permute-start | bytes 589832 | tf_op jit(solution)/shard_map/ppermute | solution.py:96
  278.0 15.0 %collective-permute-start.41 = (bf16[64,1536]{1,0:T(8,128)(2,1)S(1)}, bf16[64,1536]{1,0:T(8,128)(2,1)S(1)}, u32[]{:S(2)}, u32[]{:S(2)}) collective-permute-start(bf16[64,1536]{1,0:T(8,128)(2,1)S(1)} %fusion.190), channel_id=1, source_target_pairs={{0,2},{1,3},{2,0},{3,1},{4,6},{5,7},{6,4},{7,5},{8,10},{9,11},{10,... | collective-permute-start | bytes 589832 | tf_op jit(solution)/shard_map/ppermute | solution.py:96
  280.9 12.1 %collective-permute-start.42 = (bf16[64,1536]{1,0:T(8,128)(2,1)S(1)}, bf16[64,1536]{1,0:T(8,128)(2,1)S(1)}, u32[]{:S(2)}, u32[]{:S(2)}) collective-permute-start(bf16[64,1536]{1,0:T(8,128)(2,1)S(1)} %fusion.190), channel_id=1, source_target_pairs={{0,3},{1,0},{2,1},{3,2},{4,7},{5,4},{6,5},{7,6},{8,11},{9,8},{10,9... | collective-permute-start | bytes 589832 | tf_op jit(solution)/shard_map/ppermute | solution.py:96
  293.1 266.0 %reduce-scatter.5.cloned.1.call-start = ((), (), s32[]{:S(2)}) async-start(), calls=%async_computation.7 | async-start | bytes 10444800 | tf_op jit(solution)/shard_map/reduce_scatter | solution.py:370
  293.2 100.3 %collective-permute-start.64 = (bf16[256,1536]{1,0:T(8,128)(2,1)S(1)}, bf16[256,1536]{1,0:T(8,128)(2,1)}, u32[]{:S(2)}, u32[]{:S(2)}) collective-permute-start(bf16[256,1536]{1,0:T(8,128)(2,1)S(1)} %pad_maximum_fusion.3.refs_0_), channel_id=1, source_target_pairs={{0,4},{4,0},{1,5},{5,1},{2,6},{6,2},{3,7},{7,3},{8,12},{12,8},{9,1... | collective-permute-start | bytes 2359304 | tf_op jit(solution)/shard_map/ppermute | solution.py:86
  298.7 55.9 %collective-permute-start.53 = (bf16[256,1536]{1,0:T(8,128)(2,1)}, bf16[256,1536]{1,0:T(8,128)(2,1)}, u32[]{:S(2)}, u32[]{:S(2)}) collective-permute-start(bf16[256,1536]{1,0:T(8,128)(2,1)} %constant_dynamic-update-slice_fusion.2), channel_id=1, source_target_pairs={{0,4},{4,0},{1,5},{5,1},{2,6},{6,2},{3,7},{7,3},{8,12},{12,8},{9,1... | collective-permute-start | bytes 2359304 | tf_op jit(solution)/shard_map/ppermute | solution.py:86
  336.7 11.5 %collective-permute-start.47 = (bf16[64,1536]{1,0:T(8,128)(2,1)}, bf16[64,1536]{1,0:T(8,128)(2,1)}, u32[]{:S(2)}, u32[]{:S(2)}) collective-permute-start(bf16[64,1536]{1,0:T(8,128)(2,1)} %get-tuple-element.285), channel_id=1, source_target_pairs={{0,2},{1,3},{2,0},{3,1},{4,6},{5,7},{6,4},{7,5},{8,10},{9,11},{10,... | collective-permute-start | bytes 589832 | tf_op jit(solution)/shard_map/ppermute | solution.py:96
  356.0 20.8 %collective-permute-start.55 = (bf16[64,1536]{1,0:T(8,128)(2,1)S(1)}, bf16[64,1536]{1,0:T(8,128)(2,1)S(1)}, u32[]{:S(2)}, u32[]{:S(2)}) collective-permute-start(bf16[64,1536]{1,0:T(8,128)(2,1)S(1)} %copy-done.12), channel_id=1, source_target_pairs={{0,3},{1,0},{2,1},{3,2},{4,7},{5,4},{6,5},{7,6},{8,11},{9,8},{10,9... | collective-permute-start | bytes 589832 | tf_op jit(solution)/shard_map/ppermute | solution.py:96
  360.4 16.4 %collective-permute-start.56 = (bf16[64,1536]{1,0:T(8,128)(2,1)S(1)}, bf16[64,1536]{1,0:T(8,128)(2,1)S(1)}, u32[]{:S(2)}, u32[]{:S(2)}) collective-permute-start(bf16[64,1536]{1,0:T(8,128)(2,1)S(1)} %copy-done.10), channel_id=1, source_target_pairs={{0,2},{1,3},{2,0},{3,1},{4,6},{5,7},{6,4},{7,5},{8,10},{9,11},{10,... | collective-permute-start | bytes 589832 | tf_op jit(solution)/shard_map/ppermute | solution.py:96
  363.2 13.6 %collective-permute-start.57 = (bf16[64,1536]{1,0:T(8,128)(2,1)S(1)}, bf16[64,1536]{1,0:T(8,128)(2,1)S(1)}, u32[]{:S(2)}, u32[]{:S(2)}) collective-permute-start(bf16[64,1536]{1,0:T(8,128)(2,1)S(1)} %copy-done.8), channel_id=1, source_target_pairs={{0,1},{1,2},{2,3},{3,0},{4,5},{5,6},{6,7},{7,4},{8,9},{9,10},{10,1... | collective-permute-start | bytes 589832 | tf_op jit(solution)/shard_map/ppermute | solution.py:96
  381.0 13.0 %collective-permute-start.66 = (bf16[256,2688]{1,0:T(8,128)(2,1)S(1)}, bf16[256,2688]{1,0:T(8,128)(2,1)S(1)}, u32[]{:S(2)}, u32[]{:S(2)}) collective-permute-start(bf16[256,2688]{1,0:T(8,128)(2,1)S(1)} %get-tuple-element.123), channel_id=1, source_target_pairs={{0,4},{4,0},{1,5},{5,1},{2,6},{6,2},{3,7},{7,3},{8,12},{12,8},{9,1... | collective-permute-start | bytes 4128776 | tf_op jit(solution)/shard_map/ppermute | solution.py:86
  389.7 14.1 %collective-permute-start.61 = (bf16[64,1536]{1,0:T(8,128)(2,1)S(1)}, bf16[64,1536]{1,0:T(8,128)(2,1)S(1)}, u32[]{:S(2)}, u32[]{:S(2)}) collective-permute-start(bf16[64,1536]{1,0:T(8,128)(2,1)S(1)} %get-tuple-element.125), channel_id=1, source_target_pairs={{0,1},{1,2},{2,3},{3,0},{4,5},{5,6},{6,7},{7,4},{8,9},{9,10},{10,1... | collective-permute-start | bytes 589832 | tf_op jit(solution)/shard_map/ppermute | solution.py:96
  391.5 12.4 %collective-permute-start.62 = (bf16[64,1536]{1,0:T(8,128)(2,1)S(1)}, bf16[64,1536]{1,0:T(8,128)(2,1)S(1)}, u32[]{:S(2)}, u32[]{:S(2)}) collective-permute-start(bf16[64,1536]{1,0:T(8,128)(2,1)S(1)} %get-tuple-element.125), channel_id=1, source_target_pairs={{0,2},{1,3},{2,0},{3,1},{4,6},{5,7},{6,4},{7,5},{8,10},{9,11},{10,... | collective-permute-start | bytes 589832 | tf_op jit(solution)/shard_map/ppermute | solution.py:96
  409.4 42.3 %collective-permute-start.71 = (bf16[256,1536]{1,0:T(8,128)(2,1)S(1)}, bf16[256,1536]{1,0:T(8,128)(2,1)S(1)}, u32[]{:S(2)}, u32[]{:S(2)}) collective-permute-start(bf16[256,1536]{1,0:T(8,128)(2,1)S(1)} %multiply_convert_fusion.refs_0_), channel_id=1, source_target_pairs={{0,4},{4,0},{1,5},{5,1},{2,6},{6,2},{3,7},{7,3},{8,12},{12,8},{9,1... | collective-permute-start | bytes 2359304 | tf_op jit(solution)/shard_map/ppermute | solution.py:86
  416.2 35.5 %collective-permute-start.72 = (bf16[256,1536]{1,0:T(8,128)(2,1)}, bf16[256,1536]{1,0:T(8,128)(2,1)}, u32[]{:S(2)}, u32[]{:S(2)}) collective-permute-start(bf16[256,1536]{1,0:T(8,128)(2,1)} %get-tuple-element.370), channel_id=1, source_target_pairs={{0,4},{4,0},{1,5},{5,1},{2,6},{6,2},{3,7},{7,3},{8,12},{12,8},{9,1... | collective-permute-start | bytes 2359304 | tf_op jit(solution)/shard_map/ppermute | solution.py:86
  432.4 11.1 %collective-permute-start.70 = (bf16[64,1536]{1,0:T(8,128)(2,1)S(1)}, bf16[64,1536]{1,0:T(8,128)(2,1)S(1)}, u32[]{:S(2)}, u32[]{:S(2)}) collective-permute-start(bf16[64,1536]{1,0:T(8,128)(2,1)S(1)} %get-tuple-element.279), channel_id=1, source_target_pairs={{0,1},{1,2},{2,3},{3,0},{4,5},{5,6},{6,7},{7,4},{8,9},{9,10},{10,1... | collective-permute-start | bytes 589832 | tf_op jit(solution)/shard_map/ppermute | solution.py:96
  443.5 11.2 %collective-permute-start.73 = (bf16[256,768]{1,0:T(8,128)(2,1)}, bf16[256,768]{1,0:T(8,128)(2,1)}, u32[]{:S(2)}, u32[]{:S(2)}) collective-permute-start(bf16[256,768]{1,0:T(8,128)(2,1)} %get-tuple-element.276), channel_id=1, source_target_pairs={{0,4},{4,0},{1,5},{5,1},{2,6},{6,2},{3,7},{7,3},{8,12},{12,8},{9,1... | collective-permute-start | bytes 1179656 | tf_op jit(solution)/shard_map/ppermute | solution.py:86
  454.7 18.7 %collective-permute-start.77 = (bf16[48,2688]{1,0:T(8,128)(2,1)}, bf16[48,2688]{1,0:T(8,128)(2,1)}, u32[]{:S(2)}, u32[]{:S(2)}) collective-permute-start(bf16[48,2688]{1,0:T(8,128)(2,1)} %constant_dynamic-slice_fusion.6), channel_id=1, source_target_pairs={{0,4},{4,0},{1,5},{5,1},{2,6},{6,2},{3,7},{7,3},{8,12},{12,8},{9,1... | collective-permute-start | bytes 774152 | tf_op jit(solution)/shard_map/ppermute | solution.py:86
  459.0 54.1 %all-to-all-start.1 = ((bf16[32,8,1536]{2,1,0:T(8,128)(2,1)}), bf16[32,8,1536]{2,1,0:T(8,128)(2,1)S(1)}, u32[]{:S(2)}, u32[]{:S(2)}) async-start(bf16[32,8,1536]{2,1,0:T(8,128)(2,1)} %bitcast.291), calls=%async_computation.1 | async-start | bytes 1572864 | tf_op jit(solution)/shard_map/all_to_all | solution.py:853
  468.4 25.5 %collective-permute-start.74 = (bf16[384,768]{1,0:T(8,128)(2,1)}, bf16[384,768]{1,0:T(8,128)(2,1)}, u32[]{:S(2)}, u32[]{:S(2)}) collective-permute-start(bf16[384,768]{1,0:T(8,128)(2,1)} %get-tuple-element.268), channel_id=1, source_target_pairs={{0,32},{32,64},{64,96},{96,0},{1,33},{33,65},{65,97},{97,1},{2,34}... | collective-permute-start | bytes 1769480 | tf_op jit(solution)/shard_map/ppermute | solution.py:91
  469.8 43.2 %collective-permute-start.75 = (bf16[384,768]{1,0:T(8,128)(2,1)}, bf16[384,768]{1,0:T(8,128)(2,1)}, u32[]{:S(2)}, u32[]{:S(2)}) collective-permute-start(bf16[384,768]{1,0:T(8,128)(2,1)} %get-tuple-element.267), channel_id=1, source_target_pairs={{0,64},{32,96},{64,0},{96,32},{1,65},{33,97},{65,1},{97,33},{2,66}... | collective-permute-start | bytes 1769480 | tf_op jit(solution)/shard_map/ppermute | solution.py:91
  472.3 40.8 %collective-permute-start.76 = (bf16[384,768]{1,0:T(8,128)(2,1)}, bf16[384,768]{1,0:T(8,128)(2,1)}, u32[]{:S(2)}, u32[]{:S(2)}) collective-permute-start(bf16[384,768]{1,0:T(8,128)(2,1)} %get-tuple-element.266), channel_id=1, source_target_pairs={{0,96},{32,0},{64,32},{96,64},{1,97},{33,1},{65,33},{97,65},{2,98}... | collective-permute-start | bytes 1769480 | tf_op jit(solution)/shard_map/ppermute | solution.py:91
  513.5 11.5 %collective-permute-start.78 = (bf16[136,1536]{1,0:T(8,128)(2,1)S(1)}, bf16[136,1536]{1,0:T(8,128)(2,1)S(1)}, u32[]{:S(2)}, u32[]{:S(2)}) collective-permute-start(bf16[136,1536]{1,0:T(8,128)(2,1)S(1)} %fusion.34), channel_id=1, source_target_pairs={{0,1},{1,2},{2,3},{3,0},{4,5},{5,6},{6,7},{7,4},{8,9},{9,10},{10,1... | collective-permute-start | bytes 1253384 | tf_op jit(solution)/shard_map/ppermute | solution.py:96
  538.7 12.8 %collective-permute-start.79 = (bf16[136,1536]{1,0:T(8,128)(2,1)S(1)}, bf16[136,1536]{1,0:T(8,128)(2,1)S(1)}, u32[]{:S(2)}, u32[]{:S(2)}) collective-permute-start(bf16[136,1536]{1,0:T(8,128)(2,1)S(1)} %fusion.34), channel_id=1, source_target_pairs={{0,2},{1,3},{2,0},{3,1},{4,6},{5,7},{6,4},{7,5},{8,10},{9,11},{10,... | collective-permute-start | bytes 1253384 | tf_op jit(solution)/shard_map/ppermute | solution.py:96
  539.5 19.7 %collective-permute-start.80 = (bf16[136,1536]{1,0:T(8,128)(2,1)S(1)}, bf16[136,1536]{1,0:T(8,128)(2,1)S(1)}, u32[]{:S(2)}, u32[]{:S(2)}) collective-permute-start(bf16[136,1536]{1,0:T(8,128)(2,1)S(1)} %fusion.34), channel_id=1, source_target_pairs={{0,3},{1,0},{2,1},{3,2},{4,7},{5,4},{6,5},{7,6},{8,11},{9,8},{10,9... | collective-permute-start | bytes 1253384 | tf_op jit(solution)/shard_map/ppermute | solution.py:96
  (211 other events, 2401.5 us)
Sparse Core Ops, SparseCore 0:
  10.9 107.5 all-gather.2
  121.3 69.4 all-gather.4
  293.2 83.8 reduce-scatter.2
  404.1 110.6 reduce-scatter.4

commit v8 on v7

--- a/solution.py
+++ b/solution.py
@@ -84,11 +84,6 @@
 
 def swap_core(block):
     return lax.ppermute(block, "core", [(0, 1), (1, 0)])
-
-
-def shift_ring(block, axis, distance):
-    ring = lax.axis_size(axis)
-    return lax.ppermute(block, axis, [(i, (i + distance) % ring) for i in range(ring)])
 
 
 def shift_tp(block, distance):
@@ -370,62 +365,21 @@
     return lax.psum_scatter(partial, CHIP_AXES, scatter_dimension=0, tiled=True)
 
 
-def along(blocks, axis):
-    ring = lax.axis_size(axis)
-    place = lax.axis_index(axis)
-    return [lax.dynamic_index_in_dim(blocks, place, 0, False)] + [
-        shift_ring(lax.dynamic_index_in_dim(blocks, (place + k) % ring, 0, False), axis, k)
-        for k in range(1, ring)
-    ]
-
-
-def add_parts(parts):
-    total = parts[0].astype(F32)
-    for part in parts[1:]:
-        total = total + part.astype(F32)
-    return total
-
-
-def fill(shape, parts):
-    result = jnp.zeros(shape, BF16)
-    for part, place in parts:
-        result = lax.dynamic_update_slice(result, part, place)
-    return result
-
-
-def gather_first(pack):
-    rows, columns = pack.shape
-    half = columns // 2
-    ring = lax.axis_size("x")
-    x, z = lax.axis_index("x"), lax.axis_index(Z_AXES)
-    low, high = pack[:, :half], pack[:, half:]
-    low_parts = [(shift_ring(low, "x", k)[None] if k else low[None], k) for k in range(ring)]
-    high_parts = [(shift_ring(high, Z_AXES, k)[None] if k else high[None], k) for k in range(ring)]
-    low = fill((ring, rows, half), [(v, ((x - k) % ring, 0, 0)) for v, k in low_parts])
-    high = fill((ring, rows, half), [(v, ((z - k) % ring, 0, 0)) for v, k in high_parts])
-    return low, high
-
-
-def gather_second(low, high):
-    ring, rows, half = low.shape
-    columns = 2 * half
-    x, z, core = lax.axis_index("x"), lax.axis_index(Z_AXES), lax.axis_index("core")
-    parts = []
-    for k in range(ring):
-        part = shift_ring(low, Z_AXES, k) if k else low
-        parts.append((part[:, None], (0, (z - k) % ring, 0, 0)))
-        part = shift_ring(high, "x", k) if k else high
-        parts.append((part[None], ((x - k) % ring, 0, 0, half)))
-    plane = fill((ring, ring, rows, columns), parts)
+def gather_pack(pack):
+    chips = lax.axis_size(CHIP_AXES)
+    core = lax.axis_index("core")
+    plane = lax.all_to_all(
+        jnp.broadcast_to(pack, (chips,) + pack.shape),
+        CHIP_AXES,
+        split_axis=0,
+        concat_axis=0,
+        tiled=True,
+    )
     other = swap_core(plane)
-    both = fill(
-        (ring, ring, CORES, rows, columns),
-        [
-            (plane[:, :, None], (0, 0, core, 0, 0)),
-            (other[:, :, None], (0, 0, 1 - core, 0, 0)),
-        ],
-    )
-    return both.reshape(-1, columns)
+    both = jnp.zeros((chips, CORES) + pack.shape, BF16)
+    both = lax.dynamic_update_slice(both, plane[:, None], (0, core, 0, 0))
+    both = lax.dynamic_update_slice(both, other[:, None], (0, 1 - core, 0, 0))
+    return both.reshape(-1, pack.shape[1])
 
 
 def ffn_gradients(low, high, steps, hidden):
@@ -525,7 +479,9 @@
     )
     arrived = lax.all_to_all(outgoing, TOKEN_AXES, split_axis=0, concat_axis=0, tiled=True)
     arrived, mixer_pack = lax.optimization_barrier((arrived, mixer_pack))
-    mixer_low, mixer_high = gather_first(mixer_pack)
+    mixer_all = gather_pack(mixer_pack)
+    project_a = mixer_all[:, : 3 * channels]
+    output_a_t = mixer_all[:, 3 * channels :]
     gains = (
         arrived[:, 2 * part_rows, : 4 * depth]
         .reshape(shards, 4, depth)
@@ -540,10 +496,6 @@
     stream0 = own_tokens.astype(F32)
     upstream = own_back.astype(F32)
     both = tp_gather(jnp.concatenate([own_tokens, own_back]))
-    both, mixer_low, mixer_high = lax.optimization_barrier((both, mixer_low, mixer_high))
-    mixer_all = gather_second(mixer_low, mixer_high)
-    project_a = mixer_all[:, : 3 * channels]
-    output_a_t = mixer_all[:, 3 * channels :]
     back_s_chunks = [slot[chunk:] for slot in both]
 
     gathered = jnp.arange(row_count)
@@ -849,7 +801,6 @@
     )
     to_leaving = (source[:, None] == jnp.arange(leaving.shape[0])[None, :]).astype(BF16)
     leaving = arrange(to_leaving, leaving)
-    leaving, partial = lax.optimization_barrier((leaving, partial))
     home = lax.all_to_all(
         leaving.reshape(shards, piece_rows, width),
         TOKEN_AXES,
@@ -857,10 +808,8 @@
         concat_axis=0,
         tiled=True,
     )
-    ring = lax.axis_size("x")
-    mixer_parts = along(partial.reshape(ring, -1, mixer_cols), "x")
     second_grads = ffn_gradients(*second_grads, steps, hidden)
-    home, mixer_parts, second_grads = lax.optimization_barrier((home, mixer_parts, second_grads))
+    home, partial, second_grads = lax.optimization_barrier((home, partial, second_grads))
     place = jnp.arange(2 * chunk + 8)
     small_line = (place == 2 * chunk) | (place == 2 * chunk + 1)
     wanted = (
@@ -877,14 +826,23 @@
     rounded = payload.astype(BF16).astype(F32)
     payload = jnp.where((place == 2 * chunk + 1)[:, None], payload - rounded, payload)
     last = tp_gather(payload.astype(BF16))
-    mixer_parts = add_parts(mixer_parts).astype(BF16).reshape(ring, -1, mixer_cols)
-    last[1], mixer_parts = lax.optimization_barrier((last[1], mixer_parts))
-    mixer_parts = along(mixer_parts, Z_AXES)
+    mixer_home = lax.all_to_all(
+        partial.reshape(shards, depth, mixer_cols),
+        TOKEN_AXES,
+        split_axis=0,
+        concat_axis=0,
+        tiled=True,
+    )
     last, first_sums = lax.optimization_barrier((last, first_sums))
     low, high = share_rows(first_sums)
     first_grads = ffn_gradients(low[:, :ffn_cols], high[:, :ffn_cols], steps, hidden)
     attend_grads = jnp.concatenate([low[:, ffn_cols:], high[:, ffn_cols:]], axis=1)
-    mixer_grads = jnp.concatenate(share_rows(add_parts(mixer_parts).astype(BF16)), axis=1)
+    first_grads, attend_grads, mixer_home = lax.optimization_barrier(
+        (first_grads, attend_grads, mixer_home)
+    )
+    mixer_home = mixer_home.reshape(shards // CORES, CORES, depth, mixer_cols)
+    mixer_grads = jnp.sum(mixer_home.astype(F32), axis=0)
+    mixer_grads = jnp.concatenate([mixer_grads[0], mixer_grads[1]], axis=1)
     home_rows = (
         jnp.repeat(jnp.tile(send_piece, members), part_rows) * piece_rows
         + member_of * part_rows

time: 590 us -> 556 us (0.942)
  the two profiles are of different devices: /device:TPU:1 before, /device:TPU:17 now
where the time goes in v8:
time: 556 us; the launch traced here: 546 us
  waiting for transfers between devices  197 us (35%)
  starting transfers between devices  108 us (19%)
  Pallas kernels  66 us (12%)
  local copies, waits for them, and re-layouts  59.3 us (11%)
  other arithmetic  51.4 us (9%)
  matrix products  46.6 us (8%)
  between operations  17.9 us (3%)
    ppermute x48, waiting for transfers between devices, shift_tp(): lax.ppermute(block, 'tp', [(i, (i + distance) % members) for i in range(m...  88.1 us
    ppermute x48, starting transfers between devices, shift_tp(): lax.ppermute(block, 'tp', [(i, (i + distance) % members) for i in range(m...  53.3 us
    all_to_all x1, waiting for transfers between devices, gather_pack(): lax.all_to_all(jnp.broadcast_to(pack, (chips,) + pack.shape), CHIP_AXES,...  37.4 us
    pallas_call x2, Pallas kernels, ffn_backward(): pl.pallas_call(functools.partial(ffn_backward_kernel, count, forward), gr...  28.4 us
    reduce_scatter x2, waiting for transfers between devices, sum_chips(): return lax.psum_scatter(partial, CHIP_AXES, scatter_dimension=0, tiled=True)  27.9 us
    pallas_call x4, Pallas kernels, gradient(): pl.pallas_call(functools.partial(gradient_kernel, edge, cut), grid=(steps...  27.1 us
    ppermute x15, starting transfers between devices, swap_core(): return lax.ppermute(block, 'core', [(0, 1), (1, 0)])  20.1 us
    unnamed x344, local copies, waits for them, and re-layouts  18.8 us
  transfers between devices with their start and end apart: 75, of which 36 were waited for; matrix products, arithmetic and copies ran while one was open for 26% of the time, Pallas kernels for 9%

profile of v8, /device:TPU:17, one launch (start us, length us, event | category | flops | bytes accessed | tf_op | source)
XLA Modules:
  0.0 545.9 jit_solution(84443825488093232)
XLA Ops:
  18.7 8.6 %all-to-all-start = ((bf16[32,5,1536]{2,1,0:T(8,128)(2,1)}), bf16[32,5,1536]{2,1,0:T(8,128)(2,1)S(1)}, u32[]{:S(2)}, u32[]{:S(2)}) async-start(bf16[32,5,1536]{2,1,0:T(8,128)(2,1)} %pad_maximum_fusion.1), calls=%async_computation | async-start | bytes 1572864 | tf_op jit(solution)/shard_map/all_to_all | solution.py:480
  31.5 15.8 %all-to-all-done = bf16[32,5,1536]{2,1,0:T(8,128)(2,1)S(1)} async-done(((bf16[32,5,1536]{2,1,0:T(8,128)(2,1)}), bf16[32,5,1536]{2,1,0:T(8,128)(2,1)S(1)}, u32[]{:S(2)}, u32[]{:S(2)}) %all-to-all-start) | async-done | bytes 491552 | tf_op jit(solution)/shard_map/all_to_all | solution.py:480
  49.0 4.4 all-to-all-start.1
  57.6 2.5 collective-permute-start.1
  61.1 5.2 collective-permute-done.2
  66.4 37.4 %all-to-all-done.1 = bf16[16,48,1536]{2,1,0:T(8,128)(2,1)} async-done(((bf16[16,48,1536]{2,1,0:T(8,128)(2,1)}), bf16[16,48,1536]{2,1,0:T(8,128)(2,1)}, u32[]{:S(2)}, u32[]{:S(2)}) %all-to-all-start.1) | async-done | bytes 2359328 | tf_op jit(solution)/shard_map/all_to_all | solution.py:371
  106.0 3.3 collective-permute-start.3
  116.2 3.0 fusion.209
  125.0 3.4 collective-permute-done.7
  128.5 3.4 collective-permute-done.6
  138.5 3.3 collective-permute-done.8.refs_1_
  141.8 4.5 collective-permute-done.9.refs_2_
  147.6 10.5 %ffn_forward.1 = (f32[64,1536]{1,0:T(8,128)S(1)}, bf16[64,1536]{1,0:T(8,128)(2,1)S(1)}, bf16[64,1536]{1,0:T(8,128)(2,1)S(1)}, bf16[64,1536]{1,0:T(8,128)(2,1)S(1)}) custom-call(bf16[64,1536]{1,0:T(8,128)(2,1)S(1)} %multiply_convert_fusion.4.refs_0_, bf16[64,1536]{1,0:T(8,128)(2,1)S(1)} %collective-permute-done.8.refs_1_, ...), custom_call_target="tpu_custom_call" | custom-call | flops 4227858432 | bytes 16515072 | tf_op jit(solution)/shard_map/ffn_forward/pallas_call | solution.py:179
  163.8 4.7 collective-permute-done.12
  179.1 2.9 collective-permute-done.15
  182.1 5.3 collective-permute-done.14
  187.4 2.5 fusion.19
  190.9 6.8 %collective-permute-done.17 = bf16[256,256]{0,1:T(8,128)(2,1)S(1)} collective-permute-done((bf16[256,256]{0,1:T(8,128)(2,1)S(1)}, bf16[256,256]{0,1:T(8,128)(2,1)S(1)}, u32[]{:S(2)}, u32[]{:S(2)}) %collective-permute-start.17) | collective-permute-done | bytes 131104 | tf_op jit(solution)/shard_map/ppermute | solution.py:82
  204.5 3.1 fusion.210
  210.9 3.0 collective-permute-done.21
  213.8 4.3 collective-permute-done.20
  228.0 4.7 collective-permute-done.23.refs_2_
  234.1 14.9 %ffn_both.1 = (f32[64,1536]{1,0:T(8,128)S(1)}, bf16[64,1536]{1,0:T(8,128)(2,1)S(1)}, bf16[64,1536]{1,0:T(8,128)(2,1)S(1)}, bf16[64,1536]{1,0:T(8,128)(2,1)S(1)},...) custom-call(s32[1]{0:T(128)} %bitcast.8.core_ref, ...), custom_call_target="tpu_custom_call" | custom-call | flops 8455716864 | bytes 22413312 | tf_op jit(solution)/shard_map/ffn_both/pallas_call | solution.py:269
  255.2 2.8 collective-permute-done.27
  258.0 5.1 collective-permute-done.26
  264.7 2.9 collective-permute-start.28
  270.9 10.4 %weight_gradient.4 = bf16[1536,2688]{1,0:T(8,128)(2,1)} custom-call(bf16[256,5760]{1,0:T(8,128)(2,1)S(1)} %copy-done, bf16[256,5760]{1,0:T(8,128)(2,1)} %copy-done.16, bf16[256,5760]{1,0:T(8,128)(2,1)S(1)} %copy-done, bf16[256,5760]{1,0:T(8,128)(2,1)} %copy-done.16, bf16[256,2688]{1,0:T(8,128)(2,1)S(1)} %get-tuple-element.87.refs_4_, ...), custom_call_target="tpu_custom_call" | custom-call | flops 4227858432 | bytes 8257536 | tf_op jit(solution)/shard_map/weight_gradient/pallas_call | solution.py:338
  291.0 7.3 %fusion = (f32[2,3,256]{2,1,0:T(4,128)S(1)}, f32[2,1024,256,3]{2,1,3,0:T(8,128)}) fusion(f32[2,1024,256,3]{2,1,3,0:T(8,128)} %copy-done.15, f32[2,3,256]{2,1,0:T(4,128)S(1)} %copy-done.90, pred[256,1024]{0,1:T(8,128)(4,1)S(1)} %copy-done.29, bf16[1024,2,64,1]{0,2,3,1:T(8,128)(2,1)S(1)} %bitcast.226, bf16[256,2,3,64]{0,3,2,1:T(8,128)(2,1)S(1)} %bitcast.238), kind=kOutput, calls=%fused_computation.5 | convolution fusion | flops 209189376 | bytes 13316096 | tf_op jit(solution)/shard_map/tkgd,nkd->kgtn/dot_general | solution.py:627
  298.4 4.6 fusion.2
  310.0 7.9 %collective-permute-done.33 = bf16[256,256]{0,1:T(8,128)(2,1)S(1)} collective-permute-done((bf16[256,256]{0,1:T(8,128)(2,1)S(1)}, bf16[256,256]{0,1:T(8,128)(2,1)S(1)}, u32[]{:S(2)}, u32[]{:S(2)}) %collective-permute-start.33) | collective-permute-done | bytes 131104 | tf_op jit(solution)/shard_map/ppermute | solution.py:82
  320.1 3.7 fusion.211
  324.8 3.3 collective-permute-start.35
  334.2 3.2 collective-permute-done.35
  347.3 3.6 weight_gradient.5.refs_6_
  353.3 13.4 %ffn_backward.1 = (f32[64,1536]{1,0:T(8,128)S(1)}, bf16[64,1536]{1,0:T(8,128)(2,1)S(1)}, bf16[64,1536]{1,0:T(8,128)(2,1)S(1)}, bf16[64,1536]{1,0:T(8,128)(2,1)S(...) custom-call(s32[1]{0:T(128)} %bitcast.8.core_ref, bf16[64,1536]{1,0:T(8,128)(2,1)S(1)} %multiply_convert_fusion.4.refs_0_, ...), custom_call_target="tpu_custom_call" | custom-call | flops 7046430720 | bytes 19267584 | tf_op jit(solution)/shard_map/ffn_backward/pallas_call | solution.py:269
  370.2 3.0 collective-permute-start.54
  373.3 2.9 collective-permute-start.53
  382.8 9.8 %weight_gradient.6 = bf16[1536,3200]{1,0:T(8,128)(2,1)} custom-call(bf16[256,1536]{1,0:T(8,128)(2,1)S(1)} %pad_maximum_fusion.3.refs_0_, bf16[256,1536]{1,0:T(8,128)(2,1)} %collective-permute-done.52.refs_1_, bf16[256,1536]{1,0:T(8,128)(2,1)S(1)} %constant_dynamic-update-slice_fusion.6.refs_2_, ...), custom_call_target="tpu_custom_call", output_to_operand_aliasing={{}: (6, {})} | custom-call | flops 4227858432 | bytes 8257536 | tf_op jit(solution)/shard_map/weight_gradient/pallas_call | solution.py:338
  395.9 3.4 collective-permute-start.59
  408.7 2.7 collective-permute-done.55
  412.6 5.0 fusion.212
  425.0 4.7 collective-permute-done.57
  439.1 8.9 %all-to-all-start.2 = ((bf16[32,8,1536]{2,1,0:T(8,128)(2,1)}), bf16[32,8,1536]{2,1,0:T(8,128)(2,1)}, u32[]{:S(2)}, u32[]{:S(2)}) async-start(bf16[32,8,1536]{2,1,0:T(8,128)(2,1)} %fusion.16), calls=%async_computation.2 | async-start | bytes 1572864 | tf_op jit(solution)/shard_map/all_to_all | solution.py:804
  451.0 3.3 weight_gradient.7
  455.6 9.7 %all-to-all-done.2 = bf16[32,8,1536]{2,1,0:T(8,128)(2,1)} async-done(((bf16[32,8,1536]{2,1,0:T(8,128)(2,1)}), bf16[32,8,1536]{2,1,0:T(8,128)(2,1)}, u32[]{:S(2)}, u32[]{:S(2)}) %all-to-all-start.2) | async-done | bytes 786464 | tf_op jit(solution)/shard_map/all_to_all | solution.py:804
  470.1 6.1 %all-to-all-start.3 = ((bf16[32,48,768]{2,1,0:T(8,128)(2,1)}), bf16[32,48,768]{2,1,0:T(8,128)(2,1)S(1)}, u32[]{:S(2)}, u32[]{:S(2)}) async-start(bf16[32,48,768]{2,1,0:T(8,128)(2,1)} %bitcast.65), calls=%async_computation.5 | async-start | bytes 4718592 | tf_op jit(solution)/shard_map/all_to_all | solution.py:829
  477.6 8.5 %collective-permute-done.64 = bf16[136,1536]{1,0:T(8,128)(2,1)} collective-permute-done((bf16[136,1536]{1,0:T(8,128)(2,1)S(1)}, bf16[136,1536]{1,0:T(8,128)(2,1)}, u32[]{:S(2)}, u32[]{:S(2)}) %collective-permute-start.64) | collective-permute-done | bytes 417824 | tf_op jit(solution)/shard_map/ppermute | solution.py:91
  488.0 27.9 %reduce-scatter.5.cloned.1.call-done = bf16[96,3200]{1,0:T(8,128)(2,1)} async-done(((bf16[1536,3200]{1,0:T(8,128)(2,1)}), bf16[96,3200]{1,0:T(8,128)(2,1)}) %reduce-scatter.5.cloned.1.call-update) | async-done | bytes 614416 | tf_op jit(solution)/shard_map/reduce_scatter | solution.py:365
  (719 shorter events, 206.5 us)
Async XLA Ops:
  7.2 140.4 %all-gather.3.cloned.1.call-start = ((), (), s32[]{:S(2)}) async-start(), calls=%async_computation.6 | async-start | bytes 20275200 | tf_op jit(solution)/shard_map/all_gather | solution.py:454
  10.3 215.5 %all-gather.5.cloned.1.call-start = ((), (), s32[]{:S(2)}) async-start(), calls=%async_computation.7 | async-start | bytes 17031168 | tf_op jit(solution)/shard_map/all_gather | solution.py:455
  18.7 28.7 %all-to-all-start = ((bf16[32,5,1536]{2,1,0:T(8,128)(2,1)}), bf16[32,5,1536]{2,1,0:T(8,128)(2,1)S(1)}, u32[]{:S(2)}, u32[]{:S(2)}) async-start(bf16[32,5,1536]{2,1,0:T(8,128)(2,1)} %pad_maximum_fusion.1), calls=%async_computation | async-start | bytes 1572864 | tf_op jit(solution)/shard_map/all_to_all | solution.py:480
  49.0 54.7 %all-to-all-start.1 = ((bf16[16,48,1536]{2,1,0:T(8,128)(2,1)}), bf16[16,48,1536]{2,1,0:T(8,128)(2,1)}, u32[]{:S(2)}, u32[]{:S(2)}) async-start(bf16[16,48,1536]{2,1,0:T(8,128)(2,1)} %broadcast_in_dim.100), calls=%async_computation.1 | async-start | bytes 4718592 | tf_op jit(solution)/shard_map/all_to_all | solution.py:371
  53.5 394.6 %reduce-scatter.3.cloned.1.call-start = ((), (), s32[]{:S(2)}) async-start(), calls=%async_computation.8 | async-start | bytes 8773632 | tf_op jit(solution)/shard_map/reduce_scatter | solution.py:365
  55.6 10.8 %collective-permute-start.2 = (bf16[128,1536]{1,0:T(8,128)(2,1)S(1)}, bf16[128,1536]{1,0:T(8,128)(2,1)S(1)}, u32[]{:S(2)}, u32[]{:S(2)}) collective-permute-start(bf16[128,1536]{1,0:T(8,128)(2,1)S(1)} %constant_dynamic-update-slice_fusion), channel_id=1, source_target_pairs={{0,3},{1,0},{2,1},{3,2},{4,7},{5,4},{6,5},{7,6},{8,11},{9,8},{10,9... | collective-permute-start | bytes 1179656 | tf_op jit(solution)/shard_map/ppermute | solution.py:91
  57.6 47.6 %collective-permute-start.1 = (bf16[128,1536]{1,0:T(8,128)(2,1)S(1)}, bf16[128,1536]{1,0:T(8,128)(2,1)S(1)}, u32[]{:S(2)}, u32[]{:S(2)}) collective-permute-start(bf16[128,1536]{1,0:T(8,128)(2,1)S(1)} %constant_dynamic-update-slice_fusion), channel_id=1, source_target_pairs={{0,2},{1,3},{2,0},{3,1},{4,6},{5,7},{6,4},{7,5},{8,10},{9,11},{10,... | collective-permute-start | bytes 1179656 | tf_op jit(solution)/shard_map/ppermute | solution.py:91
  60.1 45.1 %collective-permute-start = (bf16[128,1536]{1,0:T(8,128)(2,1)S(1)}, bf16[128,1536]{1,0:T(8,128)(2,1)S(1)}, u32[]{:S(2)}, u32[]{:S(2)}) collective-permute-start(bf16[128,1536]{1,0:T(8,128)(2,1)S(1)} %constant_dynamic-update-slice_fusion), channel_id=1, source_target_pairs={{0,1},{1,2},{2,3},{3,0},{4,5},{5,6},{6,7},{7,4},{8,9},{9,10},{10,1... | collective-permute-start | bytes 1179656 | tf_op jit(solution)/shard_map/ppermute | solution.py:91
  122.2 9.7 %collective-permute-start.6 = (bf16[64,1536]{1,0:T(8,128)(2,1)}, bf16[64,1536]{1,0:T(8,128)(2,1)}, u32[]{:S(2)}, u32[]{:S(2)}) collective-permute-start(bf16[64,1536]{1,0:T(8,128)(2,1)} %get-tuple-element.269), channel_id=1, source_target_pairs={{0,2},{1,3},{2,0},{3,1},{4,6},{5,7},{6,4},{7,5},{8,10},{9,11},{10,... | collective-permute-start | bytes 589832 | tf_op jit(solution)/shard_map/ppermute | solution.py:91
  122.7 11.4 %collective-permute-start.5 = (bf16[64,1536]{1,0:T(8,128)(2,1)S(1)}, bf16[64,1536]{1,0:T(8,128)(2,1)}, u32[]{:S(2)}, u32[]{:S(2)}) collective-permute-start(bf16[64,1536]{1,0:T(8,128)(2,1)S(1)} %get-tuple-element.267), channel_id=1, source_target_pairs={{0,3},{1,0},{2,1},{3,2},{4,7},{5,4},{6,5},{7,6},{8,11},{9,8},{10,9... | collective-permute-start | bytes 589832 | tf_op jit(solution)/shard_map/ppermute | solution.py:91
  136.6 9.7 %collective-permute-start.9 = (bf16[64,1536]{1,0:T(8,128)(2,1)S(1)}, bf16[64,1536]{1,0:T(8,128)(2,1)S(1)}, u32[]{:S(2)}, u32[]{:S(2)}) collective-permute-start(bf16[64,1536]{1,0:T(8,128)(2,1)S(1)} %multiply_convert_fusion.4.refs_0_), channel_id=1, source_target_pairs={{0,2},{1,3},{2,0},{3,1},{4,6},{5,7},{6,4},{7,5},{8,10},{9,11},{10,... | collective-permute-start | bytes 589832 | tf_op jit(solution)/shard_map/ppermute | solution.py:91
  137.5 10.2 %collective-permute-start.10 = (bf16[64,1536]{1,0:T(8,128)(2,1)S(1)}, bf16[64,1536]{1,0:T(8,128)(2,1)S(1)}, u32[]{:S(2)}, u32[]{:S(2)}) collective-permute-start(bf16[64,1536]{1,0:T(8,128)(2,1)S(1)} %multiply_convert_fusion.4.refs_0_), channel_id=1, source_target_pairs={{0,3},{1,0},{2,1},{3,2},{4,7},{5,4},{6,5},{7,6},{8,11},{9,8},{10,9... | collective-permute-start | bytes 589832 | tf_op jit(solution)/shard_map/ppermute | solution.py:91
  160.2 9.8 %collective-permute-start.11 = (bf16[64,1536]{1,0:T(8,128)(2,1)S(1)}, bf16[64,1536]{1,0:T(8,128)(2,1)}, u32[]{:S(2)}, u32[]{:S(2)}) collective-permute-start(bf16[64,1536]{1,0:T(8,128)(2,1)S(1)} %get-tuple-element.79), channel_id=1, source_target_pairs={{0,3},{1,0},{2,1},{3,2},{4,7},{5,4},{6,5},{7,6},{8,11},{9,8},{10,9... | collective-permute-start | bytes 589832 | tf_op jit(solution)/shard_map/ppermute | solution.py:91
  176.3 11.1 %collective-permute-start.14 = (bf16[64,1536]{1,0:T(8,128)(2,1)S(1)}, bf16[64,1536]{1,0:T(8,128)(2,1)S(1)}, u32[]{:S(2)}, u32[]{:S(2)}) collective-permute-start(bf16[64,1536]{1,0:T(8,128)(2,1)S(1)} %multiply_convert_fusion.3), channel_id=1, source_target_pairs={{0,1},{1,2},{2,3},{3,0},{4,5},{5,6},{6,7},{7,4},{8,9},{9,10},{10,1... | collective-permute-start | bytes 589832 | tf_op jit(solution)/shard_map/ppermute | solution.py:91
  209.1 10.6 %collective-permute-start.19 = (bf16[64,1536]{1,0:T(8,128)(2,1)S(1)}, bf16[64,1536]{1,0:T(8,128)(2,1)}, u32[]{:S(2)}, u32[]{:S(2)}) collective-permute-start(bf16[64,1536]{1,0:T(8,128)(2,1)S(1)} %get-tuple-element.264), channel_id=1, source_target_pairs={{0,3},{1,0},{2,1},{3,2},{4,7},{5,4},{6,5},{7,6},{8,11},{9,8},{10,9... | collective-permute-start | bytes 589832 | tf_op jit(solution)/shard_map/ppermute | solution.py:91
  224.5 9.6 %collective-permute-start.24 = (bf16[64,1536]{1,0:T(8,128)(2,1)S(1)}, bf16[64,1536]{1,0:T(8,128)(2,1)S(1)}, u32[]{:S(2)}, u32[]{:S(2)}) collective-permute-start(bf16[64,1536]{1,0:T(8,128)(2,1)S(1)} %multiply_convert_fusion.2.refs_0_), channel_id=1, source_target_pairs={{0,3},{1,0},{2,1},{3,2},{4,7},{5,4},{6,5},{7,6},{8,11},{9,8},{10,9... | collective-permute-start | bytes 589832 | tf_op jit(solution)/shard_map/ppermute | solution.py:91
  249.8 19.5 %collective-permute-start.31 = (bf16[256,5760]{1,0:T(8,128)(2,1)}, bf16[256,5760]{1,0:T(8,128)(2,1)S(1)}, u32[]{:S(2)}, u32[]{:S(2)}) collective-permute-start(bf16[256,5760]{1,0:T(8,128)(2,1)} %get-tuple-element.86.refs_0_.refs_2_), channel_id=1, source_target_pairs={{0,4},{4,0},{1,5},{5,1},{2,6},{6,2},{3,7},{7,3},{8,12},{12,8},{9,1... | collective-permute-start | bytes 8847368 | tf_op jit(solution)/shard_map/ppermute | solution.py:86
  253.4 9.7 %collective-permute-start.26 = (bf16[64,1536]{1,0:T(8,128)(2,1)S(1)}, bf16[64,1536]{1,0:T(8,128)(2,1)S(1)}, u32[]{:S(2)}, u32[]{:S(2)}) collective-permute-start(bf16[64,1536]{1,0:T(8,128)(2,1)S(1)} %get-tuple-element.84), channel_id=1, source_target_pairs={{0,2},{1,3},{2,0},{3,1},{4,6},{5,7},{6,4},{7,5},{8,10},{9,11},{10,... | collective-permute-start | bytes 589832 | tf_op jit(solution)/shard_map/ppermute | solution.py:91
  253.9 9.8 %collective-permute-start.25 = (bf16[64,1536]{1,0:T(8,128)(2,1)S(1)}, bf16[64,1536]{1,0:T(8,128)(2,1)S(1)}, u32[]{:S(2)}, u32[]{:S(2)}) collective-permute-start(bf16[64,1536]{1,0:T(8,128)(2,1)S(1)} %get-tuple-element.83), channel_id=1, source_target_pairs={{0,3},{1,0},{2,1},{3,2},{4,7},{5,4},{6,5},{7,6},{8,11},{9,8},{10,9... | collective-permute-start | bytes 589832 | tf_op jit(solution)/shard_map/ppermute | solution.py:91
  264.7 16.5 %collective-permute-start.28 = (bf16[64,1536]{1,0:T(8,128)(2,1)S(1)}, bf16[64,1536]{1,0:T(8,128)(2,1)S(1)}, u32[]{:S(2)}, u32[]{:S(2)}) collective-permute-start(bf16[64,1536]{1,0:T(8,128)(2,1)S(1)} %fusion.184), channel_id=1, source_target_pairs={{0,1},{1,2},{2,3},{3,0},{4,5},{5,6},{6,7},{7,4},{8,9},{9,10},{10,1... | collective-permute-start | bytes 589832 | tf_op jit(solution)/shard_map/ppermute | solution.py:91
  267.6 13.7 %collective-permute-start.29 = (bf16[64,1536]{1,0:T(8,128)(2,1)S(1)}, bf16[64,1536]{1,0:T(8,128)(2,1)S(1)}, u32[]{:S(2)}, u32[]{:S(2)}) collective-permute-start(bf16[64,1536]{1,0:T(8,128)(2,1)S(1)} %fusion.184), channel_id=1, source_target_pairs={{0,2},{1,3},{2,0},{3,1},{4,6},{5,7},{6,4},{7,5},{8,10},{9,11},{10,... | collective-permute-start | bytes 589832 | tf_op jit(solution)/shard_map/ppermute | solution.py:91
  267.8 13.5 %collective-permute-start.30 = (bf16[64,1536]{1,0:T(8,128)(2,1)S(1)}, bf16[64,1536]{1,0:T(8,128)(2,1)S(1)}, u32[]{:S(2)}, u32[]{:S(2)}) collective-permute-start(bf16[64,1536]{1,0:T(8,128)(2,1)S(1)} %fusion.184), channel_id=1, source_target_pairs={{0,3},{1,0},{2,1},{3,2},{4,7},{5,4},{6,5},{7,6},{8,11},{9,8},{10,9... | collective-permute-start | bytes 589832 | tf_op jit(solution)/shard_map/ppermute | solution.py:91
  281.3 234.6 %reduce-scatter.5.cloned.1.call-start = ((), (), s32[]{:S(2)}) async-start(), calls=%async_computation.9 | async-start | bytes 10444800 | tf_op jit(solution)/shard_map/reduce_scatter | solution.py:365
  281.5 101.1 %collective-permute-start.52 = (bf16[256,1536]{1,0:T(8,128)(2,1)S(1)}, bf16[256,1536]{1,0:T(8,128)(2,1)}, u32[]{:S(2)}, u32[]{:S(2)}) collective-permute-start(bf16[256,1536]{1,0:T(8,128)(2,1)S(1)} %pad_maximum_fusion.3.refs_0_), channel_id=1, source_target_pairs={{0,4},{4,0},{1,5},{5,1},{2,6},{6,2},{3,7},{7,3},{8,12},{12,8},{9,1... | collective-permute-start | bytes 2359304 | tf_op jit(solution)/shard_map/ppermute | solution.py:86
  288.0 55.4 %collective-permute-start.41 = (bf16[256,1536]{1,0:T(8,128)(2,1)}, bf16[256,1536]{1,0:T(8,128)(2,1)}, u32[]{:S(2)}, u32[]{:S(2)}) collective-permute-start(bf16[256,1536]{1,0:T(8,128)(2,1)} %constant_dynamic-update-slice_fusion.2), channel_id=1, source_target_pairs={{0,4},{4,0},{1,5},{5,1},{2,6},{6,2},{3,7},{7,3},{8,12},{12,8},{9,1... | collective-permute-start | bytes 2359304 | tf_op jit(solution)/shard_map/ppermute | solution.py:86
  324.8 12.7 %collective-permute-start.35 = (bf16[64,1536]{1,0:T(8,128)(2,1)}, bf16[64,1536]{1,0:T(8,128)(2,1)}, u32[]{:S(2)}, u32[]{:S(2)}) collective-permute-start(bf16[64,1536]{1,0:T(8,128)(2,1)} %get-tuple-element.263), channel_id=1, source_target_pairs={{0,2},{1,3},{2,0},{3,1},{4,6},{5,7},{6,4},{7,5},{8,10},{9,11},{10,... | collective-permute-start | bytes 589832 | tf_op jit(solution)/shard_map/ppermute | solution.py:91
  328.1 10.4 %collective-permute-start.34 = (bf16[64,1536]{1,0:T(8,128)(2,1)}, bf16[64,1536]{1,0:T(8,128)(2,1)}, u32[]{:S(2)}, u32[]{:S(2)}) collective-permute-start(bf16[64,1536]{1,0:T(8,128)(2,1)} %get-tuple-element.261), channel_id=1, source_target_pairs={{0,3},{1,0},{2,1},{3,2},{4,7},{5,4},{6,5},{7,6},{8,11},{9,8},{10,9... | collective-permute-start | bytes 589832 | tf_op jit(solution)/shard_map/ppermute | solution.py:91
  333.0 9.7 %collective-permute-start.40 = (bf16[256,1536]{1,0:T(8,128)(2,1)S(1)}, bf16[256,1536]{1,0:T(8,128)(2,1)S(1)}, u32[]{:S(2)}, u32[]{:S(2)}) collective-permute-start(bf16[256,1536]{1,0:T(8,128)(2,1)S(1)} %get-tuple-element.260.refs_0_), channel_id=1, source_target_pairs={{0,4},{4,0},{1,5},{5,1},{2,6},{6,2},{3,7},{7,3},{8,12},{12,8},{9,1... | collective-permute-start | bytes 2359304 | tf_op jit(solution)/shard_map/ppermute | solution.py:86
  341.0 9.9 %collective-permute-start.37 = (bf16[64,1536]{1,0:T(8,128)(2,1)S(1)}, bf16[64,1536]{1,0:T(8,128)(2,1)S(1)}, u32[]{:S(2)}, u32[]{:S(2)}) collective-permute-start(bf16[64,1536]{1,0:T(8,128)(2,1)S(1)} %get-tuple-element.92.refs_4_), channel_id=1, source_target_pairs={{0,1},{1,2},{2,3},{3,0},{4,5},{5,6},{6,7},{7,4},{8,9},{9,10},{10,1... | collective-permute-start | bytes 589832 | tf_op jit(solution)/shard_map/ppermute | solution.py:91
  343.5 9.8 %collective-permute-start.39 = (bf16[64,1536]{1,0:T(8,128)(2,1)S(1)}, bf16[64,1536]{1,0:T(8,128)(2,1)S(1)}, u32[]{:S(2)}, u32[]{:S(2)}) collective-permute-start(bf16[64,1536]{1,0:T(8,128)(2,1)S(1)} %get-tuple-element.92.refs_4_), channel_id=1, source_target_pairs={{0,3},{1,0},{2,1},{3,2},{4,7},{5,4},{6,5},{7,6},{8,11},{9,8},{10,9... | collective-permute-start | bytes 589832 | tf_op jit(solution)/shard_map/ppermute | solution.py:91
  345.3 21.4 %collective-permute-start.43 = (bf16[64,1536]{1,0:T(8,128)(2,1)S(1)}, bf16[64,1536]{1,0:T(8,128)(2,1)S(1)}, u32[]{:S(2)}, u32[]{:S(2)}) collective-permute-start(bf16[64,1536]{1,0:T(8,128)(2,1)S(1)} %copy-done.14), channel_id=1, source_target_pairs={{0,3},{1,0},{2,1},{3,2},{4,7},{5,4},{6,5},{7,6},{8,11},{9,8},{10,9... | collective-permute-start | bytes 589832 | tf_op jit(solution)/shard_map/ppermute | solution.py:91
  350.9 15.8 %collective-permute-start.44 = (bf16[64,1536]{1,0:T(8,128)(2,1)S(1)}, bf16[64,1536]{1,0:T(8,128)(2,1)S(1)}, u32[]{:S(2)}, u32[]{:S(2)}) collective-permute-start(bf16[64,1536]{1,0:T(8,128)(2,1)S(1)} %copy-done.12), channel_id=1, source_target_pairs={{0,2},{1,3},{2,0},{3,1},{4,6},{5,7},{6,4},{7,5},{8,10},{9,11},{10,... | collective-permute-start | bytes 589832 | tf_op jit(solution)/shard_map/ppermute | solution.py:91
  352.1 14.6 %collective-permute-start.45 = (bf16[64,1536]{1,0:T(8,128)(2,1)S(1)}, bf16[64,1536]{1,0:T(8,128)(2,1)S(1)}, u32[]{:S(2)}, u32[]{:S(2)}) collective-permute-start(bf16[64,1536]{1,0:T(8,128)(2,1)S(1)} %copy-done.10), channel_id=1, source_target_pairs={{0,1},{1,2},{2,3},{3,0},{4,5},{5,6},{6,7},{7,4},{8,9},{9,10},{10,1... | collective-permute-start | bytes 589832 | tf_op jit(solution)/shard_map/ppermute | solution.py:91
  369.0 9.5 %collective-permute-start.47 = (bf16[64,1536]{1,0:T(8,128)(2,1)S(1)}, bf16[64,1536]{1,0:T(8,128)(2,1)S(1)}, u32[]{:S(2)}, u32[]{:S(2)}) collective-permute-start(bf16[64,1536]{1,0:T(8,128)(2,1)S(1)} %get-tuple-element.105), channel_id=1, source_target_pairs={{0,2},{1,3},{2,0},{3,1},{4,6},{5,7},{6,4},{7,5},{8,10},{9,11},{10,... | collective-permute-start | bytes 589832 | tf_op jit(solution)/shard_map/ppermute | solution.py:91
  370.2 12.6 %collective-permute-start.54 = (bf16[256,2688]{1,0:T(8,128)(2,1)S(1)}, bf16[256,2688]{1,0:T(8,128)(2,1)S(1)}, u32[]{:S(2)}, u32[]{:S(2)}) collective-permute-start(bf16[256,2688]{1,0:T(8,128)(2,1)S(1)} %get-tuple-element.108), channel_id=1, source_target_pairs={{0,4},{4,0},{1,5},{5,1},{2,6},{6,2},{3,7},{7,3},{8,12},{12,8},{9,1... | collective-permute-start | bytes 4128776 | tf_op jit(solution)/shard_map/ppermute | solution.py:86
  373.3 9.5 %collective-permute-start.53 = (bf16[256,1536]{1,0:T(8,128)(2,1)S(1)}, bf16[256,1536]{1,0:T(8,128)(2,1)S(1)}, u32[]{:S(2)}, u32[]{:S(2)}) collective-permute-start(bf16[256,1536]{1,0:T(8,128)(2,1)S(1)} %constant_dynamic-update-slice_fusion.6.refs_2_), channel_id=1, source_target_pairs={{0,4},{4,0},{1,5},{5,1},{2,6},{6,2},{3,7},{7,3},{8,12},{12,8},{9,1... | collective-permute-start | bytes 2359304 | tf_op jit(solution)/shard_map/ppermute | solution.py:86
  379.6 13.1 %collective-permute-start.49 = (bf16[64,1536]{1,0:T(8,128)(2,1)S(1)}, bf16[64,1536]{1,0:T(8,128)(2,1)S(1)}, u32[]{:S(2)}, u32[]{:S(2)}) collective-permute-start(bf16[64,1536]{1,0:T(8,128)(2,1)S(1)} %get-tuple-element.110), channel_id=1, source_target_pairs={{0,1},{1,2},{2,3},{3,0},{4,5},{5,6},{6,7},{7,4},{8,9},{9,10},{10,1... | collective-permute-start | bytes 589832 | tf_op jit(solution)/shard_map/ppermute | solution.py:91
  381.1 11.6 %collective-permute-start.50 = (bf16[64,1536]{1,0:T(8,128)(2,1)S(1)}, bf16[64,1536]{1,0:T(8,128)(2,1)}, u32[]{:S(2)}, u32[]{:S(2)}) collective-permute-start(bf16[64,1536]{1,0:T(8,128)(2,1)S(1)} %get-tuple-element.110), channel_id=1, source_target_pairs={{0,2},{1,3},{2,0},{3,1},{4,6},{5,7},{6,4},{7,5},{8,10},{9,11},{10,... | collective-permute-start | bytes 589832 | tf_op jit(solution)/shard_map/ppermute | solution.py:91
  382.6 10.1 %collective-permute-start.51 = (bf16[64,1536]{1,0:T(8,128)(2,1)S(1)}, bf16[64,1536]{1,0:T(8,128)(2,1)}, u32[]{:S(2)}, u32[]{:S(2)}) collective-permute-start(bf16[64,1536]{1,0:T(8,128)(2,1)S(1)} %get-tuple-element.110), channel_id=1, source_target_pairs={{0,3},{1,0},{2,1},{3,2},{4,7},{5,4},{6,5},{7,6},{8,11},{9,8},{10,9... | collective-permute-start | bytes 589832 | tf_op jit(solution)/shard_map/ppermute | solution.py:91
  395.9 53.8 %collective-permute-start.59 = (bf16[256,1536]{1,0:T(8,128)(2,1)S(1)}, bf16[256,1536]{1,0:T(8,128)(2,1)S(1)}, u32[]{:S(2)}, u32[]{:S(2)}) collective-permute-start(bf16[256,1536]{1,0:T(8,128)(2,1)S(1)} %multiply_convert_fusion.refs_0_), channel_id=1, source_target_pairs={{0,4},{4,0},{1,5},{5,1},{2,6},{6,2},{3,7},{7,3},{8,12},{12,8},{9,1... | collective-permute-start | bytes 2359304 | tf_op jit(solution)/shard_map/ppermute | solution.py:86
  403.5 46.3 %collective-permute-start.60 = (bf16[256,1536]{1,0:T(8,128)(2,1)}, bf16[256,1536]{1,0:T(8,128)(2,1)}, u32[]{:S(2)}, u32[]{:S(2)}) collective-permute-start(bf16[256,1536]{1,0:T(8,128)(2,1)} %get-tuple-element.341), channel_id=1, source_target_pairs={{0,4},{4,0},{1,5},{5,1},{2,6},{6,2},{3,7},{7,3},{8,12},{12,8},{9,1... | collective-permute-start | bytes 2359304 | tf_op jit(solution)/shard_map/ppermute | solution.py:86
  419.3 10.5 %collective-permute-start.57 = (bf16[64,1536]{1,0:T(8,128)(2,1)S(1)}, bf16[64,1536]{1,0:T(8,128)(2,1)S(1)}, u32[]{:S(2)}, u32[]{:S(2)}) collective-permute-start(bf16[64,1536]{1,0:T(8,128)(2,1)S(1)} %get-tuple-element.258), channel_id=1, source_target_pairs={{0,2},{1,3},{2,0},{3,1},{4,6},{5,7},{6,4},{7,5},{8,10},{9,11},{10,... | collective-permute-start | bytes 589832 | tf_op jit(solution)/shard_map/ppermute | solution.py:91
  425.0 25.9 %collective-permute-start.61 = (bf16[256,768]{1,0:T(8,128)(2,1)}, bf16[256,768]{1,0:T(8,128)(2,1)S(1)}, u32[]{:S(2)}, u32[]{:S(2)}) collective-permute-start(bf16[256,768]{1,0:T(8,128)(2,1)} %get-tuple-element.254), channel_id=1, source_target_pairs={{0,4},{4,0},{1,5},{5,1},{2,6},{6,2},{3,7},{7,3},{8,12},{12,8},{9,1... | collective-permute-start | bytes 1179656 | tf_op jit(solution)/shard_map/ppermute | solution.py:86
  439.1 26.1 %all-to-all-start.2 = ((bf16[32,8,1536]{2,1,0:T(8,128)(2,1)}), bf16[32,8,1536]{2,1,0:T(8,128)(2,1)}, u32[]{:S(2)}, u32[]{:S(2)}) async-start(bf16[32,8,1536]{2,1,0:T(8,128)(2,1)} %fusion.16), calls=%async_computation.2 | async-start | bytes 1572864 | tf_op jit(solution)/shard_map/all_to_all | solution.py:804
  466.7 10.8 %collective-permute-start.63 = (bf16[136,1536]{1,0:T(8,128)(2,1)S(1)}, bf16[136,1536]{1,0:T(8,128)(2,1)}, u32[]{:S(2)}, u32[]{:S(2)}) collective-permute-start(bf16[136,1536]{1,0:T(8,128)(2,1)S(1)} %fusion.35), channel_id=1, source_target_pairs={{0,1},{1,2},{2,3},{3,0},{4,5},{5,6},{6,7},{7,4},{8,9},{9,10},{10,1... | collective-permute-start | bytes 1253384 | tf_op jit(solution)/shard_map/ppermute | solution.py:91
  468.0 18.0 %collective-permute-start.64 = (bf16[136,1536]{1,0:T(8,128)(2,1)S(1)}, bf16[136,1536]{1,0:T(8,128)(2,1)}, u32[]{:S(2)}, u32[]{:S(2)}) collective-permute-start(bf16[136,1536]{1,0:T(8,128)(2,1)S(1)} %fusion.35), channel_id=1, source_target_pairs={{0,2},{1,3},{2,0},{3,1},{4,6},{5,7},{6,4},{7,5},{8,10},{9,11},{10,... | collective-permute-start | bytes 1253384 | tf_op jit(solution)/shard_map/ppermute | solution.py:91
  468.6 19.5 %collective-permute-start.65 = (bf16[136,1536]{1,0:T(8,128)(2,1)S(1)}, bf16[136,1536]{1,0:T(8,128)(2,1)}, u32[]{:S(2)}, u32[]{:S(2)}) collective-permute-start(bf16[136,1536]{1,0:T(8,128)(2,1)S(1)} %fusion.35), channel_id=1, source_target_pairs={{0,3},{1,0},{2,1},{3,2},{4,7},{5,4},{6,5},{7,6},{8,11},{9,8},{10,9... | collective-permute-start | bytes 1253384 | tf_op jit(solution)/shard_map/ppermute | solution.py:91
  470.1 64.5 %all-to-all-start.3 = ((bf16[32,48,768]{2,1,0:T(8,128)(2,1)}), bf16[32,48,768]{2,1,0:T(8,128)(2,1)S(1)}, u32[]{:S(2)}, u32[]{:S(2)}) async-start(bf16[32,48,768]{2,1,0:T(8,128)(2,1)} %bitcast.65), calls=%async_computation.5 | async-start | bytes 4718592 | tf_op jit(solution)/shard_map/all_to_all | solution.py:829
  (191 other events, 2211.9 us)
Sparse Core Ops, SparseCore 0:
  10.9 113.7 all-gather.2
  127.5 71.5 all-gather.4
  281.4 88.8 reduce-scatter.2
  392.9 123.0 reduce-scatter.4

commit v9 on v8

--- a/solution.py
+++ b/solution.py
@@ -350,6 +350,71 @@
         ),
         name="weight_gradient",
     )(*operands)
+
+
+def attend_backward_kernel(scale, groups, *refs):
+    q_ref, do_ref, k_ref, v_ref, log_ref, place_ref, key_ref, dq_ref, dk_ref, dv_ref = refs
+    head = pl.program_id(0)
+    query, d_out, key = q_ref[0], do_ref[0], k_ref[0]
+    scores = times_t(key, query) * scale
+    same = key_ref[:, 0:1] == place_ref[0:1, :]
+    allowed = same & (key_ref[:, 1:2] <= place_ref[1:2, :])
+    probs = jnp.where(allowed, jnp.exp(scores - log_ref[0]), 0.0)
+    d_probs = times_t(v_ref[0], d_out)
+    inner = jnp.sum(probs * d_probs, axis=0, keepdims=True)
+    d_scores = (probs * (d_probs - inner)).astype(BF16)
+    d_value = times(probs.astype(BF16), d_out)
+    d_key = times(d_scores, query) * scale
+    dq_ref[0] = (times_rows(key, d_scores) * scale).T
+
+    @pl.when(head % groups == 0)
+    def _():
+        dk_ref[0] = d_key
+        dv_ref[0] = d_value
+
+    @pl.when(head % groups != 0)
+    def _():
+        dk_ref[0] += d_key
+        dv_ref[0] += d_value
+
+
+def attend_backward(query, d_out, key, value, log_total, place, key_place, scale):
+    heads, rows, size = query.shape
+    kv_heads, keys = key.shape[:2]
+    groups = heads // kv_heads
+
+    def by_head(shape):
+        return pl.BlockSpec((1,) + shape, lambda h: (h, 0, 0))
+
+    def by_group(shape):
+        return pl.BlockSpec((1,) + shape, lambda h: (h // groups, 0, 0))
+
+    return pl.pallas_call(
+        functools.partial(attend_backward_kernel, scale, groups),
+        grid=(heads,),
+        in_specs=[
+            by_head((rows, size)),
+            by_head((rows, size)),
+            by_group((keys, size)),
+            by_group((keys, size)),
+            by_head((1, rows)),
+            whole(place.shape),
+            whole(key_place.shape),
+        ],
+        out_specs=[by_head((rows, size)), by_group((keys, size)), by_group((keys, size))],
+        out_shape=[
+            jax.ShapeDtypeStruct((heads, rows, size), F32),
+            jax.ShapeDtypeStruct((kv_heads, keys, size), F32),
+            jax.ShapeDtypeStruct((kv_heads, keys, size), F32),
+        ],
+        compiler_params=pltpu.CompilerParams(vmem_limit_bytes=VMEM_LIMIT),
+        cost_estimate=pl.CostEstimate(
+            flops=10 * heads * rows * keys * size,
+            bytes_accessed=4 * heads * rows * size * 2 + 12 * kv_heads * keys * size,
+            transcendentals=heads * rows * keys,
+        ),
+        name="attend_backward",
+    )(query, d_out, key, value, log_total, place, key_place)
 
 
 def share_rows(summed):
@@ -619,26 +684,20 @@
     back_b = jnp.concatenate(back_b)
     back_b_other = swap_core(back_b)
     attend_in_other = swap_core(attend_in)
-    d_attended_b = times(back_b, output_b_t).astype(BF16).reshape(row_count, -1, groups, HD)
-    scores_again = (
-        jnp.einsum("tkgd,nkd->kgtn", query_b, key_all, preferred_element_type=F32) * score_scale
-    )
-    probs_again = jnp.where(allowed, jnp.exp(scores_again - log_total), 0.0)
-    d_probs = jnp.einsum("tkgd,nkd->kgtn", d_attended_b, value_all, preferred_element_type=F32)
-    d_values = jnp.einsum(
-        "kgtn,tkgd->nkd", probs_again.astype(BF16), d_attended_b, preferred_element_type=F32
-    )
-    inner_sum = jnp.sum(probs_again * d_probs, axis=-1, keepdims=True)
-    d_scores = (probs_again * (d_probs - inner_sum)).astype(BF16)
-    d_query = (
-        jnp.einsum("kgtn,nkd->tkgd", d_scores, key_all, preferred_element_type=F32) * score_scale
-    )
-    d_keys = (
-        jnp.einsum("kgtn,tkgd->nkd", d_scores, query_b, preferred_element_type=F32) * score_scale
-    )
-    d_key_value = jnp.concatenate(
-        [d_keys.reshape(-1, kv_heads * HD), d_values.reshape(-1, kv_heads * HD)], axis=1
-    )
+    d_attended_b = times(back_b, output_b_t).astype(BF16).reshape(row_count, -1, HD)
+    d_query, d_keys, d_values = attend_backward(
+        query_b.reshape(row_count, -1, HD).transpose(1, 0, 2),
+        d_attended_b.transpose(1, 0, 2),
+        key_all.transpose(1, 0, 2),
+        value_all.transpose(1, 0, 2),
+        log_total.reshape(-1, 1, row_count),
+        jnp.stack([segment, places]),
+        jnp.stack([key_segment, key_places], axis=1),
+        score_scale,
+    )
+    d_query = d_query.transpose(1, 0, 2).reshape(row_count, kv_heads, groups, HD)
+    d_key_value = jnp.concatenate([d_keys, d_values]).transpose(1, 0, 2)
+    d_key_value = d_key_value.reshape(-1, 2 * kv_heads * HD)
     d_slots = d_key_value.reshape(contexts, row_count, -1)
     d_others = jnp.concatenate([d_slots[1], d_slots[3]]).astype(BF16)
     d_others = swap_core(d_others).astype(F32)
@@ -683,18 +742,21 @@
     back_f = tp_gather(d_stream2.astype(BF16))
     back_f, third = lax.optimization_barrier((back_f, third))
     left_x, left_b = jnp.concatenate(normed_f), jnp.concatenate(back_f)
-    ffn_lefts = [(left_x, 0), (swap_core(left_x), 0), (left_b, 0), (swap_core(left_b), 0)]
+    left_others = [swap_core(left_x), swap_core(left_b)]
     d_chunks, unused, keep, side = ffn_backward(
         core_ref, normed_f, back_f, first_all, steps, False
     )
-    d_chunks, out_others = lax.optimization_barrier((d_chunks, out_others))
+    d_chunks, out_others, left_others, side_other = lax.optimization_barrier(
+        (d_chunks, out_others, left_others, swap_core(side))
+    )
+    ffn_lefts = [(left_x, 0), (left_others[0], 0), (left_b, 0), (left_others[1], 0)]
     stream4 = stream3 + out_chunks[0]
     for part in out_others:
         stream4 = stream4 + part.astype(F32)
     partial = gradient(
         ffn_lefts,
         keep,
-        swap_core(side),
+        side_other,
         0,
         block,
         steps,
@@ -705,12 +767,12 @@
         third,
     )
 
+    d_normed, partial = lax.optimization_barrier((tp_reduce(d_chunks), partial))
     unused, pullback = jax.vjp(norm_rows, stream1, gain_f)
-    d_stream, gain_f_grad = pullback(tp_reduce(d_chunks))
+    d_stream, gain_f_grad = pullback(d_normed)
     d_stream1 = d_stream2 + d_stream
 
     back_a = tp_gather(d_stream1.astype(BF16))
-    back_a, partial = lax.optimization_barrier((back_a, partial))
     first_sums = sum_chips(partial)
     back_a = arrange(to_dealt, jnp.concatenate(back_a))
     back_a_other = swap_core(back_a)
@@ -833,13 +895,6 @@
         concat_axis=0,
         tiled=True,
     )
-    last, first_sums = lax.optimization_barrier((last, first_sums))
-    low, high = share_rows(first_sums)
-    first_grads = ffn_gradients(low[:, :ffn_cols], high[:, :ffn_cols], steps, hidden)
-    attend_grads = jnp.concatenate([low[:, ffn_cols:], high[:, ffn_cols:]], axis=1)
-    first_grads, attend_grads, mixer_home = lax.optimization_barrier(
-        (first_grads, attend_grads, mixer_home)
-    )
     mixer_home = mixer_home.reshape(shards // CORES, CORES, depth, mixer_cols)
     mixer_grads = jnp.sum(mixer_home.astype(F32), axis=0)
     mixer_grads = jnp.concatenate([mixer_grads[0], mixer_grads[1]], axis=1)
@@ -851,6 +906,12 @@
     to_arrival = (home_rows[None, :] == gathered[:, None]).astype(BF16)
     input_gradient = arrange(to_arrival, jnp.concatenate([slot[:chunk] for slot in last]))
     layer_out = arrange(to_arrival, jnp.concatenate([slot[chunk : 2 * chunk] for slot in last]))
+    first_sums, layer_out, input_gradient, mixer_grads = lax.optimization_barrier(
+        (first_sums, layer_out, input_gradient, mixer_grads)
+    )
+    low, high = share_rows(first_sums)
+    first_grads = ffn_gradients(low[:, :ffn_cols], high[:, :ffn_cols], steps, hidden)
+    attend_grads = jnp.concatenate([low[:, ffn_cols:], high[:, ffn_cols:]], axis=1)
     smalls = [
         slot[2 * chunk].astype(F32) + slot[2 * chunk + 1].astype(F32) for slot in last
     ]

time: 556 us -> 581 us (1.045)
  the two profiles are of different devices: /device:TPU:17 before, /device:TPU:1 now
where the time goes in v9:
time: 581 us; the launch traced here: 570 us
  waiting for transfers between devices  209 us (36%)
  starting transfers between devices  97.1 us (17%)
  local copies, waits for them, and re-layouts  84.8 us (15%)
  Pallas kernels  74.7 us (13%)
  other arithmetic  52 us (9%)
  matrix products  35.5 us (6%)
  between operations  17.6 us (3%)
    ppermute x48, waiting for transfers between devices, shift_tp(): lax.ppermute(block, 'tp', [(i, (i + distance) % members) for i in range(m...  126 us
    ppermute x48, starting transfers between devices, shift_tp(): lax.ppermute(block, 'tp', [(i, (i + distance) % members) for i in range(m...  52 us
    unnamed x374, local copies, waits for them, and re-layouts  35.2 us
    all_to_all x1, waiting for transfers between devices, gather_pack(): lax.all_to_all(jnp.broadcast_to(pack, (chips,) + pack.shape), CHIP_AXES,...  29.7 us
    pallas_call x2, Pallas kernels, ffn_backward(): pl.pallas_call(functools.partial(ffn_backward_kernel, count, forward), gr...  29.1 us
    pallas_call x4, Pallas kernels, gradient(): pl.pallas_call(functools.partial(gradient_kernel, edge, cut), grid=(steps...  27.3 us
    dot_general x10, matrix products, times(): lax.dot_general(left, right, (((1,), (0,)), ((), ())), preferred_element_...  18.6 us
    all_to_all x1, waiting for transfers between devices, body(): lax.all_to_all(outgoing, TOKEN_AXES, split_axis=0, concat_axis=0, tiled=T...  16.5 us
  transfers between devices with their start and end apart: 75, of which 39 were waited for; matrix products, arithmetic and copies ran while one was open for 24% of the time, Pallas kernels for 10%

profile of v9, /device:TPU:1, one launch (start us, length us, event | category | flops | bytes accessed | tf_op | source)
XLA Modules:
  0.0 570.5 jit_solution(756464834041323273)
XLA Ops:
  18.7 9.4 %all-to-all-start = ((bf16[32,5,1536]{2,1,0:T(8,128)(2,1)}), bf16[32,5,1536]{2,1,0:T(8,128)(2,1)S(1)}, u32[]{:S(2)}, u32[]{:S(2)}) async-start(bf16[32,5,1536]{2,1,0:T(8,128)(2,1)} %pad_maximum_fusion), calls=%async_computation | async-start | bytes 1572864 | tf_op jit(solution)/shard_map/all_to_all | solution.py:545
  31.9 16.5 %all-to-all-done = bf16[32,5,1536]{2,1,0:T(8,128)(2,1)S(1)} async-done(((bf16[32,5,1536]{2,1,0:T(8,128)(2,1)}), bf16[32,5,1536]{2,1,0:T(8,128)(2,1)S(1)}, u32[]{:S(2)}, u32[]{:S(2)}) %all-to-all-start) | async-done | bytes 491552 | tf_op jit(solution)/shard_map/all_to_all | solution.py:545
  50.1 4.4 all-to-all-start.1
  56.2 2.6 collective-permute-start.2
  62.6 12.9 %collective-permute-done.2 = bf16[128,1536]{1,0:T(8,128)(2,1)S(1)} collective-permute-done((bf16[128,1536]{1,0:T(8,128)(2,1)S(1)}, bf16[128,1536]{1,0:T(8,128)(2,1)S(1)}, u32[]{:S(2)}, u32[]{:S(2)}) %collective-permute-start.2) | collective-permute-done | bytes 393248 | tf_op jit(solution)/shard_map/ppermute | solution.py:91
  75.6 29.7 %all-to-all-done.1 = bf16[16,48,1536]{2,1,0:T(8,128)(2,1)} async-done(((bf16[16,48,1536]{2,1,0:T(8,128)(2,1)}), bf16[16,48,1536]{2,1,0:T(8,128)(2,1)}, u32[]{:S(2)}, u32[]{:S(2)}) %all-to-all-start.1) | async-done | bytes 2359328 | tf_op jit(solution)/shard_map/all_to_all | solution.py:436
  108.2 3.4 collective-permute-start.3
  118.6 3.2 fusion.206
  121.9 2.5 collective-permute-start.5
  125.7 7.4 %collective-permute-done.5 = bf16[64,1536]{1,0:T(8,128)(2,1)S(1)} collective-permute-done((bf16[64,1536]{1,0:T(8,128)(2,1)S(1)}, bf16[64,1536]{1,0:T(8,128)(2,1)S(1)}, u32[]{:S(2)}, u32[]{:S(2)}) %collective-permute-start.5) | collective-permute-done | bytes 196640 | tf_op jit(solution)/shard_map/ppermute | solution.py:91
  133.2 3.9 collective-permute-done.7
  141.0 3.7 collective-permute-done.10.refs_3_
  149.0 10.5 %ffn_forward.1 = (f32[64,1536]{1,0:T(8,128)S(1)}, bf16[64,1536]{1,0:T(8,128)(2,1)S(1)}, bf16[64,1536]{1,0:T(8,128)(2,1)S(1)}, bf16[64,1536]{1,0:T(8,128)(2,1)S(1)}) custom-call(bf16[64,1536]{1,0:T(8,128)(2,1)S(1)} %multiply_convert_fusion.4.refs_0_, bf16[64,1536]{1,0:T(8,128)(2,1)S(1)} %collective-permute-done.8.refs_1_, ...), custom_call_target="tpu_custom_call" | custom-call | flops 4227858432 | bytes 16515072 | tf_op jit(solution)/shard_map/ffn_forward/pallas_call | solution.py:179
  168.4 6.1 %collective-permute-done.13 = bf16[64,1536]{1,0:T(8,128)(2,1)} collective-permute-done((bf16[64,1536]{1,0:T(8,128)(2,1)S(1)}, bf16[64,1536]{1,0:T(8,128)(2,1)}, u32[]{:S(2)}, u32[]{:S(2)}) %collective-permute-start.13) | collective-permute-done | bytes 196640 | tf_op jit(solution)/shard_map/ppermute | solution.py:91
  179.6 8.2 %collective-permute-done.14 = bf16[64,1536]{1,0:T(8,128)(2,1)S(1)} collective-permute-done((bf16[64,1536]{1,0:T(8,128)(2,1)S(1)}, bf16[64,1536]{1,0:T(8,128)(2,1)S(1)}, u32[]{:S(2)}, u32[]{:S(2)}) %collective-permute-start.14) | collective-permute-done | bytes 196640 | tf_op jit(solution)/shard_map/ppermute | solution.py:91
  187.8 2.7 fusion.10
  192.7 5.7 %collective-permute-done.17 = bf16[256,256]{0,1:T(8,128)(2,1)S(1)} collective-permute-done((bf16[256,256]{0,1:T(8,128)(2,1)S(1)}, bf16[256,256]{0,1:T(8,128)(2,1)S(1)}, u32[]{:S(2)}, u32[]{:S(2)}) %collective-permute-start.17) | collective-permute-done | bytes 131104 | tf_op jit(solution)/shard_map/ppermute | solution.py:82
  205.6 3.1 fusion.207
  208.8 2.5 collective-permute-start.19
  212.7 6.6 %collective-permute-done.19 = bf16[64,1536]{1,0:T(8,128)(2,1)S(1)} collective-permute-done((bf16[64,1536]{1,0:T(8,128)(2,1)S(1)}, bf16[64,1536]{1,0:T(8,128)(2,1)S(1)}, u32[]{:S(2)}, u32[]{:S(2)}) %collective-permute-start.19) | collective-permute-done | bytes 196640 | tf_op jit(solution)/shard_map/ppermute | solution.py:91
  219.3 4.7 collective-permute-done.21
  228.9 8.4 %collective-permute-done.22.refs_1_ = bf16[64,1536]{1,0:T(8,128)(2,1)S(1)} collective-permute-done((bf16[64,1536]{1,0:T(8,128)(2,1)S(1)}, bf16[64,1536]{1,0:T(8,128)(2,1)S(1)}, u32[]{:S(2)}, u32[]{:S(2)}) %collective-permute-start.22) | collective-permute-done | bytes 196640 | tf_op jit(solution)/shard_map/ppermute | solution.py:91
  244.9 14.9 %ffn_both.1 = (f32[64,1536]{1,0:T(8,128)S(1)}, bf16[64,1536]{1,0:T(8,128)(2,1)S(1)}, bf16[64,1536]{1,0:T(8,128)(2,1)S(1)}, bf16[64,1536]{1,0:T(8,128)(2,1)S(1)},...) custom-call(s32[1]{0:T(128)} %bitcast.core_ref, ...), custom_call_target="tpu_custom_call" | custom-call | flops 8455716864 | bytes 22413312 | tf_op jit(solution)/shard_map/ffn_both/pallas_call | solution.py:269
  265.5 4.6 collective-permute-done.25
  270.1 2.5 collective-permute-done.26
  272.7 4.2 collective-permute-done.27
  282.4 10.4 %weight_gradient.4 = bf16[1536,2688]{1,0:T(8,128)(2,1)} custom-call(bf16[256,5760]{1,0:T(8,128)(2,1)S(1)} %copy-done, bf16[256,5760]{1,0:T(8,128)(2,1)} %copy-done.29, bf16[256,5760]{1,0:T(8,128)(2,1)S(1)} %copy-done, bf16[256,5760]{1,0:T(8,128)(2,1)} %copy-done.29, bf16[256,2688]{1,0:T(8,128)(2,1)S(1)} %get-tuple-element.85.refs_4_, ...), custom_call_target="tpu_custom_call" | custom-call | flops 4227858432 | bytes 8257536 | tf_op jit(solution)/shard_map/weight_gradient/pallas_call | solution.py:338
  312.8 7.8 %attend_backward.1 = (f32[6,256,64]{2,1,0:T(8,128)S(1)}, f32[2,1024,64]{2,1,0:T(8,128)S(1)}, f32[2,1024,64]{2,1,0:T(8,128)S(1)}) custom-call(bf16[6,256,64]{2,1,0:T(8,128)(2,1)S(1)} %copy-done.16, bf16[6,256,64]{2,1,0:T(8,128)(2,1)S(1)} %bitcast.180, bf16[2,1024,64]{2,1,0:T(8,128)(2,1)S(1)} %bitcast.178, bf16[2,1024,64]{2,1,0:T(8,128)(2,1)S(1)} %bitcast.179, ...), custom_call_target="tpu_custom_call" | custom-call | flops 1006632960 | bytes 2359296 | tf_op jit(solution)/shard_map/attend_backward/pallas_call | solution.py:392
  344.3 7.5 %collective-permute-done.33 = bf16[256,256]{0,1:T(8,128)(2,1)S(1)} collective-permute-done((bf16[256,256]{0,1:T(8,128)(2,1)S(1)}, bf16[256,256]{0,1:T(8,128)(2,1)S(1)}, u32[]{:S(2)}, u32[]{:S(2)}) %collective-permute-start.33) | collective-permute-done | bytes 131104 | tf_op jit(solution)/shard_map/ppermute | solution.py:82
  366.3 2.8 collective-permute-done.36
  375.4 3.6 weight_gradient.5.refs_6_
  382.3 14.2 %ffn_backward.1 = (f32[64,1536]{1,0:T(8,128)S(1)}, bf16[64,1536]{1,0:T(8,128)(2,1)}, bf16[64,1536]{1,0:T(8,128)(2,1)}, bf16[64,1536]{1,0:T(8,128)(2,1)}, bf16[25...) custom-call(s32[1]{0:T(128)} %bitcast.core_ref, bf16[64,1536]{1,0:T(8,128)(2,1)S(1)} %multiply_convert_fusion.4.refs_0_, ...), custom_call_target="tpu_custom_call" | custom-call | flops 7046430720 | bytes 19267584 | tf_op jit(solution)/shard_map/ffn_backward/pallas_call | solution.py:269
  398.2 2.6 collective-permute-start.43
  401.5 7.3 %collective-permute-done.43 = bf16[64,1536]{1,0:T(8,128)(2,1)S(1)} collective-permute-done((bf16[64,1536]{1,0:T(8,128)(2,1)S(1)}, bf16[64,1536]{1,0:T(8,128)(2,1)S(1)}, u32[]{:S(2)}, u32[]{:S(2)}) %collective-permute-start.43) | collective-permute-done | bytes 196640 | tf_op jit(solution)/shard_map/ppermute | solution.py:91
  408.8 4.5 collective-permute-done.45
  414.9 10.0 %weight_gradient.6 = bf16[1536,3200]{1,0:T(8,128)(2,1)} custom-call(bf16[256,1536]{1,0:T(8,128)(2,1)} %pad_maximum_fusion.2.refs_0_, bf16[256,1536]{1,0:T(8,128)(2,1)} %collective-permute-done.46.refs_1_, bf16[256,1536]{1,0:T(8,128)(2,1)S(1)} %constant_dynamic-update-slice_fusion.6.refs_2_, ...), custom_call_target="tpu_custom_call", output_to_operand_aliasing={{}: (6, {})} | custom-call | flops 4227858432 | bytes 8257536 | tf_op jit(solution)/shard_map/weight_gradient/pallas_call | solution.py:338
  443.4 4.9 collective-permute-done.53
  457.0 2.5 collective-permute-done.55
  460.8 5.2 fusion.209
  467.2 2.5 collective-permute-start.56
  477.9 2.8 collective-permute-done.58
  488.9 6.5 %all-to-all-start.2 = ((bf16[32,8,1536]{2,1,0:T(8,128)(2,1)}), bf16[32,8,1536]{2,1,0:T(8,128)(2,1)}, u32[]{:S(2)}, u32[]{:S(2)}) async-start(bf16[32,8,1536]{2,1,0:T(8,128)(2,1)} %fusion.7), calls=%async_computation.3 | async-start | bytes 1572864 | tf_op jit(solution)/shard_map/all_to_all | solution.py:866
  498.1 3.3 weight_gradient.7
  502.7 11.1 %all-to-all-done.2 = bf16[32,8,1536]{2,1,0:T(8,128)(2,1)} async-done(((bf16[32,8,1536]{2,1,0:T(8,128)(2,1)}), bf16[32,8,1536]{2,1,0:T(8,128)(2,1)}, u32[]{:S(2)}, u32[]{:S(2)}) %all-to-all-start.2) | async-done | bytes 786464 | tf_op jit(solution)/shard_map/all_to_all | solution.py:866
  516.0 2.7 collective-permute-start.65
  518.7 5.7 all-to-all-start.3
  526.8 10.6 %collective-permute-done.63 = bf16[136,1536]{1,0:T(8,128)(2,1)} collective-permute-done((bf16[136,1536]{1,0:T(8,128)(2,1)}, bf16[136,1536]{1,0:T(8,128)(2,1)}, u32[]{:S(2)}, u32[]{:S(2)}) %collective-permute-start.63) | collective-permute-done | bytes 417824 | tf_op jit(solution)/shard_map/ppermute | solution.py:91
  546.4 9.0 %all-to-all-done.3 = bf16[32,48,768]{2,1,0:T(8,128)(2,1)S(1)} async-done(((bf16[32,48,768]{2,1,0:T(8,128)(2,1)}), bf16[32,48,768]{2,1,0:T(8,128)(2,1)S(1)}, u32[]{:S(2)}, u32[]{:S(2)}) %all-to-all-start.3) | async-done | bytes 2359328 | tf_op jit(solution)/shard_map/all_to_all | solution.py:891
  (764 shorter events, 230.7 us)
Async XLA Ops:
  7.2 141.7 %all-gather.3.cloned.1.call-start = ((), (), s32[]{:S(2)}) async-start(), calls=%async_computation.6 | async-start | bytes 20275200 | tf_op jit(solution)/shard_map/all_gather | solution.py:519
  10.3 218.7 %all-gather.5.cloned.1.call-start = ((), (), s32[]{:S(2)}) async-start(), calls=%async_computation.7 | async-start | bytes 17031168 | tf_op jit(solution)/shard_map/all_gather | solution.py:520
  18.7 29.6 %all-to-all-start = ((bf16[32,5,1536]{2,1,0:T(8,128)(2,1)}), bf16[32,5,1536]{2,1,0:T(8,128)(2,1)S(1)}, u32[]{:S(2)}, u32[]{:S(2)}) async-start(bf16[32,5,1536]{2,1,0:T(8,128)(2,1)} %pad_maximum_fusion), calls=%async_computation | async-start | bytes 1572864 | tf_op jit(solution)/shard_map/all_to_all | solution.py:545
  50.1 55.2 %all-to-all-start.1 = ((bf16[16,48,1536]{2,1,0:T(8,128)(2,1)}), bf16[16,48,1536]{2,1,0:T(8,128)(2,1)}, u32[]{:S(2)}, u32[]{:S(2)}) async-start(bf16[16,48,1536]{2,1,0:T(8,128)(2,1)} %broadcast_in_dim.89), calls=%async_computation.1 | async-start | bytes 4718592 | tf_op jit(solution)/shard_map/all_to_all | solution.py:436
  54.5 441.0 %reduce-scatter.5.cloned.1.call-start = ((), (), s32[]{:S(2)}) async-start(), calls=%async_computation.9 | async-start | bytes 8773632 | tf_op jit(solution)/shard_map/reduce_scatter | solution.py:430
  56.2 19.3 %collective-permute-start.2 = (bf16[128,1536]{1,0:T(8,128)(2,1)S(1)}, bf16[128,1536]{1,0:T(8,128)(2,1)S(1)}, u32[]{:S(2)}, u32[]{:S(2)}) collective-permute-start(bf16[128,1536]{1,0:T(8,128)(2,1)S(1)} %constant_dynamic-update-slice_fusion), channel_id=1, source_target_pairs={{0,3},{1,0},{2,1},{3,2},{4,7},{5,4},{6,5},{7,6},{8,11},{9,8},{10,9... | collective-permute-start | bytes 1179656 | tf_op jit(solution)/shard_map/ppermute | solution.py:91
  60.4 45.7 %collective-permute-start.1 = (bf16[128,1536]{1,0:T(8,128)(2,1)S(1)}, bf16[128,1536]{1,0:T(8,128)(2,1)S(1)}, u32[]{:S(2)}, u32[]{:S(2)}) collective-permute-start(bf16[128,1536]{1,0:T(8,128)(2,1)S(1)} %constant_dynamic-update-slice_fusion), channel_id=1, source_target_pairs={{0,2},{1,3},{2,0},{3,1},{4,6},{5,7},{6,4},{7,5},{8,10},{9,11},{10,... | collective-permute-start | bytes 1179656 | tf_op jit(solution)/shard_map/ppermute | solution.py:91
  60.9 45.9 %collective-permute-start = (bf16[128,1536]{1,0:T(8,128)(2,1)S(1)}, bf16[128,1536]{1,0:T(8,128)(2,1)S(1)}, u32[]{:S(2)}, u32[]{:S(2)}) collective-permute-start(bf16[128,1536]{1,0:T(8,128)(2,1)S(1)} %constant_dynamic-update-slice_fusion), channel_id=1, source_target_pairs={{0,1},{1,2},{2,3},{3,0},{4,5},{5,6},{6,7},{7,4},{8,9},{9,10},{10,1... | collective-permute-start | bytes 1179656 | tf_op jit(solution)/shard_map/ppermute | solution.py:91
  121.9 11.2 %collective-permute-start.5 = (bf16[64,1536]{1,0:T(8,128)(2,1)S(1)}, bf16[64,1536]{1,0:T(8,128)(2,1)S(1)}, u32[]{:S(2)}, u32[]{:S(2)}) collective-permute-start(bf16[64,1536]{1,0:T(8,128)(2,1)S(1)} %get-tuple-element.285), channel_id=1, source_target_pairs={{0,3},{1,0},{2,1},{3,2},{4,7},{5,4},{6,5},{7,6},{8,11},{9,8},{10,9... | collective-permute-start | bytes 589832 | tf_op jit(solution)/shard_map/ppermute | solution.py:91
  124.9 12.2 %collective-permute-start.7 = (bf16[64,1536]{1,0:T(8,128)(2,1)S(1)}, bf16[64,1536]{1,0:T(8,128)(2,1)S(1)}, u32[]{:S(2)}, u32[]{:S(2)}) collective-permute-start(bf16[64,1536]{1,0:T(8,128)(2,1)S(1)} %get-tuple-element.286), channel_id=1, source_target_pairs={{0,1},{1,2},{2,3},{3,0},{4,5},{5,6},{6,7},{7,4},{8,9},{9,10},{10,1... | collective-permute-start | bytes 589832 | tf_op jit(solution)/shard_map/ppermute | solution.py:91
  162.3 12.2 %collective-permute-start.13 = (bf16[64,1536]{1,0:T(8,128)(2,1)S(1)}, bf16[64,1536]{1,0:T(8,128)(2,1)}, u32[]{:S(2)}, u32[]{:S(2)}) collective-permute-start(bf16[64,1536]{1,0:T(8,128)(2,1)S(1)} %get-tuple-element.79), channel_id=1, source_target_pairs={{0,1},{1,2},{2,3},{3,0},{4,5},{5,6},{6,7},{7,4},{8,9},{9,10},{10,1... | collective-permute-start | bytes 589832 | tf_op jit(solution)/shard_map/ppermute | solution.py:91
  175.9 11.9 %collective-permute-start.14 = (bf16[64,1536]{1,0:T(8,128)(2,1)S(1)}, bf16[64,1536]{1,0:T(8,128)(2,1)S(1)}, u32[]{:S(2)}, u32[]{:S(2)}) collective-permute-start(bf16[64,1536]{1,0:T(8,128)(2,1)S(1)} %multiply_convert_fusion.3), channel_id=1, source_target_pairs={{0,1},{1,2},{2,3},{3,0},{4,5},{5,6},{6,7},{7,4},{8,9},{9,10},{10,1... | collective-permute-start | bytes 589832 | tf_op jit(solution)/shard_map/ppermute | solution.py:91
  176.0 11.8 %collective-permute-start.15 = (bf16[64,1536]{1,0:T(8,128)(2,1)S(1)}, bf16[64,1536]{1,0:T(8,128)(2,1)S(1)}, u32[]{:S(2)}, u32[]{:S(2)}) collective-permute-start(bf16[64,1536]{1,0:T(8,128)(2,1)S(1)} %multiply_convert_fusion.3), channel_id=1, source_target_pairs={{0,2},{1,3},{2,0},{3,1},{4,6},{5,7},{6,4},{7,5},{8,10},{9,11},{10,... | collective-permute-start | bytes 589832 | tf_op jit(solution)/shard_map/ppermute | solution.py:91
  176.3 11.4 %collective-permute-start.16 = (bf16[64,1536]{1,0:T(8,128)(2,1)S(1)}, bf16[64,1536]{1,0:T(8,128)(2,1)S(1)}, u32[]{:S(2)}, u32[]{:S(2)}) collective-permute-start(bf16[64,1536]{1,0:T(8,128)(2,1)S(1)} %multiply_convert_fusion.3), channel_id=1, source_target_pairs={{0,3},{1,0},{2,1},{3,2},{4,7},{5,4},{6,5},{7,6},{8,11},{9,8},{10,9... | collective-permute-start | bytes 589832 | tf_op jit(solution)/shard_map/ppermute | solution.py:91
  208.8 10.5 %collective-permute-start.19 = (bf16[64,1536]{1,0:T(8,128)(2,1)S(1)}, bf16[64,1536]{1,0:T(8,128)(2,1)S(1)}, u32[]{:S(2)}, u32[]{:S(2)}) collective-permute-start(bf16[64,1536]{1,0:T(8,128)(2,1)S(1)} %get-tuple-element.282), channel_id=1, source_target_pairs={{0,3},{1,0},{2,1},{3,2},{4,7},{5,4},{6,5},{7,6},{8,11},{9,8},{10,9... | collective-permute-start | bytes 589832 | tf_op jit(solution)/shard_map/ppermute | solution.py:91
  211.8 12.1 %collective-permute-start.21 = (bf16[64,1536]{1,0:T(8,128)(2,1)S(1)}, bf16[64,1536]{1,0:T(8,128)(2,1)}, u32[]{:S(2)}, u32[]{:S(2)}) collective-permute-start(bf16[64,1536]{1,0:T(8,128)(2,1)S(1)} %get-tuple-element.283), channel_id=1, source_target_pairs={{0,1},{1,2},{2,3},{3,0},{4,5},{5,6},{6,7},{7,4},{8,9},{9,10},{10,1... | collective-permute-start | bytes 589832 | tf_op jit(solution)/shard_map/ppermute | solution.py:91
  225.5 11.8 %collective-permute-start.22 = (bf16[64,1536]{1,0:T(8,128)(2,1)S(1)}, bf16[64,1536]{1,0:T(8,128)(2,1)S(1)}, u32[]{:S(2)}, u32[]{:S(2)}) collective-permute-start(bf16[64,1536]{1,0:T(8,128)(2,1)S(1)} %multiply_convert_fusion.2.refs_0_), channel_id=1, source_target_pairs={{0,1},{1,2},{2,3},{3,0},{4,5},{5,6},{6,7},{7,4},{8,9},{9,10},{10,1... | collective-permute-start | bytes 589832 | tf_op jit(solution)/shard_map/ppermute | solution.py:91
  225.6 12.4 %collective-permute-start.23 = (bf16[64,1536]{1,0:T(8,128)(2,1)S(1)}, bf16[64,1536]{1,0:T(8,128)(2,1)S(1)}, u32[]{:S(2)}, u32[]{:S(2)}) collective-permute-start(bf16[64,1536]{1,0:T(8,128)(2,1)S(1)} %multiply_convert_fusion.2.refs_0_), channel_id=1, source_target_pairs={{0,2},{1,3},{2,0},{3,1},{4,6},{5,7},{6,4},{7,5},{8,10},{9,11},{10,... | collective-permute-start | bytes 589832 | tf_op jit(solution)/shard_map/ppermute | solution.py:91
  226.2 12.4 %collective-permute-start.24 = (bf16[64,1536]{1,0:T(8,128)(2,1)S(1)}, bf16[64,1536]{1,0:T(8,128)(2,1)S(1)}, u32[]{:S(2)}, u32[]{:S(2)}) collective-permute-start(bf16[64,1536]{1,0:T(8,128)(2,1)S(1)} %multiply_convert_fusion.2.refs_0_), channel_id=1, source_target_pairs={{0,3},{1,0},{2,1},{3,2},{4,7},{5,4},{6,5},{7,6},{8,11},{9,8},{10,9... | collective-permute-start | bytes 589832 | tf_op jit(solution)/shard_map/ppermute | solution.py:91
  262.6 18.2 %collective-permute-start.31 = (bf16[256,5760]{1,0:T(8,128)(2,1)}, bf16[256,5760]{1,0:T(8,128)(2,1)S(1)}, u32[]{:S(2)}, u32[]{:S(2)}) collective-permute-start(bf16[256,5760]{1,0:T(8,128)(2,1)} %get-tuple-element.84.refs_0_.refs_2_), channel_id=1, source_target_pairs={{0,4},{4,0},{1,5},{5,1},{2,6},{6,2},{3,7},{7,3},{8,12},{12,8},{9,1... | collective-permute-start | bytes 8847368 | tf_op jit(solution)/shard_map/ppermute | solution.py:86
  264.9 12.0 %collective-permute-start.27 = (bf16[64,1536]{1,0:T(8,128)(2,1)S(1)}, bf16[64,1536]{1,0:T(8,128)(2,1)S(1)}, u32[]{:S(2)}, u32[]{:S(2)}) collective-permute-start(bf16[64,1536]{1,0:T(8,128)(2,1)S(1)} %get-tuple-element.83), channel_id=1, source_target_pairs={{0,1},{1,2},{2,3},{3,0},{4,5},{5,6},{6,7},{7,4},{8,9},{9,10},{10,1... | collective-permute-start | bytes 589832 | tf_op jit(solution)/shard_map/ppermute | solution.py:91
  277.9 15.0 %collective-permute-start.28 = (bf16[64,1536]{1,0:T(8,128)(2,1)S(1)}, bf16[64,1536]{1,0:T(8,128)(2,1)S(1)}, u32[]{:S(2)}, u32[]{:S(2)}) collective-permute-start(bf16[64,1536]{1,0:T(8,128)(2,1)S(1)} %fusion.174), channel_id=1, source_target_pairs={{0,1},{1,2},{2,3},{3,0},{4,5},{5,6},{6,7},{7,4},{8,9},{9,10},{10,1... | collective-permute-start | bytes 589832 | tf_op jit(solution)/shard_map/ppermute | solution.py:91
  278.0 15.0 %collective-permute-start.29 = (bf16[64,1536]{1,0:T(8,128)(2,1)S(1)}, bf16[64,1536]{1,0:T(8,128)(2,1)S(1)}, u32[]{:S(2)}, u32[]{:S(2)}) collective-permute-start(bf16[64,1536]{1,0:T(8,128)(2,1)S(1)} %fusion.174), channel_id=1, source_target_pairs={{0,2},{1,3},{2,0},{3,1},{4,6},{5,7},{6,4},{7,5},{8,10},{9,11},{10,... | collective-permute-start | bytes 589832 | tf_op jit(solution)/shard_map/ppermute | solution.py:91
  279.4 13.5 %collective-permute-start.30 = (bf16[64,1536]{1,0:T(8,128)(2,1)S(1)}, bf16[64,1536]{1,0:T(8,128)(2,1)S(1)}, u32[]{:S(2)}, u32[]{:S(2)}) collective-permute-start(bf16[64,1536]{1,0:T(8,128)(2,1)S(1)} %fusion.174), channel_id=1, source_target_pairs={{0,3},{1,0},{2,1},{3,2},{4,7},{5,4},{6,5},{7,6},{8,11},{9,8},{10,9... | collective-permute-start | bytes 589832 | tf_op jit(solution)/shard_map/ppermute | solution.py:91
  293.7 262.1 %reduce-scatter.3.cloned.1.call-start = ((), (), s32[]{:S(2)}) async-start(), calls=%async_computation.8 | async-start | bytes 10444800 | tf_op jit(solution)/shard_map/reduce_scatter | solution.py:430
  295.9 105.3 %collective-permute-start.46 = (bf16[256,1536]{1,0:T(8,128)(2,1)}, bf16[256,1536]{1,0:T(8,128)(2,1)}, u32[]{:S(2)}, u32[]{:S(2)}) collective-permute-start(bf16[256,1536]{1,0:T(8,128)(2,1)} %pad_maximum_fusion.2.refs_0_), channel_id=1, source_target_pairs={{0,4},{4,0},{1,5},{5,1},{2,6},{6,2},{3,7},{7,3},{8,12},{12,8},{9,1... | collective-permute-start | bytes 2359304 | tf_op jit(solution)/shard_map/ppermute | solution.py:86
  304.3 67.9 %collective-permute-start.41 = (bf16[256,1536]{1,0:T(8,128)(2,1)}, bf16[256,1536]{1,0:T(8,128)(2,1)}, u32[]{:S(2)}, u32[]{:S(2)}) collective-permute-start(bf16[256,1536]{1,0:T(8,128)(2,1)} %constant_dynamic-update-slice_fusion.2), channel_id=1, source_target_pairs={{0,4},{4,0},{1,5},{5,1},{2,6},{6,2},{3,7},{7,3},{8,12},{12,8},{9,1... | collective-permute-start | bytes 2359304 | tf_op jit(solution)/shard_map/ppermute | solution.py:86
  358.8 10.4 %collective-permute-start.36 = (bf16[64,1536]{1,0:T(8,128)(2,1)S(1)}, bf16[64,1536]{1,0:T(8,128)(2,1)S(1)}, u32[]{:S(2)}, u32[]{:S(2)}) collective-permute-start(bf16[64,1536]{1,0:T(8,128)(2,1)S(1)} %get-tuple-element.278), channel_id=1, source_target_pairs={{0,1},{1,2},{2,3},{3,0},{4,5},{5,6},{6,7},{7,4},{8,9},{9,10},{10,1... | collective-permute-start | bytes 589832 | tf_op jit(solution)/shard_map/ppermute | solution.py:91
  364.1 11.2 %collective-permute-start.42 = (bf16[256,512]{1,0:T(8,128)(2,1)S(1)}, bf16[256,512]{1,0:T(8,128)(2,1)S(1)}, u32[]{:S(2)}, u32[]{:S(2)}) collective-permute-start(bf16[256,512]{1,0:T(8,128)(2,1)S(1)} %get-tuple-element.290), channel_id=1, source_target_pairs={{0,4},{4,0},{1,5},{5,1},{2,6},{6,2},{3,7},{7,3},{8,12},{12,8},{9,1... | collective-permute-start | bytes 786440 | tf_op jit(solution)/shard_map/ppermute | solution.py:86
  370.9 10.2 %collective-permute-start.38 = (bf16[64,1536]{1,0:T(8,128)(2,1)S(1)}, bf16[64,1536]{1,0:T(8,128)(2,1)S(1)}, u32[]{:S(2)}, u32[]{:S(2)}) collective-permute-start(bf16[64,1536]{1,0:T(8,128)(2,1)S(1)} %get-tuple-element.93.refs_4_), channel_id=1, source_target_pairs={{0,2},{1,3},{2,0},{3,1},{4,6},{5,7},{6,4},{7,5},{8,10},{9,11},{10,... | collective-permute-start | bytes 589832 | tf_op jit(solution)/shard_map/ppermute | solution.py:91
  372.2 10.1 %collective-permute-start.39 = (bf16[64,1536]{1,0:T(8,128)(2,1)S(1)}, bf16[64,1536]{1,0:T(8,128)(2,1)S(1)}, u32[]{:S(2)}, u32[]{:S(2)}) collective-permute-start(bf16[64,1536]{1,0:T(8,128)(2,1)S(1)} %get-tuple-element.93.refs_4_), channel_id=1, source_target_pairs={{0,3},{1,0},{2,1},{3,2},{4,7},{5,4},{6,5},{7,6},{8,11},{9,8},{10,9... | collective-permute-start | bytes 589832 | tf_op jit(solution)/shard_map/ppermute | solution.py:91
  396.5 16.9 %collective-permute-start.48 = (bf16[256,2688]{1,0:T(8,128)(2,1)S(1)}, bf16[256,2688]{1,0:T(8,128)(2,1)S(1)}, u32[]{:S(2)}, u32[]{:S(2)}) collective-permute-start(bf16[256,2688]{1,0:T(8,128)(2,1)S(1)} %get-tuple-element.104), channel_id=1, source_target_pairs={{0,4},{4,0},{1,5},{5,1},{2,6},{6,2},{3,7},{7,3},{8,12},{12,8},{9,1... | collective-permute-start | bytes 4128776 | tf_op jit(solution)/shard_map/ppermute | solution.py:86
  398.1 15.3 %collective-permute-start.47 = (bf16[256,1536]{1,0:T(8,128)(2,1)S(1)}, bf16[256,1536]{1,0:T(8,128)(2,1)S(1)}, u32[]{:S(2)}, u32[]{:S(2)}) collective-permute-start(bf16[256,1536]{1,0:T(8,128)(2,1)S(1)} %constant_dynamic-update-slice_fusion.6.refs_2_), channel_id=1, source_target_pairs={{0,4},{4,0},{1,5},{5,1},{2,6},{6,2},{3,7},{7,3},{8,12},{12,8},{9,1... | collective-permute-start | bytes 2359304 | tf_op jit(solution)/shard_map/ppermute | solution.py:86
  398.2 10.6 %collective-permute-start.43 = (bf16[64,1536]{1,0:T(8,128)(2,1)S(1)}, bf16[64,1536]{1,0:T(8,128)(2,1)S(1)}, u32[]{:S(2)}, u32[]{:S(2)}) collective-permute-start(bf16[64,1536]{1,0:T(8,128)(2,1)S(1)} %copy-done.28), channel_id=1, source_target_pairs={{0,3},{1,0},{2,1},{3,2},{4,7},{5,4},{6,5},{7,6},{8,11},{9,8},{10,9... | collective-permute-start | bytes 589832 | tf_op jit(solution)/shard_map/ppermute | solution.py:91
  401.2 12.1 %collective-permute-start.45 = (bf16[64,1536]{1,0:T(8,128)(2,1)S(1)}, bf16[64,1536]{1,0:T(8,128)(2,1)S(1)}, u32[]{:S(2)}, u32[]{:S(2)}) collective-permute-start(bf16[64,1536]{1,0:T(8,128)(2,1)S(1)} %copy-done.24), channel_id=1, source_target_pairs={{0,1},{1,2},{2,3},{3,0},{4,5},{5,6},{6,7},{7,4},{8,9},{9,10},{10,1... | collective-permute-start | bytes 589832 | tf_op jit(solution)/shard_map/ppermute | solution.py:91
  413.4 11.6 %collective-permute-start.49 = (bf16[64,1536]{1,0:T(8,128)(2,1)}, bf16[64,1536]{1,0:T(8,128)(2,1)S(1)}, u32[]{:S(2)}, u32[]{:S(2)}) collective-permute-start(bf16[64,1536]{1,0:T(8,128)(2,1)} %get-tuple-element.106), channel_id=1, source_target_pairs={{0,3},{1,0},{2,1},{3,2},{4,7},{5,4},{6,5},{7,6},{8,11},{9,8},{10,9... | collective-permute-start | bytes 589832 | tf_op jit(solution)/shard_map/ppermute | solution.py:91
  413.4 11.5 %collective-permute-start.50 = (bf16[64,1536]{1,0:T(8,128)(2,1)}, bf16[64,1536]{1,0:T(8,128)(2,1)S(1)}, u32[]{:S(2)}, u32[]{:S(2)}) collective-permute-start(bf16[64,1536]{1,0:T(8,128)(2,1)} %get-tuple-element.107), channel_id=1, source_target_pairs={{0,2},{1,3},{2,0},{3,1},{4,6},{5,7},{6,4},{7,5},{8,10},{9,11},{10,... | collective-permute-start | bytes 589832 | tf_op jit(solution)/shard_map/ppermute | solution.py:91
  413.9 12.3 %collective-permute-start.51 = (bf16[64,1536]{1,0:T(8,128)(2,1)}, bf16[64,1536]{1,0:T(8,128)(2,1)S(1)}, u32[]{:S(2)}, u32[]{:S(2)}) collective-permute-start(bf16[64,1536]{1,0:T(8,128)(2,1)} %get-tuple-element.108), channel_id=1, source_target_pairs={{0,1},{1,2},{2,3},{3,0},{4,5},{5,6},{6,7},{7,4},{8,9},{9,10},{10,1... | collective-permute-start | bytes 589832 | tf_op jit(solution)/shard_map/ppermute | solution.py:91
  431.1 65.7 %collective-permute-start.59 = (bf16[256,1536]{1,0:T(8,128)(2,1)S(1)}, bf16[256,1536]{1,0:T(8,128)(2,1)S(1)}, u32[]{:S(2)}, u32[]{:S(2)}) collective-permute-start(bf16[256,1536]{1,0:T(8,128)(2,1)S(1)} %multiply_convert_fusion.refs_0_), channel_id=1, source_target_pairs={{0,4},{4,0},{1,5},{5,1},{2,6},{6,2},{3,7},{7,3},{8,12},{12,8},{9,1... | collective-permute-start | bytes 2359304 | tf_op jit(solution)/shard_map/ppermute | solution.py:86
  436.6 11.7 %collective-permute-start.53 = (bf16[64,1536]{1,0:T(8,128)(2,1)S(1)}, bf16[64,1536]{1,0:T(8,128)(2,1)}, u32[]{:S(2)}, u32[]{:S(2)}) collective-permute-start(bf16[64,1536]{1,0:T(8,128)(2,1)S(1)} %get-tuple-element.244), channel_id=1, source_target_pairs={{0,2},{1,3},{2,0},{3,1},{4,6},{5,7},{6,4},{7,5},{8,10},{9,11},{10,... | collective-permute-start | bytes 589832 | tf_op jit(solution)/shard_map/ppermute | solution.py:91
  450.8 46.1 %collective-permute-start.60 = (bf16[256,1536]{1,0:T(8,128)(2,1)}, bf16[256,1536]{1,0:T(8,128)(2,1)}, u32[]{:S(2)}, u32[]{:S(2)}) collective-permute-start(bf16[256,1536]{1,0:T(8,128)(2,1)} %get-tuple-element.355), channel_id=1, source_target_pairs={{0,4},{4,0},{1,5},{5,1},{2,6},{6,2},{3,7},{7,3},{8,12},{12,8},{9,1... | collective-permute-start | bytes 2359304 | tf_op jit(solution)/shard_map/ppermute | solution.py:86
  470.6 10.1 %collective-permute-start.58 = (bf16[64,1536]{1,0:T(8,128)(2,1)S(1)}, bf16[64,1536]{1,0:T(8,128)(2,1)S(1)}, u32[]{:S(2)}, u32[]{:S(2)}) collective-permute-start(bf16[64,1536]{1,0:T(8,128)(2,1)S(1)} %get-tuple-element.273), channel_id=1, source_target_pairs={{0,1},{1,2},{2,3},{3,0},{4,5},{5,6},{6,7},{7,4},{8,9},{9,10},{10,1... | collective-permute-start | bytes 589832 | tf_op jit(solution)/shard_map/ppermute | solution.py:91
  476.6 21.5 %collective-permute-start.61 = (bf16[256,768]{1,0:T(8,128)(2,1)}, bf16[256,768]{1,0:T(8,128)(2,1)S(1)}, u32[]{:S(2)}, u32[]{:S(2)}) collective-permute-start(bf16[256,768]{1,0:T(8,128)(2,1)} %get-tuple-element.270), channel_id=1, source_target_pairs={{0,4},{4,0},{1,5},{5,1},{2,6},{6,2},{3,7},{7,3},{8,12},{12,8},{9,1... | collective-permute-start | bytes 1179656 | tf_op jit(solution)/shard_map/ppermute | solution.py:86
  488.9 24.8 %all-to-all-start.2 = ((bf16[32,8,1536]{2,1,0:T(8,128)(2,1)}), bf16[32,8,1536]{2,1,0:T(8,128)(2,1)}, u32[]{:S(2)}, u32[]{:S(2)}) async-start(bf16[32,8,1536]{2,1,0:T(8,128)(2,1)} %fusion.7), calls=%async_computation.3 | async-start | bytes 1572864 | tf_op jit(solution)/shard_map/all_to_all | solution.py:866
  516.0 21.4 %collective-permute-start.63 = (bf16[136,1536]{1,0:T(8,128)(2,1)}, bf16[136,1536]{1,0:T(8,128)(2,1)}, u32[]{:S(2)}, u32[]{:S(2)}) collective-permute-start(bf16[136,1536]{1,0:T(8,128)(2,1)} %fusion.23), channel_id=1, source_target_pairs={{0,1},{1,2},{2,3},{3,0},{4,5},{5,6},{6,7},{7,4},{8,9},{9,10},{10,1... | collective-permute-start | bytes 1253384 | tf_op jit(solution)/shard_map/ppermute | solution.py:91
  516.0 21.4 %collective-permute-start.64 = (bf16[136,1536]{1,0:T(8,128)(2,1)}, bf16[136,1536]{1,0:T(8,128)(2,1)}, u32[]{:S(2)}, u32[]{:S(2)}) collective-permute-start(bf16[136,1536]{1,0:T(8,128)(2,1)} %fusion.23), channel_id=1, source_target_pairs={{0,2},{1,3},{2,0},{3,1},{4,6},{5,7},{6,4},{7,5},{8,10},{9,11},{10,... | collective-permute-start | bytes 1253384 | tf_op jit(solution)/shard_map/ppermute | solution.py:91
  516.0 22.3 %collective-permute-start.65 = (bf16[136,1536]{1,0:T(8,128)(2,1)}, bf16[136,1536]{1,0:T(8,128)(2,1)}, u32[]{:S(2)}, u32[]{:S(2)}) collective-permute-start(bf16[136,1536]{1,0:T(8,128)(2,1)} %fusion.23), channel_id=1, source_target_pairs={{0,3},{1,0},{2,1},{3,2},{4,7},{5,4},{6,5},{7,6},{8,11},{9,8},{10,9... | collective-permute-start | bytes 1253384 | tf_op jit(solution)/shard_map/ppermute | solution.py:91
  518.7 36.7 %all-to-all-start.3 = ((bf16[32,48,768]{2,1,0:T(8,128)(2,1)}), bf16[32,48,768]{2,1,0:T(8,128)(2,1)S(1)}, u32[]{:S(2)}, u32[]{:S(2)}) async-start(bf16[32,48,768]{2,1,0:T(8,128)(2,1)} %bitcast.69), calls=%async_computation.5 | async-start | bytes 4718592 | tf_op jit(solution)/shard_map/all_to_all | solution.py:891
  (205 other events, 2897.1 us)
Sparse Core Ops, SparseCore 0:
  10.9 114.7 all-gather.2
  128.5 71.4 all-gather.4
  293.8 86.9 reduce-scatter.4
  426.6 93.4 reduce-scatter.2

commit v10 on v8

--- a/solution.py
+++ b/solution.py
@@ -22,7 +22,7 @@
 Z_AXES = ("z_hi", "z_lo")
 CORES = 2
 TILE = 256
-VMEM_LIMIT = 48 * 1024 * 1024
+MIB = 1024 * 1024
 F32 = jnp.float32
 BF16 = jnp.bfloat16
 
@@ -183,7 +183,7 @@
         out_specs=[whole((rows, width))] * count,
         out_shape=chunk_shapes(count, rows, width),
         scratch_shapes=[pltpu.VMEM((tokens, width), BF16), pltpu.VMEM((tokens, width), F32)],
-        compiler_params=pltpu.CompilerParams(vmem_limit_bytes=VMEM_LIMIT),
+        compiler_params=pltpu.CompilerParams(vmem_limit_bytes=20 * MIB),
         cost_estimate=pl.CostEstimate(
             flops=2 * tokens * width * 3 * TILE * steps,
             bytes_accessed=2 * width * 3 * TILE * steps,
@@ -281,7 +281,7 @@
         ],
         scratch_shapes=[pltpu.VMEM((tokens, width), BF16)] * 2
         + [pltpu.VMEM((tokens, width), F32)] * ways,
-        compiler_params=pltpu.CompilerParams(vmem_limit_bytes=VMEM_LIMIT),
+        compiler_params=pltpu.CompilerParams(vmem_limit_bytes=(36 if forward else 28) * MIB),
         cost_estimate=pl.CostEstimate(
             flops=2 * tokens * width * (4 + ways) * TILE * steps,
             bytes_accessed=2 * width * 3 * TILE * steps + 4 * tokens * side_width,
@@ -342,13 +342,83 @@
         out_specs=pl.BlockSpec((width, block), lambda j: (0, out_start + j)),
         out_shape=jax.ShapeDtypeStruct((width, out_width), BF16),
         input_output_aliases=aliases,
-        compiler_params=pltpu.CompilerParams(vmem_limit_bytes=VMEM_LIMIT),
+        compiler_params=pltpu.CompilerParams(vmem_limit_bytes=28 * MIB),
         cost_estimate=pl.CostEstimate(
             flops=4 * tokens * width * block * steps,
             bytes_accessed=2 * width * block * steps,
             transcendentals=0,
         ),
         name="weight_gradient",
+    )(*operands)
+
+
+def attend_backward_kernel(
+    scale, kv_heads, size, q_ref, do_ref, kv_ref, raw_ref, cos_ref, sin_ref, gain_ref, place_ref, key_ref,
+    dq_ref, dkv_ref, dgain_ref,
+):
+    groups = q_ref.shape[1] // (kv_heads * size)
+    half = size // 2
+    cosine, sine, gain = cos_ref[...], sin_ref[...], gain_ref[...]
+    allowed = key_ref[:, 0:1] == place_ref[0:1, :]
+    allowed = allowed & (key_ref[:, 1:2] <= place_ref[1:2, :])
+    d_gain = jnp.zeros_like(gain)
+    for group in range(kv_heads):
+        columns = slice(group * size, (group + 1) * size)
+        value_columns = slice((kv_heads + group) * size, (kv_heads + group + 1) * size)
+        key, value = kv_ref[:, columns], kv_ref[:, value_columns]
+        d_key = d_value = None
+        for member in range(groups):
+            head = group * groups + member
+            head_columns = slice(head * size, (head + 1) * size)
+            query, d_out = q_ref[:, head_columns], do_ref[:, head_columns]
+            scores = jnp.where(allowed, times_t(key, query) * scale, NEGATIVE)
+            probs = jnp.exp(scores - jnp.max(scores, axis=0, keepdims=True))
+            probs = probs / jnp.sum(probs, axis=0, keepdims=True)
+            d_probs = times_t(value, d_out)
+            inner = jnp.sum(probs * d_probs, axis=0, keepdims=True)
+            d_scores = (probs * (d_probs - inner)).astype(BF16)
+            part_value = times(probs.astype(BF16), d_out)
+            part_key = times(d_scores, query) * scale
+            d_value = part_value if d_value is None else d_value + part_value
+            d_key = part_key if d_key is None else d_key + part_key
+            d_query = (times_rows(key, d_scores) * scale).T
+            first, second = d_query[:, :half], d_query[:, half:]
+            d_query = jnp.concatenate(
+                [first * cosine + second * sine, second * cosine - first * sine], axis=1
+            )
+            start = (group * (groups + 2) + member) * size
+            raw = raw_ref[:, start : start + size]
+            spread_of = lax.rsqrt(jnp.mean(raw * raw, axis=1, keepdims=True) + EPSILON)
+            d_gain += jnp.sum(d_query * raw * spread_of, axis=0, keepdims=True)
+            scaled = d_query * gain
+            d_raw = spread_of * scaled - raw * (
+                spread_of * spread_of * spread_of * jnp.mean(scaled * raw, axis=1, keepdims=True)
+            )
+            dq_ref[:, head_columns] = d_raw.astype(BF16)
+        dkv_ref[:, columns] = d_key
+        dkv_ref[:, value_columns] = d_value
+    dgain_ref[...] = d_gain
+
+
+def attend_backward(query, d_out, key_value, raw, cosine, sine, gain, place, key_place, kv_heads, scale):
+    rows, width = query.shape
+    keys = key_value.shape[0]
+    size = key_value.shape[1] // (2 * kv_heads)
+    operands = (query, d_out, key_value, raw, cosine, sine, gain, place, key_place)
+    return pl.pallas_call(
+        functools.partial(attend_backward_kernel, scale, kv_heads, size),
+        out_shape=[
+            jax.ShapeDtypeStruct((rows, width), BF16),
+            jax.ShapeDtypeStruct(key_value.shape, F32),
+            jax.ShapeDtypeStruct((1, size), F32),
+        ],
+        compiler_params=pltpu.CompilerParams(vmem_limit_bytes=36 * MIB),
+        cost_estimate=pl.CostEstimate(
+            flops=10 * rows * keys * width,
+            bytes_accessed=4 * rows * width * 2 + 12 * keys * kv_heads * size,
+            transcendentals=rows * keys * width // size,
+        ),
+        name="attend_backward",
     )(*operands)
 
 
@@ -451,11 +521,6 @@
         pack_ffn(first_gateup, first_down) + [attend_project, attend_output.T], axis=1
     )
     second_pack = jnp.concatenate(pack_ffn(second_gateup, second_down), axis=1)
-    first_all = lax.all_gather(first_pack, TOKEN_AXES, axis=0, tiled=True)
-    second_all = lax.all_gather(second_pack, TOKEN_AXES, axis=0, tiled=True)
-    project_b = first_all[:, ffn_width : ffn_width + attend_project.shape[1]]
-    output_b_t = first_all[:, ffn_width + attend_project.shape[1] :]
-
     piece_table = deal_order.reshape(shards, shards, piece_rows)[:, :, 0]
     anchor = piece_table // row_count
     anchor_piece = piece_table % row_count // piece_rows
@@ -478,7 +543,11 @@
         axis=1,
     )
     arrived = lax.all_to_all(outgoing, TOKEN_AXES, split_axis=0, concat_axis=0, tiled=True)
-    arrived, mixer_pack = lax.optimization_barrier((arrived, mixer_pack))
+    arrived, mixer_pack, first_pack = lax.optimization_barrier((arrived, mixer_pack, first_pack))
+    first_all = lax.all_gather(first_pack, TOKEN_AXES, axis=0, tiled=True)
+    second_all = lax.all_gather(second_pack, TOKEN_AXES, axis=0, tiled=True)
+    project_b = first_all[:, ffn_width : ffn_width + attend_project.shape[1]]
+    output_b_t = first_all[:, ffn_width + attend_project.shape[1] :]
     mixer_all = gather_pack(mixer_pack)
     project_a = mixer_all[:, : 3 * channels]
     output_a_t = mixer_all[:, 3 * channels :]
@@ -587,7 +656,6 @@
     exponent = jnp.exp(masked - row_top)
     row_total = jnp.sum(exponent, axis=-1, keepdims=True)
     softmax_rows = exponent / row_total
-    log_total = row_top + jnp.log(row_total)
     attended = (
         jnp.einsum(
             "kgtn,nkd->tkgd", softmax_rows.astype(BF16), value_all, preferred_element_type=F32
@@ -619,26 +687,21 @@
     back_b = jnp.concatenate(back_b)
     back_b_other = swap_core(back_b)
     attend_in_other = swap_core(attend_in)
-    d_attended_b = times(back_b, output_b_t).astype(BF16).reshape(row_count, -1, groups, HD)
-    scores_again = (
-        jnp.einsum("tkgd,nkd->kgtn", query_b, key_all, preferred_element_type=F32) * score_scale
-    )
-    probs_again = jnp.where(allowed, jnp.exp(scores_again - log_total), 0.0)
-    d_probs = jnp.einsum("tkgd,nkd->kgtn", d_attended_b, value_all, preferred_element_type=F32)
-    d_values = jnp.einsum(
-        "kgtn,tkgd->nkd", probs_again.astype(BF16), d_attended_b, preferred_element_type=F32
-    )
-    inner_sum = jnp.sum(probs_again * d_probs, axis=-1, keepdims=True)
-    d_scores = (probs_again * (d_probs - inner_sum)).astype(BF16)
-    d_query = (
-        jnp.einsum("kgtn,nkd->tkgd", d_scores, key_all, preferred_element_type=F32) * score_scale
-    )
-    d_keys = (
-        jnp.einsum("kgtn,tkgd->nkd", d_scores, query_b, preferred_element_type=F32) * score_scale
-    )
-    d_key_value = jnp.concatenate(
-        [d_keys.reshape(-1, kv_heads * HD), d_values.reshape(-1, kv_heads * HD)], axis=1
-    )
+    d_attended_b = times(back_b, output_b_t).astype(BF16)
+    d_query_raw, d_key_value, qgain_grad = attend_backward(
+        query_b.reshape(row_count, -1),
+        d_attended_b,
+        key_value_all,
+        proj_b.reshape(row_count, -1),
+        cosine,
+        sine,
+        qgain_f[None],
+        jnp.stack([segment, places]),
+        jnp.stack([key_segment, key_places], axis=1),
+        kv_heads,
+        score_scale,
+    )
+    qgain_grad = qgain_grad[0]
     d_slots = d_key_value.reshape(contexts, row_count, -1)
     d_others = jnp.concatenate([d_slots[1], d_slots[3]]).astype(BF16)
     d_others = swap_core(d_others).astype(F32)
@@ -646,13 +709,18 @@
     d_local = d_slots[0] + d_others[:row_count] + swap_ctx(d_far, 2).astype(F32)
     d_key_local = d_local[:, : kv_heads * HD].reshape(row_count, kv_heads, HD)
     d_value_local = d_local[:, kv_heads * HD :].reshape(row_count, kv_heads, HD)
-    unused, pullback = jax.vjp(qk_maps, query_raw, key_raw, qgain_f, kgain_f)
-    d_query_raw, d_key_raw, qgain_grad, kgain_grad = pullback((d_query, d_key_local))
-    d_proj_b = (
-        jnp.concatenate([d_query_raw, d_key_raw[:, :, None], d_value_local[:, :, None]], axis=2)
-        .astype(BF16)
-        .reshape(row_count, -1)
-    )
+    unused, pullback = jax.vjp(
+        lambda key_in, gain_k: rotate(norm_rows(key_in, gain_k), cosine, sine), key_raw, kgain_f
+    )
+    d_key_raw, kgain_grad = pullback(d_key_local)
+    d_proj_b = jnp.concatenate(
+        [
+            d_query_raw.reshape(row_count, kv_heads, groups, HD),
+            d_key_raw[:, :, None].astype(BF16),
+            d_value_local[:, :, None].astype(BF16),
+        ],
+        axis=2,
+    ).reshape(row_count, -1)
     d_attend_in = tp_reduce(tp_chunks(times_t(d_proj_b, project_b)))
     unused, pullback = jax.vjp(norm_rows, stream2, gain_b)
     d_norm_b, gain_b_grad = pullback(d_attend_in)
@@ -833,7 +901,17 @@
         concat_axis=0,
         tiled=True,
     )
-    last, first_sums = lax.optimization_barrier((last, first_sums))
+    home_rows = (
+        jnp.repeat(jnp.tile(send_piece, members), part_rows) * piece_rows
+        + member_of * part_rows
+        + gathered % part_rows
+    )
+    to_arrival = (home_rows[None, :] == gathered[:, None]).astype(BF16)
+    input_gradient = arrange(to_arrival, jnp.concatenate([slot[:chunk] for slot in last]))
+    layer_out = arrange(to_arrival, jnp.concatenate([slot[chunk : 2 * chunk] for slot in last]))
+    first_sums, layer_out, input_gradient = lax.optimization_barrier(
+        (first_sums, layer_out, input_gradient)
+    )
     low, high = share_rows(first_sums)
     first_grads = ffn_gradients(low[:, :ffn_cols], high[:, :ffn_cols], steps, hidden)
     attend_grads = jnp.concatenate([low[:, ffn_cols:], high[:, ffn_cols:]], axis=1)
@@ -843,14 +921,6 @@
     mixer_home = mixer_home.reshape(shards // CORES, CORES, depth, mixer_cols)
     mixer_grads = jnp.sum(mixer_home.astype(F32), axis=0)
     mixer_grads = jnp.concatenate([mixer_grads[0], mixer_grads[1]], axis=1)
-    home_rows = (
-        jnp.repeat(jnp.tile(send_piece, members), part_rows) * piece_rows
-        + member_of * part_rows
-        + gathered % part_rows
-    )
-    to_arrival = (home_rows[None, :] == gathered[:, None]).astype(BF16)
-    input_gradient = arrange(to_arrival, jnp.concatenate([slot[:chunk] for slot in last]))
-    layer_out = arrange(to_arrival, jnp.concatenate([slot[chunk : 2 * chunk] for slot in last]))
     smalls = [
         slot[2 * chunk].astype(F32) + slot[2 * chunk + 1].astype(F32) for slot in last
     ]

time: 556 us -> 577 us (1.038)
  the two profiles are of different devices: /device:TPU:17 before, /device:TPU:1 now
where the time goes in v10:
time: 577 us; the launch traced here: 567 us
  waiting for transfers between devices  187 us (32%)
  starting transfers between devices  112 us (19%)
  local copies, waits for them, and re-layouts  82.3 us (14%)
  Pallas kernels  69.1 us (12%)
  other arithmetic  56.4 us (10%)
  matrix products  42.3 us (7%)
  between operations  17.7 us (3%)
    ppermute x48, waiting for transfers between devices, shift_tp(): lax.ppermute(block, 'tp', [(i, (i + distance) % members) for i in range(m...  119 us
    ppermute x48, starting transfers between devices, shift_tp(): lax.ppermute(block, 'tp', [(i, (i + distance) % members) for i in range(m...  46.3 us
    unnamed x348, local copies, waits for them, and re-layouts  40.4 us
    ppermute x15, starting transfers between devices, swap_core(): return lax.ppermute(block, 'core', [(0, 1), (1, 0)])  31.9 us
    pallas_call x2, Pallas kernels, ffn_backward(): pl.pallas_call(functools.partial(ffn_backward_kernel, count, forward), gr...  27.8 us
    pallas_call x4, Pallas kernels, gradient(): pl.pallas_call(functools.partial(gradient_kernel, edge, cut), grid=(steps...  24.8 us
    dot_general x10, matrix products, times(): lax.dot_general(left, right, (((1,), (0,)), ((), ())), preferred_element_...  18.9 us
    all_to_all x1, waiting for transfers between devices, gather_pack(): lax.all_to_all(jnp.broadcast_to(pack, (chips,) + pack.shape), CHIP_AXES,...  16 us
  transfers between devices with their start and end apart: 75, of which 38 were waited for; matrix products, arithmetic and copies ran while one was open for 24% of the time, Pallas kernels for 10%

profile of v10, /device:TPU:1, one launch (start us, length us, event | category | flops | bytes accessed | tf_op | source)
XLA Modules:
  0.0 566.7 jit_solution(15339983882923330803)
XLA Ops:
  14.4 9.4 %all-to-all-start = ((bf16[32,5,1536]{2,1,0:T(8,128)(2,1)}), bf16[32,5,1536]{2,1,0:T(8,128)(2,1)S(1)}, u32[]{:S(2)}, u32[]{:S(2)}) async-start(bf16[32,5,1536]{2,1,0:T(8,128)(2,1)} %pad_maximum_fusion), calls=%async_computation | async-start | bytes 1572864 | tf_op jit(solution)/shard_map/all_to_all | solution.py:545
  26.0 12.1 %all-to-all-done = bf16[32,5,1536]{2,1,0:T(8,128)(2,1)S(1)} async-done(((bf16[32,5,1536]{2,1,0:T(8,128)(2,1)}), bf16[32,5,1536]{2,1,0:T(8,128)(2,1)S(1)}, u32[]{:S(2)}, u32[]{:S(2)}) %all-to-all-start) | async-done | bytes 491552 | tf_op jit(solution)/shard_map/all_to_all | solution.py:545
  46.3 4.4 all-to-all-start.1
  59.9 14.3 %collective-permute-done.2 = bf16[128,1536]{1,0:T(8,128)(2,1)S(1)} collective-permute-done((bf16[128,1536]{1,0:T(8,128)(2,1)}, bf16[128,1536]{1,0:T(8,128)(2,1)S(1)}, u32[]{:S(2)}, u32[]{:S(2)}) %collective-permute-start.2) | collective-permute-done | bytes 393248 | tf_op jit(solution)/shard_map/ppermute | solution.py:91
  74.3 16.0 %all-to-all-done.1 = bf16[16,48,1536]{2,1,0:T(8,128)(2,1)} async-done(((bf16[16,48,1536]{2,1,0:T(8,128)(2,1)}), bf16[16,48,1536]{2,1,0:T(8,128)(2,1)}, u32[]{:S(2)}, u32[]{:S(2)}) %all-to-all-start.1) | async-done | bytes 2359328 | tf_op jit(solution)/shard_map/all_to_all | solution.py:441
  92.6 4.1 collective-permute-start.3
  102.9 3.3 fusion.201
  110.3 7.6 %collective-permute-done.5 = bf16[64,1536]{1,0:T(8,128)(2,1)S(1)} collective-permute-done((bf16[64,1536]{1,0:T(8,128)(2,1)S(1)}, bf16[64,1536]{1,0:T(8,128)(2,1)S(1)}, u32[]{:S(2)}, u32[]{:S(2)}) %collective-permute-start.5) | collective-permute-done | bytes 196640 | tf_op jit(solution)/shard_map/ppermute | solution.py:91
  118.0 3.7 collective-permute-done.7
  125.2 4.2 collective-permute-done.10.refs_3_
  129.4 5.8 %collective-permute-done.8.refs_1_ = bf16[64,1536]{1,0:T(8,128)(2,1)S(1)} collective-permute-done((bf16[64,1536]{1,0:T(8,128)(2,1)S(1)}, bf16[64,1536]{1,0:T(8,128)(2,1)S(1)}, u32[]{:S(2)}, u32[]{:S(2)}) %collective-permute-start.8) | collective-permute-done | bytes 196640 | tf_op jit(solution)/shard_map/ppermute | solution.py:91
  135.2 5.1 all-gather.3.cloned.1.call-done.refs_4_.refs_5_.refs_8_.refs_9_
  140.3 6.6 %copy-done = bf16[1536,6400]{1,0:T(8,128)(2,1)S(1)} copy-done((bf16[1536,6400]{1,0:T(8,128)(2,1)S(1)}, bf16[1536,6400]{1,0:T(8,128)(2,1)}, u32[]{:S(2)}) %copy-start) | copy-done | bytes 19660824
  146.9 8.4 %ffn_forward.1 = (f32[64,1536]{1,0:T(8,128)S(1)}, bf16[64,1536]{1,0:T(8,128)(2,1)}, bf16[64,1536]{1,0:T(8,128)(2,1)S(1)}, bf16[64,1536]{1,0:T(8,128)(2,1)S(1)}) custom-call(bf16[64,1536]{1,0:T(8,128)(2,1)S(1)} %multiply_convert_fusion.4.refs_0_, bf16[64,1536]{1,0:T(8,128)(2,1)S(1)} %collective-permute-done.8.refs_1_, ...), custom_call_target="tpu_custom_call" | custom-call | flops 4227858432 | bytes 16515072 | tf_op jit(solution)/shard_map/ffn_forward/pallas_call | solution.py:179
  160.1 6.2 %collective-permute-done.11 = bf16[64,1536]{1,0:T(8,128)(2,1)S(1)} collective-permute-done((bf16[64,1536]{1,0:T(8,128)(2,1)}, bf16[64,1536]{1,0:T(8,128)(2,1)S(1)}, u32[]{:S(2)}, u32[]{:S(2)}) %collective-permute-start.11) | collective-permute-done | bytes 196640 | tf_op jit(solution)/shard_map/ppermute | solution.py:91
  166.3 4.2 collective-permute-done.13
  174.9 8.8 %collective-permute-done.14 = bf16[64,1536]{1,0:T(8,128)(2,1)S(1)} collective-permute-done((bf16[64,1536]{1,0:T(8,128)(2,1)S(1)}, bf16[64,1536]{1,0:T(8,128)(2,1)S(1)}, u32[]{:S(2)}, u32[]{:S(2)}) %collective-permute-start.14) | collective-permute-done | bytes 196640 | tf_op jit(solution)/shard_map/ppermute | solution.py:91
  194.8 6.1 %collective-permute-done.17 = bf16[256,256]{1,0:T(8,128)(2,1)S(1)} collective-permute-done((bf16[256,256]{1,0:T(8,128)(2,1)S(1)}, bf16[256,256]{1,0:T(8,128)(2,1)S(1)}, u32[]{:S(2)}, u32[]{:S(2)}) %collective-permute-start.17) | collective-permute-done | bytes 131104 | tf_op jit(solution)/shard_map/ppermute | solution.py:82
  200.9 12.0 %collective-permute-start.18 = (bf16[512,256]{1,0:T(8,128)(2,1)S(1)}, bf16[512,256]{1,0:T(8,128)(2,1)S(1)}, u32[]{:S(2)}, u32[]{:S(2)}) collective-permute-start(bf16[512,256]{1,0:T(8,128)(2,1)S(1)} %pad_maximum_fusion.11), channel_id=1, source_target_pairs={{0,4},{4,0},{1,5},{5,1},{2,6},{6,2},{3,7},{7,3},{8,12},{12,8},{9,1... | collective-permute-start | bytes 786440 | tf_op jit(solution)/shard_map/ppermute | solution.py:86
  215.9 5.7 %fusion.202 = (f32[2,3,256]{2,1,0:T(4,128)S(1)}, f32[2,3,256,1024]{2,3,1,0:T(8,128)}) fusion(pred[256,1024]{0,1:T(8,128)(4,1)} %compare_and_fusion, bf16[1024,2,64,1]{0,2,3,1:T(8,128)(2,1)} %bitcast.192, bf16[256,2,3,32]{0,3,2,1:T(8,128)(2,1)S(1)} %copy-done.68, bf16[256,2,3,32]{0,3,2,1:T(8,128)(2,1)S(1)} %get-tuple-element.314), kind=kOutput, calls=%fused_computation.482 | convolution fusion | flops 208012288 | bytes 7018496 | tf_op jit(solution)/shard_map/sub | solution.py:656
  221.6 3.4 fusion.17
  225.1 3.1 fusion.203
  231.2 7.6 %collective-permute-done.19 = bf16[64,1536]{1,0:T(8,128)(2,1)} collective-permute-done((bf16[64,1536]{1,0:T(8,128)(2,1)S(1)}, bf16[64,1536]{1,0:T(8,128)(2,1)}, u32[]{:S(2)}, u32[]{:S(2)}) %collective-permute-start.19) | collective-permute-done | bytes 196640 | tf_op jit(solution)/shard_map/ppermute | solution.py:91
  238.9 3.7 collective-permute-done.21
  247.8 5.8 %collective-permute-done.22.refs_1_ = bf16[64,1536]{1,0:T(8,128)(2,1)S(1)} collective-permute-done((bf16[64,1536]{1,0:T(8,128)(2,1)S(1)}, bf16[64,1536]{1,0:T(8,128)(2,1)S(1)}, u32[]{:S(2)}, u32[]{:S(2)}) %collective-permute-start.22) | collective-permute-done | bytes 196640 | tf_op jit(solution)/shard_map/ppermute | solution.py:91
  258.5 14.1 %ffn_both.1 = (f32[64,1536]{1,0:T(8,128)S(1)}, bf16[64,1536]{1,0:T(8,128)(2,1)S(1)}, bf16[64,1536]{1,0:T(8,128)(2,1)S(1)}, bf16[64,1536]{1,0:T(8,128)(2,1)S(1)},...) custom-call(s32[1]{0:T(128)} %bitcast.11.core_ref, ...), custom_call_target="tpu_custom_call" | custom-call | flops 8455716864 | bytes 22413312 | tf_op jit(solution)/shard_map/ffn_both/pallas_call | solution.py:269
  277.2 4.5 collective-permute-done.25
  284.3 4.3 collective-permute-done.27
  292.3 8.8 %weight_gradient.4 = bf16[1536,2688]{1,0:T(8,128)(2,1)S(1)} custom-call(bf16[256,5760]{1,0:T(8,128)(2,1)S(1)} %get-tuple-element.89.refs_0_.refs_2_, bf16[256,5760]{1,0:T(8,128)(2,1)S(1)} %collective-permute-done.31.refs_1_.refs_3_.refs_5_, bf16[256,5760]{1,0:T(8,128)(2,1)S(1)} %get-tuple-element.89.refs_0_.refs_2_, ...), custom_call_target="tpu_custom_call" | custom-call | flops 4227858432 | bytes 8257536 | tf_op jit(solution)/shard_map/weight_gradient/pallas_call | solution.py:338
  301.1 3.3 copy-done.3
  312.2 8.0 %attend_backward.1 = (bf16[256,384]{1,0:T(8,128)(2,1)S(1)}, f32[1024,256]{1,0:T(8,128)S(1)}, f32[1,64]{1,0:T(1,128)S(1)}) custom-call(bf16[256,384]{1,0:T(8,128)(2,1)S(1)} %copy.198.q_ref, bf16[256,384]{1,0:T(8,128)(2,1)S(1)} %convolution_convert_fusion.5.do_ref, bf16[1024,256]{1,0:T(8,128)(2,1)S(1)} %pad_maximum_fusion.5.kv_ref, f32[256,640]{1,0:T(8,128)S(1)} %copy-done.9, ...), custom_call_target="tpu_custom_call" | custom-call | flops 1006632960 | bytes 2359296 | tf_op jit(solution)/shard_map/attend_backward/pallas_call | solution.py:408
  332.0 4.5 collective-permute-done.33
  354.7 3.1 collective-permute-start.40
  375.7 6.8 %copy-done.1 = bf16[1536,6400]{1,0:T(8,128)(2,1)S(1)} copy-done((bf16[1536,6400]{1,0:T(8,128)(2,1)S(1)}, bf16[1536,6400]{1,0:T(8,128)(2,1)}, u32[]{:S(2)}) %copy-start.1) | copy-done | bytes 19660824
  382.5 13.7 %ffn_backward.1 = (f32[64,1536]{1,0:T(8,128)S(1)}, bf16[64,1536]{1,0:T(8,128)(2,1)S(1)}, bf16[64,1536]{1,0:T(8,128)(2,1)}, bf16[64,1536]{1,0:T(8,128)(2,1)S(1)},...) custom-call(s32[1]{0:T(128)} %bitcast.11.core_ref, bf16[64,1536]{1,0:T(8,128)(2,1)S(1)} %multiply_convert_fusion.4.refs_0_, ...), custom_call_target="tpu_custom_call" | custom-call | flops 7046430720 | bytes 19267584 | tf_op jit(solution)/shard_map/ffn_backward/pallas_call | solution.py:269
  396.1 3.2 collective-permute-start.54
  402.2 3.7 collective-permute-done.46
  408.0 4.8 collective-permute-done.48
  417.0 9.9 %weight_gradient.6 = bf16[1536,3200]{1,0:T(8,128)(2,1)S(1)} custom-call(bf16[256,1536]{1,0:T(8,128)(2,1)S(1)} %pad_maximum_fusion.2.refs_0_, bf16[256,1536]{1,0:T(8,128)(2,1)} %collective-permute-done.52.refs_1_, bf16[256,1536]{1,0:T(8,128)(2,1)S(1)} %constant_dynamic-update-slice_fusion.6.refs_2_, ...), custom_call_target="tpu_custom_call", output_to_operand_aliasing={{}: (6, {})} | custom-call | flops 4227858432 | bytes 8257536 | tf_op jit(solution)/shard_map/weight_gradient/pallas_call | solution.py:338
  426.9 3.7 copy-done.2
  453.4 5.2 fusion.205
  468.2 3.2 collective-permute-done.58
  479.7 6.5 %all-to-all-start.2 = ((bf16[32,8,1536]{2,1,0:T(8,128)(2,1)}), bf16[32,8,1536]{2,1,0:T(8,128)(2,1)}, u32[]{:S(2)}, u32[]{:S(2)}) async-start(bf16[32,8,1536]{2,1,0:T(8,128)(2,1)} %fusion.10), calls=%async_computation.3 | async-start | bytes 1572864 | tf_op jit(solution)/shard_map/all_to_all | solution.py:872
  489.1 3.2 weight_gradient.7
  493.7 8.6 %all-to-all-done.2 = bf16[32,8,1536]{2,1,0:T(8,128)(2,1)} async-done(((bf16[32,8,1536]{2,1,0:T(8,128)(2,1)}), bf16[32,8,1536]{2,1,0:T(8,128)(2,1)}, u32[]{:S(2)}, u32[]{:S(2)}) %all-to-all-start.2) | async-done | bytes 786464 | tf_op jit(solution)/shard_map/all_to_all | solution.py:872
  507.7 5.2 all-to-all-start.3
  515.4 11.2 %collective-permute-done.63 = bf16[136,1536]{1,0:T(8,128)(2,1)S(1)} collective-permute-done((bf16[136,1536]{1,0:T(8,128)(2,1)}, bf16[136,1536]{1,0:T(8,128)(2,1)S(1)}, u32[]{:S(2)}, u32[]{:S(2)}) %collective-permute-start.63) | collective-permute-done | bytes 417824 | tf_op jit(solution)/shard_map/ppermute | solution.py:91
  533.9 12.3 %reduce-scatter.3.cloned.1.call-done = bf16[96,3200]{1,0:T(8,128)(2,1)} async-done(((bf16[1536,3200]{1,0:T(8,128)(2,1)}), bf16[96,3200]{1,0:T(8,128)(2,1)}) %reduce-scatter.3.cloned.1.call-update) | async-done | bytes 614416 | tf_op jit(solution)/shard_map/reduce_scatter | solution.py:435
  (728 shorter events, 225.3 us)
Async XLA Ops:
  14.4 23.7 %all-to-all-start = ((bf16[32,5,1536]{2,1,0:T(8,128)(2,1)}), bf16[32,5,1536]{2,1,0:T(8,128)(2,1)S(1)}, u32[]{:S(2)}, u32[]{:S(2)}) async-start(bf16[32,5,1536]{2,1,0:T(8,128)(2,1)} %pad_maximum_fusion), calls=%async_computation | async-start | bytes 1572864 | tf_op jit(solution)/shard_map/all_to_all | solution.py:545
  23.9 116.4 %all-gather.3.cloned.1.call-start = ((), (), s32[]{:S(2)}) async-start(), calls=%async_computation.6 | async-start | bytes 20275200 | tf_op jit(solution)/shard_map/all_gather | solution.py:547
  38.1 209.6 %all-gather.5.cloned.1.call-start = ((), (), s32[]{:S(2)}) async-start(), calls=%async_computation.7 | async-start | bytes 17031168 | tf_op jit(solution)/shard_map/all_gather | solution.py:548
  46.3 44.0 %all-to-all-start.1 = ((bf16[16,48,1536]{2,1,0:T(8,128)(2,1)}), bf16[16,48,1536]{2,1,0:T(8,128)(2,1)}, u32[]{:S(2)}, u32[]{:S(2)}) async-start(bf16[16,48,1536]{2,1,0:T(8,128)(2,1)} %broadcast_in_dim.86), calls=%async_computation.1 | async-start | bytes 4718592 | tf_op jit(solution)/shard_map/all_to_all | solution.py:441
  50.8 435.5 %reduce-scatter.5.cloned.1.call-start = ((), (), s32[]{:S(2)}) async-start(), calls=%async_computation.9 | async-start | bytes 8773632 | tf_op jit(solution)/shard_map/reduce_scatter | solution.py:435
  54.3 20.0 %collective-permute-start.2 = (bf16[128,1536]{1,0:T(8,128)(2,1)}, bf16[128,1536]{1,0:T(8,128)(2,1)S(1)}, u32[]{:S(2)}, u32[]{:S(2)}) collective-permute-start(bf16[128,1536]{1,0:T(8,128)(2,1)} %constant_dynamic-update-slice_fusion), channel_id=1, source_target_pairs={{0,3},{1,0},{2,1},{3,2},{4,7},{5,4},{6,5},{7,6},{8,11},{9,8},{10,9... | collective-permute-start | bytes 1179656 | tf_op jit(solution)/shard_map/ppermute | solution.py:91
  57.8 33.0 %collective-permute-start.1 = (bf16[128,1536]{1,0:T(8,128)(2,1)}, bf16[128,1536]{1,0:T(8,128)(2,1)}, u32[]{:S(2)}, u32[]{:S(2)}) collective-permute-start(bf16[128,1536]{1,0:T(8,128)(2,1)} %constant_dynamic-update-slice_fusion), channel_id=1, source_target_pairs={{0,2},{1,3},{2,0},{3,1},{4,6},{5,7},{6,4},{7,5},{8,10},{9,11},{10,... | collective-permute-start | bytes 1179656 | tf_op jit(solution)/shard_map/ppermute | solution.py:91
  58.2 33.6 %collective-permute-start = (bf16[128,1536]{1,0:T(8,128)(2,1)}, bf16[128,1536]{1,0:T(8,128)(2,1)S(1)}, u32[]{:S(2)}, u32[]{:S(2)}) collective-permute-start(bf16[128,1536]{1,0:T(8,128)(2,1)} %constant_dynamic-update-slice_fusion), channel_id=1, source_target_pairs={{0,1},{1,2},{2,3},{3,0},{4,5},{5,6},{6,7},{7,4},{8,9},{9,10},{10,1... | collective-permute-start | bytes 1179656 | tf_op jit(solution)/shard_map/ppermute | solution.py:91
  106.3 11.7 %collective-permute-start.5 = (bf16[64,1536]{1,0:T(8,128)(2,1)S(1)}, bf16[64,1536]{1,0:T(8,128)(2,1)S(1)}, u32[]{:S(2)}, u32[]{:S(2)}) collective-permute-start(bf16[64,1536]{1,0:T(8,128)(2,1)S(1)} %get-tuple-element.303), channel_id=1, source_target_pairs={{0,3},{1,0},{2,1},{3,2},{4,7},{5,4},{6,5},{7,6},{8,11},{9,8},{10,9... | collective-permute-start | bytes 589832 | tf_op jit(solution)/shard_map/ppermute | solution.py:91
  109.4 12.3 %collective-permute-start.7 = (bf16[64,1536]{1,0:T(8,128)(2,1)S(1)}, bf16[64,1536]{1,0:T(8,128)(2,1)S(1)}, u32[]{:S(2)}, u32[]{:S(2)}) collective-permute-start(bf16[64,1536]{1,0:T(8,128)(2,1)S(1)} %get-tuple-element.304), channel_id=1, source_target_pairs={{0,1},{1,2},{2,3},{3,0},{4,5},{5,6},{6,7},{7,4},{8,9},{9,10},{10,1... | collective-permute-start | bytes 589832 | tf_op jit(solution)/shard_map/ppermute | solution.py:91
  123.8 11.4 %collective-permute-start.8 = (bf16[64,1536]{1,0:T(8,128)(2,1)S(1)}, bf16[64,1536]{1,0:T(8,128)(2,1)S(1)}, u32[]{:S(2)}, u32[]{:S(2)}) collective-permute-start(bf16[64,1536]{1,0:T(8,128)(2,1)S(1)} %multiply_convert_fusion.4.refs_0_), channel_id=1, source_target_pairs={{0,1},{1,2},{2,3},{3,0},{4,5},{5,6},{6,7},{7,4},{8,9},{9,10},{10,1... | collective-permute-start | bytes 589832 | tf_op jit(solution)/shard_map/ppermute | solution.py:91
  124.7 10.5 %collective-permute-start.9 = (bf16[64,1536]{1,0:T(8,128)(2,1)S(1)}, bf16[64,1536]{1,0:T(8,128)(2,1)S(1)}, u32[]{:S(2)}, u32[]{:S(2)}) collective-permute-start(bf16[64,1536]{1,0:T(8,128)(2,1)S(1)} %multiply_convert_fusion.4.refs_0_), channel_id=1, source_target_pairs={{0,2},{1,3},{2,0},{3,1},{4,6},{5,7},{6,4},{7,5},{8,10},{9,11},{10,... | collective-permute-start | bytes 589832 | tf_op jit(solution)/shard_map/ppermute | solution.py:91
  155.3 11.0 %collective-permute-start.11 = (bf16[64,1536]{1,0:T(8,128)(2,1)}, bf16[64,1536]{1,0:T(8,128)(2,1)S(1)}, u32[]{:S(2)}, u32[]{:S(2)}) collective-permute-start(bf16[64,1536]{1,0:T(8,128)(2,1)} %get-tuple-element.82), channel_id=1, source_target_pairs={{0,3},{1,0},{2,1},{3,2},{4,7},{5,4},{6,5},{7,6},{8,11},{9,8},{10,9... | collective-permute-start | bytes 589832 | tf_op jit(solution)/shard_map/ppermute | solution.py:91
  158.4 12.1 %collective-permute-start.13 = (bf16[64,1536]{1,0:T(8,128)(2,1)S(1)}, bf16[64,1536]{1,0:T(8,128)(2,1)}, u32[]{:S(2)}, u32[]{:S(2)}) collective-permute-start(bf16[64,1536]{1,0:T(8,128)(2,1)S(1)} %get-tuple-element.84), channel_id=1, source_target_pairs={{0,1},{1,2},{2,3},{3,0},{4,5},{5,6},{6,7},{7,4},{8,9},{9,10},{10,1... | collective-permute-start | bytes 589832 | tf_op jit(solution)/shard_map/ppermute | solution.py:91
  172.1 11.6 %collective-permute-start.14 = (bf16[64,1536]{1,0:T(8,128)(2,1)S(1)}, bf16[64,1536]{1,0:T(8,128)(2,1)S(1)}, u32[]{:S(2)}, u32[]{:S(2)}) collective-permute-start(bf16[64,1536]{1,0:T(8,128)(2,1)S(1)} %multiply_convert_fusion.3), channel_id=1, source_target_pairs={{0,1},{1,2},{2,3},{3,0},{4,5},{5,6},{6,7},{7,4},{8,9},{9,10},{10,1... | collective-permute-start | bytes 589832 | tf_op jit(solution)/shard_map/ppermute | solution.py:91
  172.2 11.5 %collective-permute-start.15 = (bf16[64,1536]{1,0:T(8,128)(2,1)S(1)}, bf16[64,1536]{1,0:T(8,128)(2,1)S(1)}, u32[]{:S(2)}, u32[]{:S(2)}) collective-permute-start(bf16[64,1536]{1,0:T(8,128)(2,1)S(1)} %multiply_convert_fusion.3), channel_id=1, source_target_pairs={{0,2},{1,3},{2,0},{3,1},{4,6},{5,7},{6,4},{7,5},{8,10},{9,11},{10,... | collective-permute-start | bytes 589832 | tf_op jit(solution)/shard_map/ppermute | solution.py:91
  173.4 10.6 %collective-permute-start.16 = (bf16[64,1536]{1,0:T(8,128)(2,1)S(1)}, bf16[64,1536]{1,0:T(8,128)(2,1)S(1)}, u32[]{:S(2)}, u32[]{:S(2)}) collective-permute-start(bf16[64,1536]{1,0:T(8,128)(2,1)S(1)} %multiply_convert_fusion.3), channel_id=1, source_target_pairs={{0,3},{1,0},{2,1},{3,2},{4,7},{5,4},{6,5},{7,6},{8,11},{9,8},{10,9... | collective-permute-start | bytes 589832 | tf_op jit(solution)/shard_map/ppermute | solution.py:91
  200.9 13.9 %collective-permute-start.18 = (bf16[512,256]{1,0:T(8,128)(2,1)S(1)}, bf16[512,256]{1,0:T(8,128)(2,1)S(1)}, u32[]{:S(2)}, u32[]{:S(2)}) collective-permute-start(bf16[512,256]{1,0:T(8,128)(2,1)S(1)} %pad_maximum_fusion.11), channel_id=1, source_target_pairs={{0,4},{4,0},{1,5},{5,1},{2,6},{6,2},{3,7},{7,3},{8,12},{12,8},{9,1... | collective-permute-start | bytes 786440 | tf_op jit(solution)/shard_map/ppermute | solution.py:86
  228.3 10.6 %collective-permute-start.19 = (bf16[64,1536]{1,0:T(8,128)(2,1)S(1)}, bf16[64,1536]{1,0:T(8,128)(2,1)}, u32[]{:S(2)}, u32[]{:S(2)}) collective-permute-start(bf16[64,1536]{1,0:T(8,128)(2,1)S(1)} %get-tuple-element.300), channel_id=1, source_target_pairs={{0,3},{1,0},{2,1},{3,2},{4,7},{5,4},{6,5},{7,6},{8,11},{9,8},{10,9... | collective-permute-start | bytes 589832 | tf_op jit(solution)/shard_map/ppermute | solution.py:91
  230.5 12.1 %collective-permute-start.21 = (bf16[64,1536]{1,0:T(8,128)(2,1)S(1)}, bf16[64,1536]{1,0:T(8,128)(2,1)}, u32[]{:S(2)}, u32[]{:S(2)}) collective-permute-start(bf16[64,1536]{1,0:T(8,128)(2,1)S(1)} %get-tuple-element.301), channel_id=1, source_target_pairs={{0,1},{1,2},{2,3},{3,0},{4,5},{5,6},{6,7},{7,4},{8,9},{9,10},{10,1... | collective-permute-start | bytes 589832 | tf_op jit(solution)/shard_map/ppermute | solution.py:91
  272.6 19.8 %collective-permute-start.31 = (bf16[256,5760]{1,0:T(8,128)(2,1)S(1)}, bf16[256,5760]{1,0:T(8,128)(2,1)S(1)}, u32[]{:S(2)}, u32[]{:S(2)}) collective-permute-start(bf16[256,5760]{1,0:T(8,128)(2,1)S(1)} %get-tuple-element.89.refs_0_.refs_2_), channel_id=1, source_target_pairs={{0,4},{4,0},{1,5},{5,1},{2,6},{6,2},{3,7},{7,3},{8,12},{12,8},{9,1... | collective-permute-start | bytes 8847368 | tf_op jit(solution)/shard_map/ppermute | solution.py:86
  276.6 12.0 %collective-permute-start.27 = (bf16[64,1536]{1,0:T(8,128)(2,1)S(1)}, bf16[64,1536]{1,0:T(8,128)(2,1)S(1)}, u32[]{:S(2)}, u32[]{:S(2)}) collective-permute-start(bf16[64,1536]{1,0:T(8,128)(2,1)S(1)} %get-tuple-element.88), channel_id=1, source_target_pairs={{0,1},{1,2},{2,3},{3,0},{4,5},{5,6},{6,7},{7,4},{8,9},{9,10},{10,1... | collective-permute-start | bytes 589832 | tf_op jit(solution)/shard_map/ppermute | solution.py:91
  289.6 14.9 %collective-permute-start.28 = (bf16[64,1536]{1,0:T(8,128)(2,1)S(1)}, bf16[64,1536]{1,0:T(8,128)(2,1)S(1)}, u32[]{:S(2)}, u32[]{:S(2)}) collective-permute-start(bf16[64,1536]{1,0:T(8,128)(2,1)S(1)} %fusion.172), channel_id=1, source_target_pairs={{0,1},{1,2},{2,3},{3,0},{4,5},{5,6},{6,7},{7,4},{8,9},{9,10},{10,1... | collective-permute-start | bytes 589832 | tf_op jit(solution)/shard_map/ppermute | solution.py:91
  289.7 14.9 %collective-permute-start.29 = (bf16[64,1536]{1,0:T(8,128)(2,1)S(1)}, bf16[64,1536]{1,0:T(8,128)(2,1)}, u32[]{:S(2)}, u32[]{:S(2)}) collective-permute-start(bf16[64,1536]{1,0:T(8,128)(2,1)S(1)} %fusion.172), channel_id=1, source_target_pairs={{0,2},{1,3},{2,0},{3,1},{4,6},{5,7},{6,4},{7,5},{8,10},{9,11},{10,... | collective-permute-start | bytes 589832 | tf_op jit(solution)/shard_map/ppermute | solution.py:91
  291.0 13.5 %collective-permute-start.30 = (bf16[64,1536]{1,0:T(8,128)(2,1)S(1)}, bf16[64,1536]{1,0:T(8,128)(2,1)}, u32[]{:S(2)}, u32[]{:S(2)}) collective-permute-start(bf16[64,1536]{1,0:T(8,128)(2,1)S(1)} %fusion.172), channel_id=1, source_target_pairs={{0,3},{1,0},{2,1},{3,2},{4,7},{5,4},{6,5},{7,6},{8,11},{9,8},{10,9... | collective-permute-start | bytes 589832 | tf_op jit(solution)/shard_map/ppermute | solution.py:91
  305.2 241.0 %reduce-scatter.3.cloned.1.call-start = ((), (), s32[]{:S(2)}) async-start(), calls=%async_computation.8 | async-start | bytes 10444800 | tf_op jit(solution)/shard_map/reduce_scatter | solution.py:435
  324.1 90.8 %collective-permute-start.52 = (bf16[256,1536]{1,0:T(8,128)(2,1)S(1)}, bf16[256,1536]{1,0:T(8,128)(2,1)}, u32[]{:S(2)}, u32[]{:S(2)}) collective-permute-start(bf16[256,1536]{1,0:T(8,128)(2,1)S(1)} %pad_maximum_fusion.2.refs_0_), channel_id=1, source_target_pairs={{0,4},{4,0},{1,5},{5,1},{2,6},{6,2},{3,7},{7,3},{8,12},{12,8},{9,1... | collective-permute-start | bytes 2359304 | tf_op jit(solution)/shard_map/ppermute | solution.py:86
  326.0 40.1 %collective-permute-start.41 = (bf16[256,1536]{1,0:T(8,128)(2,1)}, bf16[256,1536]{1,0:T(8,128)(2,1)}, u32[]{:S(2)}, u32[]{:S(2)}) collective-permute-start(bf16[256,1536]{1,0:T(8,128)(2,1)} %copy-done.49), channel_id=1, source_target_pairs={{0,4},{4,0},{1,5},{5,1},{2,6},{6,2},{3,7},{7,3},{8,12},{12,8},{9,1... | collective-permute-start | bytes 2359304 | tf_op jit(solution)/shard_map/ppermute | solution.py:86
  357.8 10.8 %collective-permute-start.42 = (bf16[256,512]{1,0:T(8,128)(2,1)S(1)}, bf16[256,512]{1,0:T(8,128)(2,1)S(1)}, u32[]{:S(2)}, u32[]{:S(2)}) collective-permute-start(bf16[256,512]{1,0:T(8,128)(2,1)S(1)} %get-tuple-element.308), channel_id=1, source_target_pairs={{0,4},{4,0},{1,5},{5,1},{2,6},{6,2},{3,7},{7,3},{8,12},{12,8},{9,1... | collective-permute-start | bytes 786440 | tf_op jit(solution)/shard_map/ppermute | solution.py:86
  364.5 10.6 %collective-permute-start.38 = (bf16[64,1536]{1,0:T(8,128)(2,1)S(1)}, bf16[64,1536]{1,0:T(8,128)(2,1)S(1)}, u32[]{:S(2)}, u32[]{:S(2)}) collective-permute-start(bf16[64,1536]{1,0:T(8,128)(2,1)S(1)} %get-tuple-element.97.refs_4_), channel_id=1, source_target_pairs={{0,2},{1,3},{2,0},{3,1},{4,6},{5,7},{6,4},{7,5},{8,10},{9,11},{10,... | collective-permute-start | bytes 589832 | tf_op jit(solution)/shard_map/ppermute | solution.py:91
  368.6 30.8 %collective-permute-start.43 = (bf16[64,1536]{1,0:T(8,128)(2,1)}, bf16[64,1536]{1,0:T(8,128)(2,1)}, u32[]{:S(2)}, u32[]{:S(2)}) collective-permute-start(bf16[64,1536]{1,0:T(8,128)(2,1)} %get-tuple-element.105), channel_id=1, source_target_pairs={{0,3},{1,0},{2,1},{3,2},{4,7},{5,4},{6,5},{7,6},{8,11},{9,8},{10,9... | collective-permute-start | bytes 589832 | tf_op jit(solution)/shard_map/ppermute | solution.py:91
  372.0 27.3 %collective-permute-start.44 = (bf16[64,1536]{1,0:T(8,128)(2,1)}, bf16[64,1536]{1,0:T(8,128)(2,1)S(1)}, u32[]{:S(2)}, u32[]{:S(2)}) collective-permute-start(bf16[64,1536]{1,0:T(8,128)(2,1)} %get-tuple-element.106), channel_id=1, source_target_pairs={{0,2},{1,3},{2,0},{3,1},{4,6},{5,7},{6,4},{7,5},{8,10},{9,11},{10,... | collective-permute-start | bytes 589832 | tf_op jit(solution)/shard_map/ppermute | solution.py:91
  375.1 24.2 %collective-permute-start.45 = (bf16[64,1536]{1,0:T(8,128)(2,1)S(1)}, bf16[64,1536]{1,0:T(8,128)(2,1)S(1)}, u32[]{:S(2)}, u32[]{:S(2)}) collective-permute-start(bf16[64,1536]{1,0:T(8,128)(2,1)S(1)} %copy-done.22), channel_id=1, source_target_pairs={{0,1},{1,2},{2,3},{3,0},{4,5},{5,6},{6,7},{7,4},{8,9},{9,10},{10,1... | collective-permute-start | bytes 589832 | tf_op jit(solution)/shard_map/ppermute | solution.py:91
  396.1 20.8 %collective-permute-start.54 = (bf16[256,2688]{1,0:T(8,128)(2,1)S(1)}, bf16[256,2688]{1,0:T(8,128)(2,1)S(1)}, u32[]{:S(2)}, u32[]{:S(2)}) collective-permute-start(bf16[256,2688]{1,0:T(8,128)(2,1)S(1)} %get-tuple-element.113), channel_id=1, source_target_pairs={{0,4},{4,0},{1,5},{5,1},{2,6},{6,2},{3,7},{7,3},{8,12},{12,8},{9,1... | collective-permute-start | bytes 4128776 | tf_op jit(solution)/shard_map/ppermute | solution.py:86
  402.1 10.8 %collective-permute-start.48 = (bf16[64,1536]{1,0:T(8,128)(2,1)S(1)}, bf16[64,1536]{1,0:T(8,128)(2,1)S(1)}, u32[]{:S(2)}, u32[]{:S(2)}) collective-permute-start(bf16[64,1536]{1,0:T(8,128)(2,1)S(1)} %get-tuple-element.111), channel_id=1, source_target_pairs={{0,1},{1,2},{2,3},{3,0},{4,5},{5,6},{6,7},{7,4},{8,9},{9,10},{10,1... | collective-permute-start | bytes 589832 | tf_op jit(solution)/shard_map/ppermute | solution.py:91
  405.9 11.0 %collective-permute-start.53 = (bf16[256,1536]{1,0:T(8,128)(2,1)S(1)}, bf16[256,1536]{1,0:T(8,128)(2,1)S(1)}, u32[]{:S(2)}, u32[]{:S(2)}) collective-permute-start(bf16[256,1536]{1,0:T(8,128)(2,1)S(1)} %constant_dynamic-update-slice_fusion.6.refs_2_), channel_id=1, source_target_pairs={{0,4},{4,0},{1,5},{5,1},{2,6},{6,2},{3,7},{7,3},{8,12},{12,8},{9,1... | collective-permute-start | bytes 2359304 | tf_op jit(solution)/shard_map/ppermute | solution.py:86
  414.1 16.5 %collective-permute-start.49 = (bf16[64,1536]{1,0:T(8,128)(2,1)}, bf16[64,1536]{1,0:T(8,128)(2,1)S(1)}, u32[]{:S(2)}, u32[]{:S(2)}) collective-permute-start(bf16[64,1536]{1,0:T(8,128)(2,1)} %get-tuple-element.116), channel_id=1, source_target_pairs={{0,1},{1,2},{2,3},{3,0},{4,5},{5,6},{6,7},{7,4},{8,9},{9,10},{10,1... | collective-permute-start | bytes 589832 | tf_op jit(solution)/shard_map/ppermute | solution.py:91
  414.1 16.6 %collective-permute-start.50 = (bf16[64,1536]{1,0:T(8,128)(2,1)}, bf16[64,1536]{1,0:T(8,128)(2,1)S(1)}, u32[]{:S(2)}, u32[]{:S(2)}) collective-permute-start(bf16[64,1536]{1,0:T(8,128)(2,1)} %get-tuple-element.116), channel_id=1, source_target_pairs={{0,2},{1,3},{2,0},{3,1},{4,6},{5,7},{6,4},{7,5},{8,10},{9,11},{10,... | collective-permute-start | bytes 589832 | tf_op jit(solution)/shard_map/ppermute | solution.py:91
  414.9 15.7 %collective-permute-start.51 = (bf16[64,1536]{1,0:T(8,128)(2,1)}, bf16[64,1536]{1,0:T(8,128)(2,1)}, u32[]{:S(2)}, u32[]{:S(2)}) collective-permute-start(bf16[64,1536]{1,0:T(8,128)(2,1)} %get-tuple-element.116), channel_id=1, source_target_pairs={{0,3},{1,0},{2,1},{3,2},{4,7},{5,4},{6,5},{7,6},{8,11},{9,8},{10,9... | collective-permute-start | bytes 589832 | tf_op jit(solution)/shard_map/ppermute | solution.py:91
  435.4 52.5 %collective-permute-start.59 = (bf16[256,1536]{1,0:T(8,128)(2,1)S(1)}, bf16[256,1536]{1,0:T(8,128)(2,1)S(1)}, u32[]{:S(2)}, u32[]{:S(2)}) collective-permute-start(bf16[256,1536]{1,0:T(8,128)(2,1)S(1)} %multiply_convert_fusion.refs_0_), channel_id=1, source_target_pairs={{0,4},{4,0},{1,5},{5,1},{2,6},{6,2},{3,7},{7,3},{8,12},{12,8},{9,1... | collective-permute-start | bytes 2359304 | tf_op jit(solution)/shard_map/ppermute | solution.py:86
  442.8 45.1 %collective-permute-start.60 = (bf16[256,1536]{1,0:T(8,128)(2,1)}, bf16[256,1536]{1,0:T(8,128)(2,1)}, u32[]{:S(2)}, u32[]{:S(2)}) collective-permute-start(bf16[256,1536]{1,0:T(8,128)(2,1)} %get-tuple-element.375), channel_id=1, source_target_pairs={{0,4},{4,0},{1,5},{5,1},{2,6},{6,2},{3,7},{7,3},{8,12},{12,8},{9,1... | collective-permute-start | bytes 2359304 | tf_op jit(solution)/shard_map/ppermute | solution.py:86
  461.3 10.2 %collective-permute-start.58 = (bf16[64,1536]{1,0:T(8,128)(2,1)S(1)}, bf16[64,1536]{1,0:T(8,128)(2,1)S(1)}, u32[]{:S(2)}, u32[]{:S(2)}) collective-permute-start(bf16[64,1536]{1,0:T(8,128)(2,1)S(1)} %get-tuple-element.293), channel_id=1, source_target_pairs={{0,1},{1,2},{2,3},{3,0},{4,5},{5,6},{6,7},{7,4},{8,9},{9,10},{10,1... | collective-permute-start | bytes 589832 | tf_op jit(solution)/shard_map/ppermute | solution.py:91
  467.0 22.1 %collective-permute-start.61 = (bf16[256,768]{1,0:T(8,128)(2,1)}, bf16[256,768]{1,0:T(8,128)(2,1)S(1)}, u32[]{:S(2)}, u32[]{:S(2)}) collective-permute-start(bf16[256,768]{1,0:T(8,128)(2,1)} %get-tuple-element.290), channel_id=1, source_target_pairs={{0,4},{4,0},{1,5},{5,1},{2,6},{6,2},{3,7},{7,3},{8,12},{12,8},{9,1... | collective-permute-start | bytes 1179656 | tf_op jit(solution)/shard_map/ppermute | solution.py:86
  479.7 22.6 %all-to-all-start.2 = ((bf16[32,8,1536]{2,1,0:T(8,128)(2,1)}), bf16[32,8,1536]{2,1,0:T(8,128)(2,1)}, u32[]{:S(2)}, u32[]{:S(2)}) async-start(bf16[32,8,1536]{2,1,0:T(8,128)(2,1)} %fusion.10), calls=%async_computation.3 | async-start | bytes 1572864 | tf_op jit(solution)/shard_map/all_to_all | solution.py:872
  504.5 22.0 %collective-permute-start.63 = (bf16[136,1536]{1,0:T(8,128)(2,1)}, bf16[136,1536]{1,0:T(8,128)(2,1)S(1)}, u32[]{:S(2)}, u32[]{:S(2)}) collective-permute-start(bf16[136,1536]{1,0:T(8,128)(2,1)} %fusion.26), channel_id=1, source_target_pairs={{0,1},{1,2},{2,3},{3,0},{4,5},{5,6},{6,7},{7,4},{8,9},{9,10},{10,1... | collective-permute-start | bytes 1253384 | tf_op jit(solution)/shard_map/ppermute | solution.py:91
  504.5 22.0 %collective-permute-start.64 = (bf16[136,1536]{1,0:T(8,128)(2,1)}, bf16[136,1536]{1,0:T(8,128)(2,1)}, u32[]{:S(2)}, u32[]{:S(2)}) collective-permute-start(bf16[136,1536]{1,0:T(8,128)(2,1)} %fusion.26), channel_id=1, source_target_pairs={{0,2},{1,3},{2,0},{3,1},{4,6},{5,7},{6,4},{7,5},{8,10},{9,11},{10,... | collective-permute-start | bytes 1253384 | tf_op jit(solution)/shard_map/ppermute | solution.py:91
  506.0 21.0 %collective-permute-start.65 = (bf16[136,1536]{1,0:T(8,128)(2,1)}, bf16[136,1536]{1,0:T(8,128)(2,1)}, u32[]{:S(2)}, u32[]{:S(2)}) collective-permute-start(bf16[136,1536]{1,0:T(8,128)(2,1)} %fusion.26), channel_id=1, source_target_pairs={{0,3},{1,0},{2,1},{3,2},{4,7},{5,4},{6,5},{7,6},{8,11},{9,8},{10,9... | collective-permute-start | bytes 1253384 | tf_op jit(solution)/shard_map/ppermute | solution.py:91
  507.7 47.6 %all-to-all-start.3 = ((bf16[32,48,768]{2,1,0:T(8,128)(2,1)}), bf16[32,48,768]{2,1,0:T(8,128)(2,1)S(1)}, u32[]{:S(2)}, u32[]{:S(2)}) async-start(bf16[32,48,768]{2,1,0:T(8,128)(2,1)} %bitcast.63), calls=%async_computation.5 | async-start | bytes 4718592 | tf_op jit(solution)/shard_map/all_to_all | solution.py:897
  (193 other events, 2407.6 us)
Sparse Core Ops, SparseCore 0:
  38.2 102.0 all-gather.2
  143.1 72.6 all-gather.4
  304.7 84.9 reduce-scatter.4
  430.8 115.3 reduce-scatter.2
